TPU v7x, 32 devices: a whole 2x2x4 slice. The times are simulated.
32 devices in a mesh: dp: 4 (over y, x), rep: 8 (over z, core).
Axes of the slice: x: 2, y: 2, z: 4, core: 2. Of those that a mesh axis runs over, the one named last changes fastest.
Arguments:
- video: float32 [112, 65536], P(None, ('dp', 'rep')), may hold values from -6 to 6
- frame_counts: int32 [64], P(('dp', 'rep')), may hold values from 1 to 7, as said below
- momentum_index: int32 [1], replicated, may hold values from 1 to 9
- expand_weight: float32 [2, 640, 112], replicated, may hold values from -0.5 to 0.5
- wide_gains: float32 [4, 640], replicated, may hold values from 0.25 to 1.75
- wide_biases: float32 [4, 640], replicated, may hold values from -3 to 3
- narrow_gains: float32 [2, 112], replicated, may hold values from 0.25 to 1.75
- narrow_biases: float32 [2, 112], replicated, may hold values from -3 to 3
- depth_weight: float32 [2, 45, 640], replicated, may hold values from -0.875 to 0.875
- squeeze_weight: float32 [2, 160, 640], replicated, may hold values from -0.25 to 0.25
- squeeze_bias: float32 [2, 160], replicated, may hold values from -3 to 3
- excite_weight: float32 [2, 640, 160], replicated, may hold values from -0.5 to 0.5
- excite_bias: float32 [2, 640], replicated, may hold values from -3 to 3
- project_weight: float32 [2, 112, 640], replicated, may hold values from -0.25 to 0.25
- wide_means: float32 [4, 640], replicated, may hold values from -3 to 3
- wide_variances: float32 [4, 640], replicated, may hold values from 0.5 to 2
- narrow_means: float32 [2, 112], replicated, may hold values from -3 to 3
- narrow_variances: float32 [2, 112], replicated, may hold values from 0.5 to 2
- cotangent: float32 [112, 16384], P(None, ('dp', 'rep')), may hold values from -6 to 6
Outputs:
- activations: float32 [112, 16384], P(None, ('dp', 'rep'))
- video_grad: float32 [112, 65536], P(None, ('dp', 'rep'))
- expand_weight_grad: float32 [2, 640, 112], replicated
- wide_gains_grad: float32 [4, 640], replicated
- wide_biases_grad: float32 [4, 640], replicated
- narrow_gains_grad: float32 [2, 112], replicated
- narrow_biases_grad: float32 [2, 112], replicated
- depth_weight_grad: float32 [2, 45, 640], replicated
- squeeze_weight_grad: float32 [2, 160, 640], replicated
- squeeze_bias_grad: float32 [2, 160], replicated
- excite_weight_grad: float32 [2, 640, 160], replicated
- excite_bias_grad: float32 [2, 640], replicated
- project_weight_grad: float32 [2, 112, 640], replicated
- new_wide_means: float32 [4, 640], replicated
- new_wide_variances: float32 [4, 640], replicated
- new_narrow_means: float32 [2, 112], replicated
- new_narrow_variances: float32 [2, 112], replicated
Inputs may be any that keep to these rules, and one draw needn't show every extreme that they name: `frame_counts`: each device's 2 entries give its clips' frame counts in order; they sum to at most 8, the slots after them are padding, and some device's entries sum to exactly 8.
All inputs are finite; a program needn't handle non-finite values.
Results may differ from a plain program's by a relative error of at most 0.0003.
Values sent between devices are 32-bit elements; how exact they have to be, the bound alone decides.
No kernel may reach another device: no remote copies, remote signals or barrier semaphores. Data moves between devices by JAX's collectives and lax.ppermute only.
A program may use at most 576 MiB of HBM per device.

v0:
```python
import functools

import jax
import jax.numpy as jnp
from jax import lax
from jax.experimental import pallas as pl
from jax.experimental.pallas import tpu as pltpu
from jax.sharding import PartitionSpec as P

SIDE = 16
LANES = 128
LAGS = 5
FULL_ROWS = 2 * SIDE
HALF_ROWS = SIDE // 2
EPSILON = 1e-05
HIGHEST = lax.Precision.HIGHEST
F32 = jnp.float32
NN = (((1,), (0,)), ((), ()))
NT = (((1,), (1,)), ((), ()))
TN = (((0,), (0,)), ((), ()))
VMEM_BYTES = 52 * 1024 * 1024


def half_tanh(half_values):
    return jnp.tanh(half_values)


def sigmoid(values):
    return 0.5 * jnp.tanh(0.5 * values) + 0.5


def silu_slope(half_values, tanh):
    return 0.5 * (1.0 + tanh + half_values * (1.0 - tanh * tanh))


def exact_dot(left, right, dims=NN):
    return lax.dot_general(left, right, dims, precision=HIGHEST, preferred_element_type=F32)


def halves(values):
    high = values.astype(jnp.bfloat16)
    return (high, (values - high.astype(F32)).astype(jnp.bfloat16))


def side_by_side(values):
    return jnp.concatenate(halves(values), axis=1)


def right_square(w):
    both = side_by_side(w)
    return jnp.concatenate([both, both], axis=0)


def right_square_t(w):
    high, low = halves(w)
    return jnp.concatenate(
        [jnp.concatenate([high, high], axis=1), jnp.concatenate([low, low], axis=1)], axis=0
    )


def plain_dot(left, right, dims=NN):
    return lax.dot_general(left, right, dims, preferred_element_type=F32)


def fold_right(values):
    lanes = values.shape[1] // 2
    return values[:, :lanes] + values[:, lanes:]


def fold_square(values):
    rows = values.shape[0] // 2
    return fold_right(values[:rows] + values[rows:])


def stacked(values):
    high = values.astype(jnp.bfloat16).astype(F32)
    return jnp.concatenate([high, values - high], axis=0).astype(jnp.bfloat16)


def skinny_dot(left, right, dims=NN):
    rows = left.shape[0]
    both = stacked(left)
    high, low = halves(right)
    values = plain_dot(both, high, dims) + plain_dot(both, low, dims)
    return values[:rows] + values[rows:]


def frame_outer(left, right):
    a_high = left.astype(jnp.bfloat16).astype(F32)
    b_high = right.astype(jnp.bfloat16).astype(F32)
    a_low = left - a_high
    b_low = right - b_high
    a = jnp.concatenate([a_high, a_high, a_low, a_low], axis=0).astype(jnp.bfloat16)
    b = jnp.concatenate([b_high, b_low, b_high, b_low], axis=0).astype(jnp.bfloat16)
    return plain_dot(a, b, TN)


def pad_rows(values):
    return jnp.concatenate([values, jnp.zeros((LANES - values.shape[0], values.shape[1]), values.dtype)], axis=0)


def column_order():
    q = lax.broadcasted_iota(jnp.int32, (LANES, LANES), 0)
    n = lax.broadcasted_iota(jnp.int32, (LANES, LANES), 1)
    source = (q // 16) * 16 + (q % 8) * 2 + (q // 8) % 2
    return (source == n).astype(jnp.bfloat16)


def live_frames(counts_ref):
    total = counts_ref[0]
    for clip in range(1, counts_ref.shape[0]):
        total = total + counts_ref[clip]
    return total


def place_of(counts_ref, frame):
    begin = jnp.int32(0)
    end = jnp.int32(0)
    for clip in range(counts_ref.shape[0]):
        end = end + counts_ref[clip]
        begin = jnp.where(frame >= end, end, begin)
    return frame - begin


def running_matrix(counts_ref, frames):
    after = lax.broadcasted_iota(jnp.int32, (frames, frames), 0)
    before = lax.broadcasted_iota(jnp.int32, (frames, frames), 1)
    begin = jnp.int32(0)
    matrix = jnp.zeros((frames, frames), F32)
    for clip in range(counts_ref.shape[0]):
        end = begin + counts_ref[clip]
        inside = (before >= begin) & (before <= after) & (after < end)
        matrix = matrix + jnp.where(inside, 1.0 / (after - begin + 1).astype(F32), 0.0)
        begin = end
    return matrix


def columns_up(values):
    spot = lax.broadcasted_iota(jnp.int32, values.shape, 1)
    return jnp.where(spot == 7, 0.0, pltpu.roll(values, 7, axis=1))


def columns_down(values):
    spot = lax.broadcasted_iota(jnp.int32, values.shape, 1)
    return jnp.where(spot == 0, 0.0, pltpu.roll(values, 1, axis=1))


def tile_sum(values):
    return jnp.sum(jnp.sum(values, axis=0), axis=0, keepdims=True)


def rows8(*rows):
    lanes = rows[0].shape[1]
    spot = lax.broadcasted_iota(jnp.int32, (8, lanes), 0)
    block = jnp.zeros((8, lanes), F32)
    for index, row in enumerate(rows):
        block = jnp.where(spot == index, row, block)
    return block


def pick_row(block, index):
    spot = lax.broadcasted_iota(jnp.int32, block.shape, 0)
    return jnp.sum(jnp.where(spot == index, block, 0.0), axis=0, keepdims=True)


def outer(left, right):
    return exact_dot(rows8(left), rows8(right), TN)


def row_dot(row, matrix, dims=NN):
    return exact_dot(rows8(row), matrix, dims)[0:1]


def clear_edges(ref):
    planes = ref.shape[1]
    edge = jnp.zeros((8, LANES), F32)
    for t in range(ref.shape[0]):
        for plane in range(planes):
            ref[t, plane, 0] = edge
            ref[t, plane, ref.shape[2] - 1] = edge


def spread_taps(taps_ref, w_ref):
    for tap in range(w_ref.shape[0]):
        w_ref[tap] = jnp.broadcast_to(taps_ref[0, tap : tap + 1, :], (8, LANES))


def conv_full(t, k, a_ref, w_ref, d_ref, fresh):
    weights = [w_ref[k * 9 + tap] for tap in range(9)]
    source = t - k
    rows = {}
    for i in range(SIDE):
        for need in (i, i + 1, i + 2):
            if need not in rows:
                rows[need] = [a_ref[source, plane, need] for plane in range(4)]
        even = None
        odd = None
        for r in range(3):
            a_even, a_odd, a_odd_down, a_even_up = rows[i + r]
            left, centre, right = weights[3 * r : 3 * r + 3]
            part_even = centre * a_even + right * a_odd + left * a_odd_down
            part_odd = centre * a_odd + left * a_even + right * a_even_up
            even = part_even if even is None else even + part_even
            odd = part_odd if odd is None else odd + part_odd
        rows.pop(i)
        at = t * FULL_ROWS + 2 * i
        if fresh:
            d_ref[at] = even
            d_ref[at + 1] = odd
        else:
            d_ref[at] = d_ref[at] + even
            d_ref[at + 1] = d_ref[at + 1] + odd


def conv_half(t, k, a_ref, w_ref, d_ref, fresh):
    weights = [w_ref[k * 9 + tap] for tap in range(9)]
    source = t - k
    carried = [a_ref[source, plane, 0] for plane in range(3)]
    for i in range(HALF_ROWS):
        rows = [carried]
        for need in (2 * i + 1, 2 * i + 2):
            rows.append([a_ref[source, plane, need] for plane in range(3)])
        carried = rows[2]
        total = None
        for r in range(3):
            a_even, a_odd, a_odd_down = rows[r]
            left, centre, right = weights[3 * r : 3 * r + 3]
            part = centre * a_even + right * a_odd + left * a_odd_down
            total = part if total is None else total + part
        at = t * HALF_ROWS + i
        d_ref[at] = total if fresh else d_ref[at] + total


def row_total(ref, lanes=None):
    values = ref[...] if lanes is None else ref[:, :, lanes]
    return jnp.sum(values, axis=0)


def send_all(send_ref, rows, lanes):
    count = rows.shape[0]

    def one(device, carry):
        send_ref[pl.ds(device, 1), 0:count, lanes] = rows[None]
        return carry

    lax.fori_loop(0, send_ref.shape[0], one, 0)


def stack_rows(*rows):
    return rows8(*rows)[0 : len(rows)]


def pick_thirds(order, values, dims, order_left):
    pieces = []
    rest = values
    for _ in range(3):
        piece = rest.astype(jnp.bfloat16)
        rest = rest - piece.astype(F32)
        args = (order, piece) if order_left else (piece, order)
        pieces.append(plain_dot(*args, dims))
    return pieces


def prepare_kernel(
    counts_ref, video_ref, cot_ref, w_ref, x_ref, rows_ref, columns_ref, cot_out_ref, gram_ref, send_ref
):
    order = column_order()
    total = live_frames(counts_ref)
    pixels = video_ref.shape[1]
    gram = jnp.zeros((2 * LANES, 2 * LANES), F32)
    summed = jnp.zeros((1, LANES), F32)
    for frame in range(pixels // 256):
        live = jnp.where(frame < total, 1.0, 0.0).astype(F32)
        for part in (2 * frame, 2 * frame + 1):
            at = slice(part * LANES, (part + 1) * LANES)
            block = pad_rows(video_ref[:, at] * live)
            high, middle, low = pick_thirds(order, block, NT, True)
            rows = high + middle + low
            x_ref[at, :] = rows
            rows_ref[at, :] = jnp.concatenate([high, middle], axis=1).astype(jnp.bfloat16)
            first, second, _ = pick_thirds(order, block, NT, False)
            columns_ref[:, at] = jnp.concatenate([first, second], axis=0).astype(jnp.bfloat16)
            summed = summed + jnp.sum(rows, axis=0, keepdims=True)
        at = slice(frame * 256, (frame + 1) * 256)
        gram = gram + plain_dot(columns_ref[:, at], rows_ref[at, :])
    gram = fold_square(gram)
    gram_ref[0:LANES, :] = gram
    gram_ref[LANES : LANES + 8, :] = rows8(summed)
    w = pad_rows(w_ref[0])
    width = w.shape[1]
    sums = stack_rows(row_dot(summed, w), jnp.sum(w * exact_dot(gram, w), axis=0, keepdims=True))
    count = jnp.full((2, LANES), 1.0, F32) * (total * (SIDE * SIDE)).astype(F32)
    send_all(send_ref, sums, slice(0, width))
    send_all(send_ref, count, slice(width, width + LANES))
    spot = lax.broadcasted_iota(jnp.int32, (LANES, LANES), 1)
    for part in range(cot_ref.shape[1] // LANES):
        at = slice(part * LANES, (part + 1) * LANES)
        frame = (spot + part * LANES) // (HALF_ROWS * 8)
        cot_out_ref[at, :] = jnp.where(frame < total, pad_rows(cot_ref[:, at]), 0.0).T


def moments_of(sums, count):
    average = sums[0:1] / count
    return (average, sums[1:2] / count - average * average)


def narrow_kernel(
    counts_ref, sums_ref, stat_ref, gram0_ref, x_ref, z_ref, ngain_ref, nbias_ref, w_ref,
    x1_ref, rows_ref, columns_ref, gram_ref, stat_out_ref, send_ref,
):
    total = live_frames(counts_ref)
    count = stat_ref[2:3, 0:LANES]
    average, variance = moments_of(row_total(sums_ref), count)
    factor = ngain_ref[0:1, :] * lax.rsqrt(variance + EPSILON)
    shift = nbias_ref[0:1, :] - factor * average
    stat_out_ref[...] = rows8(average, variance, count)
    frames = x_ref.shape[0] // 256

    def frame(t, carry):
        gram, cross, summed = carry
        at = pl.ds(pl.multiple_of(t * 256, 256), 256)
        z = z_ref[at, :]
        rows = (x_ref[at, :] + factor * z + shift) * live_value(t, total)
        x1_ref[at, :] = rows
        both = side_by_side(rows)
        rows_ref[at, :] = both
        columns = jnp.concatenate(halves(rows.T), axis=0)
        columns_ref[:, at] = columns
        gram = gram + plain_dot(columns, both)
        cross = cross + plain_dot(columns, side_by_side(z))
        return (gram, cross, summed + jnp.sum(rows, axis=0, keepdims=True))

    zero = jnp.zeros((2 * LANES, 2 * LANES), F32)
    gram, cross, summed = each_frame(frames, frame, (zero, zero, jnp.zeros((1, LANES), F32)))

    gram = fold_square(gram)
    tiles = LANES // 8
    gram_ref[0:tiles] = gram.reshape(tiles, 8, LANES)
    gram_ref[tiles : 2 * tiles] = fold_square(cross).reshape(tiles, 8, LANES)
    gram_ref[2 * tiles : 3 * tiles] = gram0_ref[0:LANES, :].reshape(tiles, 8, LANES)
    gram_ref[3 * tiles] = rows8(summed, gram0_ref[LANES : LANES + 1, :])
    w = pad_rows(w_ref[0])
    sums = stack_rows(row_dot(summed, w), jnp.sum(w * exact_dot(gram, w), axis=0, keepdims=True))
    send_all(send_ref, sums, slice(0, w.shape[1]))


def write_first(t, total, values, scale, shift, a_ref, planes):
    half_pre = values * scale + shift
    first = (half_pre + half_pre * half_tanh(half_pre)) * live_value(t, total)
    first = first.reshape(SIDE, 2, 8, LANES)
    even = first[:, 0]
    odd = first[:, 1]
    a_ref[t, 0, 1 : SIDE + 1] = even
    a_ref[t, 1, 1 : SIDE + 1] = odd
    if planes >= 3:
        a_ref[t, 2, 1 : SIDE + 1] = columns_down(odd)
    if planes >= 4:
        a_ref[t, 3, 1 : SIDE + 1] = columns_up(even)


def expand_kernel(
    block, counts_ref, sums_ref, count_ref, rows_ref, w_ref, gain_ref, bias_ref, taps_ref,
    e_ref, d_ref, stat_ref, send_ref, a_ref, taps8_ref,
):
    @pl.when(pl.program_id(0) == 0)
    def start():
        clear_edges(a_ref)

    total = live_frames(counts_ref)
    frames = a_ref.shape[0]
    count = count_ref[2:3, :] if block else row_total(count_ref)[0:1]
    average, variance = moments_of(row_total(sums_ref), count)
    stat_ref[...] = rows8(average, variance, count)
    norm_row = 2 * block
    scale = gain_ref[norm_row : norm_row + 1, :] * lax.rsqrt(variance + EPSILON)
    shift = 0.5 * (bias_ref[norm_row : norm_row + 1, :] - average * scale)
    scale = 0.5 * scale
    square = right_square(pad_rows(w_ref[0]))

    def expand(t, carry):
        at = pl.ds(pl.multiple_of(t * 256, 256), 256)
        values = fold_right(plain_dot(rows_ref[at, :], square)).reshape(FULL_ROWS, 8, LANES)
        e_ref[pl.ds(pl.multiple_of(t * FULL_ROWS, FULL_ROWS), FULL_ROWS)] = values
        write_first(t, total, values, scale, shift, a_ref, 3 if block else 4)
        return carry

    each_frame(frames, expand, 0)
    spread_taps(taps_ref, taps8_ref)
    per_frame = HALF_ROWS if block else FULL_ROWS
    conv = conv_half if block else conv_full

    def frame(t, carry):
        conv(t, 0, a_ref, taps8_ref, d_ref, True)
        last = jnp.minimum(place_of(counts_ref, t), LAGS - 1)

        def lag(k, inner):
            conv(t, k, a_ref, taps8_ref, d_ref, False)
            return inner

        lax.fori_loop(1, last + 1, lag, 0)
        values = d_ref[pl.ds(t * per_frame, per_frame)]
        return (carry[0] + jnp.sum(values, axis=0), carry[1] + jnp.sum(values * values, axis=0))

    zero = jnp.zeros((8, LANES), F32)
    summed, squares = lax.fori_loop(0, total, frame, (zero, zero))

    def dead(t, carry):
        d_ref[pl.ds(t * per_frame, per_frame)] = jnp.zeros((per_frame, 8, LANES), F32)
        return carry

    lax.fori_loop(total, frames, dead, 0)
    sums = stack_rows(jnp.sum(summed, axis=0, keepdims=True), jnp.sum(squares, axis=0, keepdims=True))
    send_all(send_ref, sums, slice(0, LANES))


def live_value(t, total):
    return jnp.where(t < total, 1.0, 0.0).astype(F32)


def each_frame(count, body, init, unroll=2):
    return lax.fori_loop(0, count, body, init, unroll=unroll)


def squeeze_forward_kernel(
    block, counts_ref, sums_ref, stat_ref, d_ref, gain_ref, bias_ref, down_ref, downb_ref, up_ref, upb_ref, proj_ref,
    cot_ref, z_ref, gates_ref, running_ref, pre_ref, stat_out_ref, send_ref, second_ref, pooled_ref,
):
    phase = pl.program_id(0)
    tile = pl.program_id(1)
    tiles = pl.num_programs(1)
    total = live_frames(counts_ref)
    per_frame = HALF_ROWS if block else FULL_ROWS
    pixels = per_frame * 8
    frames = second_ref.shape[1] // per_frame
    group = 256 // pixels
    chunks = frames // group
    norm_row = 2 * block + 1

    @pl.when(phase == 0)
    def activate():
        count = stat_ref[2:3, 0:LANES] * (0.25 if block else 1.0)
        average, variance = moments_of(row_total(sums_ref), count)
        stat_out_ref[...] = rows8(average, variance, count)
        scale = gain_ref[norm_row : norm_row + 1, :] * lax.rsqrt(variance + EPSILON)
        shift = 0.5 * (bias_ref[norm_row : norm_row + 1, :] - average * scale)
        scale = 0.5 * scale

        def chunk(index, carry):
            for inner in range(group):
                t = index * group + inner
                at = pl.ds(t * per_frame, per_frame)
                half_pre = d_ref[at] * scale + shift
                second = half_pre + half_pre * half_tanh(half_pre)
                second = second * live_value(t, total)
                second_ref[tile, at] = second
                pooled_ref[tile, pl.ds(t, 1), :] = tile_sum(second) * (1.0 / pixels)
            return carry

        each_frame(chunks, chunk, 0)

    @pl.when((phase == 1) & (tile == 0))
    def gate():
        matrix = running_matrix(counts_ref, frames)
        pooled = jnp.concatenate([pooled_ref[index] for index in range(pooled_ref.shape[0])], axis=1)
        running = exact_dot(matrix, pooled)
        running_ref[...] = running
        pre = skinny_dot(running, down_ref[0], NT) + downb_ref[block : block + 1, :]
        pre_ref[...] = pre
        gates_ref[...] = sigmoid(skinny_dot(pre * sigmoid(pre), up_ref[0]) + upb_ref[block : block + 1, :])
        z_ref[...] = jnp.zeros_like(z_ref)

    @pl.when(phase == 1)
    def project():
        square = right_square_t(pad_rows(proj_ref[0]))
        lanes = pl.ds(pl.multiple_of(tile * LANES, LANES), LANES)
        gates = gates_ref[:, lanes]

        def chunk(index, carry):
            parts = []
            for inner in range(group):
                t = index * group + inner
                second = second_ref[tile, pl.ds(t * per_frame, per_frame)].reshape(pixels, LANES)
                parts.append(second * pick_row(gates, t))
            excited = parts[0] if group == 1 else jnp.concatenate(parts, axis=0)
            at = pl.ds(pl.multiple_of(index * 256, 256), 256)
            z_ref[at, :] = z_ref[at, :] + fold_right(plain_dot(side_by_side(excited), square, NT))
            return carry

        each_frame(chunks, chunk, 0)

    @pl.when((phase == 1) & (tile == tiles - 1))
    def finish():
        def chunk(index, carry):
            at = pl.ds(pl.multiple_of(index * 256, 256), 256)
            z = z_ref[at, :].reshape(32, 8, LANES)
            values = [z, z * z]
            if block:
                dy = cot_ref[at, :].reshape(32, 8, LANES)
                values = values + [dy, dy * z]
            return tuple(old + jnp.sum(new, axis=0) for old, new in zip(carry, values))

        zero = jnp.zeros((8, LANES), F32)
        sums = each_frame(chunks, chunk, (zero,) * (4 if block else 2))
        rows = stack_rows(*(jnp.sum(value, axis=0, keepdims=True) for value in sums))
        send_all(send_ref, rows, slice(0, LANES))


def pack_tiles(narrow, squeeze):
    return narrow // 8 + 2 * (squeeze // 8) + 1


def squeeze_backward_body(
    block, counts_ref, stat_ref, d_ref, gain_ref, bias_ref, down_ref, up_ref, proj_ref, gates_ref, running_ref,
    pre_ref, dy2_ref, send_ref, pack_ref, dz3_ref, dz3t_ref, excited_ref, dexc_ref, dgate_ref, head,
):
    phase = pl.program_id(0)
    tile = pl.program_id(1)
    total = live_frames(counts_ref)
    per_frame = HALF_ROWS if block else FULL_ROWS
    pixels = per_frame * 8
    frames = dz3_ref.shape[0] // pixels
    group = 256 // pixels
    chunks = frames // group
    norm_row = 2 * block + 1
    tiles = dexc_ref.shape[0]
    narrow = proj_ref.shape[1]
    squeeze = down_ref.shape[1]
    per_tile = pack_tiles(narrow, squeeze)
    lanes = pl.ds(pl.multiple_of(tile * LANES, LANES), LANES)

    @pl.when((phase == 0) & (tile == 0))
    def start():
        head()

    average = stat_ref[0:1, :]
    root = lax.rsqrt(stat_ref[1:2, :] + EPSILON)
    scale = gain_ref[norm_row : norm_row + 1, :] * root
    shift = 0.5 * (bias_ref[norm_row : norm_row + 1, :] - average * scale)
    scale = 0.5 * scale
    gates = gates_ref[:, lanes]

    @pl.when(phase == 0)
    def excite():
        square = right_square(pad_rows(proj_ref[0]))

        def chunk(index, carry):
            flat = pl.ds(pl.multiple_of(index * 256, 256), 256)
            dexc = fold_right(plain_dot(dz3_ref[flat, :], square)).reshape(32, 8, LANES)
            dexc_ref[tile, pl.ds(pl.multiple_of(index * 32, 32), 32)] = dexc
            parts = []
            for inner in range(group):
                t = index * group + inner
                half_pre = d_ref[pl.ds(t * per_frame, per_frame)] * scale + shift
                second = half_pre + half_pre * half_tanh(half_pre)
                second = second * live_value(t, total)
                own = dexc[inner * per_frame : (inner + 1) * per_frame]
                dgate_ref[tile, pl.ds(t, 1), :] = tile_sum(own * second)
                parts.append(second.reshape(pixels, LANES) * pick_row(gates, t))
            excited = parts[0] if group == 1 else jnp.concatenate(parts, axis=0)
            excited_ref[flat, :] = side_by_side(excited)
            return carry

        each_frame(chunks, chunk, 0)
        dproj = fold_square(plain_dot(dz3t_ref[...], excited_ref[...]))
        pack_ref[pl.ds(tile * per_tile, narrow // 8)] = dproj[0:narrow].reshape(narrow // 8, 8, LANES)

    @pl.when((phase == 1) & (tile == 0))
    def squeeze_part():
        pre = pre_ref[...]
        half_pre = 0.5 * pre
        tanh = half_tanh(half_pre)
        squeezed = half_pre + half_pre * tanh
        all_gates = gates_ref[...]
        dgate = jnp.concatenate([dgate_ref[index] for index in range(tiles)], axis=1)
        du = dgate * all_gates * (1.0 - all_gates)
        dpre = skinny_dot(du, up_ref[0], NT) * silu_slope(half_pre, tanh)
        ddown = frame_outer(dpre, running_ref[...])
        dup = frame_outer(squeezed, du)
        dpre_row = jnp.sum(dpre, axis=0, keepdims=True)
        dpre_row = jnp.concatenate([dpre_row, jnp.zeros((1, du.shape[1] - squeeze), F32)], axis=1)
        biases = rows8(jnp.sum(du, axis=0, keepdims=True), dpre_row)
        for index in range(tiles):
            own = slice(index * LANES, (index + 1) * LANES)
            at = index * per_tile + narrow // 8
            pack_ref[at : at + squeeze // 8] = ddown[:, own].reshape(squeeze // 8, 8, LANES)
            at = at + squeeze // 8
            pack_ref[at : at + squeeze // 8] = dup[:, own].reshape(squeeze // 8, 8, LANES)
            pack_ref[at + squeeze // 8] = biases[:, own]
        drunning = skinny_dot(dpre, down_ref[0])
        dpooled = exact_dot(running_matrix(counts_ref, frames), drunning, TN) * (1.0 / pixels)
        for index in range(tiles):
            dgate_ref[index] = dpooled[:, index * LANES : (index + 1) * LANES]

    @pl.when(phase == 1)
    def slope():
        def chunk(index, carry):
            summed, cross = carry
            for inner in range(group):
                t = index * group + inner
                at = pl.ds(t * per_frame, per_frame)
                depth = d_ref[at]
                half_pre = depth * scale + shift
                dsecond = dexc_ref[tile, at] * pick_row(gates, t) + pick_row(dgate_ref[tile], t)
                dy = dsecond * silu_slope(half_pre, half_tanh(half_pre))
                dy = dy * live_value(t, total)
                dy2_ref[at] = dy
                summed = summed + jnp.sum(dy, axis=0)
                cross = cross + jnp.sum(dy * (depth - average), axis=0)
            return (summed, cross)

        zero = jnp.zeros((8, LANES), F32)
        summed, cross = each_frame(chunks, chunk, (zero, zero))
        rows = stack_rows(jnp.sum(summed, axis=0, keepdims=True), root * jnp.sum(cross, axis=0, keepdims=True))
        send_all(send_ref, rows, slice(0, LANES))


def squeeze_one_backward_kernel(
    counts_ref, third_ref, z_ref, cot_ref, ngain_ref, nbias_ref, stat_ref, d_ref, gain_ref, bias_ref, down_ref,
    up_ref, proj_ref, gates_ref, running_ref, pre_ref, act_ref, nsum_ref, dy2_ref, send_ref, pack_ref,
    dz3_ref, dz3t_ref, excited_ref, dexc_ref, dgate_ref,
):
    total = live_frames(counts_ref)
    pixels = HALF_ROWS * 8

    def head():
        count = stat_ref[2:3, :]
        sums = row_total(third_ref)
        mean, variance = moments_of(sums, count)
        root = lax.rsqrt(variance + EPSILON)
        gain = ngain_ref[1:2, :]
        bias_sum = sums[2:3, :]
        gain_sum = root * (sums[3:4, :] - mean * bias_sum)
        nsum_ref[...] = rows8(gain_sum, bias_sum, mean, variance)
        row = lax.broadcasted_iota(jnp.int32, z_ref.shape, 0) // pixels
        live = row < total
        normed = (z_ref[...] - mean) * root
        act = jnp.where(live, gain * normed + nbias_ref[1:2, :], 0.0)
        act_ref[...] = act.T[0 : act_ref.shape[0]]
        dz3 = gain * root * (cot_ref[...] - bias_sum / count - normed * (gain_sum / count))
        dz3 = jnp.where(live, dz3, 0.0)
        dz3_ref[...] = side_by_side(dz3)
        dz3t_ref[...] = jnp.concatenate(halves(dz3.T), axis=0)

    squeeze_backward_body(
        1, counts_ref, stat_ref, d_ref, gain_ref, bias_ref, down_ref, up_ref, proj_ref, gates_ref, running_ref,
        pre_ref, dy2_ref, send_ref, pack_ref, dz3_ref, dz3t_ref, excited_ref, dexc_ref, dgate_ref, head,
    )


def input_factors(sums, stat_ref, count, gain, w):
    root = lax.rsqrt(stat_ref[1:2, :] + EPSILON)
    factor = gain * root
    matrix = exact_dot(w * (factor * root * sums[1:2] / count), w, NT)
    return (matrix, row_dot(factor * sums[0:1] / count, w, NT))


def covariance(gram, summed, count):
    mean = summed / count
    return (mean, gram / count - outer(mean, mean))


def squeeze_zero_backward_kernel(
    counts_ref, top_ref, stat1_ref, gram_ref, nstat_ref, dxpre_ref, x1_ref, z_ref, ngain_ref, w_ref, gains_ref, q_one_ref,
    stat_ref, d_ref, gain_ref, bias_ref, down_ref, up_ref, proj_ref, gates_ref, running_ref, pre_ref,
    dx1_ref, nsum_ref, dy2_ref, send_ref, pack_ref, dz3_ref, dz3t_ref, excited_ref, dexc_ref, dgate_ref,
):
    total = live_frames(counts_ref)
    width = gains_ref.shape[1]

    def head():
        start = pack_tiles(proj_ref.shape[1], down_ref.shape[1]) * (width // LANES)
        pack_ref[start : start + q_one_ref.shape[0]] = q_one_ref[...]
        count = stat_ref[2:3, :]
        wide_count = jnp.broadcast_to(count[:, 0:1], (1, width))
        sums = row_total(top_ref, slice(0, width))
        extra = row_total(top_ref, slice(width, width + LANES))
        matrix, shift = input_factors(sums, stat1_ref, wide_count, gains_ref[2:3, :], pad_rows(w_ref[0]))
        mean = nstat_ref[0:1, :]
        root = lax.rsqrt(nstat_ref[1:2, :] + EPSILON)
        mean_x1 = gram_ref[3 * LANES : 3 * LANES + 1, :] / count
        cross = (gram_ref[LANES : 2 * LANES, :] - count * outer(mean_x1, mean)) * root
        gain_sum = extra[0:1] - jnp.sum(matrix * cross, axis=0, keepdims=True)
        bias_sum = extra[1:2] - count * shift
        nsum_ref[...] = rows8(gain_sum, bias_sum, mean, nstat_ref[1:2, :])
        factor = ngain_ref[0:1, :] * root
        square = right_square(matrix)
        bias_mean = bias_sum / count
        gain_mean = gain_sum / count

        def frame(t, carry):
            at = pl.ds(pl.multiple_of(t * 256, 256), 256)
            centred = side_by_side(x1_ref[at, :] - mean_x1)
            live = live_value(t, total)
            dx1 = (dxpre_ref[at, :] - fold_right(plain_dot(centred, square)) - shift) * live
            dx1_ref[at, :] = dx1
            normed = (z_ref[at, :] - mean) * root
            dz3 = factor * (dx1 - bias_mean - normed * gain_mean) * live
            dz3_ref[at, :] = side_by_side(dz3)
            dz3t_ref[:, at] = jnp.concatenate(halves(dz3.T), axis=0)
            return carry

        each_frame(dz3_ref.shape[0] // 256, frame, 0)

    squeeze_backward_body(
        0, counts_ref, stat_ref, d_ref, gain_ref, bias_ref, down_ref, up_ref, proj_ref, gates_ref, running_ref,
        pre_ref, dy2_ref, send_ref, pack_ref, dz3_ref, dz3t_ref, excited_ref, dexc_ref, dgate_ref, head,
    )

def back_full(t, k, a_ref, w_ref, z_ref, f_ref, dw_ref, fresh):
    weights = [w_ref[k * 9 + tap] for tap in range(9)]
    target = t - k
    sums = [None] * 9
    a_rows = {}
    z_rows = {}
    for i in range(SIDE):
        for need in (i, i + 1, i + 2):
            if need not in a_rows:
                a_rows[need] = [a_ref[target, plane, need] for plane in range(2)]
                z_rows[need] = [z_ref[t, plane, need] for plane in range(4)]
        even = None
        odd = None
        z_even, z_odd, z_odd_down, z_even_up = z_rows[i + 1]
        for r in range(3):
            b_even, b_odd, b_odd_down, b_even_up = z_rows[i + 2 - r]
            left, centre, right = weights[3 * r : 3 * r + 3]
            part_even = centre * b_even + right * b_odd_down + left * b_odd
            part_odd = centre * b_odd + right * b_even + left * b_even_up
            even = part_even if even is None else even + part_even
            odd = part_odd if odd is None else odd + part_odd
            a_even, a_odd = a_rows[i + r]
            pieces = (
                z_even_up * a_odd + z_odd * a_even,
                z_even * a_even + z_odd * a_odd,
                z_even * a_odd + z_odd_down * a_even,
            )
            for c in range(3):
                at = 3 * r + c
                sums[at] = pieces[c] if sums[at] is None else sums[at] + pieces[c]
        a_rows.pop(i)
        z_rows.pop(i)
        at = target * FULL_ROWS + 2 * i
        if fresh:
            f_ref[at] = even
            f_ref[at + 1] = odd
        else:
            f_ref[at] = f_ref[at] + even
            f_ref[at + 1] = f_ref[at + 1] + odd
    for tap in range(9):
        dw_ref[k * 9 + tap] = dw_ref[k * 9 + tap] + sums[tap]


def back_half(t, k, a_ref, w_ref, z_ref, f_ref, dw_ref, fresh):
    weights = [w_ref[k * 9 + tap] for tap in range(9)]
    target = t - k
    sums = [None] * 9

    def put(row, parity, value):
        at = target * FULL_ROWS + 2 * row + parity
        f_ref[at] = value if fresh else f_ref[at] + value

    carried = [a_ref[target, plane, 0] for plane in range(2)]
    here = [z_ref[t, plane, 0] for plane in range(2)]
    for i in range(HALF_ROWS):
        below = [z_ref[t, plane, i + 1] for plane in range(2)]
        dz, dz_up = here
        rows = [carried]
        for need in (2 * i + 1, 2 * i + 2):
            rows.append([a_ref[target, plane, need] for plane in range(2)])
        carried = rows[2]
        put(2 * i, 0, weights[4] * dz)
        put(2 * i, 1, weights[5] * dz + weights[3] * dz_up)
        put(2 * i + 1, 0, weights[7] * dz + weights[1] * below[0])
        put(
            2 * i + 1,
            1,
            weights[8] * dz + weights[6] * dz_up + (weights[2] * below[0] + weights[0] * below[1]),
        )
        for r in range(3):
            a_even, a_odd = rows[r]
            pieces = (dz_up * a_odd, dz * a_even, dz * a_odd)
            for c in range(3):
                at = 3 * r + c
                sums[at] = pieces[c] if sums[at] is None else sums[at] + pieces[c]
        here = below
    for tap in range(9):
        dw_ref[k * 9 + tap] = dw_ref[k * 9 + tap] + sums[tap]


def depth_backward_kernel(
    block, before, final, counts_ref, grads_ref, stat2_ref, stat_ref, nstat_ref, dy2_ref, d_ref, e_ref, columns_ref, w_ref,
    gain_ref, bias_ref, taps_ref, z3_ref, dx_in_ref, sums_in_ref, list_in_ref, dxpre_ref, send_ref, q_ref, grad_rows_ref,
    a_ref, z_ref, f_ref, taps8_ref, dw_ref, pair_ref,
):
    tile = pl.program_id(0)
    tiles = pl.num_programs(0)
    total = live_frames(counts_ref)
    frames = a_ref.shape[0]
    norm_row = 2 * block
    half = block == 1
    per_frame = HALF_ROWS if half else FULL_ROWS
    taps = dw_ref.shape[0]

    @pl.when(tile == 0)
    def start():
        clear_edges(a_ref)
        clear_edges(z_ref)
        if before:
            dxpre_ref[...] = dx_in_ref[...]
            send_all(send_ref, sums_in_ref[0:2, :], slice(0, before * LANES))
            q_ref[0 : list_in_ref.shape[0]] = list_in_ref[...]
        else:
            dxpre_ref[...] = jnp.zeros_like(dxpre_ref)

        def dead(t, carry):
            f_ref[pl.ds(t * FULL_ROWS, FULL_ROWS)] = jnp.zeros((FULL_ROWS, 8, LANES), F32)
            return carry

        lax.fori_loop(total, frames, dead, 0)

    count = stat2_ref[2:3, :]
    grads = row_total(grads_ref)
    grad_rows_ref[...] = rows8(grads[0:1], grads[1:2])
    average = stat2_ref[0:1, :]
    root = lax.rsqrt(stat2_ref[1:2, :] + EPSILON)
    scale_two = gain_ref[norm_row + 1 : norm_row + 2, :] * root
    slope = scale_two * root * grads[1:2] / count
    level = scale_two * grads[0:1] / count - slope * average
    average_one = stat_ref[0:1, :]
    root_one = lax.rsqrt(stat_ref[1:2, :] + EPSILON)
    scale_one = gain_ref[norm_row : norm_row + 1, :] * root_one
    shift_half = 0.5 * (bias_ref[norm_row : norm_row + 1, :] - average_one * scale_one)
    scale_half = 0.5 * scale_one

    def fill(t, carry):
        at = pl.ds(t * per_frame, per_frame)
        dz = scale_two * dy2_ref[at] - (slope * d_ref[at] + level)
        if half:
            z_ref[t, 0, 0:HALF_ROWS] = dz
            z_ref[t, 1, 0:HALF_ROWS] = columns_up(dz)
        else:
            pair = dz.reshape(SIDE, 2, 8, LANES)
            z_ref[t, 0, 1 : SIDE + 1] = pair[:, 0]
            z_ref[t, 1, 1 : SIDE + 1] = pair[:, 1]
            z_ref[t, 2, 1 : SIDE + 1] = columns_down(pair[:, 1])
            z_ref[t, 3, 1 : SIDE + 1] = columns_up(pair[:, 0])
        values = e_ref[pl.ds(pl.multiple_of(t * FULL_ROWS, FULL_ROWS), FULL_ROWS)]
        write_first(t, total, values, scale_half, shift_half, a_ref, 2)
        return carry

    each_frame(frames, fill, 0)
    spread_taps(taps_ref, taps8_ref)
    dw_ref[...] = jnp.zeros_like(dw_ref)
    back = back_half if half else back_full

    def frame(t, carry):
        back(t, 0, a_ref, taps8_ref, z_ref, f_ref, dw_ref, True)
        last = jnp.minimum(place_of(counts_ref, t), LAGS - 1)

        def lag(k, inner):
            back(t, k, a_ref, taps8_ref, z_ref, f_ref, dw_ref, False)
            return inner

        return lax.fori_loop(1, last + 1, lag, carry)

    lax.fori_loop(0, total, frame, 0)
    square = right_square_t(pad_rows(w_ref[0]))

    def finish(t, carry):
        rows = pl.ds(pl.multiple_of(t * FULL_ROWS, FULL_ROWS), FULL_ROWS)
        flat = pl.ds(pl.multiple_of(t * 256, 256), 256)
        values = e_ref[rows]
        half_pre = values * scale_half + shift_half
        dy = f_ref[rows] * silu_slope(half_pre, half_tanh(half_pre))
        summed = carry[0] + jnp.sum(dy, axis=0)
        cross = carry[1] + jnp.sum(dy * (values - average_one), axis=0)
        dy = dy.reshape(256, LANES)
        pair_ref[flat, :] = side_by_side(dy)
        scaled = side_by_side(dy * scale_one)
        dxpre_ref[flat, :] = dxpre_ref[flat, :] + fold_right(plain_dot(scaled, square, NT))
        return (summed, cross)

    zero = jnp.zeros((8, LANES), F32)
    summed, cross = each_frame(frames, finish, (zero, zero))
    rows = stack_rows(jnp.sum(summed, axis=0, keepdims=True), root_one * jnp.sum(cross, axis=0, keepdims=True))
    if final:
        send_all(send_ref, rows, pl.ds(pl.multiple_of((tile + before) * LANES, LANES), LANES))
    else:
        send_ref[...] = rows8(rows[0:1], rows[1:2])
    gathered = fold_square(plain_dot(columns_ref[...], pair_ref[...]))
    narrow = w_ref.shape[1]
    dtaps = jnp.sum(dw_ref[...], axis=1)
    unused = (-taps) % 8
    dtaps = jnp.concatenate([dtaps, jnp.zeros((unused, LANES), F32)], axis=0)
    values = jnp.concatenate([gathered[0:narrow], dtaps], axis=0)
    listed = values.shape[0] // 8
    q_ref[pl.ds((tile + before) * listed, listed)] = values.reshape(listed, 8, LANES)

    if half:
        @pl.when(tile == tiles - 1)
        def tail():
            mean = nstat_ref[0:1, :]
            root_three = lax.rsqrt(nstat_ref[1:2, :] + EPSILON)

            def part(t, carry):
                flat = pl.ds(pl.multiple_of(t * 256, 256), 256)
                dx = dxpre_ref[flat, :].reshape(32, 8, LANES)
                normed = ((z3_ref[flat, :] - mean) * root_three).reshape(32, 8, LANES)
                return (carry[0] + jnp.sum(dx * normed, axis=0), carry[1] + jnp.sum(dx, axis=0))

            cross_three, summed_three = each_frame(frames, part, (zero, zero))
            rows = stack_rows(
                jnp.sum(cross_three, axis=0, keepdims=True), jnp.sum(summed_three, axis=0, keepdims=True)
            )
            width = send_ref.shape[2] - LANES
            send_all(send_ref, rows, slice(width, width + LANES))


def finish_kernel(
    counts_ref, momentum_ref, gram_ref, stat01_ref, stat02_ref, stat11_ref, stat12_ref, grad0_ref,
    grad1_ref, one_ref, zero_ref, nsum0_ref, nsum1_ref, dxpre_ref, x_ref, dx1_ref, w_ref, gain_ref, means_ref, vars_ref,
    nmeans_ref, nvars_ref,
    video_ref, less_ref, factor_ref, wgain_ref, wbias_ref, ngain_ref, nbias_ref, newm_ref, newv_ref, newnm_ref, newnv_ref,
):
    total = live_frames(counts_ref)
    full = stat01_ref[2:3, :]
    count = full[:, 0:LANES]
    width = full.shape[1]
    top_zero = row_total(zero_ref)
    top_one = row_total(one_ref, slice(0, width))
    w_zero = pad_rows(w_ref[0])
    matrix, shift = input_factors(top_zero, stat01_ref, full, gain_ref[0:1, :], w_zero)
    square = right_square(matrix)
    mean_x, cov_zero = covariance(
        gram_ref[2 * LANES : 3 * LANES, :], gram_ref[3 * LANES + 1 : 3 * LANES + 2, :], count
    )
    order = column_order()
    narrow = video_ref.shape[0]

    def frame(t, carry):
        at = pl.ds(pl.multiple_of(t * 256, 256), 256)
        centred = side_by_side(x_ref[at, :] - mean_x)
        dx = (dxpre_ref[at, :] - fold_right(plain_dot(centred, square)) - shift) * live_value(t, total) + dx1_ref[at, :]
        for part in range(2):
            own = dx[part * LANES : (part + 1) * LANES].T[0:narrow]
            pieces = pick_thirds(order, own, NN, False)
            start = pl.multiple_of(t * 256 + part * LANES, LANES)
            video_ref[:, pl.ds(start, LANES)] = pieces[0] + pieces[1] + pieces[2]
        return carry

    each_frame(x_ref.shape[0] // 256, frame, 0)
    mean_one, cov_one = covariance(gram_ref[0:LANES, :], gram_ref[3 * LANES : 3 * LANES + 1, :], count)
    plan = ((mean_x, cov_zero, stat01_ref, top_zero, w_zero), (mean_one, cov_one, stat11_ref, top_one, pad_rows(w_ref[1])))
    for block, (mean_row, cov, stat_ref, top, w) in enumerate(plan):
        root = lax.rsqrt(stat_ref[1:2, :] + EPSILON)
        factor = gain_ref[2 * block : 2 * block + 1, :] * root
        less = outer(mean_row, top[0:1]) + exact_dot(cov, w) * (root * top[1:2])
        less_ref[block] = (less * factor)[0:narrow]
        factor_ref[8 * block : 8 * block + 8, :] = rows8(factor)
    momentum = momentum_ref[0].astype(F32) / 10.0
    wgain_ref[...] = stack_rows(top_zero[1:2], grad0_ref[1:2, :], top_one[1:2], grad1_ref[1:2, :])
    wbias_ref[...] = stack_rows(top_zero[0:1], grad0_ref[0:1, :], top_one[0:1], grad1_ref[0:1, :])
    stats = (stat01_ref, stat02_ref, stat11_ref, stat12_ref)
    means = stack_rows(*(ref[0:1, :] for ref in stats))
    variances = stack_rows(*(ref[1:2, :] * (ref[2:3, :] / (ref[2:3, :] - 1.0)) for ref in stats))
    newm_ref[...] = (1.0 - momentum) * means_ref[...] + momentum * means
    newv_ref[...] = (1.0 - momentum) * vars_ref[...] + momentum * variances
    ngain_ref[...] = stack_rows(nsum0_ref[0:1, :], nsum1_ref[0:1, :])[:, 0:narrow]
    nbias_ref[...] = stack_rows(nsum0_ref[1:2, :], nsum1_ref[1:2, :])[:, 0:narrow]
    means = stack_rows(nsum0_ref[2:3, :], nsum1_ref[2:3, :])[:, 0:narrow]
    quarter = 0.25 * count
    variances = stack_rows(
        nsum0_ref[3:4, :] * (count / (count - 1.0)), nsum1_ref[3:4, :] * (quarter / (quarter - 1.0))
    )[:, 0:narrow]
    newnm_ref[...] = (1.0 - momentum) * nmeans_ref[...] + momentum * means
    newnv_ref[...] = (1.0 - momentum) * nvars_ref[...] + momentum * variances


def gradient_kernel(
    core_ref, pack0_ref, pack0_other_ref, pack1_ref, pack1_other_ref, late_ref, late_other_ref, less_ref, factor_ref,
    dw_ref, dtaps_ref, ddown_ref, dup_ref, dproj_ref, dupb_ref, ddownb_ref,
):
    narrow = dw_ref.shape[1]
    taps = dtaps_ref.shape[1]
    squeeze = ddown_ref.shape[1]
    tiles = dw_ref.shape[2] // LANES
    per_pack = pack_tiles(narrow, squeeze)
    per_tile = narrow // 8 + -(-taps // 8)
    first_core = core_ref[0] == 0

    def rows_of(pair, at, count):
        mine, other = pair
        half = mine.shape[0]
        pieces = []
        if at < half:
            size = min(count, half - at)
            here = slice(at, at + size)
            pieces.append(jnp.where(first_core, mine[here], other[here]))
            count = count - size
            at = at + size
        if count:
            here = slice(at - half, at - half + count)
            pieces.append(jnp.where(first_core, other[here], mine[here]))
        values = pieces[0] if len(pieces) == 1 else jnp.concatenate(pieces, axis=0)
        return values.reshape(-1, LANES)

    packs = ((pack0_ref, pack0_other_ref), (pack1_ref, pack1_other_ref))
    lists = ((late_ref, late_other_ref), packs[0])
    for block in range(2):
        down_rows = []
        for tile in range(tiles):
            lanes = slice(tile * LANES, (tile + 1) * LANES)
            at = tile * per_pack
            dproj_ref[block, :, lanes] = rows_of(packs[block], at, narrow // 8)
            at = at + narrow // 8
            ddown_ref[block, :, lanes] = rows_of(packs[block], at, squeeze // 8)
            at = at + squeeze // 8
            dup_ref[block, :, lanes] = rows_of(packs[block], at, squeeze // 8)
            biases = rows_of(packs[block], at + squeeze // 8, 1)
            dupb_ref[block : block + 1, lanes] = biases[0:1]
            down_rows.append(biases[1:2])
            values = rows_of(lists[block], (per_pack * tiles if block else 0) + tile * per_tile, per_tile)
            dw = values[0:narrow] * factor_ref[8 * block : 8 * block + 1, lanes] - less_ref[block, :, lanes]
            dw_ref[block, :, lanes] = dw
            dtaps_ref[block, :, lanes] = values[narrow : narrow + taps]
        ddownb_ref[block : block + 1, :] = jnp.concatenate(down_rows, axis=1)[:, 0:squeeze]


AXES = ("dp", "z", "core")
CHIPS = ("dp", "z")


def exchange(send):
    return lax.all_to_all(send, AXES, 0, 0, tiled=True)


def together(*values):
    return lax.optimization_barrier(values)


def swap_cores(values):
    return lax.ppermute(values, "core", [(0, 1), (1, 0)])


def add_cores(tiles):
    core = lax.axis_index("core")
    pair = tiles.reshape(2, tiles.shape[0] // 2, *tiles.shape[1:])
    mine = lax.dynamic_index_in_dim(pair, core, 0, keepdims=False)
    return mine + swap_cores(lax.dynamic_index_in_dim(pair, 1 - core, 0, keepdims=False))


def share_out(tiles, names=CHIPS):
    count = 1
    for name in names:
        count = count * lax.axis_size(name)
    return lax.all_to_all(tiles.reshape(count, -1, *tiles.shape[1:]), names, 0, 0, tiled=True)


def share_back(pieces, names=CHIPS):
    own = jnp.sum(pieces, axis=0)
    everyone = lax.all_to_all(jnp.broadcast_to(own[None], pieces.shape), names, 0, 0, tiled=True)
    return everyone.reshape(-1, *pieces.shape[2:])


def shape(*dims, kind=F32):
    return jax.ShapeDtypeStruct(dims, kind)


def whole(array):
    rank = len(array.shape)
    return pl.BlockSpec(array.shape, lambda *ids: (0,) * rank)


SCALARS = pl.BlockSpec(memory_space=pltpu.SMEM)


def call(kernel, grid, in_specs, out_specs, out_shape, scratch, args, micros=10):
    return pl.pallas_call(
        kernel,
        grid=grid,
        in_specs=in_specs,
        out_specs=out_specs,
        out_shape=out_shape,
        scratch_shapes=scratch,
        compiler_params=pltpu.CompilerParams(vmem_limit_bytes=VMEM_BYTES),
        cost_estimate=pl.CostEstimate(
            flops=micros * 1_000_000_000, bytes_accessed=micros * 3_000_000, transcendentals=0
        ),
    )(*args)


def simple_call(kernel, scalars, args, outs):
    return call(
        kernel, (1,), [SCALARS] * scalars + [whole(array) for array in args[scalars:]], [whole(item) for item in outs],
        outs, [], args,
    )


def local(
    video, frame_counts, momentum_index, expand_weight, wide_gains, wide_biases, narrow_gains, narrow_biases, depth_weight,
    squeeze_weight, squeeze_bias, excite_weight, excite_bias, project_weight, wide_means, wide_variances, narrow_means,
    narrow_variances, cotangent,
):
    devices = lax.axis_size("dp") * lax.axis_size("z") * lax.axis_size("core")
    cin, pixels = video.shape
    half_pixels = cotangent.shape[1]
    width = expand_weight.shape[1]
    squeeze = squeeze_weight.shape[1]
    frames = pixels // (SIDE * SIDE)
    tiles = width // LANES
    taps = depth_weight.shape[1]
    w_t = jnp.swapaxes(expand_weight, 1, 2)
    up_t = jnp.swapaxes(excite_weight, 1, 2)
    lanes_pad = ((0, 0), (0, LANES - cin))
    ngains = jnp.pad(narrow_gains, lanes_pad)
    nbiases = jnp.pad(narrow_biases, lanes_pad)
    full_rows = frames * FULL_ROWS
    half_rows = frames * HALF_ROWS
    low = jnp.bfloat16

    def round_up(count):
        return -(-count // devices) * devices

    def fixed(*dims):
        return pl.BlockSpec(dims, lambda *ids: (0,) * len(dims))

    def tile_rows(rows):
        return pl.BlockSpec((rows, LANES), lambda j: (0, j))

    def tile_cube(rows):
        return pl.BlockSpec((rows, 8, LANES), lambda j: (0, 0, j))

    def tile_sums(rows=2):
        return pl.BlockSpec((devices, rows, LANES), lambda j: (0, 0, j))

    def weight_tile(block, rows):
        return pl.BlockSpec((1, rows, LANES), lambda j, block=block: (block, 0, j))

    def of_block(block, rows, lanes):
        return pl.BlockSpec((1, rows, lanes), lambda *ids: (block, 0, 0))

    def early(make):
        return make(lambda p, j: j * (1 - p) + (tiles - 1) * p)

    def late(make):
        return make(lambda p, j: j * p)

    def both(make):
        return make(lambda p, j: j)

    def rows_at(rows):
        return lambda at: pl.BlockSpec((rows, LANES), lambda p, j: (0, at(p, j)))

    def cube_at(rows):
        return lambda at: pl.BlockSpec((rows, 8, LANES), lambda p, j: (0, 0, at(p, j)))

    def sums_at(rows):
        return lambda at: pl.BlockSpec((devices, rows, LANES), lambda p, j: (0, 0, at(p, j)))

    def weight_at(block, rows):
        return lambda at: pl.BlockSpec((1, rows, LANES), lambda p, j: (block, 0, at(p, j)))

    x, x_rows, x_columns, cot, gram_zero, sums = call(
        prepare_kernel, (1,), [SCALARS, whole(video), whole(cotangent), of_block(0, cin, width)],
        [fixed(pixels, LANES), fixed(pixels, 2 * LANES), fixed(2 * LANES, pixels), fixed(half_pixels, LANES),
         fixed(LANES + 8, LANES), fixed(devices, 2, width + LANES)],
        [shape(pixels, LANES), shape(pixels, 2 * LANES, kind=low), shape(2 * LANES, pixels, kind=low),
         shape(half_pixels, LANES), shape(LANES + 8, LANES), shape(devices, 2, width + LANES)],
        [], (frame_counts, video, cotangent, w_t),
    )
    sums = exchange(sums)

    def expand(block, sums, count, count_spec, rows):
        depth_rows = half_rows if block else full_rows
        return call(
            functools.partial(expand_kernel, block), (tiles,),
            [SCALARS, tile_sums(), count_spec, whole(rows), weight_tile(block, cin), tile_rows(4), tile_rows(4),
             weight_tile(block, taps)],
            [tile_cube(full_rows), tile_cube(depth_rows), tile_rows(8), tile_sums()],
            [shape(full_rows, 8, width), shape(depth_rows, 8, width), shape(8, width), shape(devices, 2, width)],
            [pltpu.VMEM((frames, 4, SIDE + 2, 8, LANES), F32), pltpu.VMEM((taps, 8, LANES), F32)],
            (frame_counts, sums, count, rows, w_t, wide_gains, wide_biases, depth_weight),
        )

    count_spec = pl.BlockSpec((devices, 2, LANES), lambda j: (0, 0, tiles))
    e_zero, d_zero, stat01, sums = expand(0, sums, sums, count_spec, x_rows)
    sums = exchange(sums)

    def squeeze_forward(block, sums, stat, depth):
        rows = half_rows if block else full_rows
        kinds = 4 if block else 2
        return call(
            functools.partial(squeeze_forward_kernel, block), (2, tiles),
            [SCALARS, early(sums_at(2)), early(rows_at(8)), early(cube_at(rows)), early(rows_at(4)), early(rows_at(4)),
             of_block(block, squeeze, width), whole(squeeze_bias), of_block(block, squeeze, width), whole(excite_bias),
             late(weight_at(block, cin)), whole(cot)],
            [fixed(rows * 8, LANES), fixed(8, width), fixed(8, width), fixed(8, squeeze), early(rows_at(8)),
             fixed(devices, kinds, LANES)],
            [shape(rows * 8, LANES), shape(8, width), shape(8, width), shape(8, squeeze), shape(8, width),
             shape(devices, kinds, LANES)],
            [pltpu.VMEM((tiles, rows, 8, LANES), F32), pltpu.VMEM((tiles, frames, LANES), F32)],
            (frame_counts, sums, stat, depth, wide_gains, wide_biases, squeeze_weight, squeeze_bias, up_t, excite_bias,
             project_weight, cot),
        )

    z_zero, gates_zero, running_zero, pre_zero, stat02, sums = squeeze_forward(0, sums, stat01, d_zero)
    sums = exchange(sums)
    narrow_args = (frame_counts, sums, stat01, gram_zero, x, z_zero, ngains, nbiases, w_t)
    narrow_outs = [
        shape(pixels, LANES), shape(pixels, 2 * LANES, kind=low), shape(2 * LANES, pixels, kind=low),
        shape(round_up(3 * LANES // 8 + 1), 8, LANES), shape(8, LANES), shape(devices, 2, width),
    ]
    x1, x1_rows, x1_columns, gram, nstat, sums = call(
        narrow_kernel, (1,), [SCALARS] + [whole(array) for array in narrow_args[1:-1]] + [of_block(1, cin, width)],
        [whole(item) for item in narrow_outs], narrow_outs, [], narrow_args,
    )
    sums, gram = together(exchange(sums), gram)
    gram = share_out(gram, AXES)
    e_one, d_one, stat11, sums = expand(1, sums, nstat, pl.BlockSpec((8, LANES), lambda j: (0, 0)), x1_rows)
    sums, gram = together(sums, gram)
    sums = exchange(sums)
    z_one, gates_one, running_one, pre_one, stat12, sums = squeeze_forward(1, sums, stat11, d_one)
    third, gram = together(exchange(sums), gram)
    gram = share_back(gram, AXES).reshape(-1, LANES)
    q_tiles = cin // 8 + -(-taps // 8)

    def backward_specs(block):
        rows = half_rows if block else full_rows
        ins = [both(rows_at(8)), both(cube_at(rows)), both(rows_at(4)), both(rows_at(4)), of_block(block, squeeze, width),
               of_block(block, squeeze, width), early(weight_at(block, cin)), fixed(8, width), fixed(8, width),
               fixed(8, squeeze)]
        packed = round_up(tiles * (pack_tiles(cin, squeeze) + (0 if block else q_tiles)))
        outs = [fixed(8, LANES), late(cube_at(rows)), late(sums_at(2)), fixed(packed, 8, LANES)]
        shapes = [shape(8, LANES), shape(rows, 8, width), shape(devices, 2, width), shape(packed, 8, LANES)]
        scratch = [pltpu.VMEM((rows * 8, 2 * LANES), low), pltpu.VMEM((2 * LANES, rows * 8), low),
                   pltpu.VMEM((rows * 8, 2 * LANES), low), pltpu.VMEM((tiles, rows, 8, LANES), F32),
                   pltpu.VMEM((tiles, frames, LANES), F32)]
        return (ins, outs, shapes, scratch)

    ins, outs, shapes, scratch = backward_specs(1)
    activations, nsum_one, dy2_one, sums, pack_one = call(
        squeeze_one_backward_kernel, (2, tiles),
        [SCALARS, whole(third), whole(z_one), whole(cot), whole(ngains), whole(nbiases)] + ins,
        [fixed(cin, half_pixels)] + outs, [shape(cin, half_pixels)] + shapes, scratch,
        (frame_counts, third, z_one, cot, ngains, nbiases, stat12, d_one, wide_gains, wide_biases, squeeze_weight, up_t,
         project_weight, gates_one, running_one, pre_one),
    )
    sums, gram = together(sums, gram)
    sums, pack_one = together(exchange(sums), add_cores(pack_one))
    pack_one = share_out(pack_one)
    nothing = jnp.zeros((8, LANES), F32)

    def depth_backward(block, begin, end, sums, stat2, stat, dy2, depth, expanded, columns, dx_in, sums_in, list_in):
        rows = half_rows if block else full_rows
        z_shape = (frames, 2, HALF_ROWS + 1, 8, LANES) if block else (frames, 4, SIDE + 2, 8, LANES)
        count = end - begin
        final = end == tiles
        listed = round_up(end * q_tiles) if final and not block else end * q_tiles
        if final:
            send = (devices, 2, width + (LANES if block else 0))
            send_spec = fixed(*send)
        else:
            send = (8, count * LANES)
            send_spec = tile_rows(8)

        def wide_rows(rows):
            return pl.BlockSpec((rows, LANES), lambda j: (0, j + begin))

        def wide_cube(rows):
            return pl.BlockSpec((rows, 8, LANES), lambda j: (0, 0, j + begin))

        def wide_weight(rows):
            return pl.BlockSpec((1, rows, LANES), lambda j: (block, 0, j + begin))

        return call(
            functools.partial(depth_backward_kernel, block, begin, final), (count,),
            [SCALARS, pl.BlockSpec((devices, 2, LANES), lambda j: (0, 0, j + begin)), wide_rows(8), wide_rows(8), whole(nstat),
             wide_cube(rows), wide_cube(rows), wide_cube(full_rows), whole(columns), wide_weight(cin), wide_rows(4),
             wide_rows(4), wide_weight(taps), whole(z_zero), whole(dx_in), whole(sums_in), whole(list_in)],
            [fixed(pixels, LANES), send_spec, fixed(listed, 8, LANES), tile_rows(8)],
            [shape(pixels, LANES), shape(*send), shape(listed, 8, LANES), shape(8, count * LANES)],
            [pltpu.VMEM((frames, 2, SIDE + 2, 8, LANES), F32), pltpu.VMEM(z_shape, F32), pltpu.VMEM((full_rows, 8, LANES), F32),
             pltpu.VMEM((taps, 8, LANES), F32), pltpu.VMEM((taps, 8, LANES), F32), pltpu.VMEM((pixels, 2 * LANES), low)],
            (frame_counts, sums, stat2, stat, nstat, dy2, depth, expanded, columns, w_t, wide_gains, wide_biases,
             depth_weight, z_zero, dx_in, sums_in, list_in),
            20,
        )

    dxpre_one, sums, q_one, grad_one = depth_backward(
        1, 0, tiles, sums, stat12, stat11, dy2_one, d_one, e_one, x1_columns, nothing, nothing, nothing
    )
    sums, pack_one = together(sums, pack_one)
    top_one, pack_one = together(exchange(sums), pack_one)
    pack_one = share_back(pack_one)
    ins, outs, shapes, scratch = backward_specs(0)
    dx1, nsum_zero, dy2_zero, sums, pack_zero = call(
        squeeze_zero_backward_kernel, (2, tiles),
        [SCALARS, whole(top_one), whole(stat11), whole(gram), whole(nstat), whole(dxpre_one), whole(x1), whole(z_zero),
         whole(ngains), of_block(1, cin, width), whole(wide_gains), whole(q_one)] + ins,
        [fixed(pixels, LANES)] + outs, [shape(pixels, LANES)] + shapes, scratch,
        (frame_counts, top_one, stat11, gram, nstat, dxpre_one, x1, z_zero, ngains, w_t, wide_gains, q_one, stat02, d_zero,
         wide_gains, wide_biases, squeeze_weight, up_t, project_weight, gates_zero, running_zero, pre_zero),
    )
    sums, pack_one = together(sums, pack_one)
    pack_one_other = swap_cores(pack_one)
    sums, pack_zero, pack_one_other = together(exchange(sums), add_cores(pack_zero), pack_one_other)
    pack_zero = share_out(pack_zero)
    first = tiles - tiles // 2
    dxpre_zero, sums_in, late, grad_a = depth_backward(
        0, 0, first, sums, stat02, stat01, dy2_zero, d_zero, e_zero, x_columns, nothing, nothing, nothing
    )
    dxpre_zero, pack_zero = together(dxpre_zero, pack_zero)
    pack_zero = share_back(pack_zero)
    dxpre_zero, sums, late, grad_b = depth_backward(
        0, first, tiles, sums, stat02, stat01, dy2_zero, d_zero, e_zero, x_columns, dxpre_zero, sums_in, late
    )
    grad_zero = jnp.concatenate([grad_a, grad_b], axis=1)
    sums, pack_zero = together(sums, pack_zero)
    pack_zero_other = swap_cores(pack_zero)
    top_zero, late, pack_zero_other = together(exchange(sums), add_cores(late), pack_zero_other)
    late = share_back(share_out(late))
    late_other = swap_cores(late)
    core = lax.axis_index("core").astype(jnp.int32).reshape(1)
    final_args = (
        frame_counts, momentum_index, gram, stat01, stat02, stat11, stat12, grad_zero, grad_one, top_one,
        top_zero, nsum_zero, nsum_one, dxpre_zero, x, dx1, w_t, wide_gains, wide_means, wide_variances, narrow_means,
        narrow_variances,
    )
    final_outs = [
        shape(cin, pixels), shape(2, cin, width), shape(16, width), shape(4, width), shape(4, width), shape(2, cin),
        shape(2, cin), shape(4, width), shape(4, width), shape(2, cin), shape(2, cin),
    ]
    video_grad, less, factor, wgain, wbias, ngain, nbias, newm, newv, newnm, newnv = simple_call(
        finish_kernel, 2, final_args, final_outs
    )
    dw_t, dtaps, ddown, dup, dproj, dupb, ddownb = simple_call(
        gradient_kernel, 1,
        (core, pack_zero, pack_zero_other, pack_one, pack_one_other, late, late_other, less, factor),
        [shape(2, cin, width), shape(2, taps, width), shape(2, squeeze, width), shape(2, squeeze, width),
         shape(2, cin, width), shape(2, width), shape(2, squeeze)],
    )
    return (
        activations, video_grad, jnp.swapaxes(dw_t, 1, 2), wgain, wbias, ngain, nbias, dtaps, ddown, ddownb,
        jnp.swapaxes(dup, 1, 2), dupb, dproj, newm, newv, newnm, newnv,
    )


def solution(mesh):
    sizes = (mesh.shape["dp"], mesh.shape["rep"] // 2, 2)
    split_mesh = jax.sharding.Mesh(mesh.devices.reshape(sizes), AXES)
    split = P(None, AXES)
    placed = (split, P(AXES)) + (P(),) * 16 + (split,)
    return jax.shard_map(
        local, mesh=split_mesh, in_specs=placed, out_specs=(split, split) + (P(),) * 15, check_vma=False
    )
```

profile of v0, /device:TPU:0, one launch (start us, length us, event | category | flops | bytes accessed | tf_op | source)
XLA Modules:
  0.0 367.7 jit_solution(13988823514716119420)
XLA Ops:
  0.7 1.1 copy-done.2
  1.7 0.9 copy-done.5
  3.3 6.4 %shard_map.314 = (f32[2048,128]{1,0:T(8,128)}, bf16[2048,256]{1,0:T(8,128)(2,1)}, bf16[256,2048]{1,0:T(8,128)(2,1)}, f32[512,128]{1,0:T(8,128)S(1)}, f32[136,128]{1,0:T(8,128)S(1)}, /*index=5*/f32[32,2,768]{2,1,0:T(2,128)}) custom-call(s32[2]{0:T(128)S(1)} %copy-done.14, f32[112,2048]{1,0:T(8,128)} %video_ref.1, f32[112,512]{1,0:T(8,128)S(1)} %copy-done.5, ...), custom_call_target="tpu_custom_call" | custom-call | flops 10000000000 | bytes 30000000 | tf_op jit(solution)/shard_map/pallas_call | solution.py:1077
  9.7 7.3 %all-to-all-start = ((f32[32,2,768]{2,1,0:T(2,128)}), f32[32,2,768]{2,1,0:T(2,128)S(1)}, u32[]{:S(2)}, u32[]{:S(2)}) async-start(f32[32,2,768]{2,1,0:T(2,128)} %get-tuple-element.115), calls=%async_computation | async-start | bytes 393216 | tf_op jit(solution)/shard_map/all_to_all | solution.py:1033
  17.0 8.7 %all-to-all-done.sums_ref.count_ref = f32[32,2,768]{2,1,0:T(2,128)S(1)} async-done(((f32[32,2,768]{2,1,0:T(2,128)}), f32[32,2,768]{2,1,0:T(2,128)S(1)}, u32[]{:S(2)}, u32[]{:S(2)}) %all-to-all-start) | async-done | bytes 196640 | tf_op jit(solution)/shard_map/all_to_all | solution.py:1033
  25.8 17.3 %shard_map.315 = (f32[256,8,640]{2,1,0:T(8,128)}, f32[256,8,640]{2,1,0:T(8,128)}, f32[8,640]{1,0:T(8,128)S(1)}, f32[32,2,640]{2,1,0:T(2,128)S(1)}) custom-call(s32[2]{0:T(128)S(1)} %copy-done.15, f32[32,2,768]{2,1,0:T(2,128)S(1)} %all-to-all-done.sums_ref.count_ref, f32[32,2,768]{2,1,0:T(2,128)S(1)} %all-to-all-done.sums_ref.count_ref, ...), custom_call_target="tpu_custom_call" | custom-call | flops 10000000000 | bytes 30000000 | tf_op jit(solution)/shard_map/pallas_call | solution.py:1077
  43.1 14.4 %all_to_all.90.sums_ref = f32[32,2,640]{2,1,0:T(2,128)S(1)} all-to-all(f32[32,2,640]{2,1,0:T(2,128)S(1)} %get-tuple-element.117), channel_id=1, replica_groups=mesh['dp'=4,'z'=4,'core'=2] {'dp','z','core'}, dimensions={0} | all-to-all | bytes 327680 | tf_op jit(solution)/shard_map/all_to_all | solution.py:1033
  57.6 12.9 %shard_map.316 = (f32[2048,128]{1,0:T(8,128)}, f32[8,640]{1,0:T(8,128)S(1)}, f32[8,640]{1,0:T(8,128)S(1)}, f32[8,160]{1,0:T(8,128)S(1)}, f32[8,640]{1,0:T(8,128)S(1)}, /*index=5*/f32[32,2,128]{2,1,0:T(2,128)}) custom-call(s32[2]{0:T(128)S(1)} %copy-done.15, f32[32,2,640]{2,1,0:T(2,128)S(1)} %all_to_all.90.sums_ref, ...), custom_call_target="tpu_custom_call" | custom-call | flops 10000000000 | bytes 30000000 | tf_op jit(solution)/shard_map/pallas_call | solution.py:1077
  70.5 2.6 all-to-all-start.2
  73.1 7.2 %all-to-all-done.2.sums_ref = f32[32,2,128]{2,1,0:T(2,128)S(1)} async-done(((f32[32,2,128]{2,1,0:T(2,128)}), f32[32,2,128]{2,1,0:T(2,128)S(1)}, u32[]{:S(2)}, u32[]{:S(2)}) %all-to-all-start.2) | async-done | bytes 32800 | tf_op jit(solution)/shard_map/all_to_all | solution.py:1033
  80.3 5.8 %shard_map.317 = (f32[2048,128]{1,0:T(8,128)}, bf16[2048,256]{1,0:T(8,128)(2,1)}, bf16[256,2048]{1,0:T(8,128)(2,1)}, f32[64,8,128]{2,1,0:T(8,128)}, f32[8,128]{1,0:T(8,128)S(1)}, /*index=5*/f32[32,2,640]{2,1,0:T(2,128)S(1)}) custom-call(s32[2]{0:T(128)S(1)} %copy-done.15, f32[32,2,128]{2,1,0:T(2,128)S(1)} %all-to-all-done.2.sums_ref, ...), custom_call_target="tpu_custom_call" | custom-call | flops 10000000000 | bytes 30000000 | tf_op jit(solution)/shard_map/pallas_call | solution.py:1077
  86.1 10.2 %all_to_all.91.sums_ref = f32[32,2,640]{2,1,0:T(2,128)S(1)} all-to-all(f32[32,2,640]{2,1,0:T(2,128)S(1)} %get-tuple-element.125), channel_id=1, replica_groups=mesh['dp'=4,'z'=4,'core'=2] {'dp','z','core'}, dimensions={0} | all-to-all | bytes 327680 | tf_op jit(solution)/shard_map/all_to_all | solution.py:1033
  96.3 2.6 all-to-all-start.4
  98.9 11.3 %shard_map.318 = (f32[256,8,640]{2,1,0:T(8,128)}, f32[64,8,640]{2,1,0:T(8,128)}, f32[8,640]{1,0:T(8,128)S(1)}, f32[32,2,640]{2,1,0:T(2,128)S(1)}) custom-call(s32[2]{0:T(128)S(1)} %copy-done.15, f32[32,2,640]{2,1,0:T(2,128)S(1)} %all_to_all.91.sums_ref, f32[8,128]{1,0:T(8,128)S(1)} %get-tuple-element.128.count_ref.nstat_ref, ...), custom_call_target="tpu_custom_call" | custom-call | flops 10000000000 | bytes 30000000 | tf_op jit(solution)/shard_map/pallas_call | solution.py:1077
  110.2 14.8 %all_to_all.92.sums_ref = f32[32,2,640]{2,1,0:T(2,128)S(1)} all-to-all(f32[32,2,640]{2,1,0:T(2,128)S(1)} %get-tuple-element.132), channel_id=1, replica_groups=mesh['dp'=4,'z'=4,'core'=2] {'dp','z','core'}, dimensions={0} | all-to-all | bytes 327680 | tf_op jit(solution)/shard_map/all_to_all | solution.py:1033
  125.1 7.0 %shard_map.319 = (f32[512,128]{1,0:T(8,128)S(1)}, f32[8,640]{1,0:T(8,128)S(1)}, f32[8,640]{1,0:T(8,128)S(1)}, f32[8,160]{1,0:T(8,128)S(1)}, f32[8,640]{1,0:T(8,128)S(1)}, /*index=5*/f32[32,4,128]{2,1,0:T(4,128)}) custom-call(s32[2]{0:T(128)S(1)} %copy-done.15, f32[32,2,640]{2,1,0:T(2,128)S(1)} %all_to_all.92.sums_ref, ...), custom_call_target="tpu_custom_call" | custom-call | flops 10000000000 | bytes 30000000 | tf_op jit(solution)/shard_map/pallas_call | solution.py:1077
  132.1 2.6 all-to-all-start.6
  134.6 7.4 %all-to-all-done.6.third_ref = f32[32,4,128]{2,1,0:T(4,128)S(1)} async-done(((f32[32,4,128]{2,1,0:T(4,128)}), f32[32,4,128]{2,1,0:T(4,128)S(1)}, u32[]{:S(2)}, u32[]{:S(2)}) %all-to-all-start.6) | async-done | bytes 65568 | tf_op jit(solution)/shard_map/all_to_all | solution.py:1033
  142.0 10.3 %shard_map.320 = (f32[112,512]{1,0:T(8,128)}, f32[8,128]{1,0:T(8,128)S(1)}, f32[64,8,640]{2,1,0:T(8,128)}, f32[32,2,640]{2,1,0:T(2,128)}, f32[288,8,128]{2,1,0:T(8,128)}) custom-call(s32[2]{0:T(128)S(1)} %copy-done.15, f32[32,4,128]{2,1,0:T(4,128)S(1)} %all-to-all-done.6.third_ref, f32[512,128]{1,0:T(8,128)S(1)} %get-tuple-element.138.z_ref, ...), custom_call_target="tpu_custom_call" | custom-call | flops 10000000000 | bytes 30000000 | tf_op jit(solution)/shard_map/pallas_call | solution.py:1077
  152.3 1.2 dynamic-slice_bitcast_fusion.1
  153.8 12.1 %all_to_all.93 = f32[32,2,8,128]{3,2,1,0:T(8,128)S(1)} all-to-all(f32[32,2,8,128]{3,2,1,0:T(8,128)S(1)} %broadcast_in_dim.10), channel_id=1, replica_groups=mesh['dp'=4,'z'=4,'core'=2] {'dp','z','core'}, dimensions={0} | all-to-all | bytes 524288 | tf_op jit(solution)/shard_map/all_to_all | solution.py:1060
  165.8 2.7 all-to-all-start.8
  168.6 1.9 bitcast_add_fusion.1
  170.5 6.5 %all-to-all-done.8.grads_ref = f32[32,2,640]{2,1,0:T(2,128)S(1)} async-done(((f32[32,2,640]{2,1,0:T(2,128)}), f32[32,2,640]{2,1,0:T(2,128)S(1)}, u32[]{:S(2)}, u32[]{:S(2)}) %all-to-all-start.8) | async-done | bytes 163872 | tf_op jit(solution)/shard_map/all_to_all | solution.py:1033
  177.0 3.6 all-to-all-start.9
  180.6 19.3 %shard_map.321 = (f32[2048,128]{1,0:T(8,128)}, f32[32,2,768]{2,1,0:T(2,128)S(1)}, f32[100,8,128]{2,1,0:T(8,128)S(1)}, f32[8,640]{1,0:T(8,128)S(1)}) custom-call(s32[2]{0:T(128)S(1)} %copy-done.15, f32[32,2,640]{2,1,0:T(2,128)S(1)} %all-to-all-done.8.grads_ref, f32[8,640]{1,0:T(8,128)S(1)} %get-tuple-element.139.stat_ref.stat2_ref.stat12_ref, ...), custom_call_target="tpu_custom_call" | custom-call | flops 20000000000 | bytes 60000000 | tf_op jit(solution)/shard_map/pallas_call | solution.py:1077
  200.0 15.6 %all_to_all.94.top_ref.one_ref = f32[32,2,768]{2,1,0:T(2,128)S(1)} all-to-all(f32[32,2,768]{2,1,0:T(2,128)S(1)} %get-tuple-element.156), channel_id=1, replica_groups=mesh['dp'=4,'z'=4,'core'=2] {'dp','z','core'}, dimensions={0} | all-to-all | bytes 393216 | tf_op jit(solution)/shard_map/all_to_all | solution.py:1033
  216.5 3.8 %all-to-all-start.11 = ((f32[16,9,8,128]{3,2,1,0:T(8,128)}), f32[16,9,8,128]{3,2,1,0:T(8,128)S(1)}, u32[]{:S(2)}, u32[]{:S(2)}) async-start(f32[16,9,8,128]{3,2,1,0:T(8,128)} %broadcast_in_dim.12), calls=%async_computation.11 | async-start | bytes 1179648 | tf_op jit(solution)/shard_map/all_to_all | solution.py:1060
  220.3 21.3 %shard_map.322 = (f32[2048,128]{1,0:T(8,128)}, f32[8,128]{1,0:T(8,128)S(1)}, f32[256,8,640]{2,1,0:T(8,128)}, f32[32,2,640]{2,1,0:T(2,128)}, f32[384,8,128]{2,1,0:T(8,128)}) custom-call(s32[2]{0:T(128)S(1)} %copy-done.15, f32[32,2,768]{2,1,0:T(2,128)S(1)} %all_to_all.94.top_ref.one_ref, f32[8,640]{1,0:T(8,128)S(1)} %get-tuple-element.133.stat_ref.stat1_ref.stat11_ref, ...), custom_call_target="tpu_custom_call" | custom-call | flops 10000000000 | bytes 30000000 | tf_op jit(solution)/shard_map/pallas_call | solution.py:1077
  241.6 2.1 dynamic-slice_bitcast_fusion
  244.4 5.6 %all-to-all-start.12 = ((f32[32,2,640]{2,1,0:T(2,128)}), f32[32,2,640]{2,1,0:T(2,128)S(1)}, u32[]{:S(2)}, u32[]{:S(2)}) async-start(f32[32,2,640]{2,1,0:T(2,128)} %get-tuple-element.167), calls=%async_computation.12 | async-start | bytes 327680 | tf_op jit(solution)/shard_map/all_to_all | solution.py:1033
  250.0 2.2 bitcast_add_fusion
  252.2 6.3 %all-to-all-done.12.grads_ref = f32[32,2,640]{2,1,0:T(2,128)S(1)} async-done(((f32[32,2,640]{2,1,0:T(2,128)}), f32[32,2,640]{2,1,0:T(2,128)S(1)}, u32[]{:S(2)}, u32[]{:S(2)}) %all-to-all-start.12) | async-done | bytes 163872 | tf_op jit(solution)/shard_map/all_to_all | solution.py:1033
  258.5 4.3 %all-to-all-start.13 = ((f32[16,12,8,128]{3,2,1,0:T(8,128)}), f32[16,12,8,128]{3,2,1,0:T(8,128)}, u32[]{:S(2)}, u32[]{:S(2)}) async-start(f32[16,12,8,128]{3,2,1,0:T(8,128)} %bitcast.12), calls=%async_computation.13 | async-start | bytes 1572864 | tf_op jit(solution)/shard_map/all_to_all | solution.py:1055
  262.8 18.8 %shard_map.323 = (f32[2048,128]{1,0:T(8,128)}, f32[8,384]{1,0:T(8,128)S(1)}, f32[60,8,128]{2,1,0:T(8,128)S(1)}, f32[8,384]{1,0:T(8,128)S(1)}) custom-call(s32[2]{0:T(128)S(1)} %copy-done.15, f32[32,2,640]{2,1,0:T(2,128)S(1)} %all-to-all-done.12.grads_ref, f32[8,640]{1,0:T(8,128)S(1)} %get-tuple-element.147.stat_ref.stat2_ref.stat02_ref, ...), custom_call_target="tpu_custom_call" | custom-call | flops 20000000000 | bytes 60000000 | tf_op jit(solution)/shard_map/pallas_call | solution.py:1077
  281.6 4.1 %all-to-all-done.13 = f32[16,12,8,128]{3,2,1,0:T(8,128)} async-done(((f32[16,12,8,128]{3,2,1,0:T(8,128)}), f32[16,12,8,128]{3,2,1,0:T(8,128)}, u32[]{:S(2)}, u32[]{:S(2)}) %all-to-all-start.13) | async-done | bytes 786464 | tf_op jit(solution)/shard_map/all_to_all | solution.py:1055
  285.7 1.2 reduce_sum.38
  286.8 1.0 broadcast_in_dim.13
  287.8 6.1 %all-to-all-start.14 = ((f32[16,12,8,128]{3,2,1,0:T(8,128)}), f32[16,12,8,128]{3,2,1,0:T(8,128)}, u32[]{:S(2)}, u32[]{:S(2)}) async-start(f32[16,12,8,128]{3,2,1,0:T(8,128)} %broadcast_in_dim.13), calls=%async_computation.14 | async-start | bytes 1572864 | tf_op jit(solution)/shard_map/all_to_all | solution.py:1060
  293.9 14.5 %shard_map.324 = (f32[2048,128]{1,0:T(8,128)}, f32[32,2,640]{2,1,0:T(2,128)}, f32[128,8,128]{2,1,0:T(8,128)S(1)}, f32[8,256]{1,0:T(8,128)S(1)}) custom-call(s32[2]{0:T(128)S(1)} %copy-done.15, f32[32,2,640]{2,1,0:T(2,128)S(1)} %all-to-all-done.12.grads_ref, f32[8,640]{1,0:T(8,128)S(1)} %get-tuple-element.147.stat_ref.stat2_ref.stat02_ref, ...), custom_call_target="tpu_custom_call" | custom-call | flops 20000000000 | bytes 60000000 | tf_op jit(solution)/shard_map/pallas_call | solution.py:1077
  308.4 7.6 %all-to-all-done.14 = f32[16,12,8,128]{3,2,1,0:T(8,128)} async-done(((f32[16,12,8,128]{3,2,1,0:T(8,128)}), f32[16,12,8,128]{3,2,1,0:T(8,128)}, u32[]{:S(2)}, u32[]{:S(2)}) %all-to-all-start.14) | async-done | bytes 786464 | tf_op jit(solution)/shard_map/all_to_all | solution.py:1060
  316.7 2.6 all-to-all-start.15
  319.3 8.4 %all-to-all-done.15.zero_ref = f32[32,2,640]{2,1,0:T(2,128)S(1)} async-done(((f32[32,2,640]{2,1,0:T(2,128)}), f32[32,2,640]{2,1,0:T(2,128)S(1)}, u32[]{:S(2)}, u32[]{:S(2)}) %all-to-all-start.15) | async-done | bytes 163872 | tf_op jit(solution)/shard_map/all_to_all | solution.py:1033
  327.8 14.2 %all_to_all.95 = f32[16,4,8,128]{3,2,1,0:T(8,128)S(1)} all-to-all(f32[16,4,8,128]{3,2,1,0:T(8,128)S(1)} %bitcast.49), channel_id=1, replica_groups=mesh['dp'=4,'z'=4,'core'=2] {'dp','z'}, dimensions={0} | all-to-all | bytes 524288 | tf_op jit(solution)/shard_map/all_to_all | solution.py:1055
  342.7 3.5 all-to-all-start.17
  346.9 9.0 %all-to-all-done.17 = f32[16,4,8,128]{3,2,1,0:T(8,128)S(1)} async-done(((f32[16,4,8,128]{3,2,1,0:T(8,128)}), f32[16,4,8,128]{3,2,1,0:T(8,128)S(1)}, u32[]{:S(2)}, u32[]{:S(2)}) %all-to-all-start.17) | async-done | bytes 262176 | tf_op jit(solution)/shard_map/all_to_all | solution.py:1060
  355.9 7.8 %shard_map.325 = (f32[112,2048]{1,0:T(8,128)}, f32[2,112,640]{2,1,0:T(8,128)S(1)}, f32[16,640]{1,0:T(8,128)S(1)}, f32[4,640]{1,0:T(4,128)}, f32[4,640]{1,0:T(4,1...) custom-call(s32[2]{0:T(128)S(1)} %copy-done.15, ...), custom_call_target="tpu_custom_call" | custom-call | flops 10000000000 | bytes 30000000 | tf_op jit(solution)/shard_map/pallas_call | solution.py:1077
  363.7 3.2 shard_map.326
  (67 shorter events, 4.9 us)
Async XLA Ops:
  0.7 1.1 copy-start.2
  1.7 0.9 copy-start.5
  2.7 0.7 copy-start.14
  3.3 13.7 %copy-start.17 = (f32[2,45,640]{2,0,1:T(2,128)S(1)}, f32[2,45,640]{2,0,1:T(2,128)}, u32[]{:S(2)}) copy-start(f32[2,45,640]{2,0,1:T(2,128)} %param.27) | copy-start | bytes 691204
  3.3 22.4 %copy-start.3 = (f32[2,640,112]{1,2,0:T(8,128)S(1)}, f32[2,640,112]{1,2,0:T(8,128)}, u32[]{:S(2)}) copy-start(f32[2,640,112]{1,2,0:T(8,128)} %param.22) | copy-start | bytes 1720324
  3.3 22.4 %copy-start.6 = (f32[4,640]{1,0:T(4,128)S(1)}, f32[4,640]{1,0:T(4,128)}, u32[]{:S(2)}) copy-start(f32[4,640]{1,0:T(4,128)} %bias_ref.17) | copy-start | bytes 30724
  3.3 22.4 %copy-start.7 = (f32[4,640]{1,0:T(4,128)S(1)}, f32[4,640]{1,0:T(4,128)}, u32[]{:S(2)}) copy-start(f32[4,640]{1,0:T(4,128)} %gain_ref.19) | copy-start | bytes 30724
  3.3 22.4 %copy-start.15 = (s32[2]{0:T(128)S(1)}, s32[2]{0:T(128)}, u32[]{:S(2)}) copy-start(s32[2]{0:T(128)} %counts_ref.23) | copy-start | bytes 28
  9.7 16.1 %all-to-all-start = ((f32[32,2,768]{2,1,0:T(2,128)}), f32[32,2,768]{2,1,0:T(2,128)S(1)}, u32[]{:S(2)}, u32[]{:S(2)}) async-start(f32[32,2,768]{2,1,0:T(2,128)} %get-tuple-element.115), calls=%async_computation | async-start | bytes 393216 | tf_op jit(solution)/shard_map/all_to_all | solution.py:1033
  25.8 31.8 %copy-start = (f32[2,160,640]{2,1,0:T(8,128)S(1)}, f32[2,160,640]{2,1,0:T(8,128)}, u32[]{:S(2)}) copy-start(f32[2,160,640]{2,1,0:T(8,128)} %down_ref.7) | copy-start | bytes 2457604
  25.8 31.8 %copy-start.1 = (f32[2,112,640]{2,1,0:T(8,128)S(1)}, f32[2,112,640]{2,1,0:T(8,128)}, u32[]{:S(2)}) copy-start(f32[2,112,640]{2,1,0:T(8,128)} %proj_ref.7) | copy-start | bytes 1720324
  25.8 31.8 %copy-start.10 = (f32[2,640]{1,0:T(2,128)S(1)}, f32[2,640]{1,0:T(2,128)}, u32[]{:S(2)}) copy-start(f32[2,640]{1,0:T(2,128)} %upb_ref.3) | copy-start | bytes 15364
  25.8 31.8 %copy-start.11 = (f32[2,160]{1,0:T(2,128)S(1)}, f32[2,160]{1,0:T(2,128)}, u32[]{:S(2)}) copy-start(f32[2,160]{1,0:T(2,128)} %downb_ref.3) | copy-start | bytes 3844
  57.6 15.5 %copy-start.18 = (f32[2,112]{1,0:T(2,128)S(1)}, f32[2,112]{1,0:T(2,128)}, u32[]{:S(2)}) copy-start(f32[2,112]{1,0:T(2,128)} %param.25) | copy-start | bytes 2692
  57.6 15.5 %copy-start.19 = (f32[2,112]{1,0:T(2,128)S(1)}, f32[2,112]{1,0:T(2,128)}, u32[]{:S(2)}) copy-start(f32[2,112]{1,0:T(2,128)} %param.26) | copy-start | bytes 2692
  70.5 9.8 %all-to-all-start.2 = ((f32[32,2,128]{2,1,0:T(2,128)}), f32[32,2,128]{2,1,0:T(2,128)S(1)}, u32[]{:S(2)}, u32[]{:S(2)}) async-start(f32[32,2,128]{2,1,0:T(2,128)} %get-tuple-element.121), calls=%async_computation.2 | async-start | bytes 65536 | tf_op jit(solution)/shard_map/all_to_all | solution.py:1033
  96.3 13.9 %all-to-all-start.4 = ((f32[32,2,8,128]{3,2,1,0:T(8,128)}), f32[32,2,8,128]{3,2,1,0:T(8,128)S(1)}, u32[]{:S(2)}, u32[]{:S(2)}) async-start(f32[32,2,8,128]{3,2,1,0:T(8,128)} %bitcast.2), calls=%async_computation.4 | async-start | bytes 524288 | tf_op jit(solution)/shard_map/all_to_all | solution.py:1055
  132.1 10.0 %all-to-all-start.6 = ((f32[32,4,128]{2,1,0:T(4,128)}), f32[32,4,128]{2,1,0:T(4,128)S(1)}, u32[]{:S(2)}, u32[]{:S(2)}) async-start(f32[32,4,128]{2,1,0:T(4,128)} %get-tuple-element.135), calls=%async_computation.6 | async-start | bytes 131072 | tf_op jit(solution)/shard_map/all_to_all | solution.py:1033
  152.3 16.3 %copy-start.16 = (f32[288,8,128]{2,1,0:T(8,128)S(1)}, f32[288,8,128]{2,1,0:T(8,128)}, u32[]{:S(2)}) copy-start(f32[288,8,128]{2,1,0:T(8,128)} %get-tuple-element.149) | copy-start | bytes 3538948
  153.5 15.1 %collective-permute-start = (f32[144,8,128]{2,1,0:T(8,128)S(1)}, f32[144,8,128]{2,1,0:T(8,128)}, u32[]{:S(2)}, u32[]{:S(2)}) collective-permute-start(f32[144,8,128]{2,1,0:T(8,128)S(1)} %dynamic-slice_bitcast_fusion.1), channel_id=1, source_target_pairs={{0,1},{1,0},{2,3},{3,2},{4,5},{5,4},{6,7},{7,6},{8,9},{9,8},{10,11... | collective-permute-start | bytes 1769480 | tf_op jit(solution)/shard_map/ppermute | solution.py:1041
  165.8 14.8 %copy-start.4 = (f32[2,640,112]{1,2,0:T(8,128)S(1)}, f32[2,640,112]{1,2,0:T(8,128)}, u32[]{:S(2)}) copy-start(f32[2,640,112]{1,2,0:T(8,128)} %param.22) | copy-start | bytes 1720324
  165.8 11.2 %all-to-all-start.8 = ((f32[32,2,640]{2,1,0:T(2,128)}), f32[32,2,640]{2,1,0:T(2,128)S(1)}, u32[]{:S(2)}, u32[]{:S(2)}) async-start(f32[32,2,640]{2,1,0:T(2,128)} %get-tuple-element.148), calls=%async_computation.8 | async-start | bytes 327680 | tf_op jit(solution)/shard_map/all_to_all | solution.py:1033
  177.0 23.0 %all-to-all-start.9 = ((f32[16,9,8,128]{3,2,1,0:T(8,128)}), f32[16,9,8,128]{3,2,1,0:T(8,128)S(1)}, u32[]{:S(2)}, u32[]{:S(2)}) async-start(f32[16,9,8,128]{3,2,1,0:T(8,128)} %bitcast.7), calls=%async_computation.9 | async-start | bytes 1179648 | tf_op jit(solution)/shard_map/all_to_all | solution.py:1055
  216.5 27.9 %all-to-all-start.11 = ((f32[16,9,8,128]{3,2,1,0:T(8,128)}), f32[16,9,8,128]{3,2,1,0:T(8,128)S(1)}, u32[]{:S(2)}, u32[]{:S(2)}) async-start(f32[16,9,8,128]{3,2,1,0:T(8,128)} %broadcast_in_dim.12), calls=%async_computation.11 | async-start | bytes 1179648 | tf_op jit(solution)/shard_map/all_to_all | solution.py:1060
  243.7 6.4 %collective-permute-start.1 = (f32[192,8,128]{2,1,0:T(8,128)}, f32[192,8,128]{2,1,0:T(8,128)S(1)}, u32[]{:S(2)}, u32[]{:S(2)}) collective-permute-start(f32[192,8,128]{2,1,0:T(8,128)} %dynamic-slice_bitcast_fusion), channel_id=1, source_target_pairs={{0,1},{1,0},{2,3},{3,2},{4,5},{5,4},{6,7},{7,6},{8,9},{9,8},{10,11... | collective-permute-start | bytes 2359304 | tf_op jit(solution)/shard_map/ppermute | solution.py:1041
  244.4 14.1 %collective-permute-start.2 = (f32[144,8,128]{2,1,0:T(8,128)S(1)}, f32[144,8,128]{2,1,0:T(8,128)}, u32[]{:S(2)}, u32[]{:S(2)}) collective-permute-start(f32[144,8,128]{2,1,0:T(8,128)S(1)} %bitcast.28), channel_id=1, source_target_pairs={{0,1},{1,0},{2,3},{3,2},{4,5},{5,4},{6,7},{7,6},{8,9},{9,8},{10,11... | collective-permute-start | bytes 1769480 | tf_op jit(solution)/shard_map/ppermute | solution.py:1041
  244.4 14.1 %all-to-all-start.12 = ((f32[32,2,640]{2,1,0:T(2,128)}), f32[32,2,640]{2,1,0:T(2,128)S(1)}, u32[]{:S(2)}, u32[]{:S(2)}) async-start(f32[32,2,640]{2,1,0:T(2,128)} %get-tuple-element.167), calls=%async_computation.12 | async-start | bytes 327680 | tf_op jit(solution)/shard_map/all_to_all | solution.py:1033
  258.5 27.2 %all-to-all-start.13 = ((f32[16,12,8,128]{3,2,1,0:T(8,128)}), f32[16,12,8,128]{3,2,1,0:T(8,128)}, u32[]{:S(2)}, u32[]{:S(2)}) async-start(f32[16,12,8,128]{3,2,1,0:T(8,128)} %bitcast.12), calls=%async_computation.13 | async-start | bytes 1572864 | tf_op jit(solution)/shard_map/all_to_all | solution.py:1055
  287.8 28.3 %all-to-all-start.14 = ((f32[16,12,8,128]{3,2,1,0:T(8,128)}), f32[16,12,8,128]{3,2,1,0:T(8,128)}, u32[]{:S(2)}, u32[]{:S(2)}) async-start(f32[16,12,8,128]{3,2,1,0:T(8,128)} %broadcast_in_dim.13), calls=%async_computation.14 | async-start | bytes 1572864 | tf_op jit(solution)/shard_map/all_to_all | solution.py:1060
  316.1 11.7 %collective-permute-start.4 = (f32[192,8,128]{2,1,0:T(8,128)}, f32[192,8,128]{2,1,0:T(8,128)}, u32[]{:S(2)}, u32[]{:S(2)}) collective-permute-start(f32[192,8,128]{2,1,0:T(8,128)} %bitcast.13.pack0_ref), channel_id=1, source_target_pairs={{0,1},{1,0},{2,3},{3,2},{4,5},{5,4},{6,7},{7,6},{8,9},{9,8},{10,11... | collective-permute-start | bytes 2359304 | tf_op jit(solution)/shard_map/ppermute | solution.py:1041
  316.1 39.8 %copy-start.8 = (f32[4,640]{1,0:T(4,128)S(1)}, f32[4,640]{1,0:T(4,128)}, u32[]{:S(2)}) copy-start(f32[4,640]{1,0:T(4,128)} %means_ref.1) | copy-start | bytes 30724
  316.1 39.8 %copy-start.9 = (f32[4,640]{1,0:T(4,128)S(1)}, f32[4,640]{1,0:T(4,128)}, u32[]{:S(2)}) copy-start(f32[4,640]{1,0:T(4,128)} %vars_ref.1) | copy-start | bytes 30724
  316.1 39.8 %copy-start.12 = (f32[2,112]{1,0:T(2,128)S(1)}, f32[2,112]{1,0:T(2,128)}, u32[]{:S(2)}) copy-start(f32[2,112]{1,0:T(2,128)} %nmeans_ref.1) | copy-start | bytes 2692
  316.1 39.8 %copy-start.13 = (f32[2,112]{1,0:T(2,128)S(1)}, f32[2,112]{1,0:T(2,128)}, u32[]{:S(2)}) copy-start(f32[2,112]{1,0:T(2,128)} %nvars_ref.1) | copy-start | bytes 2692
  316.1 3.1 collective-permute-start.3
  316.7 11.1 %all-to-all-start.15 = ((f32[32,2,640]{2,1,0:T(2,128)}), f32[32,2,640]{2,1,0:T(2,128)S(1)}, u32[]{:S(2)}, u32[]{:S(2)}) async-start(f32[32,2,640]{2,1,0:T(2,128)} %get-tuple-element.184), calls=%async_computation.15 | async-start | bytes 327680 | tf_op jit(solution)/shard_map/all_to_all | solution.py:1033
  342.7 13.2 %all-to-all-start.17 = ((f32[16,4,8,128]{3,2,1,0:T(8,128)}), f32[16,4,8,128]{3,2,1,0:T(8,128)S(1)}, u32[]{:S(2)}, u32[]{:S(2)}) async-start(f32[16,4,8,128]{3,2,1,0:T(8,128)} %broadcast_in_dim.14), calls=%async_computation.17 | async-start | bytes 524288 | tf_op jit(solution)/shard_map/all_to_all | solution.py:1060
  355.9 7.8 %collective-permute-start.5 = (f32[64,8,128]{2,1,0:T(8,128)S(1)}, f32[64,8,128]{2,1,0:T(8,128)S(1)}, u32[]{:S(2)}, u32[]{:S(2)}) collective-permute-start(f32[64,8,128]{2,1,0:T(8,128)S(1)} %bitcast.34), channel_id=1, source_target_pairs={{0,1},{1,0},{2,3},{3,2},{4,5},{5,4},{6,7},{7,6},{8,9},{9,8},{10,11... | collective-permute-start | bytes 786440 | tf_op jit(solution)/shard_map/ppermute | solution.py:1041
where the time goes:
time: 370 us; the launch traced here: 368 us
  Pallas kernels  156 us (42%)
  blocking collectives  81.3 us (22%)
  waiting for transfers between devices  65.3 us (18%)
  starting transfers between devices  48.8 us (13%)
  local copies, waits for them, and re-layouts  9.43 us (3%)
  other arithmetic  5.42 us (1%)
    pallas_call x13, Pallas kernels, call(): pl.pallas_call(kernel, grid=grid, in_specs=in_specs, out_specs=out_specs,...  156 us
    all_to_all x4, blocking collectives, exchange(): return lax.all_to_all(send, AXES, 0, 0, tiled=True)  55 us
    all_to_all x6, waiting for transfers between devices, exchange(): return lax.all_to_all(send, AXES, 0, 0, tiled=True)  44.5 us
    all_to_all x6, starting transfers between devices, exchange(): return lax.all_to_all(send, AXES, 0, 0, tiled=True)  23.3 us
    all_to_all x3, waiting for transfers between devices, share_back(): lax.all_to_all(jnp.broadcast_to(own[None], pieces.shape), names, 0, 0, ti...  16.7 us
    all_to_all x1, blocking collectives, share_out(): lax.all_to_all(tiles.reshape(count, -1, *tiles.shape[1:]), names, 0, 0, t...  14.2 us
    all_to_all x3, starting transfers between devices, share_back(): lax.all_to_all(jnp.broadcast_to(own[None], pieces.shape), names, 0, 0, ti...  13.5 us
    all_to_all x1, blocking collectives, share_back(): lax.all_to_all(jnp.broadcast_to(own[None], pieces.shape), names, 0, 0, ti...  12.1 us
  transfers between devices with their start and end apart: 18, of which 9 were waited for; matrix products, arithmetic and copies ran while one was open for 2% of the time, Pallas kernels for 25%

commit v1 on v0

--- a/solution.py
+++ b/solution.py
@@ -232,7 +232,7 @@
 
 
 def row_total(ref, lanes=None):
-    values = ref[...] if lanes is None else ref[:, :, lanes]
+    values = ref[...] if lanes is None or lanes == slice(None) else ref[:, :, lanes]
     return jnp.sum(values, axis=0)
 
 
@@ -421,13 +421,19 @@
     return lax.fori_loop(0, count, body, init, unroll=unroll)
 
 
+def lanes_of(ref, tile):
+    if ref.shape[-1] == LANES:
+        return slice(None)
+    return pl.ds(pl.multiple_of(tile * LANES, LANES), LANES)
+
+
 def squeeze_forward_kernel(
     block, counts_ref, sums_ref, stat_ref, d_ref, gain_ref, bias_ref, down_ref, downb_ref, up_ref, upb_ref, proj_ref,
     cot_ref, z_ref, gates_ref, running_ref, pre_ref, stat_out_ref, send_ref, second_ref, pooled_ref,
 ):
-    phase = pl.program_id(0)
-    tile = pl.program_id(1)
-    tiles = pl.num_programs(1)
+    step = pl.program_id(0)
+    steps = pl.num_programs(0)
+    tiles = second_ref.shape[0]
     total = live_frames(counts_ref)
     per_frame = HALF_ROWS if block else FULL_ROWS
     pixels = per_frame * 8
@@ -436,46 +442,40 @@
     chunks = frames // group
     norm_row = 2 * block + 1
 
-    @pl.when(phase == 0)
-    def activate():
-        count = stat_ref[2:3, 0:LANES] * (0.25 if block else 1.0)
-        average, variance = moments_of(row_total(sums_ref), count)
-        stat_out_ref[...] = rows8(average, variance, count)
-        scale = gain_ref[norm_row : norm_row + 1, :] * lax.rsqrt(variance + EPSILON)
-        shift = 0.5 * (bias_ref[norm_row : norm_row + 1, :] - average * scale)
+    def activate(tile, carry):
+        lanes = lanes_of(d_ref, tile)
+        count = stat_ref[2:3, lanes] * (0.25 if block else 1.0)
+        average, variance = moments_of(row_total(sums_ref, lanes), count)
+        stat_out_ref[:, lanes] = rows8(average, variance, count)
+        scale = gain_ref[norm_row : norm_row + 1, lanes] * lax.rsqrt(variance + EPSILON)
+        shift = 0.5 * (bias_ref[norm_row : norm_row + 1, lanes] - average * scale)
         scale = 0.5 * scale
 
-        def chunk(index, carry):
+        def chunk(index, inside):
             for inner in range(group):
                 t = index * group + inner
                 at = pl.ds(t * per_frame, per_frame)
-                half_pre = d_ref[at] * scale + shift
+                half_pre = d_ref[at, :, lanes] * scale + shift
                 second = half_pre + half_pre * half_tanh(half_pre)
                 second = second * live_value(t, total)
                 second_ref[tile, at] = second
                 pooled_ref[tile, pl.ds(t, 1), :] = tile_sum(second) * (1.0 / pixels)
-            return carry
+            return inside
 
         each_frame(chunks, chunk, 0)
-
-    @pl.when((phase == 1) & (tile == 0))
-    def gate():
-        matrix = running_matrix(counts_ref, frames)
-        pooled = jnp.concatenate([pooled_ref[index] for index in range(pooled_ref.shape[0])], axis=1)
-        running = exact_dot(matrix, pooled)
-        running_ref[...] = running
-        pre = skinny_dot(running, down_ref[0], NT) + downb_ref[block : block + 1, :]
-        pre_ref[...] = pre
-        gates_ref[...] = sigmoid(skinny_dot(pre * sigmoid(pre), up_ref[0]) + upb_ref[block : block + 1, :])
-        z_ref[...] = jnp.zeros_like(z_ref)
-
-    @pl.when(phase == 1)
-    def project():
-        square = right_square_t(pad_rows(proj_ref[0]))
-        lanes = pl.ds(pl.multiple_of(tile * LANES, LANES), LANES)
+        return carry
+
+    if block:
+        lax.fori_loop(0, tiles, activate, 0)
+    else:
+        activate(step, 0)
+
+    def project(tile, carry):
+        lanes = lanes_of(gates_ref, tile)
+        square = right_square_t(pad_rows(proj_ref[0, :, lanes]))
         gates = gates_ref[:, lanes]
 
-        def chunk(index, carry):
+        def chunk(index, inside):
             parts = []
             for inner in range(group):
                 t = index * group + inner
@@ -484,12 +484,23 @@
             excited = parts[0] if group == 1 else jnp.concatenate(parts, axis=0)
             at = pl.ds(pl.multiple_of(index * 256, 256), 256)
             z_ref[at, :] = z_ref[at, :] + fold_right(plain_dot(side_by_side(excited), square, NT))
-            return carry
+            return inside
 
         each_frame(chunks, chunk, 0)
-
-    @pl.when((phase == 1) & (tile == tiles - 1))
-    def finish():
+        return carry
+
+    @pl.when(step == steps - 1)
+    def gate_and_project():
+        matrix = running_matrix(counts_ref, frames)
+        pooled = jnp.concatenate([pooled_ref[index] for index in range(tiles)], axis=1)
+        running = exact_dot(matrix, pooled)
+        running_ref[...] = running
+        pre = skinny_dot(running, down_ref[0], NT) + downb_ref[block : block + 1, :]
+        pre_ref[...] = pre
+        gates_ref[...] = sigmoid(skinny_dot(pre * sigmoid(pre), up_ref[0]) + upb_ref[block : block + 1, :])
+        z_ref[...] = jnp.zeros_like(z_ref)
+        lax.fori_loop(0, tiles, project, 0)
+
         def chunk(index, carry):
             at = pl.ds(pl.multiple_of(index * 256, 256), 256)
             z = z_ref[at, :].reshape(32, 8, LANES)
@@ -513,8 +524,6 @@
     block, counts_ref, stat_ref, d_ref, gain_ref, bias_ref, down_ref, up_ref, proj_ref, gates_ref, running_ref,
     pre_ref, dy2_ref, send_ref, pack_ref, dz3_ref, dz3t_ref, excited_ref, dexc_ref, dgate_ref, head,
 ):
-    phase = pl.program_id(0)
-    tile = pl.program_id(1)
     total = live_frames(counts_ref)
     per_frame = HALF_ROWS if block else FULL_ROWS
     pixels = per_frame * 8
@@ -526,31 +535,28 @@
     narrow = proj_ref.shape[1]
     squeeze = down_ref.shape[1]
     per_tile = pack_tiles(narrow, squeeze)
-    lanes = pl.ds(pl.multiple_of(tile * LANES, LANES), LANES)
-
-    @pl.when((phase == 0) & (tile == 0))
-    def start():
-        head()
-
-    average = stat_ref[0:1, :]
-    root = lax.rsqrt(stat_ref[1:2, :] + EPSILON)
-    scale = gain_ref[norm_row : norm_row + 1, :] * root
-    shift = 0.5 * (bias_ref[norm_row : norm_row + 1, :] - average * scale)
-    scale = 0.5 * scale
-    gates = gates_ref[:, lanes]
-
-    @pl.when(phase == 0)
-    def excite():
-        square = right_square(pad_rows(proj_ref[0]))
-
-        def chunk(index, carry):
+
+    def norm_of(tile):
+        lanes = lanes_of(d_ref, tile)
+        average = stat_ref[0:1, lanes]
+        root = lax.rsqrt(stat_ref[1:2, lanes] + EPSILON)
+        scale = gain_ref[norm_row : norm_row + 1, lanes] * root
+        shift = 0.5 * (bias_ref[norm_row : norm_row + 1, lanes] - average * scale)
+        return (lanes, average, root, 0.5 * scale, shift)
+
+    def excite(tile, carry):
+        lanes, _, _, scale, shift = norm_of(tile)
+        gates = gates_ref[:, lanes_of(gates_ref, tile)]
+        square = right_square(pad_rows(proj_ref[0, :, lanes]))
+
+        def chunk(index, inside):
             flat = pl.ds(pl.multiple_of(index * 256, 256), 256)
             dexc = fold_right(plain_dot(dz3_ref[flat, :], square)).reshape(32, 8, LANES)
             dexc_ref[tile, pl.ds(pl.multiple_of(index * 32, 32), 32)] = dexc
             parts = []
             for inner in range(group):
                 t = index * group + inner
-                half_pre = d_ref[pl.ds(t * per_frame, per_frame)] * scale + shift
+                half_pre = d_ref[pl.ds(t * per_frame, per_frame), :, lanes] * scale + shift
                 second = half_pre + half_pre * half_tanh(half_pre)
                 second = second * live_value(t, total)
                 own = dexc[inner * per_frame : (inner + 1) * per_frame]
@@ -558,13 +564,13 @@
                 parts.append(second.reshape(pixels, LANES) * pick_row(gates, t))
             excited = parts[0] if group == 1 else jnp.concatenate(parts, axis=0)
             excited_ref[flat, :] = side_by_side(excited)
-            return carry
+            return inside
 
         each_frame(chunks, chunk, 0)
         dproj = fold_square(plain_dot(dz3t_ref[...], excited_ref[...]))
         pack_ref[pl.ds(tile * per_tile, narrow // 8)] = dproj[0:narrow].reshape(narrow // 8, 8, LANES)
-
-    @pl.when((phase == 1) & (tile == 0))
+        return carry
+
     def squeeze_part():
         pre = pre_ref[...]
         half_pre = 0.5 * pre
@@ -591,19 +597,21 @@
         for index in range(tiles):
             dgate_ref[index] = dpooled[:, index * LANES : (index + 1) * LANES]
 
-    @pl.when(phase == 1)
-    def slope():
-        def chunk(index, carry):
-            summed, cross = carry
+    def slope(tile, carry):
+        lanes, average, root, scale, shift = norm_of(tile)
+        gates = gates_ref[:, lanes_of(gates_ref, tile)]
+
+        def chunk(index, inside):
+            summed, cross = inside
             for inner in range(group):
                 t = index * group + inner
                 at = pl.ds(t * per_frame, per_frame)
-                depth = d_ref[at]
+                depth = d_ref[at, :, lanes]
                 half_pre = depth * scale + shift
                 dsecond = dexc_ref[tile, at] * pick_row(gates, t) + pick_row(dgate_ref[tile], t)
                 dy = dsecond * silu_slope(half_pre, half_tanh(half_pre))
                 dy = dy * live_value(t, total)
-                dy2_ref[at] = dy
+                dy2_ref[at, :, lanes] = dy
                 summed = summed + jnp.sum(dy, axis=0)
                 cross = cross + jnp.sum(dy * (depth - average), axis=0)
             return (summed, cross)
@@ -611,7 +619,33 @@
         zero = jnp.zeros((8, LANES), F32)
         summed, cross = each_frame(chunks, chunk, (zero, zero))
         rows = stack_rows(jnp.sum(summed, axis=0, keepdims=True), root * jnp.sum(cross, axis=0, keepdims=True))
-        send_all(send_ref, rows, slice(0, LANES))
+        send_all(send_ref, rows, lanes)
+        return carry
+
+    if block:
+        head()
+        lax.fori_loop(0, tiles, excite, 0)
+        squeeze_part()
+        lax.fori_loop(0, tiles, slope, 0)
+    else:
+        phase = pl.program_id(0)
+        tile = pl.program_id(1)
+
+        @pl.when((phase == 0) & (tile == 0))
+        def start():
+            head()
+
+        @pl.when(phase == 0)
+        def first():
+            excite(tile, 0)
+
+        @pl.when((phase == 1) & (tile == 0))
+        def between():
+            squeeze_part()
+
+        @pl.when(phase == 1)
+        def second():
+            slope(tile, 0)
 
 
 def squeeze_one_backward_kernel(
@@ -623,7 +657,7 @@
     pixels = HALF_ROWS * 8
 
     def head():
-        count = stat_ref[2:3, :]
+        count = stat_ref[2:3, 0:LANES]
         sums = row_total(third_ref)
         mean, variance = moments_of(sums, count)
         root = lax.rsqrt(variance + EPSILON)
@@ -976,7 +1010,7 @@
 
 
 def gradient_kernel(
-    core_ref, pack0_ref, pack0_other_ref, pack1_ref, pack1_other_ref, late_ref, late_other_ref, less_ref, factor_ref,
+    core_ref, pack0_ref, pack0_other_ref, pack1_ref, late_ref, late_other_ref, less_ref, factor_ref,
     dw_ref, dtaps_ref, ddown_ref, dup_ref, dproj_ref, dupb_ref, ddownb_ref,
 ):
     narrow = dw_ref.shape[1]
@@ -989,6 +1023,8 @@
 
     def rows_of(pair, at, count):
         mine, other = pair
+        if other is None:
+            return mine[at : at + count].reshape(-1, LANES)
         half = mine.shape[0]
         pieces = []
         if at < half:
@@ -1003,7 +1039,7 @@
         values = pieces[0] if len(pieces) == 1 else jnp.concatenate(pieces, axis=0)
         return values.reshape(-1, LANES)
 
-    packs = ((pack0_ref, pack0_other_ref), (pack1_ref, pack1_other_ref))
+    packs = ((pack0_ref, pack0_other_ref), (pack1_ref, None))
     lists = ((late_ref, late_other_ref), packs[0])
     for block in range(2):
         down_rows = []
@@ -1073,7 +1109,7 @@
 SCALARS = pl.BlockSpec(memory_space=pltpu.SMEM)
 
 
-def call(kernel, grid, in_specs, out_specs, out_shape, scratch, args, micros=10):
+def call(kernel, grid, in_specs, out_specs, out_shape, scratch, args):
     return pl.pallas_call(
         kernel,
         grid=grid,
@@ -1083,7 +1119,7 @@
         scratch_shapes=scratch,
         compiler_params=pltpu.CompilerParams(vmem_limit_bytes=VMEM_BYTES),
         cost_estimate=pl.CostEstimate(
-            flops=micros * 1_000_000_000, bytes_accessed=micros * 3_000_000, transcendentals=0
+            flops=1_000_000_000, bytes_accessed=1_000_000, transcendentals=0
         ),
     )(*args)
 
@@ -1188,13 +1224,16 @@
     def squeeze_forward(block, sums, stat, depth):
         rows = half_rows if block else full_rows
         kinds = 4 if block else 2
+        moving = [tile_sums(), tile_rows(8), tile_cube(rows), tile_rows(4), tile_rows(4)]
+        if block:
+            moving = [whole(array) for array in (sums, stat, depth, wide_gains, wide_biases)]
         return call(
-            functools.partial(squeeze_forward_kernel, block), (2, tiles),
-            [SCALARS, early(sums_at(2)), early(rows_at(8)), early(cube_at(rows)), early(rows_at(4)), early(rows_at(4)),
-             of_block(block, squeeze, width), whole(squeeze_bias), of_block(block, squeeze, width), whole(excite_bias),
-             late(weight_at(block, cin)), whole(cot)],
-            [fixed(rows * 8, LANES), fixed(8, width), fixed(8, width), fixed(8, squeeze), early(rows_at(8)),
-             fixed(devices, kinds, LANES)],
+            functools.partial(squeeze_forward_kernel, block), (1 if block else tiles,),
+            [SCALARS] + moving
+            + [of_block(block, squeeze, width), whole(squeeze_bias), of_block(block, squeeze, width), whole(excite_bias),
+               of_block(block, cin, width), whole(cot)],
+            [fixed(rows * 8, LANES), fixed(8, width), fixed(8, width), fixed(8, squeeze),
+             fixed(8, width) if block else tile_rows(8), fixed(devices, kinds, LANES)],
             [shape(rows * 8, LANES), shape(8, width), shape(8, width), shape(8, squeeze), shape(8, width),
              shape(devices, kinds, LANES)],
             [pltpu.VMEM((tiles, rows, 8, LANES), F32), pltpu.VMEM((tiles, frames, LANES), F32)],
@@ -1225,11 +1264,16 @@
 
     def backward_specs(block):
         rows = half_rows if block else full_rows
-        ins = [both(rows_at(8)), both(cube_at(rows)), both(rows_at(4)), both(rows_at(4)), of_block(block, squeeze, width),
-               of_block(block, squeeze, width), early(weight_at(block, cin)), fixed(8, width), fixed(8, width),
+        ins = [fixed(8, width), fixed(rows, 8, width), fixed(4, width), fixed(4, width), of_block(block, squeeze, width),
+               of_block(block, squeeze, width), of_block(block, cin, width), fixed(8, width), fixed(8, width),
                fixed(8, squeeze)]
-        packed = round_up(tiles * (pack_tiles(cin, squeeze) + (0 if block else q_tiles)))
-        outs = [fixed(8, LANES), late(cube_at(rows)), late(sums_at(2)), fixed(packed, 8, LANES)]
+        if not block:
+            ins[0:4] = [both(rows_at(8)), both(cube_at(rows)), both(rows_at(4)), both(rows_at(4))]
+            ins[6] = early(weight_at(block, cin))
+        packed = tiles * pack_tiles(cin, squeeze)
+        packed = packed if block else round_up(packed + tiles * q_tiles)
+        wide_outs = [fixed(rows, 8, width), fixed(devices, 2, width)] if block else [late(cube_at(rows)), late(sums_at(2))]
+        outs = [fixed(8, LANES)] + wide_outs + [fixed(packed, 8, LANES)]
         shapes = [shape(8, LANES), shape(rows, 8, width), shape(devices, 2, width), shape(packed, 8, LANES)]
         scratch = [pltpu.VMEM((rows * 8, 2 * LANES), low), pltpu.VMEM((2 * LANES, rows * 8), low),
                    pltpu.VMEM((rows * 8, 2 * LANES), low), pltpu.VMEM((tiles, rows, 8, LANES), F32),
@@ -1238,15 +1282,15 @@
 
     ins, outs, shapes, scratch = backward_specs(1)
     activations, nsum_one, dy2_one, sums, pack_one = call(
-        squeeze_one_backward_kernel, (2, tiles),
+        squeeze_one_backward_kernel, (1,),
         [SCALARS, whole(third), whole(z_one), whole(cot), whole(ngains), whole(nbiases)] + ins,
         [fixed(cin, half_pixels)] + outs, [shape(cin, half_pixels)] + shapes, scratch,
         (frame_counts, third, z_one, cot, ngains, nbiases, stat12, d_one, wide_gains, wide_biases, squeeze_weight, up_t,
          project_weight, gates_one, running_one, pre_one),
     )
     sums, gram = together(sums, gram)
-    sums, pack_one = together(exchange(sums), add_cores(pack_one))
-    pack_one = share_out(pack_one)
+    pack_one = lax.psum(pack_one, AXES)
+    sums = exchange(sums)
     nothing = jnp.zeros((8, LANES), F32)
 
     def depth_backward(block, begin, end, sums, stat2, stat, dy2, depth, expanded, columns, dx_in, sums_in, list_in):
@@ -1282,15 +1326,12 @@
              pltpu.VMEM((taps, 8, LANES), F32), pltpu.VMEM((taps, 8, LANES), F32), pltpu.VMEM((pixels, 2 * LANES), low)],
             (frame_counts, sums, stat2, stat, nstat, dy2, depth, expanded, columns, w_t, wide_gains, wide_biases,
              depth_weight, z_zero, dx_in, sums_in, list_in),
-            20,
         )
 
     dxpre_one, sums, q_one, grad_one = depth_backward(
         1, 0, tiles, sums, stat12, stat11, dy2_one, d_one, e_one, x1_columns, nothing, nothing, nothing
     )
-    sums, pack_one = together(sums, pack_one)
-    top_one, pack_one = together(exchange(sums), pack_one)
-    pack_one = share_back(pack_one)
+    top_one = exchange(sums)
     ins, outs, shapes, scratch = backward_specs(0)
     dx1, nsum_zero, dy2_zero, sums, pack_zero = call(
         squeeze_zero_backward_kernel, (2, tiles),
@@ -1300,9 +1341,7 @@
         (frame_counts, top_one, stat11, gram, nstat, dxpre_one, x1, z_zero, ngains, w_t, wide_gains, q_one, stat02, d_zero,
          wide_gains, wide_biases, squeeze_weight, up_t, project_weight, gates_zero, running_zero, pre_zero),
     )
-    sums, pack_one = together(sums, pack_one)
-    pack_one_other = swap_cores(pack_one)
-    sums, pack_zero, pack_one_other = together(exchange(sums), add_cores(pack_zero), pack_one_other)
+    sums, pack_zero = together(exchange(sums), add_cores(pack_zero))
     pack_zero = share_out(pack_zero)
     first = tiles - tiles // 2
     dxpre_zero, sums_in, late, grad_a = depth_backward(
@@ -1317,8 +1356,7 @@
     sums, pack_zero = together(sums, pack_zero)
     pack_zero_other = swap_cores(pack_zero)
     top_zero, late, pack_zero_other = together(exchange(sums), add_cores(late), pack_zero_other)
-    late = share_back(share_out(late))
-    late_other = swap_cores(late)
+    late = share_out(late)
     core = lax.axis_index("core").astype(jnp.int32).reshape(1)
     final_args = (
         frame_counts, momentum_index, gram, stat01, stat02, stat11, stat12, grad_zero, grad_one, top_one,
@@ -1332,9 +1370,12 @@
     video_grad, less, factor, wgain, wbias, ngain, nbias, newm, newv, newnm, newnv = simple_call(
         finish_kernel, 2, final_args, final_outs
     )
+    less, late = together(less, late)
+    late = share_back(late)
+    late_other = swap_cores(late)
     dw_t, dtaps, ddown, dup, dproj, dupb, ddownb = simple_call(
         gradient_kernel, 1,
-        (core, pack_zero, pack_zero_other, pack_one, pack_one_other, late, late_other, less, factor),
+        (core, pack_zero, pack_zero_other, pack_one, late, late_other, less, factor),
         [shape(2, cin, width), shape(2, taps, width), shape(2, squeeze, width), shape(2, squeeze, width),
          shape(2, cin, width), shape(2, width), shape(2, squeeze)],
     )

time: 370 us -> 475 us (1.28)
  waiting for transfers between devices: 65.3 us -> 192 us
  blocking collectives: 81.3 us -> 56.3 us
  between operations: 1.71 us -> 15.1 us
  starting transfers between devices: 48.8 us -> 39.8 us
    psum x0 -> x1, waiting for transfers between devices: none -> 127 us  [local(): pack_one = lax.psum(pack_one, AXES)]
    all_to_all x2 -> x0, blocking collectives: 26.2 us -> none  [the longest x1 14.2 us: share_out(): lax.all_to_all(tiles.reshape(count, -1, *tiles.shape[1:]), names, 0, 0, t...]
    all_to_all x6 -> x5, waiting for transfers between devices: 44.5 us -> 38.5 us  [exchange(): return lax.all_to_all(send, AXES, 0, 0, tiled=True)]
    all_to_all x6 -> x5, starting transfers between devices: 23.3 us -> 17.8 us  [exchange(): return lax.all_to_all(send, AXES, 0, 0, tiled=True)]
    all_to_all x4 -> x5, blocking collectives: 55 us -> 56.3 us  [exchange(): return lax.all_to_all(send, AXES, 0, 0, tiled=True)]
  transfers between devices with their start and end apart: 18 -> 16, of which waited for: 9 -> 11; matrix products, arithmetic and copies ran while one was open for 2% -> 1% of each run, Pallas kernels for 25% -> 14%
where the time goes in v1:
time: 475 us; the launch traced here: 472 us
  waiting for transfers between devices  192 us (40%)
  Pallas kernels  158 us (33%)
  blocking collectives  56.3 us (12%)
  starting transfers between devices  39.8 us (8%)
  between operations  15.1 us (3%)
  local copies, waits for them, and re-layouts  8.06 us (2%)
    pallas_call x13, Pallas kernels, call(): pl.pallas_call(kernel, grid=grid, in_specs=in_specs, out_specs=out_specs,...  158 us
    psum x1, waiting for transfers between devices, local(): pack_one = lax.psum(pack_one, AXES)  127 us
    all_to_all x5, blocking collectives, exchange(): return lax.all_to_all(send, AXES, 0, 0, tiled=True)  56.3 us
    all_to_all x5, waiting for transfers between devices, exchange(): return lax.all_to_all(send, AXES, 0, 0, tiled=True)  38.5 us
    all_to_all x3, waiting for transfers between devices, share_back(): lax.all_to_all(jnp.broadcast_to(own[None], pieces.shape), names, 0, 0, ti...  20.2 us
    all_to_all x5, starting transfers between devices, exchange(): return lax.all_to_all(send, AXES, 0, 0, tiled=True)  17.8 us
    all_to_all x3, starting transfers between devices, share_back(): lax.all_to_all(jnp.broadcast_to(own[None], pieces.shape), names, 0, 0, ti...  10.8 us
    all_to_all x3, starting transfers between devices, share_out(): lax.all_to_all(tiles.reshape(count, -1, *tiles.shape[1:]), names, 0, 0, t...  9.74 us
  transfers between devices with their start and end apart: 16, of which 11 were waited for; matrix products, arithmetic and copies ran while one was open for 1% of the time, Pallas kernels for 14%

profile of v1, /device:TPU:0, one launch (start us, length us, event | category | flops | bytes accessed | tf_op | source)
XLA Modules:
  0.0 471.7 jit_solution(17070301308942357354)
XLA Ops:
  7.2 1.1 copy-done
  8.9 0.9 copy-done.14
  9.9 6.4 %shard_map.314 = (f32[2048,128]{1,0:T(8,128)}, bf16[2048,256]{1,0:T(8,128)(2,1)}, bf16[256,2048]{1,0:T(8,128)(2,1)}, f32[512,128]{1,0:T(8,128)S(1)}, f32[136,128]{1,0:T(8,128)S(1)}, /*index=5*/f32[32,2,768]{2,1,0:T(2,128)}) custom-call(s32[2]{0:T(128)S(1)} %copy-done.6, f32[112,2048]{1,0:T(8,128)} %video_ref.1, f32[112,512]{1,0:T(8,128)S(1)} %copy-done.14, ...), custom_call_target="tpu_custom_call" | custom-call | flops 1000000000 | bytes 1000000 | tf_op jit(solution)/shard_map/pallas_call | solution.py:1113
  16.2 7.3 %all-to-all-start = ((f32[32,2,768]{2,1,0:T(2,128)}), f32[32,2,768]{2,1,0:T(2,128)S(1)}, u32[]{:S(2)}, u32[]{:S(2)}) async-start(f32[32,2,768]{2,1,0:T(2,128)} %get-tuple-element.108), calls=%async_computation | async-start | bytes 393216 | tf_op jit(solution)/shard_map/all_to_all | solution.py:1069
  23.6 8.7 %all-to-all-done.sums_ref.count_ref = f32[32,2,768]{2,1,0:T(2,128)S(1)} async-done(((f32[32,2,768]{2,1,0:T(2,128)}), f32[32,2,768]{2,1,0:T(2,128)S(1)}, u32[]{:S(2)}, u32[]{:S(2)}) %all-to-all-start) | async-done | bytes 196640 | tf_op jit(solution)/shard_map/all_to_all | solution.py:1069
  32.3 19.4 %shard_map.315 = (f32[256,8,640]{2,1,0:T(8,128)}, f32[256,8,640]{2,1,0:T(8,128)}, f32[8,640]{1,0:T(8,128)S(1)}, f32[32,2,640]{2,1,0:T(2,128)S(1)}) custom-call(s32[2]{0:T(128)S(1)} %copy-done.7, f32[32,2,768]{2,1,0:T(2,128)S(1)} %all-to-all-done.sums_ref.count_ref, f32[32,2,768]{2,1,0:T(2,128)S(1)} %all-to-all-done.sums_ref.count_ref, ...), custom_call_target="tpu_custom_call" | custom-call | flops 1000000000 | bytes 1000000 | tf_op jit(solution)/shard_map/pallas_call | solution.py:1113
  51.8 11.8 %all_to_all.80.sums_ref = f32[32,2,640]{2,1,0:T(2,128)S(1)} all-to-all(f32[32,2,640]{2,1,0:T(2,128)S(1)} %get-tuple-element.110), channel_id=1, replica_groups=mesh['dp'=4,'z'=4,'core'=2] {'dp','z','core'}, dimensions={0} | all-to-all | bytes 327680 | tf_op jit(solution)/shard_map/all_to_all | solution.py:1069
  63.6 12.5 %shard_map.316 = (f32[2048,128]{1,0:T(8,128)}, f32[8,640]{1,0:T(8,128)S(1)}, f32[8,640]{1,0:T(8,128)S(1)}, f32[8,160]{1,0:T(8,128)S(1)}, f32[8,640]{1,0:T(8,128)S(1)}, /*index=5*/f32[32,2,128]{2,1,0:T(2,128)}) custom-call(s32[2]{0:T(128)S(1)} %copy-done.7, f32[32,2,640]{2,1,0:T(2,128)S(1)} %all_to_all.80.sums_ref, ...), custom_call_target="tpu_custom_call" | custom-call | flops 1000000000 | bytes 1000000 | tf_op jit(solution)/shard_map/pallas_call | solution.py:1113
  76.1 2.6 all-to-all-start.2
  78.7 7.2 %all-to-all-done.2.sums_ref = f32[32,2,128]{2,1,0:T(2,128)S(1)} async-done(((f32[32,2,128]{2,1,0:T(2,128)}), f32[32,2,128]{2,1,0:T(2,128)S(1)}, u32[]{:S(2)}, u32[]{:S(2)}) %all-to-all-start.2) | async-done | bytes 32800 | tf_op jit(solution)/shard_map/all_to_all | solution.py:1069
  85.9 5.8 %shard_map.317 = (f32[2048,128]{1,0:T(8,128)}, bf16[2048,256]{1,0:T(8,128)(2,1)}, bf16[256,2048]{1,0:T(8,128)(2,1)}, f32[64,8,128]{2,1,0:T(8,128)}, f32[8,128]{1,0:T(8,128)S(1)}, /*index=5*/f32[32,2,640]{2,1,0:T(2,128)S(1)}) custom-call(s32[2]{0:T(128)S(1)} %copy-done.7, f32[32,2,128]{2,1,0:T(2,128)S(1)} %all-to-all-done.2.sums_ref, ...), custom_call_target="tpu_custom_call" | custom-call | flops 1000000000 | bytes 1000000 | tf_op jit(solution)/shard_map/pallas_call | solution.py:1113
  91.7 10.2 %all_to_all.81.sums_ref = f32[32,2,640]{2,1,0:T(2,128)S(1)} all-to-all(f32[32,2,640]{2,1,0:T(2,128)S(1)} %get-tuple-element.118), channel_id=1, replica_groups=mesh['dp'=4,'z'=4,'core'=2] {'dp','z','core'}, dimensions={0} | all-to-all | bytes 327680 | tf_op jit(solution)/shard_map/all_to_all | solution.py:1069
  101.9 2.6 all-to-all-start.4
  104.5 12.1 %shard_map.318 = (f32[256,8,640]{2,1,0:T(8,128)}, f32[64,8,640]{2,1,0:T(8,128)}, f32[8,640]{1,0:T(8,128)S(1)}, f32[32,2,640]{2,1,0:T(2,128)S(1)}) custom-call(s32[2]{0:T(128)S(1)} %copy-done.7, f32[32,2,640]{2,1,0:T(2,128)S(1)} %all_to_all.81.sums_ref, f32[8,128]{1,0:T(8,128)S(1)} %get-tuple-element.121.count_ref.nstat_ref, ...), custom_call_target="tpu_custom_call" | custom-call | flops 1000000000 | bytes 1000000 | tf_op jit(solution)/shard_map/pallas_call | solution.py:1113
  116.6 13.4 %all_to_all.82.sums_ref = f32[32,2,640]{2,1,0:T(2,128)S(1)} all-to-all(f32[32,2,640]{2,1,0:T(2,128)S(1)} %get-tuple-element.125), channel_id=1, replica_groups=mesh['dp'=4,'z'=4,'core'=2] {'dp','z','core'}, dimensions={0} | all-to-all | bytes 327680 | tf_op jit(solution)/shard_map/all_to_all | solution.py:1069
  129.9 4.5 shard_map.319
  134.4 9.5 %all_to_all.83.third_ref = f32[32,4,128]{2,1,0:T(4,128)S(1)} all-to-all(f32[32,4,128]{2,1,0:T(4,128)S(1)} %get-tuple-element.128), channel_id=1, replica_groups=mesh['dp'=4,'z'=4,'core'=2] {'dp','z','core'}, dimensions={0} | all-to-all | bytes 131072 | tf_op jit(solution)/shard_map/all_to_all | solution.py:1069
  144.7 2.6 all-to-all-start.7
  147.3 7.8 %shard_map.320 = (f32[112,512]{1,0:T(8,128)}, f32[8,128]{1,0:T(8,128)S(1)}, f32[64,8,640]{2,1,0:T(8,128)}, f32[32,2,640]{2,1,0:T(2,128)S(1)}, f32[275,8,128]{2,1,0:T(8,128)}) custom-call(s32[2]{0:T(128)S(1)} %copy-done.7, f32[32,4,128]{2,1,0:T(4,128)S(1)} %all_to_all.83.third_ref, f32[512,128]{1,0:T(8,128)S(1)} %get-tuple-element.131.z_ref, ...), custom_call_target="tpu_custom_call" | custom-call | flops 1000000000 | bytes 1000000 | tf_op jit(solution)/shard_map/pallas_call | solution.py:1113
  155.1 2.6 all-to-all-done.7
  157.7 11.5 %all_to_all.84.grads_ref = f32[32,2,640]{2,1,0:T(2,128)S(1)} all-to-all(f32[32,2,640]{2,1,0:T(2,128)S(1)} %get-tuple-element.141), channel_id=1, replica_groups=mesh['dp'=4,'z'=4,'core'=2] {'dp','z','core'}, dimensions={0} | all-to-all | bytes 327680 | tf_op jit(solution)/shard_map/all_to_all | solution.py:1069
  169.2 20.5 %shard_map.321 = (f32[2048,128]{1,0:T(8,128)}, f32[32,2,768]{2,1,0:T(2,128)}, f32[100,8,128]{2,1,0:T(8,128)S(1)}, f32[8,640]{1,0:T(8,128)S(1)}) custom-call(s32[2]{0:T(128)S(1)} %copy-done.7, f32[32,2,640]{2,1,0:T(2,128)S(1)} %all_to_all.84.grads_ref, f32[8,640]{1,0:T(8,128)S(1)} %get-tuple-element.132.stat_ref.stat2_ref.stat12_ref, ...), custom_call_target="tpu_custom_call" | custom-call | flops 1000000000 | bytes 1000000 | tf_op jit(solution)/shard_map/pallas_call | solution.py:1113
  189.7 2.8 all-to-all-start.9
  192.5 8.6 %all-to-all-done.9.top_ref.one_ref = f32[32,2,768]{2,1,0:T(2,128)S(1)} async-done(((f32[32,2,768]{2,1,0:T(2,128)}), f32[32,2,768]{2,1,0:T(2,128)S(1)}, u32[]{:S(2)}, u32[]{:S(2)}) %all-to-all-start.9) | async-done | bytes 196640 | tf_op jit(solution)/shard_map/all_to_all | solution.py:1069
  201.0 21.4 %shard_map.322 = (f32[2048,128]{1,0:T(8,128)}, f32[8,128]{1,0:T(8,128)S(1)}, f32[256,8,640]{2,1,0:T(8,128)}, f32[32,2,640]{2,1,0:T(2,128)}, f32[384,8,128]{2,1,0:T(8,128)}) custom-call(s32[2]{0:T(128)S(1)} %copy-done.7, f32[32,2,768]{2,1,0:T(2,128)S(1)} %all-to-all-done.9.top_ref.one_ref, f32[8,640]{1,0:T(8,128)S(1)} %get-tuple-element.126.stat_ref.stat1_ref.stat11_ref, ...), custom_call_target="tpu_custom_call" | custom-call | flops 1000000000 | bytes 1000000 | tf_op jit(solution)/shard_map/pallas_call | solution.py:1113
  222.4 2.1 dynamic-slice_bitcast_fusion
  224.5 0.8 collective-permute-start
  225.3 2.6 all-to-all-start.10
  227.9 2.1 bitcast_add_fusion
  230.0 6.4 %all-to-all-done.10.grads_ref = f32[32,2,640]{2,1,0:T(2,128)S(1)} async-done(((f32[32,2,640]{2,1,0:T(2,128)}), f32[32,2,640]{2,1,0:T(2,128)S(1)}, u32[]{:S(2)}, u32[]{:S(2)}) %all-to-all-start.10) | async-done | bytes 163872 | tf_op jit(solution)/shard_map/all_to_all | solution.py:1069
  236.4 3.6 all-to-all-start.11
  240.0 20.7 %shard_map.323 = (f32[2048,128]{1,0:T(8,128)}, f32[8,384]{1,0:T(8,128)S(1)}, f32[60,8,128]{2,1,0:T(8,128)S(1)}, f32[8,384]{1,0:T(8,128)S(1)}) custom-call(s32[2]{0:T(128)S(1)} %copy-done.7, f32[32,2,640]{2,1,0:T(2,128)S(1)} %all-to-all-done.10.grads_ref, f32[8,640]{1,0:T(8,128)S(1)} %get-tuple-element.140.stat_ref.stat2_ref.stat02_ref, ...), custom_call_target="tpu_custom_call" | custom-call | flops 1000000000 | bytes 1000000 | tf_op jit(solution)/shard_map/pallas_call | solution.py:1113
  260.7 2.1 all-to-all-done.11
  262.8 1.0 broadcast_in_dim.10
  263.8 4.4 all-to-all-start.12
  268.2 15.8 %shard_map.324 = (f32[2048,128]{1,0:T(8,128)}, f32[32,2,640]{2,1,0:T(2,128)}, f32[128,8,128]{2,1,0:T(8,128)S(1)}, f32[8,256]{1,0:T(8,128)S(1)}) custom-call(s32[2]{0:T(128)S(1)} %copy-done.7, f32[32,2,640]{2,1,0:T(2,128)S(1)} %all-to-all-done.10.grads_ref, f32[8,640]{1,0:T(8,128)S(1)} %get-tuple-element.140.stat_ref.stat2_ref.stat02_ref, ...), custom_call_target="tpu_custom_call" | custom-call | flops 1000000000 | bytes 1000000 | tf_op jit(solution)/shard_map/pallas_call | solution.py:1113
  284.1 7.4 %all-to-all-done.12 = f32[16,12,8,128]{3,2,1,0:T(8,128)S(1)} async-done(((f32[16,12,8,128]{3,2,1,0:T(8,128)}), f32[16,12,8,128]{3,2,1,0:T(8,128)S(1)}, u32[]{:S(2)}, u32[]{:S(2)}) %all-to-all-start.12) | async-done | bytes 786464 | tf_op jit(solution)/shard_map/all_to_all | solution.py:1096
  292.1 2.6 all-to-all-start.13
  294.7 0.7 bitcast_add_fusion.1
  295.4 7.7 %all-to-all-done.13.zero_ref = f32[32,2,640]{2,1,0:T(2,128)S(1)} async-done(((f32[32,2,640]{2,1,0:T(2,128)}), f32[32,2,640]{2,1,0:T(2,128)S(1)}, u32[]{:S(2)}, u32[]{:S(2)}) %all-to-all-start.13) | async-done | bytes 163872 | tf_op jit(solution)/shard_map/all_to_all | solution.py:1069
  303.1 3.5 all-to-all-start.14
  307.4 7.7 %shard_map.325 = (f32[112,2048]{1,0:T(8,128)}, f32[2,112,640]{2,1,0:T(8,128)S(1)}, f32[16,640]{1,0:T(8,128)S(1)}, f32[4,640]{1,0:T(4,128)}, f32[4,640]{1,0:T(4,1...) custom-call(s32[2]{0:T(128)S(1)} %copy-done.7, ...), custom_call_target="tpu_custom_call" | custom-call | flops 1000000000 | bytes 1000000 | tf_op jit(solution)/shard_map/pallas_call | solution.py:1113
  315.1 3.1 all-to-all-done.14
  318.9 3.8 all-to-all-start.15
  323.5 10.3 %all-to-all-done.15 = f32[16,4,8,128]{3,2,1,0:T(8,128)S(1)} async-done(((f32[16,4,8,128]{3,2,1,0:T(8,128)}), f32[16,4,8,128]{3,2,1,0:T(8,128)S(1)}, u32[]{:S(2)}, u32[]{:S(2)}) %all-to-all-start.15) | async-done | bytes 262176 | tf_op jit(solution)/shard_map/all_to_all | solution.py:1096
  333.8 126.9 %all-reduce.4.cloned.1.call-done.pack1_ref = f32[275,8,128]{2,1,0:T(8,128)} async-done(((f32[275,8,128]{2,1,0:T(8,128)}), f32[275,8,128]{2,1,0:T(8,128)}) %all-reduce.4.cloned.1.call-update) | async-done | bytes 1126416 | tf_op jit(solution)/shard_map/psum | solution.py:1292
  460.7 3.4 shard_map.326
  464.1 0.8 copy.41
  (57 shorter events, 3.7 us)
Async XLA Ops:
  7.2 1.1 copy-start
  8.3 0.7 copy-start.6
  8.9 0.9 copy-start.14
  9.8 13.7 %copy-start.16 = (f32[2,45,640]{2,0,1:T(2,128)S(1)}, f32[2,45,640]{2,0,1:T(2,128)}, u32[]{:S(2)}) copy-start(f32[2,45,640]{2,0,1:T(2,128)} %param.27) | copy-start | bytes 691204
  9.8 22.4 %copy-start.1 = (f32[2,640,112]{1,2,0:T(8,128)S(1)}, f32[2,640,112]{1,2,0:T(8,128)}, u32[]{:S(2)}) copy-start(f32[2,640,112]{1,2,0:T(8,128)} %param.22) | copy-start | bytes 1720324
  9.9 22.4 %copy-start.4 = (f32[4,640]{1,0:T(4,128)S(1)}, f32[4,640]{1,0:T(4,128)}, u32[]{:S(2)}) copy-start(f32[4,640]{1,0:T(4,128)} %gain_ref.19) | copy-start | bytes 30724
  9.9 22.4 %copy-start.5 = (f32[4,640]{1,0:T(4,128)S(1)}, f32[4,640]{1,0:T(4,128)}, u32[]{:S(2)}) copy-start(f32[4,640]{1,0:T(4,128)} %bias_ref.17) | copy-start | bytes 30724
  9.9 22.4 %copy-start.7 = (s32[2]{0:T(128)S(1)}, s32[2]{0:T(128)}, u32[]{:S(2)}) copy-start(s32[2]{0:T(128)} %counts_ref.23) | copy-start | bytes 28
  16.2 16.0 %all-to-all-start = ((f32[32,2,768]{2,1,0:T(2,128)}), f32[32,2,768]{2,1,0:T(2,128)S(1)}, u32[]{:S(2)}, u32[]{:S(2)}) async-start(f32[32,2,768]{2,1,0:T(2,128)} %get-tuple-element.108), calls=%async_computation | async-start | bytes 393216 | tf_op jit(solution)/shard_map/all_to_all | solution.py:1069
  32.3 31.2 %copy-start.2 = (f32[2,160,640]{2,1,0:T(8,128)S(1)}, f32[2,160,640]{2,1,0:T(8,128)}, u32[]{:S(2)}) copy-start(f32[2,160,640]{2,1,0:T(8,128)} %down_ref.7) | copy-start | bytes 2457604
  32.3 31.2 %copy-start.3 = (f32[2,112,640]{2,1,0:T(8,128)S(1)}, f32[2,112,640]{2,1,0:T(8,128)}, u32[]{:S(2)}) copy-start(f32[2,112,640]{2,1,0:T(8,128)} %proj_ref.7) | copy-start | bytes 1720324
  32.3 31.2 %copy-start.8 = (f32[2,640]{1,0:T(2,128)S(1)}, f32[2,640]{1,0:T(2,128)}, u32[]{:S(2)}) copy-start(f32[2,640]{1,0:T(2,128)} %upb_ref.3) | copy-start | bytes 15364
  32.3 31.2 %copy-start.11 = (f32[2,160]{1,0:T(2,128)S(1)}, f32[2,160]{1,0:T(2,128)}, u32[]{:S(2)}) copy-start(f32[2,160]{1,0:T(2,128)} %downb_ref.3) | copy-start | bytes 3844
  63.6 15.1 %copy-start.17 = (f32[2,112]{1,0:T(2,128)S(1)}, f32[2,112]{1,0:T(2,128)}, u32[]{:S(2)}) copy-start(f32[2,112]{1,0:T(2,128)} %param.25) | copy-start | bytes 2692
  63.6 15.2 %copy-start.18 = (f32[2,112]{1,0:T(2,128)S(1)}, f32[2,112]{1,0:T(2,128)}, u32[]{:S(2)}) copy-start(f32[2,112]{1,0:T(2,128)} %param.26) | copy-start | bytes 2692
  76.1 9.8 %all-to-all-start.2 = ((f32[32,2,128]{2,1,0:T(2,128)}), f32[32,2,128]{2,1,0:T(2,128)S(1)}, u32[]{:S(2)}, u32[]{:S(2)}) async-start(f32[32,2,128]{2,1,0:T(2,128)} %get-tuple-element.114), calls=%async_computation.2 | async-start | bytes 65536 | tf_op jit(solution)/shard_map/all_to_all | solution.py:1069
  101.9 14.7 %all-to-all-start.4 = ((f32[32,2,8,128]{3,2,1,0:T(8,128)}), f32[32,2,8,128]{3,2,1,0:T(8,128)S(1)}, u32[]{:S(2)}, u32[]{:S(2)}) async-start(f32[32,2,8,128]{3,2,1,0:T(8,128)} %bitcast.2), calls=%async_computation.4 | async-start | bytes 524288 | tf_op jit(solution)/shard_map/all_to_all | solution.py:1091
  144.7 13.0 %all-to-all-start.7 = ((f32[32,2,8,128]{3,2,1,0:T(8,128)}), f32[32,2,8,128]{3,2,1,0:T(8,128)S(1)}, u32[]{:S(2)}, u32[]{:S(2)}) async-start(f32[32,2,8,128]{3,2,1,0:T(8,128)} %broadcast_in_dim.8), calls=%async_computation.7 | async-start | bytes 524288 | tf_op jit(solution)/shard_map/all_to_all | solution.py:1096
  189.7 11.3 %all-to-all-start.9 = ((f32[32,2,768]{2,1,0:T(2,128)}), f32[32,2,768]{2,1,0:T(2,128)S(1)}, u32[]{:S(2)}, u32[]{:S(2)}) async-start(f32[32,2,768]{2,1,0:T(2,128)} %get-tuple-element.145), calls=%async_computation.9 | async-start | bytes 393216 | tf_op jit(solution)/shard_map/all_to_all | solution.py:1069
  224.5 3.4 collective-permute-start
  225.3 11.1 %all-to-all-start.10 = ((f32[32,2,640]{2,1,0:T(2,128)}), f32[32,2,640]{2,1,0:T(2,128)S(1)}, u32[]{:S(2)}, u32[]{:S(2)}) async-start(f32[32,2,640]{2,1,0:T(2,128)} %get-tuple-element.152), calls=%async_computation.10 | async-start | bytes 327680 | tf_op jit(solution)/shard_map/all_to_all | solution.py:1069
  236.4 26.4 %all-to-all-start.11 = ((f32[16,12,8,128]{3,2,1,0:T(8,128)}), f32[16,12,8,128]{3,2,1,0:T(8,128)S(1)}, u32[]{:S(2)}, u32[]{:S(2)}) async-start(f32[16,12,8,128]{3,2,1,0:T(8,128)} %bitcast.7), calls=%async_computation.11 | async-start | bytes 1572864 | tf_op jit(solution)/shard_map/all_to_all | solution.py:1091
  263.8 27.7 %all-to-all-start.12 = ((f32[16,12,8,128]{3,2,1,0:T(8,128)}), f32[16,12,8,128]{3,2,1,0:T(8,128)S(1)}, u32[]{:S(2)}, u32[]{:S(2)}) async-start(f32[16,12,8,128]{3,2,1,0:T(8,128)} %broadcast_in_dim.10), calls=%async_computation.12 | async-start | bytes 1572864 | tf_op jit(solution)/shard_map/all_to_all | solution.py:1096
  284.0 23.3 %copy-start.9 = (f32[4,640]{1,0:T(4,128)S(1)}, f32[4,640]{1,0:T(4,128)}, u32[]{:S(2)}) copy-start(f32[4,640]{1,0:T(4,128)} %means_ref.1) | copy-start | bytes 30724
  284.0 23.3 %copy-start.10 = (f32[4,640]{1,0:T(4,128)S(1)}, f32[4,640]{1,0:T(4,128)}, u32[]{:S(2)}) copy-start(f32[4,640]{1,0:T(4,128)} %vars_ref.1) | copy-start | bytes 30724
  284.0 23.3 %copy-start.12 = (f32[2,112]{1,0:T(2,128)S(1)}, f32[2,112]{1,0:T(2,128)}, u32[]{:S(2)}) copy-start(f32[2,112]{1,0:T(2,128)} %nmeans_ref.1) | copy-start | bytes 2692
  284.1 23.3 %copy-start.13 = (f32[2,112]{1,0:T(2,128)S(1)}, f32[2,112]{1,0:T(2,128)}, u32[]{:S(2)}) copy-start(f32[2,112]{1,0:T(2,128)} %nvars_ref.1) | copy-start | bytes 2692
  291.5 23.6 %copy-start.15 = (f32[16,12,8,128]{3,2,1,0:T(8,128)}, f32[16,12,8,128]{3,2,1,0:T(8,128)S(1)}, u32[]{:S(2)}) copy-start(f32[16,12,8,128]{3,2,1,0:T(8,128)S(1)} %all-to-all-done.12) | copy-start | bytes 2359300
  291.5 11.7 %collective-permute-start.2 = (f32[192,8,128]{2,1,0:T(8,128)S(1)}, f32[192,8,128]{2,1,0:T(8,128)}, u32[]{:S(2)}, u32[]{:S(2)}) collective-permute-start(f32[192,8,128]{2,1,0:T(8,128)S(1)} %bitcast.40), channel_id=1, source_target_pairs={{0,1},{1,0},{2,3},{3,2},{4,5},{5,4},{6,7},{7,6},{8,9},{9,8},{10,11... | collective-permute-start | bytes 2359304 | tf_op jit(solution)/shard_map/ppermute | solution.py:1077
  291.5 3.1 collective-permute-start.1
  292.1 11.1 %all-to-all-start.13 = ((f32[32,2,640]{2,1,0:T(2,128)}), f32[32,2,640]{2,1,0:T(2,128)S(1)}, u32[]{:S(2)}, u32[]{:S(2)}) async-start(f32[32,2,640]{2,1,0:T(2,128)} %get-tuple-element.168), calls=%async_computation.13 | async-start | bytes 327680 | tf_op jit(solution)/shard_map/all_to_all | solution.py:1069
  303.1 15.1 %all-to-all-start.14 = ((f32[16,4,8,128]{3,2,1,0:T(8,128)}), f32[16,4,8,128]{3,2,1,0:T(8,128)S(1)}, u32[]{:S(2)}, u32[]{:S(2)}) async-start(f32[16,4,8,128]{3,2,1,0:T(8,128)} %bitcast.13), calls=%async_computation.14 | async-start | bytes 524288 | tf_op jit(solution)/shard_map/all_to_all | solution.py:1091
  318.9 14.8 %all-to-all-start.15 = ((f32[16,4,8,128]{3,2,1,0:T(8,128)}), f32[16,4,8,128]{3,2,1,0:T(8,128)S(1)}, u32[]{:S(2)}, u32[]{:S(2)}) async-start(f32[16,4,8,128]{3,2,1,0:T(8,128)} %broadcast_in_dim.11), calls=%async_computation.15 | async-start | bytes 524288 | tf_op jit(solution)/shard_map/all_to_all | solution.py:1096
  322.8 137.9 %all-reduce.4.cloned.1.call-start = ((), (), s32[]{:S(2)}) async-start(), calls=%async_computation.16 | async-start | bytes 2252800 | tf_op jit(solution)/shard_map/psum | solution.py:1292
  333.8 126.9 %collective-permute-start.3 = (f32[64,8,128]{2,1,0:T(8,128)S(1)}, f32[64,8,128]{2,1,0:T(8,128)S(1)}, u32[]{:S(2)}, u32[]{:S(2)}) collective-permute-start(f32[64,8,128]{2,1,0:T(8,128)S(1)} %bitcast.32), channel_id=1, source_target_pairs={{0,1},{1,0},{2,3},{3,2},{4,5},{5,4},{6,7},{7,6},{8,9},{9,8},{10,11... | collective-permute-start | bytes 786440 | tf_op jit(solution)/shard_map/ppermute | solution.py:1077
Sparse Core Ops, SparseCore 0:
  329.0 131.5 all-reduce.3

commit v2 on v1

--- a/solution.py
+++ b/solution.py
@@ -261,29 +261,20 @@
     return pieces
 
 
-def prepare_kernel(
-    counts_ref, video_ref, cot_ref, w_ref, x_ref, rows_ref, columns_ref, cot_out_ref, gram_ref, send_ref
-):
-    order = column_order()
+def gram_kernel(counts_ref, video_ref, w_ref, gram_ref, send_ref):
     total = live_frames(counts_ref)
-    pixels = video_ref.shape[1]
-    gram = jnp.zeros((2 * LANES, 2 * LANES), F32)
-    summed = jnp.zeros((1, LANES), F32)
-    for frame in range(pixels // 256):
-        live = jnp.where(frame < total, 1.0, 0.0).astype(F32)
-        for part in (2 * frame, 2 * frame + 1):
-            at = slice(part * LANES, (part + 1) * LANES)
-            block = pad_rows(video_ref[:, at] * live)
-            high, middle, low = pick_thirds(order, block, NT, True)
-            rows = high + middle + low
-            x_ref[at, :] = rows
-            rows_ref[at, :] = jnp.concatenate([high, middle], axis=1).astype(jnp.bfloat16)
-            first, second, _ = pick_thirds(order, block, NT, False)
-            columns_ref[:, at] = jnp.concatenate([first, second], axis=0).astype(jnp.bfloat16)
-            summed = summed + jnp.sum(rows, axis=0, keepdims=True)
-        at = slice(frame * 256, (frame + 1) * 256)
-        gram = gram + plain_dot(columns_ref[:, at], rows_ref[at, :])
+    frames = video_ref.shape[1] // 256
+    ones = jnp.ones((8, 256), jnp.bfloat16)
+
+    def frame(t, carry):
+        at = pl.ds(pl.multiple_of(t * 256, 256), 256)
+        both = jnp.concatenate(halves(pad_rows(video_ref[:, at] * live_value(t, total))), axis=0)
+        return (carry[0] + plain_dot(both, both, NT), carry[1] + plain_dot(ones, both, NT))
+
+    init = (jnp.zeros((2 * LANES, 2 * LANES), F32), jnp.zeros((8, 2 * LANES), F32))
+    gram, summed = each_frame(frames, frame, init)
     gram = fold_square(gram)
+    summed = fold_right(summed)[0:1]
     gram_ref[0:LANES, :] = gram
     gram_ref[LANES : LANES + 8, :] = rows8(summed)
     w = pad_rows(w_ref[0])
@@ -292,6 +283,18 @@
     count = jnp.full((2, LANES), 1.0, F32) * (total * (SIDE * SIDE)).astype(F32)
     send_all(send_ref, sums, slice(0, width))
     send_all(send_ref, count, slice(width, width + LANES))
+
+
+def prepare_kernel(counts_ref, video_ref, cot_ref, x_ref, rows_ref, columns_ref, cot_out_ref):
+    order = column_order()
+    total = live_frames(counts_ref)
+    for part in range(video_ref.shape[1] // LANES):
+        at = slice(part * LANES, (part + 1) * LANES)
+        block = pad_rows(video_ref[:, at] * live_value(part // 2, total))
+        high, middle, low = pick_thirds(order, block, NT, True)
+        x_ref[at, :] = high + middle + low
+        rows_ref[at, :] = jnp.concatenate([high, middle], axis=1).astype(jnp.bfloat16)
+        columns_ref[:, at] = jnp.concatenate([high.T, middle.T], axis=0).astype(jnp.bfloat16)
     spot = lax.broadcasted_iota(jnp.int32, (LANES, LANES), 1)
     for part in range(cot_ref.shape[1] // LANES):
         at = slice(part * LANES, (part + 1) * LANES)
@@ -362,10 +365,7 @@
     block, counts_ref, sums_ref, count_ref, rows_ref, w_ref, gain_ref, bias_ref, taps_ref,
     e_ref, d_ref, stat_ref, send_ref, a_ref, taps8_ref,
 ):
-    @pl.when(pl.program_id(0) == 0)
-    def start():
-        clear_edges(a_ref)
-
+    clear_edges(a_ref)
     total = live_frames(counts_ref)
     frames = a_ref.shape[0]
     count = count_ref[2:3, :] if block else row_total(count_ref)[0:1]
@@ -821,9 +821,9 @@
 
 
 def depth_backward_kernel(
-    block, before, final, counts_ref, grads_ref, stat2_ref, stat_ref, nstat_ref, dy2_ref, d_ref, e_ref, columns_ref, w_ref,
+    block, before, final, counts_ref, grads_ref, stat2_ref, stat_ref, nstat_ref, dy2_ref, d_ref, e_ref, a_ref, columns_ref, w_ref,
     gain_ref, bias_ref, taps_ref, z3_ref, dx_in_ref, sums_in_ref, list_in_ref, dxpre_ref, send_ref, q_ref, grad_rows_ref,
-    a_ref, z_ref, f_ref, taps8_ref, dw_ref, pair_ref,
+    z_ref, f_ref, taps8_ref, dw_ref, pair_ref,
 ):
     tile = pl.program_id(0)
     tiles = pl.num_programs(0)
@@ -836,7 +836,6 @@
 
     @pl.when(tile == 0)
     def start():
-        clear_edges(a_ref)
         clear_edges(z_ref)
         if before:
             dxpre_ref[...] = dx_in_ref[...]
@@ -877,8 +876,6 @@
             z_ref[t, 1, 1 : SIDE + 1] = pair[:, 1]
             z_ref[t, 2, 1 : SIDE + 1] = columns_down(pair[:, 1])
             z_ref[t, 3, 1 : SIDE + 1] = columns_up(pair[:, 0])
-        values = e_ref[pl.ds(pl.multiple_of(t * FULL_ROWS, FULL_ROWS), FULL_ROWS)]
-        write_first(t, total, values, scale_half, shift_half, a_ref, 2)
         return carry
 
     each_frame(frames, fill, 0)
@@ -1010,7 +1007,7 @@
 
 
 def gradient_kernel(
-    core_ref, pack0_ref, pack0_other_ref, pack1_ref, late_ref, late_other_ref, less_ref, factor_ref,
+    core_ref, pack0_ref, pack0_other_ref, pack1_ref, pack1_other_ref, late_ref, late_other_ref, less_ref, factor_ref,
     dw_ref, dtaps_ref, ddown_ref, dup_ref, dproj_ref, dupb_ref, ddownb_ref,
 ):
     narrow = dw_ref.shape[1]
@@ -1023,8 +1020,6 @@
 
     def rows_of(pair, at, count):
         mine, other = pair
-        if other is None:
-            return mine[at : at + count].reshape(-1, LANES)
         half = mine.shape[0]
         pieces = []
         if at < half:
@@ -1039,7 +1034,7 @@
         values = pieces[0] if len(pieces) == 1 else jnp.concatenate(pieces, axis=0)
         return values.reshape(-1, LANES)
 
-    packs = ((pack0_ref, pack0_other_ref), (pack1_ref, None))
+    packs = ((pack0_ref, pack0_other_ref), (pack1_ref, pack1_other_ref))
     lists = ((late_ref, late_other_ref), packs[0])
     for block in range(2):
         down_rows = []
@@ -1195,30 +1190,38 @@
     def weight_at(block, rows):
         return lambda at: pl.BlockSpec((1, rows, LANES), lambda p, j: (block, 0, at(p, j)))
 
-    x, x_rows, x_columns, cot, gram_zero, sums = call(
-        prepare_kernel, (1,), [SCALARS, whole(video), whole(cotangent), of_block(0, cin, width)],
-        [fixed(pixels, LANES), fixed(pixels, 2 * LANES), fixed(2 * LANES, pixels), fixed(half_pixels, LANES),
-         fixed(LANES + 8, LANES), fixed(devices, 2, width + LANES)],
+    gram_zero, sums = call(
+        gram_kernel, (1,), [SCALARS, whole(video), of_block(0, cin, width)],
+        [fixed(LANES + 8, LANES), fixed(devices, 2, width + LANES)],
+        [shape(LANES + 8, LANES), shape(devices, 2, width + LANES)],
+        [], (frame_counts, video, w_t),
+    )
+    x, x_rows, x_columns, cot = simple_call(
+        prepare_kernel, 1, (frame_counts, video, cotangent),
         [shape(pixels, LANES), shape(pixels, 2 * LANES, kind=low), shape(2 * LANES, pixels, kind=low),
-         shape(half_pixels, LANES), shape(LANES + 8, LANES), shape(devices, 2, width + LANES)],
-        [], (frame_counts, video, cotangent, w_t),
+         shape(half_pixels, LANES)],
     )
     sums = exchange(sums)
+
+    def planes_of(planes, begin=0):
+        return pl.BlockSpec((frames, planes, SIDE + 2, 8, LANES), lambda j: (0, 0, 0, 0, j + begin))
 
     def expand(block, sums, count, count_spec, rows):
         depth_rows = half_rows if block else full_rows
+        planes = 3 if block else 4
         return call(
             functools.partial(expand_kernel, block), (tiles,),
             [SCALARS, tile_sums(), count_spec, whole(rows), weight_tile(block, cin), tile_rows(4), tile_rows(4),
              weight_tile(block, taps)],
-            [tile_cube(full_rows), tile_cube(depth_rows), tile_rows(8), tile_sums()],
-            [shape(full_rows, 8, width), shape(depth_rows, 8, width), shape(8, width), shape(devices, 2, width)],
-            [pltpu.VMEM((frames, 4, SIDE + 2, 8, LANES), F32), pltpu.VMEM((taps, 8, LANES), F32)],
+            [tile_cube(full_rows), tile_cube(depth_rows), tile_rows(8), tile_sums(), planes_of(planes)],
+            [shape(full_rows, 8, width), shape(depth_rows, 8, width), shape(8, width), shape(devices, 2, width),
+             shape(frames, planes, SIDE + 2, 8, width)],
+            [pltpu.VMEM((taps, 8, LANES), F32)],
             (frame_counts, sums, count, rows, w_t, wide_gains, wide_biases, depth_weight),
         )
 
     count_spec = pl.BlockSpec((devices, 2, LANES), lambda j: (0, 0, tiles))
-    e_zero, d_zero, stat01, sums = expand(0, sums, sums, count_spec, x_rows)
+    e_zero, d_zero, stat01, sums, planes_zero = expand(0, sums, sums, count_spec, x_rows)
     sums = exchange(sums)
 
     def squeeze_forward(block, sums, stat, depth):
@@ -1254,7 +1257,7 @@
     )
     sums, gram = together(exchange(sums), gram)
     gram = share_out(gram, AXES)
-    e_one, d_one, stat11, sums = expand(1, sums, nstat, pl.BlockSpec((8, LANES), lambda j: (0, 0)), x1_rows)
+    e_one, d_one, stat11, sums, planes_one = expand(1, sums, nstat, pl.BlockSpec((8, LANES), lambda j: (0, 0)), x1_rows)
     sums, gram = together(sums, gram)
     sums = exchange(sums)
     z_one, gates_one, running_one, pre_one, stat12, sums = squeeze_forward(1, sums, stat11, d_one)
@@ -1270,8 +1273,7 @@
         if not block:
             ins[0:4] = [both(rows_at(8)), both(cube_at(rows)), both(rows_at(4)), both(rows_at(4))]
             ins[6] = early(weight_at(block, cin))
-        packed = tiles * pack_tiles(cin, squeeze)
-        packed = packed if block else round_up(packed + tiles * q_tiles)
+        packed = round_up(tiles * (pack_tiles(cin, squeeze) + (0 if block else q_tiles)))
         wide_outs = [fixed(rows, 8, width), fixed(devices, 2, width)] if block else [late(cube_at(rows)), late(sums_at(2))]
         outs = [fixed(8, LANES)] + wide_outs + [fixed(packed, 8, LANES)]
         shapes = [shape(8, LANES), shape(rows, 8, width), shape(devices, 2, width), shape(packed, 8, LANES)]
@@ -1289,11 +1291,11 @@
          project_weight, gates_one, running_one, pre_one),
     )
     sums, gram = together(sums, gram)
-    pack_one = lax.psum(pack_one, AXES)
-    sums = exchange(sums)
+    sums, pack_one = together(exchange(sums), add_cores(pack_one))
+    pack_one = share_out(pack_one)
     nothing = jnp.zeros((8, LANES), F32)
 
-    def depth_backward(block, begin, end, sums, stat2, stat, dy2, depth, expanded, columns, dx_in, sums_in, list_in):
+    def depth_backward(block, begin, end, sums, stat2, stat, dy2, depth, expanded, planes, columns, dx_in, sums_in, list_in):
         rows = half_rows if block else full_rows
         z_shape = (frames, 2, HALF_ROWS + 1, 8, LANES) if block else (frames, 4, SIDE + 2, 8, LANES)
         count = end - begin
@@ -1318,20 +1320,22 @@
         return call(
             functools.partial(depth_backward_kernel, block, begin, final), (count,),
             [SCALARS, pl.BlockSpec((devices, 2, LANES), lambda j: (0, 0, j + begin)), wide_rows(8), wide_rows(8), whole(nstat),
-             wide_cube(rows), wide_cube(rows), wide_cube(full_rows), whole(columns), wide_weight(cin), wide_rows(4),
+             wide_cube(rows), wide_cube(rows), wide_cube(full_rows), planes_of(2, begin), whole(columns), wide_weight(cin), wide_rows(4),
              wide_rows(4), wide_weight(taps), whole(z_zero), whole(dx_in), whole(sums_in), whole(list_in)],
             [fixed(pixels, LANES), send_spec, fixed(listed, 8, LANES), tile_rows(8)],
             [shape(pixels, LANES), shape(*send), shape(listed, 8, LANES), shape(8, count * LANES)],
-            [pltpu.VMEM((frames, 2, SIDE + 2, 8, LANES), F32), pltpu.VMEM(z_shape, F32), pltpu.VMEM((full_rows, 8, LANES), F32),
+            [pltpu.VMEM(z_shape, F32), pltpu.VMEM((full_rows, 8, LANES), F32),
              pltpu.VMEM((taps, 8, LANES), F32), pltpu.VMEM((taps, 8, LANES), F32), pltpu.VMEM((pixels, 2 * LANES), low)],
-            (frame_counts, sums, stat2, stat, nstat, dy2, depth, expanded, columns, w_t, wide_gains, wide_biases,
+            (frame_counts, sums, stat2, stat, nstat, dy2, depth, expanded, planes, columns, w_t, wide_gains, wide_biases,
              depth_weight, z_zero, dx_in, sums_in, list_in),
         )
 
     dxpre_one, sums, q_one, grad_one = depth_backward(
-        1, 0, tiles, sums, stat12, stat11, dy2_one, d_one, e_one, x1_columns, nothing, nothing, nothing
-    )
-    top_one = exchange(sums)
+        1, 0, tiles, sums, stat12, stat11, dy2_one, d_one, e_one, planes_one, x1_columns, nothing, nothing, nothing
+    )
+    sums, pack_one = together(sums, pack_one)
+    top_one, pack_one = together(exchange(sums), pack_one)
+    pack_one = share_back(pack_one)
     ins, outs, shapes, scratch = backward_specs(0)
     dx1, nsum_zero, dy2_zero, sums, pack_zero = call(
         squeeze_zero_backward_kernel, (2, tiles),
@@ -1341,16 +1345,18 @@
         (frame_counts, top_one, stat11, gram, nstat, dxpre_one, x1, z_zero, ngains, w_t, wide_gains, q_one, stat02, d_zero,
          wide_gains, wide_biases, squeeze_weight, up_t, project_weight, gates_zero, running_zero, pre_zero),
     )
-    sums, pack_zero = together(exchange(sums), add_cores(pack_zero))
+    sums, pack_one = together(sums, pack_one)
+    pack_one_other = swap_cores(pack_one)
+    sums, pack_zero, pack_one_other = together(exchange(sums), add_cores(pack_zero), pack_one_other)
     pack_zero = share_out(pack_zero)
     first = tiles - tiles // 2
     dxpre_zero, sums_in, late, grad_a = depth_backward(
-        0, 0, first, sums, stat02, stat01, dy2_zero, d_zero, e_zero, x_columns, nothing, nothing, nothing
+        0, 0, first, sums, stat02, stat01, dy2_zero, d_zero, e_zero, planes_zero, x_columns, nothing, nothing, nothing
     )
     dxpre_zero, pack_zero = together(dxpre_zero, pack_zero)
     pack_zero = share_back(pack_zero)
     dxpre_zero, sums, late, grad_b = depth_backward(
-        0, first, tiles, sums, stat02, stat01, dy2_zero, d_zero, e_zero, x_columns, dxpre_zero, sums_in, late
+        0, first, tiles, sums, stat02, stat01, dy2_zero, d_zero, e_zero, planes_zero, x_columns, dxpre_zero, sums_in, late
     )
     grad_zero = jnp.concatenate([grad_a, grad_b], axis=1)
     sums, pack_zero = together(sums, pack_zero)
@@ -1375,7 +1381,7 @@
     late_other = swap_cores(late)
     dw_t, dtaps, ddown, dup, dproj, dupb, ddownb = simple_call(
         gradient_kernel, 1,
-        (core, pack_zero, pack_zero_other, pack_one, late, late_other, less, factor),
+        (core, pack_zero, pack_zero_other, pack_one, pack_one_other, late, late_other, less, factor),
         [shape(2, cin, width), shape(2, taps, width), shape(2, squeeze, width), shape(2, squeeze, width),
          shape(2, cin, width), shape(2, width), shape(2, squeeze)],
     )

time: 475 us -> 361 us (0.76)
  waiting for transfers between devices: 192 us -> 55.6 us
  blocking collectives: 56.3 us -> 79.8 us
  between operations: 15.1 us -> 1.74 us
  starting transfers between devices: 39.8 us -> 47 us
    psum x1 -> x0, waiting for transfers between devices: 127 us -> none  [local(): pack_one = lax.psum(pack_one, AXES)]
    all_to_all x0 -> x2, blocking collectives: none -> 26.7 us  [share_back(): lax.all_to_all(jnp.broadcast_to(own[None], pieces.shape), names, 0, 0, ti...]
    all_to_all x3 -> x2, waiting for transfers between devices: 20.2 us -> 7.86 us  [share_back(): lax.all_to_all(jnp.broadcast_to(own[None], pieces.shape), names, 0, 0, ti...]
    all_to_all x5 -> x6, starting transfers between devices: 17.8 us -> 23.2 us  [exchange(): return lax.all_to_all(send, AXES, 0, 0, tiled=True)]
    all_to_all x3 -> x4, starting transfers between devices: 9.74 us -> 14 us  [share_out(): lax.all_to_all(tiles.reshape(count, -1, *tiles.shape[1:]), names, 0, 0, t...]
    pallas_call x13 -> x14, Pallas kernels: 158 us -> 155 us  [call(): pl.pallas_call(kernel, grid=grid, in_specs=in_specs, out_specs=out_specs,...]
    all_to_all x5 -> x4, blocking collectives: 56.3 us -> 53.1 us  [exchange(): return lax.all_to_all(send, AXES, 0, 0, tiled=True)]
    all_to_all x3 -> x2, starting transfers between devices: 10.8 us -> 8.43 us  [share_back(): lax.all_to_all(jnp.broadcast_to(own[None], pieces.shape), names, 0, 0, ti...]
  transfers between devices with their start and end apart: 16 -> 18, of which waited for: 11 -> 10; matrix products, arithmetic and copies ran while one was open for 1% -> 2% of each run, Pallas kernels for 14% -> 27%
where the time goes in v2:
time: 361 us; the launch traced here: 357 us
  Pallas kernels  155 us (43%)
  blocking collectives  79.8 us (22%)
  waiting for transfers between devices  55.6 us (15%)
  starting transfers between devices  47 us (13%)
  local copies, waits for them, and re-layouts  11.4 us (3%)
  other arithmetic  7.07 us (2%)
    pallas_call x14, Pallas kernels, call(): pl.pallas_call(kernel, grid=grid, in_specs=in_specs, out_specs=out_specs,...  155 us
    all_to_all x4, blocking collectives, exchange(): return lax.all_to_all(send, AXES, 0, 0, tiled=True)  53.1 us
    all_to_all x6, waiting for transfers between devices, exchange(): return lax.all_to_all(send, AXES, 0, 0, tiled=True)  39.4 us
    all_to_all x2, blocking collectives, share_back(): lax.all_to_all(jnp.broadcast_to(own[None], pieces.shape), names, 0, 0, ti...  26.7 us
    all_to_all x6, starting transfers between devices, exchange(): return lax.all_to_all(send, AXES, 0, 0, tiled=True)  23.2 us
    all_to_all x4, starting transfers between devices, share_out(): lax.all_to_all(tiles.reshape(count, -1, *tiles.shape[1:]), names, 0, 0, t...  14 us
    all_to_all x2, starting transfers between devices, share_back(): lax.all_to_all(jnp.broadcast_to(own[None], pieces.shape), names, 0, 0, ti...  8.43 us
    all_to_all x2, waiting for transfers between devices, share_back(): lax.all_to_all(jnp.broadcast_to(own[None], pieces.shape), names, 0, 0, ti...  7.86 us
  transfers between devices with their start and end apart: 18, of which 10 were waited for; matrix products, arithmetic and copies ran while one was open for 2% of the time, Pallas kernels for 27%

profile of v2, /device:TPU:0, one launch (start us, length us, event | category | flops | bytes accessed | tf_op | source)
XLA Modules:
  0.0 357.3 jit_solution(17229298809353603508)
XLA Ops:
  3.6 3.5 shard_map.314
  7.1 7.3 %all-to-all-start = ((f32[32,2,768]{2,1,0:T(2,128)}), f32[32,2,768]{2,1,0:T(2,128)S(1)}, u32[]{:S(2)}, u32[]{:S(2)}) async-start(f32[32,2,768]{2,1,0:T(2,128)} %get-tuple-element.119), calls=%async_computation | async-start | bytes 393216 | tf_op jit(solution)/shard_map/all_to_all | solution.py:1064
  14.5 3.4 shard_map.315
  17.8 5.3 %all-to-all-done.sums_ref.count_ref = f32[32,2,768]{2,1,0:T(2,128)S(1)} async-done(((f32[32,2,768]{2,1,0:T(2,128)}), f32[32,2,768]{2,1,0:T(2,128)S(1)}, u32[]{:S(2)}, u32[]{:S(2)}) %all-to-all-start) | async-done | bytes 196640 | tf_op jit(solution)/shard_map/all_to_all | solution.py:1064
  23.2 18.8 %shard_map.316 = (f32[256,8,640]{2,1,0:T(8,128)}, f32[256,8,640]{2,1,0:T(8,128)}, f32[8,640]{1,0:T(8,128)S(1)}, f32[32,2,640]{2,1,0:T(2,128)S(1)}, f32[8,4,18,8,640]{4,3,2,1,0:T(8,128)}) custom-call(s32[2]{0:T(128)S(1)} %copy-done.7, f32[32,2,768]{2,1,0:T(2,128)S(1)} %all-to-all-done.sums_ref.count_ref, f32[32,2,768]{2,1,0:T(2,128)S(1)} %all-to-all-done.sums_ref.count_ref, ...), custom_call_target="tpu_custom_call" | custom-call | flops 1000000000 | bytes 1000000 | tf_op jit(solution)/shard_map/pallas_call | solution.py:1108
  42.0 13.1 %all_to_all.90.sums_ref = f32[32,2,640]{2,1,0:T(2,128)S(1)} all-to-all(f32[32,2,640]{2,1,0:T(2,128)S(1)} %get-tuple-element.121), channel_id=1, replica_groups=mesh['dp'=4,'z'=4,'core'=2] {'dp','z','core'}, dimensions={0} | all-to-all | bytes 327680 | tf_op jit(solution)/shard_map/all_to_all | solution.py:1064
  55.1 12.6 %shard_map.317 = (f32[2048,128]{1,0:T(8,128)}, f32[8,640]{1,0:T(8,128)S(1)}, f32[8,640]{1,0:T(8,128)S(1)}, f32[8,160]{1,0:T(8,128)S(1)}, f32[8,640]{1,0:T(8,128)S(1)}, /*index=5*/f32[32,2,128]{2,1,0:T(2,128)}) custom-call(s32[2]{0:T(128)S(1)} %copy-done.7, f32[32,2,640]{2,1,0:T(2,128)S(1)} %all_to_all.90.sums_ref, ...), custom_call_target="tpu_custom_call" | custom-call | flops 1000000000 | bytes 1000000 | tf_op jit(solution)/shard_map/pallas_call | solution.py:1108
  67.7 2.6 all-to-all-start.2
  70.3 7.2 %all-to-all-done.2.sums_ref = f32[32,2,128]{2,1,0:T(2,128)S(1)} async-done(((f32[32,2,128]{2,1,0:T(2,128)}), f32[32,2,128]{2,1,0:T(2,128)S(1)}, u32[]{:S(2)}, u32[]{:S(2)}) %all-to-all-start.2) | async-done | bytes 32800 | tf_op jit(solution)/shard_map/all_to_all | solution.py:1064
  77.5 5.8 %shard_map.318 = (f32[2048,128]{1,0:T(8,128)}, bf16[2048,256]{1,0:T(8,128)(2,1)}, bf16[256,2048]{1,0:T(8,128)(2,1)}, f32[64,8,128]{2,1,0:T(8,128)}, f32[8,128]{1,0:T(8,128)S(1)}, /*index=5*/f32[32,2,640]{2,1,0:T(2,128)S(1)}) custom-call(s32[2]{0:T(128)S(1)} %copy-done.7, f32[32,2,128]{2,1,0:T(2,128)S(1)} %all-to-all-done.2.sums_ref, ...), custom_call_target="tpu_custom_call" | custom-call | flops 1000000000 | bytes 1000000 | tf_op jit(solution)/shard_map/pallas_call | solution.py:1108
  83.3 10.2 %all_to_all.91.sums_ref = f32[32,2,640]{2,1,0:T(2,128)S(1)} all-to-all(f32[32,2,640]{2,1,0:T(2,128)S(1)} %get-tuple-element.129), channel_id=1, replica_groups=mesh['dp'=4,'z'=4,'core'=2] {'dp','z','core'}, dimensions={0} | all-to-all | bytes 327680 | tf_op jit(solution)/shard_map/all_to_all | solution.py:1064
  93.5 2.6 all-to-all-start.4
  96.1 12.1 %shard_map.319 = (f32[256,8,640]{2,1,0:T(8,128)}, f32[64,8,640]{2,1,0:T(8,128)}, f32[8,640]{1,0:T(8,128)S(1)}, f32[32,2,640]{2,1,0:T(2,128)S(1)}, f32[8,3,18,8,640]{4,3,2,1,0:T(8,128)}) custom-call(s32[2]{0:T(128)S(1)} %copy-done.7, f32[32,2,640]{2,1,0:T(2,128)S(1)} %all_to_all.91.sums_ref, f32[8,128]{1,0:T(8,128)S(1)} %get-tuple-element.132.count_ref.nstat_ref, ...), custom_call_target="tpu_custom_call" | custom-call | flops 1000000000 | bytes 1000000 | tf_op jit(solution)/shard_map/pallas_call | solution.py:1108
  108.2 14.5 %all_to_all.92.sums_ref = f32[32,2,640]{2,1,0:T(2,128)S(1)} all-to-all(f32[32,2,640]{2,1,0:T(2,128)S(1)} %get-tuple-element.136), channel_id=1, replica_groups=mesh['dp'=4,'z'=4,'core'=2] {'dp','z','core'}, dimensions={0} | all-to-all | bytes 327680 | tf_op jit(solution)/shard_map/all_to_all | solution.py:1064
  122.7 5.1 %shard_map.320 = (f32[512,128]{1,0:T(8,128)S(1)}, f32[8,640]{1,0:T(8,128)S(1)}, f32[8,640]{1,0:T(8,128)S(1)}, f32[8,160]{1,0:T(8,128)S(1)}, f32[8,640]{1,0:T(8,128)S(1)}, /*index=5*/f32[32,4,128]{2,1,0:T(4,128)}) custom-call(s32[2]{0:T(128)S(1)} %copy-done.7, f32[32,2,640]{2,1,0:T(2,128)S(1)} %all_to_all.92.sums_ref, ...), custom_call_target="tpu_custom_call" | custom-call | flops 1000000000 | bytes 1000000 | tf_op jit(solution)/shard_map/pallas_call | solution.py:1108
  127.8 2.6 all-to-all-start.6
  130.4 7.4 %all-to-all-done.6.third_ref = f32[32,4,128]{2,1,0:T(4,128)S(1)} async-done(((f32[32,4,128]{2,1,0:T(4,128)}), f32[32,4,128]{2,1,0:T(4,128)S(1)}, u32[]{:S(2)}, u32[]{:S(2)}) %all-to-all-start.6) | async-done | bytes 65568 | tf_op jit(solution)/shard_map/all_to_all | solution.py:1064
  137.8 7.9 %shard_map.321 = (f32[112,512]{1,0:T(8,128)}, f32[8,128]{1,0:T(8,128)S(1)}, f32[64,8,640]{2,1,0:T(8,128)}, f32[32,2,640]{2,1,0:T(2,128)}, f32[288,8,128]{2,1,0:T(8,128)}) custom-call(s32[2]{0:T(128)S(1)} %copy-done.7, f32[32,4,128]{2,1,0:T(4,128)S(1)} %all-to-all-done.6.third_ref, f32[512,128]{1,0:T(8,128)S(1)} %get-tuple-element.142.z_ref, ...), custom_call_target="tpu_custom_call" | custom-call | flops 1000000000 | bytes 1000000 | tf_op jit(solution)/shard_map/pallas_call | solution.py:1108
  145.6 2.0 dynamic-slice_bitcast_fusion.1
  147.8 12.1 %all_to_all.93 = f32[32,2,8,128]{3,2,1,0:T(8,128)S(1)} all-to-all(f32[32,2,8,128]{3,2,1,0:T(8,128)S(1)} %broadcast_in_dim.10), channel_id=1, replica_groups=mesh['dp'=4,'z'=4,'core'=2] {'dp','z','core'}, dimensions={0} | all-to-all | bytes 524288 | tf_op jit(solution)/shard_map/all_to_all | solution.py:1091
  159.9 2.6 all-to-all-start.8
  162.5 2.0 bitcast_add_fusion.1
  164.5 6.5 %all-to-all-done.8.grads_ref = f32[32,2,640]{2,1,0:T(2,128)S(1)} async-done(((f32[32,2,640]{2,1,0:T(2,128)}), f32[32,2,640]{2,1,0:T(2,128)S(1)}, u32[]{:S(2)}, u32[]{:S(2)}) %all-to-all-start.8) | async-done | bytes 163872 | tf_op jit(solution)/shard_map/all_to_all | solution.py:1064
  171.0 3.6 %all-to-all-start.9 = ((f32[16,9,8,128]{3,2,1,0:T(8,128)}), f32[16,9,8,128]{3,2,1,0:T(8,128)S(1)}, u32[]{:S(2)}, u32[]{:S(2)}) async-start(f32[16,9,8,128]{3,2,1,0:T(8,128)} %bitcast.7), calls=%async_computation.9 | async-start | bytes 1179648 | tf_op jit(solution)/shard_map/all_to_all | solution.py:1086
  174.6 19.2 %shard_map.322 = (f32[2048,128]{1,0:T(8,128)}, f32[32,2,768]{2,1,0:T(2,128)S(1)}, f32[100,8,128]{2,1,0:T(8,128)S(1)}, f32[8,640]{1,0:T(8,128)S(1)}) custom-call(s32[2]{0:T(128)S(1)} %copy-done.7, f32[32,2,640]{2,1,0:T(2,128)S(1)} %all-to-all-done.8.grads_ref, f32[8,640]{1,0:T(8,128)S(1)} %get-tuple-element.143.stat_ref.stat2_ref.stat12_ref, ...), custom_call_target="tpu_custom_call" | custom-call | flops 1000000000 | bytes 1000000 | tf_op jit(solution)/shard_map/pallas_call | solution.py:1108
  193.8 15.3 %all_to_all.94.top_ref.one_ref = f32[32,2,768]{2,1,0:T(2,128)S(1)} all-to-all(f32[32,2,768]{2,1,0:T(2,128)S(1)} %get-tuple-element.161), channel_id=1, replica_groups=mesh['dp'=4,'z'=4,'core'=2] {'dp','z','core'}, dimensions={0} | all-to-all | bytes 393216 | tf_op jit(solution)/shard_map/all_to_all | solution.py:1064
  210.0 3.8 %all-to-all-start.11 = ((f32[16,9,8,128]{3,2,1,0:T(8,128)}), f32[16,9,8,128]{3,2,1,0:T(8,128)S(1)}, u32[]{:S(2)}, u32[]{:S(2)}) async-start(f32[16,9,8,128]{3,2,1,0:T(8,128)} %broadcast_in_dim.12), calls=%async_computation.11 | async-start | bytes 1179648 | tf_op jit(solution)/shard_map/all_to_all | solution.py:1091
  213.8 21.4 %shard_map.323 = (f32[2048,128]{1,0:T(8,128)}, f32[8,128]{1,0:T(8,128)S(1)}, f32[256,8,640]{2,1,0:T(8,128)}, f32[32,2,640]{2,1,0:T(2,128)}, f32[384,8,128]{2,1,0:T(8,128)}) custom-call(s32[2]{0:T(128)S(1)} %copy-done.7, f32[32,2,768]{2,1,0:T(2,128)S(1)} %all_to_all.94.top_ref.one_ref, f32[8,640]{1,0:T(8,128)S(1)} %get-tuple-element.137.stat_ref.stat1_ref.stat11_ref, ...), custom_call_target="tpu_custom_call" | custom-call | flops 1000000000 | bytes 1000000 | tf_op jit(solution)/shard_map/pallas_call | solution.py:1108
  235.2 2.1 dynamic-slice_bitcast_fusion
  238.0 5.6 %all-to-all-start.12 = ((f32[32,2,640]{2,1,0:T(2,128)}), f32[32,2,640]{2,1,0:T(2,128)S(1)}, u32[]{:S(2)}, u32[]{:S(2)}) async-start(f32[32,2,640]{2,1,0:T(2,128)} %get-tuple-element.172), calls=%async_computation.12 | async-start | bytes 327680 | tf_op jit(solution)/shard_map/all_to_all | solution.py:1064
  243.6 2.1 bitcast_add_fusion
  245.7 6.3 %all-to-all-done.12.grads_ref = f32[32,2,640]{2,1,0:T(2,128)S(1)} async-done(((f32[32,2,640]{2,1,0:T(2,128)}), f32[32,2,640]{2,1,0:T(2,128)S(1)}, u32[]{:S(2)}, u32[]{:S(2)}) %all-to-all-start.12) | async-done | bytes 163872 | tf_op jit(solution)/shard_map/all_to_all | solution.py:1064
  252.1 4.3 %all-to-all-start.13 = ((f32[16,12,8,128]{3,2,1,0:T(8,128)}), f32[16,12,8,128]{3,2,1,0:T(8,128)}, u32[]{:S(2)}, u32[]{:S(2)}) async-start(f32[16,12,8,128]{3,2,1,0:T(8,128)} %bitcast.12), calls=%async_computation.13 | async-start | bytes 1572864 | tf_op jit(solution)/shard_map/all_to_all | solution.py:1086
  256.4 19.1 %shard_map.324 = (f32[2048,128]{1,0:T(8,128)}, f32[8,384]{1,0:T(8,128)S(1)}, f32[60,8,128]{2,1,0:T(8,128)S(1)}, f32[8,384]{1,0:T(8,128)S(1)}) custom-call(s32[2]{0:T(128)S(1)} %copy-done.7, f32[32,2,640]{2,1,0:T(2,128)S(1)} %all-to-all-done.12.grads_ref, f32[8,640]{1,0:T(8,128)S(1)} %get-tuple-element.151.stat_ref.stat2_ref.stat02_ref, ...), custom_call_target="tpu_custom_call" | custom-call | flops 1000000000 | bytes 1000000 | tf_op jit(solution)/shard_map/pallas_call | solution.py:1108
  275.5 3.7 %all-to-all-done.13 = f32[16,12,8,128]{3,2,1,0:T(8,128)} async-done(((f32[16,12,8,128]{3,2,1,0:T(8,128)}), f32[16,12,8,128]{3,2,1,0:T(8,128)}, u32[]{:S(2)}, u32[]{:S(2)}) %all-to-all-start.13) | async-done | bytes 786464 | tf_op jit(solution)/shard_map/all_to_all | solution.py:1086
  279.2 1.2 reduce_sum.38
  281.4 4.6 %all-to-all-start.14 = ((f32[16,12,8,128]{3,2,1,0:T(8,128)}), f32[16,12,8,128]{3,2,1,0:T(8,128)}, u32[]{:S(2)}, u32[]{:S(2)}) async-start(f32[16,12,8,128]{3,2,1,0:T(8,128)} %broadcast_in_dim.13), calls=%async_computation.14 | async-start | bytes 1572864 | tf_op jit(solution)/shard_map/all_to_all | solution.py:1091
  286.0 14.9 %shard_map.325 = (f32[2048,128]{1,0:T(8,128)}, f32[32,2,640]{2,1,0:T(2,128)}, f32[128,8,128]{2,1,0:T(8,128)S(1)}, f32[8,256]{1,0:T(8,128)S(1)}) custom-call(s32[2]{0:T(128)S(1)} %copy-done.7, f32[32,2,640]{2,1,0:T(2,128)S(1)} %all-to-all-done.12.grads_ref, f32[8,640]{1,0:T(8,128)S(1)} %get-tuple-element.151.stat_ref.stat2_ref.stat02_ref, ...), custom_call_target="tpu_custom_call" | custom-call | flops 1000000000 | bytes 1000000 | tf_op jit(solution)/shard_map/pallas_call | solution.py:1108
  300.9 7.9 %all-to-all-done.14 = f32[16,12,8,128]{3,2,1,0:T(8,128)} async-done(((f32[16,12,8,128]{3,2,1,0:T(8,128)}), f32[16,12,8,128]{3,2,1,0:T(8,128)}, u32[]{:S(2)}, u32[]{:S(2)}) %all-to-all-start.14) | async-done | bytes 786464 | tf_op jit(solution)/shard_map/all_to_all | solution.py:1091
  310.0 2.6 all-to-all-start.15
  312.6 1.7 bitcast_add_fusion.2
  314.3 6.8 %all-to-all-done.15.zero_ref = f32[32,2,640]{2,1,0:T(2,128)S(1)} async-done(((f32[32,2,640]{2,1,0:T(2,128)}), f32[32,2,640]{2,1,0:T(2,128)S(1)}, u32[]{:S(2)}, u32[]{:S(2)}) %all-to-all-start.15) | async-done | bytes 163872 | tf_op jit(solution)/shard_map/all_to_all | solution.py:1064
  321.9 3.5 all-to-all-start.16
  326.2 7.8 %shard_map.326 = (f32[112,2048]{1,0:T(8,128)}, f32[2,112,640]{2,1,0:T(8,128)S(1)}, f32[16,640]{1,0:T(8,128)S(1)}, f32[4,640]{1,0:T(4,128)}, f32[4,640]{1,0:T(4,1...) custom-call(s32[2]{0:T(128)S(1)} %copy-done.7, ...), custom_call_target="tpu_custom_call" | custom-call | flops 1000000000 | bytes 1000000 | tf_op jit(solution)/shard_map/pallas_call | solution.py:1108
  333.9 3.1 all-to-all-done.16
  337.0 14.6 %all_to_all.95 = f32[16,4,8,128]{3,2,1,0:T(8,128)S(1)} all-to-all(f32[16,4,8,128]{3,2,1,0:T(8,128)S(1)} %broadcast_in_dim.14), channel_id=1, replica_groups=mesh['dp'=4,'z'=4,'core'=2] {'dp','z'}, dimensions={0} | all-to-all | bytes 524288 | tf_op jit(solution)/shard_map/all_to_all | solution.py:1091
  351.7 1.5 collective-permute-done.5.late_other_ref
  353.2 3.2 shard_map.327
  (72 shorter events, 8.8 us)
Async XLA Ops:
  0.7 1.1 copy-start
  1.7 0.7 copy-start.6
  2.4 1.2 copy-start.14
  3.6 10.8 %copy-start.19 = (f32[2,45,640]{2,0,1:T(2,128)S(1)}, f32[2,45,640]{2,0,1:T(2,128)}, u32[]{:S(2)}) copy-start(f32[2,45,640]{2,0,1:T(2,128)} %param.27) | copy-start | bytes 691204
  3.6 10.8 %copy-start.7 = (s32[2]{0:T(128)S(1)}, s32[2]{0:T(128)}, u32[]{:S(2)}) copy-start(s32[2]{0:T(128)} %counts_ref.25) | copy-start | bytes 28
  3.6 10.9 %copy-start.15 = (f32[112,2048]{1,0:T(8,128)S(1)}, f32[112,2048]{1,0:T(8,128)}, u32[]{:S(2)}) copy-start(f32[112,2048]{1,0:T(8,128)} %video_ref.3) | copy-start | bytes 2752516
  3.6 10.9 %copy-start.16 = (f32[112,512]{1,0:T(8,128)S(1)}, f32[112,512]{1,0:T(8,128)}, u32[]{:S(2)}) copy-start(f32[112,512]{1,0:T(8,128)} %cot_ref.1) | copy-start | bytes 688132
  7.1 16.1 %all-to-all-start = ((f32[32,2,768]{2,1,0:T(2,128)}), f32[32,2,768]{2,1,0:T(2,128)S(1)}, u32[]{:S(2)}, u32[]{:S(2)}) async-start(f32[32,2,768]{2,1,0:T(2,128)} %get-tuple-element.119), calls=%async_computation | async-start | bytes 393216 | tf_op jit(solution)/shard_map/all_to_all | solution.py:1064
  14.4 8.7 %copy-start.1 = (f32[2,640,112]{1,2,0:T(8,128)S(1)}, f32[2,640,112]{1,2,0:T(8,128)}, u32[]{:S(2)}) copy-start(f32[2,640,112]{1,2,0:T(8,128)} %param.22) | copy-start | bytes 1720324
  14.4 8.7 %copy-start.4 = (f32[4,640]{1,0:T(4,128)S(1)}, f32[4,640]{1,0:T(4,128)}, u32[]{:S(2)}) copy-start(f32[4,640]{1,0:T(4,128)} %gain_ref.19) | copy-start | bytes 30724
  14.5 8.7 %copy-start.5 = (f32[4,640]{1,0:T(4,128)S(1)}, f32[4,640]{1,0:T(4,128)}, u32[]{:S(2)}) copy-start(f32[4,640]{1,0:T(4,128)} %bias_ref.17) | copy-start | bytes 30724
  23.1 32.0 %copy-start.2 = (f32[2,160,640]{2,1,0:T(8,128)S(1)}, f32[2,160,640]{2,1,0:T(8,128)}, u32[]{:S(2)}) copy-start(f32[2,160,640]{2,1,0:T(8,128)} %down_ref.7) | copy-start | bytes 2457604
  23.1 32.0 %copy-start.3 = (f32[2,112,640]{2,1,0:T(8,128)S(1)}, f32[2,112,640]{2,1,0:T(8,128)}, u32[]{:S(2)}) copy-start(f32[2,112,640]{2,1,0:T(8,128)} %proj_ref.7) | copy-start | bytes 1720324
  23.1 32.0 %copy-start.8 = (f32[2,640]{1,0:T(2,128)S(1)}, f32[2,640]{1,0:T(2,128)}, u32[]{:S(2)}) copy-start(f32[2,640]{1,0:T(2,128)} %upb_ref.3) | copy-start | bytes 15364
  23.2 32.0 %copy-start.11 = (f32[2,160]{1,0:T(2,128)S(1)}, f32[2,160]{1,0:T(2,128)}, u32[]{:S(2)}) copy-start(f32[2,160]{1,0:T(2,128)} %downb_ref.3) | copy-start | bytes 3844
  55.1 15.2 %copy-start.20 = (f32[2,112]{1,0:T(2,128)S(1)}, f32[2,112]{1,0:T(2,128)}, u32[]{:S(2)}) copy-start(f32[2,112]{1,0:T(2,128)} %param.25) | copy-start | bytes 2692
  55.1 15.2 %copy-start.21 = (f32[2,112]{1,0:T(2,128)S(1)}, f32[2,112]{1,0:T(2,128)}, u32[]{:S(2)}) copy-start(f32[2,112]{1,0:T(2,128)} %param.26) | copy-start | bytes 2692
  67.7 9.8 %all-to-all-start.2 = ((f32[32,2,128]{2,1,0:T(2,128)}), f32[32,2,128]{2,1,0:T(2,128)S(1)}, u32[]{:S(2)}, u32[]{:S(2)}) async-start(f32[32,2,128]{2,1,0:T(2,128)} %get-tuple-element.125), calls=%async_computation.2 | async-start | bytes 65536 | tf_op jit(solution)/shard_map/all_to_all | solution.py:1064
  93.5 14.7 %all-to-all-start.4 = ((f32[32,2,8,128]{3,2,1,0:T(8,128)}), f32[32,2,8,128]{3,2,1,0:T(8,128)S(1)}, u32[]{:S(2)}, u32[]{:S(2)}) async-start(f32[32,2,8,128]{3,2,1,0:T(8,128)} %bitcast.2), calls=%async_computation.4 | async-start | bytes 524288 | tf_op jit(solution)/shard_map/all_to_all | solution.py:1086
  127.8 10.0 %all-to-all-start.6 = ((f32[32,4,128]{2,1,0:T(4,128)}), f32[32,4,128]{2,1,0:T(4,128)S(1)}, u32[]{:S(2)}, u32[]{:S(2)}) async-start(f32[32,4,128]{2,1,0:T(4,128)} %get-tuple-element.139), calls=%async_computation.6 | async-start | bytes 131072 | tf_op jit(solution)/shard_map/all_to_all | solution.py:1064
  145.6 16.9 %copy-start.17 = (f32[288,8,128]{2,1,0:T(8,128)S(1)}, f32[288,8,128]{2,1,0:T(8,128)}, u32[]{:S(2)}) copy-start(f32[288,8,128]{2,1,0:T(8,128)} %get-tuple-element.153) | copy-start | bytes 3538948
  147.6 14.9 %collective-permute-start = (f32[144,8,128]{2,1,0:T(8,128)}, f32[144,8,128]{2,1,0:T(8,128)}, u32[]{:S(2)}, u32[]{:S(2)}) collective-permute-start(f32[144,8,128]{2,1,0:T(8,128)} %dynamic-slice_bitcast_fusion.1), channel_id=1, source_target_pairs={{0,1},{1,0},{2,3},{3,2},{4,5},{5,4},{6,7},{7,6},{8,9},{9,8},{10,11... | collective-permute-start | bytes 1769480 | tf_op jit(solution)/shard_map/ppermute | solution.py:1072
  159.9 11.1 %all-to-all-start.8 = ((f32[32,2,640]{2,1,0:T(2,128)}), f32[32,2,640]{2,1,0:T(2,128)S(1)}, u32[]{:S(2)}, u32[]{:S(2)}) async-start(f32[32,2,640]{2,1,0:T(2,128)} %get-tuple-element.152), calls=%async_computation.8 | async-start | bytes 327680 | tf_op jit(solution)/shard_map/all_to_all | solution.py:1064
  171.0 22.8 %all-to-all-start.9 = ((f32[16,9,8,128]{3,2,1,0:T(8,128)}), f32[16,9,8,128]{3,2,1,0:T(8,128)S(1)}, u32[]{:S(2)}, u32[]{:S(2)}) async-start(f32[16,9,8,128]{3,2,1,0:T(8,128)} %bitcast.7), calls=%async_computation.9 | async-start | bytes 1179648 | tf_op jit(solution)/shard_map/all_to_all | solution.py:1086
  210.0 28.0 %all-to-all-start.11 = ((f32[16,9,8,128]{3,2,1,0:T(8,128)}), f32[16,9,8,128]{3,2,1,0:T(8,128)S(1)}, u32[]{:S(2)}, u32[]{:S(2)}) async-start(f32[16,9,8,128]{3,2,1,0:T(8,128)} %broadcast_in_dim.12), calls=%async_computation.11 | async-start | bytes 1179648 | tf_op jit(solution)/shard_map/all_to_all | solution.py:1091
  237.2 6.4 %collective-permute-start.1 = (f32[192,8,128]{2,1,0:T(8,128)}, f32[192,8,128]{2,1,0:T(8,128)S(1)}, u32[]{:S(2)}, u32[]{:S(2)}) collective-permute-start(f32[192,8,128]{2,1,0:T(8,128)} %dynamic-slice_bitcast_fusion), channel_id=1, source_target_pairs={{0,1},{1,0},{2,3},{3,2},{4,5},{5,4},{6,7},{7,6},{8,9},{9,8},{10,11... | collective-permute-start | bytes 2359304 | tf_op jit(solution)/shard_map/ppermute | solution.py:1072
  238.0 14.1 %collective-permute-start.2 = (f32[144,8,128]{2,1,0:T(8,128)S(1)}, f32[144,8,128]{2,1,0:T(8,128)}, u32[]{:S(2)}, u32[]{:S(2)}) collective-permute-start(f32[144,8,128]{2,1,0:T(8,128)S(1)} %bitcast.39), channel_id=1, source_target_pairs={{0,1},{1,0},{2,3},{3,2},{4,5},{5,4},{6,7},{7,6},{8,9},{9,8},{10,11... | collective-permute-start | bytes 1769480 | tf_op jit(solution)/shard_map/ppermute | solution.py:1072
  238.0 14.1 %all-to-all-start.12 = ((f32[32,2,640]{2,1,0:T(2,128)}), f32[32,2,640]{2,1,0:T(2,128)S(1)}, u32[]{:S(2)}, u32[]{:S(2)}) async-start(f32[32,2,640]{2,1,0:T(2,128)} %get-tuple-element.172), calls=%async_computation.12 | async-start | bytes 327680 | tf_op jit(solution)/shard_map/all_to_all | solution.py:1064
  252.1 27.2 %all-to-all-start.13 = ((f32[16,12,8,128]{3,2,1,0:T(8,128)}), f32[16,12,8,128]{3,2,1,0:T(8,128)}, u32[]{:S(2)}, u32[]{:S(2)}) async-start(f32[16,12,8,128]{3,2,1,0:T(8,128)} %bitcast.12), calls=%async_computation.13 | async-start | bytes 1572864 | tf_op jit(solution)/shard_map/all_to_all | solution.py:1086
  281.4 27.4 %all-to-all-start.14 = ((f32[16,12,8,128]{3,2,1,0:T(8,128)}), f32[16,12,8,128]{3,2,1,0:T(8,128)}, u32[]{:S(2)}, u32[]{:S(2)}) async-start(f32[16,12,8,128]{3,2,1,0:T(8,128)} %broadcast_in_dim.13), calls=%async_computation.14 | async-start | bytes 1572864 | tf_op jit(solution)/shard_map/all_to_all | solution.py:1091
  300.8 25.3 %copy-start.9 = (f32[4,640]{1,0:T(4,128)S(1)}, f32[4,640]{1,0:T(4,128)}, u32[]{:S(2)}) copy-start(f32[4,640]{1,0:T(4,128)} %means_ref.1) | copy-start | bytes 30724
  300.8 25.3 %copy-start.10 = (f32[4,640]{1,0:T(4,128)S(1)}, f32[4,640]{1,0:T(4,128)}, u32[]{:S(2)}) copy-start(f32[4,640]{1,0:T(4,128)} %vars_ref.1) | copy-start | bytes 30724
  300.9 25.3 %copy-start.12 = (f32[2,112]{1,0:T(2,128)S(1)}, f32[2,112]{1,0:T(2,128)}, u32[]{:S(2)}) copy-start(f32[2,112]{1,0:T(2,128)} %nmeans_ref.1) | copy-start | bytes 2692
  300.9 25.3 %copy-start.13 = (f32[2,112]{1,0:T(2,128)S(1)}, f32[2,112]{1,0:T(2,128)}, u32[]{:S(2)}) copy-start(f32[2,112]{1,0:T(2,128)} %nvars_ref.1) | copy-start | bytes 2692
  308.7 12.3 %collective-permute-start.4 = (f32[192,8,128]{2,1,0:T(8,128)}, f32[192,8,128]{2,1,0:T(8,128)S(1)}, u32[]{:S(2)}, u32[]{:S(2)}) collective-permute-start(f32[192,8,128]{2,1,0:T(8,128)} %bitcast.13.pack0_ref), channel_id=1, source_target_pairs={{0,1},{1,0},{2,3},{3,2},{4,5},{5,4},{6,7},{7,6},{8,9},{9,8},{10,11... | collective-permute-start | bytes 2359304 | tf_op jit(solution)/shard_map/ppermute | solution.py:1072
  309.9 2.7 collective-permute-start.3
  310.0 11.1 %all-to-all-start.15 = ((f32[32,2,640]{2,1,0:T(2,128)}), f32[32,2,640]{2,1,0:T(2,128)S(1)}, u32[]{:S(2)}, u32[]{:S(2)}) async-start(f32[32,2,640]{2,1,0:T(2,128)} %get-tuple-element.190), calls=%async_computation.15 | async-start | bytes 327680 | tf_op jit(solution)/shard_map/all_to_all | solution.py:1064
  321.0 0.9 copy-start.18
  321.9 15.1 %all-to-all-start.16 = ((f32[16,4,8,128]{3,2,1,0:T(8,128)}), f32[16,4,8,128]{3,2,1,0:T(8,128)S(1)}, u32[]{:S(2)}, u32[]{:S(2)}) async-start(f32[16,4,8,128]{3,2,1,0:T(8,128)} %bitcast.18), calls=%async_computation.16 | async-start | bytes 524288 | tf_op jit(solution)/shard_map/all_to_all | solution.py:1086
  351.7 1.5 collective-permute-start.5

commit v3 on v2

--- a/solution.py
+++ b/solution.py
@@ -185,31 +185,51 @@
         w_ref[tap] = jnp.broadcast_to(taps_ref[0, tap : tap + 1, :], (8, LANES))
 
 
-def conv_full(t, k, a_ref, w_ref, d_ref, fresh):
-    weights = [w_ref[k * 9 + tap] for tap in range(9)]
+PAIRS = SIDE // 2
+
+
+def row_pairs(plane):
+    pair = plane.reshape(PAIRS, 2, 8, LANES)
+    d1 = pair[:, 0]
+    d2 = pair[:, 1]
+    edge = jnp.zeros((1, 8, LANES), F32)
+    d0 = jnp.concatenate([edge, d2[:-1]], axis=0)
+    d3 = jnp.concatenate([d1[1:], edge], axis=0)
+    return (d0 - d2, d1 + d2, d2 - d1, d1 - d3)
+
+
+def pair_rows(parts):
+    upper = parts[:, 0] + parts[:, 1] + parts[:, 2]
+    lower = parts[:, 1] - parts[:, 2] - parts[:, 3]
+    return jnp.stack([upper, lower], axis=1).reshape(FULL_ROWS, 8, LANES)
+
+
+def spread_pairs(taps_ref, w_ref):
+    for k in range(LAGS):
+        for c in range(3):
+            g0, g1, g2 = (taps_ref[0, k * 9 + 3 * r + c : k * 9 + 3 * r + c + 1, :] for r in range(3))
+            outside = 0.5 * (g0 + g2)
+            combined = (g0, outside + 0.5 * g1, outside - 0.5 * g1, g2)
+            for place in range(4):
+                w_ref[k * 12 + 3 * place + c] = jnp.broadcast_to(combined[place], (8, LANES))
+
+
+def conv_full(t, k, a_ref, b_ref, w_ref, m_ref, fresh):
+    weights = [w_ref[k * 12 + tap] for tap in range(12)]
     source = t - k
-    rows = {}
-    for i in range(SIDE):
-        for need in (i, i + 1, i + 2):
-            if need not in rows:
-                rows[need] = [a_ref[source, plane, need] for plane in range(4)]
-        even = None
-        odd = None
-        for r in range(3):
-            a_even, a_odd, a_odd_down, a_even_up = rows[i + r]
-            left, centre, right = weights[3 * r : 3 * r + 3]
-            part_even = centre * a_even + right * a_odd + left * a_odd_down
-            part_odd = centre * a_odd + left * a_even + right * a_even_up
-            even = part_even if even is None else even + part_even
-            odd = part_odd if odd is None else odd + part_odd
-        rows.pop(i)
-        at = t * FULL_ROWS + 2 * i
-        if fresh:
-            d_ref[at] = even
-            d_ref[at + 1] = odd
-        else:
-            d_ref[at] = d_ref[at] + even
-            d_ref[at + 1] = d_ref[at + 1] + odd
+    for m in range(PAIRS):
+        for place in range(4):
+            left, centre, right = weights[3 * place : 3 * place + 3]
+            a_even, a_odd = (a_ref[source, plane, place, m] for plane in range(2))
+            a_odd_down, a_even_up = (b_ref[source, plane, place, m] for plane in range(2))
+            even = centre * a_even + right * a_odd + left * a_odd_down
+            odd = centre * a_odd + left * a_even + right * a_even_up
+            if fresh:
+                m_ref[m, place, 0] = even
+                m_ref[m, place, 1] = odd
+            else:
+                m_ref[m, place, 0] = m_ref[m, place, 0] + even
+                m_ref[m, place, 1] = m_ref[m, place, 1] + odd
 
 
 def conv_half(t, k, a_ref, w_ref, d_ref, fresh):
@@ -347,25 +367,29 @@
     send_all(send_ref, sums, slice(0, w.shape[1]))
 
 
-def write_first(t, total, values, scale, shift, a_ref, planes):
+def write_first(t, total, values, scale, shift, a_ref, b_ref):
     half_pre = values * scale + shift
     first = (half_pre + half_pre * half_tanh(half_pre)) * live_value(t, total)
     first = first.reshape(SIDE, 2, 8, LANES)
     even = first[:, 0]
     odd = first[:, 1]
-    a_ref[t, 0, 1 : SIDE + 1] = even
-    a_ref[t, 1, 1 : SIDE + 1] = odd
-    if planes >= 3:
+    if b_ref is None:
+        a_ref[t, 0, 1 : SIDE + 1] = even
+        a_ref[t, 1, 1 : SIDE + 1] = odd
         a_ref[t, 2, 1 : SIDE + 1] = columns_down(odd)
-    if planes >= 4:
-        a_ref[t, 3, 1 : SIDE + 1] = columns_up(even)
+        return
+    for ref, plane, values in ((a_ref, 0, even), (a_ref, 1, odd), (b_ref, 0, columns_down(odd)), (b_ref, 1, columns_up(even))):
+        for place, part in enumerate(row_pairs(values)):
+            ref[t, plane, place] = part
 
 
 def expand_kernel(
     block, counts_ref, sums_ref, count_ref, rows_ref, w_ref, gain_ref, bias_ref, taps_ref,
-    e_ref, d_ref, stat_ref, send_ref, a_ref, taps8_ref,
+    e_ref, d_ref, stat_ref, send_ref, a_ref, taps8_ref, *pair_refs,
 ):
-    clear_edges(a_ref)
+    b_ref, m_ref = pair_refs if pair_refs else (None, None)
+    if block:
+        clear_edges(a_ref)
     total = live_frames(counts_ref)
     frames = a_ref.shape[0]
     count = count_ref[2:3, :] if block else row_total(count_ref)[0:1]
@@ -381,23 +405,29 @@
         at = pl.ds(pl.multiple_of(t * 256, 256), 256)
         values = fold_right(plain_dot(rows_ref[at, :], square)).reshape(FULL_ROWS, 8, LANES)
         e_ref[pl.ds(pl.multiple_of(t * FULL_ROWS, FULL_ROWS), FULL_ROWS)] = values
-        write_first(t, total, values, scale, shift, a_ref, 3 if block else 4)
+        write_first(t, total, values, scale, shift, a_ref, b_ref)
         return carry
 
     each_frame(frames, expand, 0)
-    spread_taps(taps_ref, taps8_ref)
     per_frame = HALF_ROWS if block else FULL_ROWS
-    conv = conv_half if block else conv_full
+    if block:
+        spread_taps(taps_ref, taps8_ref)
+        conv = functools.partial(conv_half, a_ref=a_ref, w_ref=taps8_ref, d_ref=d_ref)
+    else:
+        spread_pairs(taps_ref, taps8_ref)
+        conv = functools.partial(conv_full, a_ref=a_ref, b_ref=b_ref, w_ref=taps8_ref, m_ref=m_ref)
 
     def frame(t, carry):
-        conv(t, 0, a_ref, taps8_ref, d_ref, True)
+        conv(t, 0, fresh=True)
         last = jnp.minimum(place_of(counts_ref, t), LAGS - 1)
 
         def lag(k, inner):
-            conv(t, k, a_ref, taps8_ref, d_ref, False)
+            conv(t, k, fresh=False)
             return inner
 
         lax.fori_loop(1, last + 1, lag, 0)
+        if not block:
+            d_ref[pl.ds(t * per_frame, per_frame)] = pair_rows(m_ref[...])
         values = d_ref[pl.ds(t * per_frame, per_frame)]
         return (carry[0] + jnp.sum(values, axis=0), carry[1] + jnp.sum(values * values, axis=0))
 
@@ -740,47 +770,46 @@
         pre_ref, dy2_ref, send_ref, pack_ref, dz3_ref, dz3t_ref, excited_ref, dexc_ref, dgate_ref, head,
     )
 
-def back_full(t, k, a_ref, w_ref, z_ref, f_ref, dw_ref, fresh):
-    weights = [w_ref[k * 9 + tap] for tap in range(9)]
+def back_full(t, k, a_ref, w_ref, z_ref, raw_ref, f_ref, dw_ref, fresh):
+    weights = [w_ref[k * 12 + tap] for tap in range(12)]
     target = t - k
-    sums = [None] * 9
-    a_rows = {}
-    z_rows = {}
-    for i in range(SIDE):
-        for need in (i, i + 1, i + 2):
-            if need not in a_rows:
-                a_rows[need] = [a_ref[target, plane, need] for plane in range(2)]
-                z_rows[need] = [z_ref[t, plane, need] for plane in range(4)]
-        even = None
-        odd = None
-        z_even, z_odd, z_odd_down, z_even_up = z_rows[i + 1]
-        for r in range(3):
-            b_even, b_odd, b_odd_down, b_even_up = z_rows[i + 2 - r]
-            left, centre, right = weights[3 * r : 3 * r + 3]
-            part_even = centre * b_even + right * b_odd_down + left * b_odd
-            part_odd = centre * b_odd + right * b_even + left * b_even_up
-            even = part_even if even is None else even + part_even
-            odd = part_odd if odd is None else odd + part_odd
-            a_even, a_odd = a_rows[i + r]
+    sums = [None] * 12
+    for m in range(PAIRS):
+        for place in range(4):
+            flipped = (3, 1, 2, 0)[place]
+            left, centre, right = weights[3 * flipped : 3 * flipped + 3]
+            b_even, b_odd, b_odd_down, b_even_up = (z_ref[t, plane, place, m] for plane in range(4))
+            even = centre * b_even + right * b_odd_down + left * b_odd
+            odd = centre * b_odd + right * b_even + left * b_even_up
+            if fresh:
+                f_ref[target, m, place, 0] = even
+                f_ref[target, m, place, 1] = odd
+            else:
+                f_ref[target, m, place, 0] = f_ref[target, m, place, 0] + even
+                f_ref[target, m, place, 1] = f_ref[target, m, place, 1] + odd
+            if place in (0, 3):
+                row = 0 if place == 0 else 1
+                b_even, b_odd, b_odd_down, b_even_up = (raw_ref[t, plane, row, m] for plane in range(4))
+            a_even, a_odd = (a_ref[target, plane, place, m] for plane in range(2))
             pieces = (
-                z_even_up * a_odd + z_odd * a_even,
-                z_even * a_even + z_odd * a_odd,
-                z_even * a_odd + z_odd_down * a_even,
+                b_even_up * a_odd + b_odd * a_even,
+                b_even * a_even + b_odd * a_odd,
+                b_even * a_odd + b_odd_down * a_even,
             )
             for c in range(3):
-                at = 3 * r + c
+                at = 3 * place + c
                 sums[at] = pieces[c] if sums[at] is None else sums[at] + pieces[c]
-        a_rows.pop(i)
-        z_rows.pop(i)
-        at = target * FULL_ROWS + 2 * i
-        if fresh:
-            f_ref[at] = even
-            f_ref[at + 1] = odd
-        else:
-            f_ref[at] = f_ref[at] + even
-            f_ref[at + 1] = f_ref[at + 1] + odd
-    for tap in range(9):
-        dw_ref[k * 9 + tap] = dw_ref[k * 9 + tap] + sums[tap]
+    for place in range(4):
+        for c in range(3):
+            at = place * 3 * LAGS + k * 3 + c
+            dw_ref[at] = dw_ref[at] + sums[3 * place + c]
+
+
+def pair_taps(totals):
+    count = 3 * LAGS
+    first, second, third, last = (totals[place * count : (place + 1) * count] for place in range(4))
+    middle = 0.5 * (second - third)
+    return (first + middle, 0.5 * (second + third), middle - last)
 
 
 def back_half(t, k, a_ref, w_ref, z_ref, f_ref, dw_ref, fresh):
@@ -823,7 +852,7 @@
 def depth_backward_kernel(
     block, before, final, counts_ref, grads_ref, stat2_ref, stat_ref, nstat_ref, dy2_ref, d_ref, e_ref, a_ref, columns_ref, w_ref,
     gain_ref, bias_ref, taps_ref, z3_ref, dx_in_ref, sums_in_ref, list_in_ref, dxpre_ref, send_ref, q_ref, grad_rows_ref,
-    z_ref, f_ref, taps8_ref, dw_ref, pair_ref,
+    z_ref, f_ref, taps8_ref, dw_ref, pair_ref, *raw_refs,
 ):
     tile = pl.program_id(0)
     tiles = pl.num_programs(0)
@@ -832,11 +861,12 @@
     norm_row = 2 * block
     half = block == 1
     per_frame = HALF_ROWS if half else FULL_ROWS
-    taps = dw_ref.shape[0]
+    taps = taps_ref.shape[1]
 
     @pl.when(tile == 0)
     def start():
-        clear_edges(z_ref)
+        if half:
+            clear_edges(z_ref)
         if before:
             dxpre_ref[...] = dx_in_ref[...]
             send_all(send_ref, sums_in_ref[0:2, :], slice(0, before * LANES))
@@ -845,7 +875,10 @@
             dxpre_ref[...] = jnp.zeros_like(dxpre_ref)
 
         def dead(t, carry):
-            f_ref[pl.ds(t * FULL_ROWS, FULL_ROWS)] = jnp.zeros((FULL_ROWS, 8, LANES), F32)
+            if half:
+                f_ref[pl.ds(t * FULL_ROWS, FULL_ROWS)] = jnp.zeros((FULL_ROWS, 8, LANES), F32)
+            else:
+                f_ref[t] = jnp.zeros(f_ref.shape[1:], F32)
             return carry
 
         lax.fori_loop(total, frames, dead, 0)
@@ -872,23 +905,32 @@
             z_ref[t, 1, 0:HALF_ROWS] = columns_up(dz)
         else:
             pair = dz.reshape(SIDE, 2, 8, LANES)
-            z_ref[t, 0, 1 : SIDE + 1] = pair[:, 0]
-            z_ref[t, 1, 1 : SIDE + 1] = pair[:, 1]
-            z_ref[t, 2, 1 : SIDE + 1] = columns_down(pair[:, 1])
-            z_ref[t, 3, 1 : SIDE + 1] = columns_up(pair[:, 0])
+            even = pair[:, 0]
+            odd = pair[:, 1]
+            for plane, values in enumerate((even, odd, columns_down(odd), columns_up(even))):
+                for place, part in enumerate(row_pairs(values)):
+                    z_ref[t, plane, place] = part
+                rows = values.reshape(PAIRS, 2, 8, LANES)
+                raw_refs[0][t, plane, 0] = rows[:, 0]
+                raw_refs[0][t, plane, 1] = rows[:, 1]
         return carry
 
     each_frame(frames, fill, 0)
-    spread_taps(taps_ref, taps8_ref)
     dw_ref[...] = jnp.zeros_like(dw_ref)
-    back = back_half if half else back_full
+    refs = dict(a_ref=a_ref, w_ref=taps8_ref, z_ref=z_ref, f_ref=f_ref, dw_ref=dw_ref)
+    if half:
+        spread_taps(taps_ref, taps8_ref)
+        back = functools.partial(back_half, **refs)
+    else:
+        spread_pairs(taps_ref, taps8_ref)
+        back = functools.partial(back_full, raw_ref=raw_refs[0], **refs)
 
     def frame(t, carry):
-        back(t, 0, a_ref, taps8_ref, z_ref, f_ref, dw_ref, True)
+        back(t, 0, fresh=True)
         last = jnp.minimum(place_of(counts_ref, t), LAGS - 1)
 
         def lag(k, inner):
-            back(t, k, a_ref, taps8_ref, z_ref, f_ref, dw_ref, False)
+            back(t, k, fresh=False)
             return inner
 
         return lax.fori_loop(1, last + 1, lag, carry)
@@ -901,7 +943,8 @@
         flat = pl.ds(pl.multiple_of(t * 256, 256), 256)
         values = e_ref[rows]
         half_pre = values * scale_half + shift_half
-        dy = f_ref[rows] * silu_slope(half_pre, half_tanh(half_pre))
+        dfirst = f_ref[rows] if half else pair_rows(f_ref[t])
+        dy = dfirst * silu_slope(half_pre, half_tanh(half_pre))
         summed = carry[0] + jnp.sum(dy, axis=0)
         cross = carry[1] + jnp.sum(dy * (values - average_one), axis=0)
         dy = dy.reshape(256, LANES)
@@ -920,9 +963,9 @@
     gathered = fold_square(plain_dot(columns_ref[...], pair_ref[...]))
     narrow = w_ref.shape[1]
     dtaps = jnp.sum(dw_ref[...], axis=1)
-    unused = (-taps) % 8
-    dtaps = jnp.concatenate([dtaps, jnp.zeros((unused, LANES), F32)], axis=0)
-    values = jnp.concatenate([gathered[0:narrow], dtaps], axis=0)
+    parts = (dtaps,) if half else pair_taps(dtaps)
+    unused = jnp.zeros(((-taps) % 8, LANES), F32)
+    values = jnp.concatenate((gathered[0:narrow],) + parts + (unused,), axis=0)
     listed = values.shape[0] // 8
     q_ref[pl.ds((tile + before) * listed, listed)] = values.reshape(listed, 8, LANES)
 
@@ -1052,7 +1095,13 @@
             values = rows_of(lists[block], (per_pack * tiles if block else 0) + tile * per_tile, per_tile)
             dw = values[0:narrow] * factor_ref[8 * block : 8 * block + 1, lanes] - less_ref[block, :, lanes]
             dw_ref[block, :, lanes] = dw
-            dtaps_ref[block, :, lanes] = values[narrow : narrow + taps]
+            if block:
+                dtaps_ref[block, :, lanes] = values[narrow : narrow + taps]
+                continue
+            for r in range(3):
+                for k in range(LAGS):
+                    source = narrow + r * 3 * LAGS + 3 * k
+                    dtaps_ref[block, k * 9 + 3 * r : k * 9 + 3 * r + 3, lanes] = values[source : source + 3]
         ddownb_ref[block : block + 1, :] = jnp.concatenate(down_rows, axis=1)[:, 0:squeeze]
 
 
@@ -1203,20 +1252,30 @@
     )
     sums = exchange(sums)
 
-    def planes_of(planes, begin=0):
-        return pl.BlockSpec((frames, planes, SIDE + 2, 8, LANES), lambda j: (0, 0, 0, 0, j + begin))
+    def planes_shape(block, lanes, planes):
+        if block:
+            return (frames, planes, SIDE + 2, 8, lanes)
+        return (frames, planes, 4, PAIRS, 8, lanes)
+
+    def planes_of(block, planes, begin=0):
+        dims = planes_shape(block, LANES, planes)
+        zeros = (0,) * (len(dims) - 1)
+        return pl.BlockSpec(dims, lambda j: zeros + (j + begin,))
 
     def expand(block, sums, count, count_spec, rows):
         depth_rows = half_rows if block else full_rows
-        planes = 3 if block else 4
+        planes = 3 if block else 2
+        scratch = [pltpu.VMEM((taps if block else 12 * LAGS, 8, LANES), F32)]
+        if not block:
+            scratch = scratch + [pltpu.VMEM(planes_shape(0, LANES, 2), F32), pltpu.VMEM((PAIRS, 4, 2, 8, LANES), F32)]
         return call(
             functools.partial(expand_kernel, block), (tiles,),
             [SCALARS, tile_sums(), count_spec, whole(rows), weight_tile(block, cin), tile_rows(4), tile_rows(4),
              weight_tile(block, taps)],
-            [tile_cube(full_rows), tile_cube(depth_rows), tile_rows(8), tile_sums(), planes_of(planes)],
+            [tile_cube(full_rows), tile_cube(depth_rows), tile_rows(8), tile_sums(), planes_of(block, planes)],
             [shape(full_rows, 8, width), shape(depth_rows, 8, width), shape(8, width), shape(devices, 2, width),
-             shape(frames, planes, SIDE + 2, 8, width)],
-            [pltpu.VMEM((taps, 8, LANES), F32)],
+             shape(*planes_shape(block, width, planes))],
+            scratch,
             (frame_counts, sums, count, rows, w_t, wide_gains, wide_biases, depth_weight),
         )
 
@@ -1290,14 +1349,21 @@
         (frame_counts, third, z_one, cot, ngains, nbiases, stat12, d_one, wide_gains, wide_biases, squeeze_weight, up_t,
          project_weight, gates_one, running_one, pre_one),
     )
-    sums, gram = together(sums, gram)
+    sums, pack_one, gram = together(sums, pack_one, gram)
     sums, pack_one = together(exchange(sums), add_cores(pack_one))
     pack_one = share_out(pack_one)
     nothing = jnp.zeros((8, LANES), F32)
 
     def depth_backward(block, begin, end, sums, stat2, stat, dy2, depth, expanded, planes, columns, dx_in, sums_in, list_in):
         rows = half_rows if block else full_rows
-        z_shape = (frames, 2, HALF_ROWS + 1, 8, LANES) if block else (frames, 4, SIDE + 2, 8, LANES)
+        if block:
+            taps_shape = (taps, 8, LANES)
+            z_shape = (frames, 2, HALF_ROWS + 1, 8, LANES)
+            f_shape = (full_rows, 8, LANES)
+        else:
+            taps_shape = (12 * LAGS, 8, LANES)
+            z_shape = planes_shape(0, LANES, 4)
+            f_shape = (frames, PAIRS, 4, 2, 8, LANES)
         count = end - begin
         final = end == tiles
         listed = round_up(end * q_tiles) if final and not block else end * q_tiles
@@ -1320,12 +1386,13 @@
         return call(
             functools.partial(depth_backward_kernel, block, begin, final), (count,),
             [SCALARS, pl.BlockSpec((devices, 2, LANES), lambda j: (0, 0, j + begin)), wide_rows(8), wide_rows(8), whole(nstat),
-             wide_cube(rows), wide_cube(rows), wide_cube(full_rows), planes_of(2, begin), whole(columns), wide_weight(cin), wide_rows(4),
+             wide_cube(rows), wide_cube(rows), wide_cube(full_rows), planes_of(block, 2, begin), whole(columns), wide_weight(cin), wide_rows(4),
              wide_rows(4), wide_weight(taps), whole(z_zero), whole(dx_in), whole(sums_in), whole(list_in)],
             [fixed(pixels, LANES), send_spec, fixed(listed, 8, LANES), tile_rows(8)],
             [shape(pixels, LANES), shape(*send), shape(listed, 8, LANES), shape(8, count * LANES)],
-            [pltpu.VMEM(z_shape, F32), pltpu.VMEM((full_rows, 8, LANES), F32),
-             pltpu.VMEM((taps, 8, LANES), F32), pltpu.VMEM((taps, 8, LANES), F32), pltpu.VMEM((pixels, 2 * LANES), low)],
+            [pltpu.VMEM(z_shape, F32), pltpu.VMEM(f_shape, F32), pltpu.VMEM(taps_shape, F32), pltpu.VMEM(taps_shape, F32),
+             pltpu.VMEM((pixels, 2 * LANES), low)]
+            + ([] if block else [pltpu.VMEM((frames, 4, 2, PAIRS, 8, LANES), F32)]),
             (frame_counts, sums, stat2, stat, nstat, dy2, depth, expanded, planes, columns, w_t, wide_gains, wide_biases,
              depth_weight, z_zero, dx_in, sums_in, list_in),
         )

time: 361 us -> 350 us (0.970)
  Pallas kernels: 155 us -> 148 us
    all_to_all x2 -> x1, blocking collectives: 26.7 us -> 14.6 us  [share_back(): lax.all_to_all(jnp.broadcast_to(own[None], pieces.shape), names, 0, 0, ti...]
    all_to_all x4 -> x5, blocking collectives: 53.1 us -> 64.1 us  [exchange(): return lax.all_to_all(send, AXES, 0, 0, tiled=True)]
    all_to_all x6 -> x5, waiting for transfers between devices: 39.4 us -> 32 us  [exchange(): return lax.all_to_all(send, AXES, 0, 0, tiled=True)]
    pallas_call x14, Pallas kernels: 155 us -> 148 us  [call(): pl.pallas_call(kernel, grid=grid, in_specs=in_specs, out_specs=out_specs,...]
    all_to_all x2 -> x3, waiting for transfers between devices: 7.86 us -> 11.2 us  [share_back(): lax.all_to_all(jnp.broadcast_to(own[None], pieces.shape), names, 0, 0, ti...]
    all_to_all x2 -> x3, starting transfers between devices: 8.43 us -> 10.7 us  [share_back(): lax.all_to_all(jnp.broadcast_to(own[None], pieces.shape), names, 0, 0, ti...]
    all_to_all x6 -> x5, starting transfers between devices: 23.2 us -> 21.2 us  [exchange(): return lax.all_to_all(send, AXES, 0, 0, tiled=True)]
  transfers between devices with their start and end apart: 18 -> 18, of which waited for: 10 -> 10; matrix products, arithmetic and copies ran while one was open for 2% -> 2% of each run, Pallas kernels for 27% -> 29%
where the time goes in v3:
time: 350 us; the launch traced here: 348 us
  Pallas kernels  148 us (42%)
  blocking collectives  78.8 us (23%)
  waiting for transfers between devices  53.8 us (15%)
  starting transfers between devices  47.6 us (14%)
  local copies, waits for them, and re-layouts  11.2 us (3%)
  other arithmetic  7.07 us (2%)
    pallas_call x14, Pallas kernels, call(): pl.pallas_call(kernel, grid=grid, in_specs=in_specs, out_specs=out_specs,...  148 us
    all_to_all x5, blocking collectives, exchange(): return lax.all_to_all(send, AXES, 0, 0, tiled=True)  64.1 us
    all_to_all x5, waiting for transfers between devices, exchange(): return lax.all_to_all(send, AXES, 0, 0, tiled=True)  32 us
    all_to_all x5, starting transfers between devices, exchange(): return lax.all_to_all(send, AXES, 0, 0, tiled=True)  21.2 us
    all_to_all x1, blocking collectives, share_back(): lax.all_to_all(jnp.broadcast_to(own[None], pieces.shape), names, 0, 0, ti...  14.6 us
    all_to_all x4, starting transfers between devices, share_out(): lax.all_to_all(tiles.reshape(count, -1, *tiles.shape[1:]), names, 0, 0, t...  14 us
    all_to_all x3, waiting for transfers between devices, share_back(): lax.all_to_all(jnp.broadcast_to(own[None], pieces.shape), names, 0, 0, ti...  11.2 us
    all_to_all x3, starting transfers between devices, share_back(): lax.all_to_all(jnp.broadcast_to(own[None], pieces.shape), names, 0, 0, ti...  10.7 us
  transfers between devices with their start and end apart: 18, of which 10 were waited for; matrix products, arithmetic and copies ran while one was open for 2% of the time, Pallas kernels for 29%

profile of v3, /device:TPU:0, one launch (start us, length us, event | category | flops | bytes accessed | tf_op | source)
XLA Modules:
  0.0 348.5 jit_solution(16062059873208621306)
XLA Ops:
  2.4 1.2 copy-done.14
  3.6 3.5 %shard_map.314 = (f32[136,128]{1,0:T(8,128)S(1)}, f32[32,2,768]{2,1,0:T(2,128)}) custom-call(s32[2]{0:T(128)S(1)} %copy-done.6, f32[112,2048]{1,0:T(8,128)S(1)} %copy-done.14, f32[2,112,640]{2,1,0:T(8,128)S(1)} %bitcast.28), custom_call_target="tpu_custom_call" | custom-call | flops 1000000000 | bytes 1000000 | tf_op jit(solution)/shard_map/pallas_call | solution.py:1157
  7.1 7.3 %all-to-all-start = ((f32[32,2,768]{2,1,0:T(2,128)}), f32[32,2,768]{2,1,0:T(2,128)S(1)}, u32[]{:S(2)}, u32[]{:S(2)}) async-start(f32[32,2,768]{2,1,0:T(2,128)} %get-tuple-element.120), calls=%async_computation | async-start | bytes 393216 | tf_op jit(solution)/shard_map/all_to_all | solution.py:1113
  14.5 3.4 shard_map.315
  17.8 5.3 %all-to-all-done.sums_ref.count_ref = f32[32,2,768]{2,1,0:T(2,128)S(1)} async-done(((f32[32,2,768]{2,1,0:T(2,128)}), f32[32,2,768]{2,1,0:T(2,128)S(1)}, u32[]{:S(2)}, u32[]{:S(2)}) %all-to-all-start) | async-done | bytes 196640 | tf_op jit(solution)/shard_map/all_to_all | solution.py:1113
  23.2 17.7 %shard_map.316 = (f32[256,8,640]{2,1,0:T(8,128)}, f32[256,8,640]{2,1,0:T(8,128)}, f32[8,640]{1,0:T(8,128)S(1)}, f32[32,2,640]{2,1,0:T(2,128)S(1)}, f32[8,2,4,8,8,640]{5,4,3,2,1,0:T(8,128)}) custom-call(s32[2]{0:T(128)S(1)} %copy-done.7, f32[32,2,768]{2,1,0:T(2,128)S(1)} %all-to-all-done.sums_ref.count_ref, ...), custom_call_target="tpu_custom_call" | custom-call | flops 1000000000 | bytes 1000000 | tf_op jit(solution)/shard_map/pallas_call | solution.py:1157
  40.9 13.7 %all_to_all.90.sums_ref = f32[32,2,640]{2,1,0:T(2,128)S(1)} all-to-all(f32[32,2,640]{2,1,0:T(2,128)S(1)} %get-tuple-element.122), channel_id=1, replica_groups=mesh['dp'=4,'z'=4,'core'=2] {'dp','z','core'}, dimensions={0} | all-to-all | bytes 327680 | tf_op jit(solution)/shard_map/all_to_all | solution.py:1113
  54.6 12.5 %shard_map.317 = (f32[2048,128]{1,0:T(8,128)}, f32[8,640]{1,0:T(8,128)S(1)}, f32[8,640]{1,0:T(8,128)S(1)}, f32[8,160]{1,0:T(8,128)S(1)}, f32[8,640]{1,0:T(8,128)S(1)}, /*index=5*/f32[32,2,128]{2,1,0:T(2,128)}) custom-call(s32[2]{0:T(128)S(1)} %copy-done.7, f32[32,2,640]{2,1,0:T(2,128)S(1)} %all_to_all.90.sums_ref, ...), custom_call_target="tpu_custom_call" | custom-call | flops 1000000000 | bytes 1000000 | tf_op jit(solution)/shard_map/pallas_call | solution.py:1157
  67.1 2.6 all-to-all-start.2
  69.7 7.2 %all-to-all-done.2.sums_ref = f32[32,2,128]{2,1,0:T(2,128)S(1)} async-done(((f32[32,2,128]{2,1,0:T(2,128)}), f32[32,2,128]{2,1,0:T(2,128)S(1)}, u32[]{:S(2)}, u32[]{:S(2)}) %all-to-all-start.2) | async-done | bytes 32800 | tf_op jit(solution)/shard_map/all_to_all | solution.py:1113
  76.9 5.8 %shard_map.318 = (f32[2048,128]{1,0:T(8,128)}, bf16[2048,256]{1,0:T(8,128)(2,1)}, bf16[256,2048]{1,0:T(8,128)(2,1)}, f32[64,8,128]{2,1,0:T(8,128)}, f32[8,128]{1,0:T(8,128)S(1)}, /*index=5*/f32[32,2,640]{2,1,0:T(2,128)S(1)}) custom-call(s32[2]{0:T(128)S(1)} %copy-done.7, f32[32,2,128]{2,1,0:T(2,128)S(1)} %all-to-all-done.2.sums_ref, ...), custom_call_target="tpu_custom_call" | custom-call | flops 1000000000 | bytes 1000000 | tf_op jit(solution)/shard_map/pallas_call | solution.py:1157
  82.7 10.2 %all_to_all.91.sums_ref = f32[32,2,640]{2,1,0:T(2,128)S(1)} all-to-all(f32[32,2,640]{2,1,0:T(2,128)S(1)} %get-tuple-element.130), channel_id=1, replica_groups=mesh['dp'=4,'z'=4,'core'=2] {'dp','z','core'}, dimensions={0} | all-to-all | bytes 327680 | tf_op jit(solution)/shard_map/all_to_all | solution.py:1113
  92.9 2.6 all-to-all-start.4
  95.4 11.8 %shard_map.319 = (f32[256,8,640]{2,1,0:T(8,128)}, f32[64,8,640]{2,1,0:T(8,128)}, f32[8,640]{1,0:T(8,128)S(1)}, f32[32,2,640]{2,1,0:T(2,128)S(1)}, f32[8,3,18,8,640]{4,3,2,1,0:T(8,128)}) custom-call(s32[2]{0:T(128)S(1)} %copy-done.7, f32[32,2,640]{2,1,0:T(2,128)S(1)} %all_to_all.91.sums_ref, f32[8,128]{1,0:T(8,128)S(1)} %get-tuple-element.133.count_ref.nstat_ref, ...), custom_call_target="tpu_custom_call" | custom-call | flops 1000000000 | bytes 1000000 | tf_op jit(solution)/shard_map/pallas_call | solution.py:1157
  107.3 14.8 %all_to_all.92.sums_ref = f32[32,2,640]{2,1,0:T(2,128)S(1)} all-to-all(f32[32,2,640]{2,1,0:T(2,128)S(1)} %get-tuple-element.137), channel_id=1, replica_groups=mesh['dp'=4,'z'=4,'core'=2] {'dp','z','core'}, dimensions={0} | all-to-all | bytes 327680 | tf_op jit(solution)/shard_map/all_to_all | solution.py:1113
  122.1 4.5 %shard_map.320 = (f32[512,128]{1,0:T(8,128)S(1)}, f32[8,640]{1,0:T(8,128)S(1)}, f32[8,640]{1,0:T(8,128)S(1)}, f32[8,160]{1,0:T(8,128)S(1)}, f32[8,640]{1,0:T(8,128)S(1)}, /*index=5*/f32[32,4,128]{2,1,0:T(4,128)S(1)}) custom-call(s32[2]{0:T(128)S(1)} %copy-done.7, f32[32,2,640]{2,1,0:T(2,128)S(1)} %all_to_all.92.sums_ref, ...), custom_call_target="tpu_custom_call" | custom-call | flops 1000000000 | bytes 1000000 | tf_op jit(solution)/shard_map/pallas_call | solution.py:1157
  126.6 9.5 %all_to_all.93.third_ref = f32[32,4,128]{2,1,0:T(4,128)S(1)} all-to-all(f32[32,4,128]{2,1,0:T(4,128)S(1)} %get-tuple-element.140), channel_id=1, replica_groups=mesh['dp'=4,'z'=4,'core'=2] {'dp','z','core'}, dimensions={0} | all-to-all | bytes 131072 | tf_op jit(solution)/shard_map/all_to_all | solution.py:1113
  136.9 2.6 all-to-all-start.7
  139.5 7.9 %shard_map.321 = (f32[112,512]{1,0:T(8,128)}, f32[8,128]{1,0:T(8,128)S(1)}, f32[64,8,640]{2,1,0:T(8,128)}, f32[32,2,640]{2,1,0:T(2,128)}, f32[288,8,128]{2,1,0:T(8,128)}) custom-call(s32[2]{0:T(128)S(1)} %copy-done.7, f32[32,4,128]{2,1,0:T(4,128)S(1)} %all_to_all.93.third_ref, f32[512,128]{1,0:T(8,128)S(1)} %get-tuple-element.143.z_ref, ...), custom_call_target="tpu_custom_call" | custom-call | flops 1000000000 | bytes 1000000 | tf_op jit(solution)/shard_map/pallas_call | solution.py:1157
  147.3 2.5 all-to-all-done.7
  151.4 3.2 all-to-all-start.8
  154.6 2.0 bitcast_add_fusion.1
  156.6 6.5 %all-to-all-done.8.grads_ref = f32[32,2,640]{2,1,0:T(2,128)S(1)} async-done(((f32[32,2,640]{2,1,0:T(2,128)}), f32[32,2,640]{2,1,0:T(2,128)S(1)}, u32[]{:S(2)}, u32[]{:S(2)}) %all-to-all-start.8) | async-done | bytes 163872 | tf_op jit(solution)/shard_map/all_to_all | solution.py:1113
  163.1 3.6 %all-to-all-start.9 = ((f32[16,9,8,128]{3,2,1,0:T(8,128)}), f32[16,9,8,128]{3,2,1,0:T(8,128)S(1)}, u32[]{:S(2)}, u32[]{:S(2)}) async-start(f32[16,9,8,128]{3,2,1,0:T(8,128)} %bitcast.7), calls=%async_computation.9 | async-start | bytes 1179648 | tf_op jit(solution)/shard_map/all_to_all | solution.py:1135
  166.7 18.7 %shard_map.322 = (f32[2048,128]{1,0:T(8,128)}, f32[32,2,768]{2,1,0:T(2,128)S(1)}, f32[100,8,128]{2,1,0:T(8,128)S(1)}, f32[8,640]{1,0:T(8,128)S(1)}) custom-call(s32[2]{0:T(128)S(1)} %copy-done.7, f32[32,2,640]{2,1,0:T(2,128)S(1)} %all-to-all-done.8.grads_ref, f32[8,640]{1,0:T(8,128)S(1)} %get-tuple-element.144.stat_ref.stat2_ref.stat12_ref, ...), custom_call_target="tpu_custom_call" | custom-call | flops 1000000000 | bytes 1000000 | tf_op jit(solution)/shard_map/pallas_call | solution.py:1157
  185.4 16.0 %all_to_all.94.top_ref.one_ref = f32[32,2,768]{2,1,0:T(2,128)S(1)} all-to-all(f32[32,2,768]{2,1,0:T(2,128)S(1)} %get-tuple-element.163), channel_id=1, replica_groups=mesh['dp'=4,'z'=4,'core'=2] {'dp','z','core'}, dimensions={0} | all-to-all | bytes 393216 | tf_op jit(solution)/shard_map/all_to_all | solution.py:1113
  202.2 3.8 %all-to-all-start.11 = ((f32[16,9,8,128]{3,2,1,0:T(8,128)}), f32[16,9,8,128]{3,2,1,0:T(8,128)S(1)}, u32[]{:S(2)}, u32[]{:S(2)}) async-start(f32[16,9,8,128]{3,2,1,0:T(8,128)} %broadcast_in_dim.12), calls=%async_computation.11 | async-start | bytes 1179648 | tf_op jit(solution)/shard_map/all_to_all | solution.py:1140
  206.0 21.4 %shard_map.323 = (f32[2048,128]{1,0:T(8,128)}, f32[8,128]{1,0:T(8,128)S(1)}, f32[256,8,640]{2,1,0:T(8,128)}, f32[32,2,640]{2,1,0:T(2,128)}, f32[384,8,128]{2,1,0:T(8,128)}) custom-call(s32[2]{0:T(128)S(1)} %copy-done.7, f32[32,2,768]{2,1,0:T(2,128)S(1)} %all_to_all.94.top_ref.one_ref, f32[8,640]{1,0:T(8,128)S(1)} %get-tuple-element.138.stat_ref.stat1_ref.stat11_ref, ...), custom_call_target="tpu_custom_call" | custom-call | flops 1000000000 | bytes 1000000 | tf_op jit(solution)/shard_map/pallas_call | solution.py:1157
  227.4 2.1 dynamic-slice_bitcast_fusion
  230.2 5.6 %all-to-all-start.12 = ((f32[32,2,640]{2,1,0:T(2,128)}), f32[32,2,640]{2,1,0:T(2,128)S(1)}, u32[]{:S(2)}, u32[]{:S(2)}) async-start(f32[32,2,640]{2,1,0:T(2,128)} %get-tuple-element.174), calls=%async_computation.12 | async-start | bytes 327680 | tf_op jit(solution)/shard_map/all_to_all | solution.py:1113
  235.8 2.1 bitcast_add_fusion
  238.0 6.3 %all-to-all-done.12.grads_ref = f32[32,2,640]{2,1,0:T(2,128)S(1)} async-done(((f32[32,2,640]{2,1,0:T(2,128)}), f32[32,2,640]{2,1,0:T(2,128)S(1)}, u32[]{:S(2)}, u32[]{:S(2)}) %all-to-all-start.12) | async-done | bytes 163872 | tf_op jit(solution)/shard_map/all_to_all | solution.py:1113
  244.3 4.3 %all-to-all-start.13 = ((f32[16,12,8,128]{3,2,1,0:T(8,128)}), f32[16,12,8,128]{3,2,1,0:T(8,128)}, u32[]{:S(2)}, u32[]{:S(2)}) async-start(f32[16,12,8,128]{3,2,1,0:T(8,128)} %bitcast.12), calls=%async_computation.13 | async-start | bytes 1572864 | tf_op jit(solution)/shard_map/all_to_all | solution.py:1135
  248.6 16.8 %shard_map.324 = (f32[2048,128]{1,0:T(8,128)}, f32[8,384]{1,0:T(8,128)S(1)}, f32[60,8,128]{2,1,0:T(8,128)S(1)}, f32[8,384]{1,0:T(8,128)S(1)}) custom-call(s32[2]{0:T(128)S(1)} %copy-done.7, f32[32,2,640]{2,1,0:T(2,128)S(1)} %all-to-all-done.12.grads_ref, f32[8,640]{1,0:T(8,128)S(1)} %get-tuple-element.153.stat_ref.stat2_ref.stat02_ref, ...), custom_call_target="tpu_custom_call" | custom-call | flops 1000000000 | bytes 1000000 | tf_op jit(solution)/shard_map/pallas_call | solution.py:1157
  265.4 6.0 %all-to-all-done.13 = f32[16,12,8,128]{3,2,1,0:T(8,128)} async-done(((f32[16,12,8,128]{3,2,1,0:T(8,128)}), f32[16,12,8,128]{3,2,1,0:T(8,128)}, u32[]{:S(2)}, u32[]{:S(2)}) %all-to-all-start.13) | async-done | bytes 786464 | tf_op jit(solution)/shard_map/all_to_all | solution.py:1135
  271.4 1.2 reduce_sum.38
  273.6 4.3 %all-to-all-start.14 = ((f32[16,12,8,128]{3,2,1,0:T(8,128)}), f32[16,12,8,128]{3,2,1,0:T(8,128)}, u32[]{:S(2)}, u32[]{:S(2)}) async-start(f32[16,12,8,128]{3,2,1,0:T(8,128)} %broadcast_in_dim.13), calls=%async_computation.14 | async-start | bytes 1572864 | tf_op jit(solution)/shard_map/all_to_all | solution.py:1140
  277.9 13.4 %shard_map.325 = (f32[2048,128]{1,0:T(8,128)}, f32[32,2,640]{2,1,0:T(2,128)}, f32[128,8,128]{2,1,0:T(8,128)S(1)}, f32[8,256]{1,0:T(8,128)S(1)}) custom-call(s32[2]{0:T(128)S(1)} %copy-done.7, f32[32,2,640]{2,1,0:T(2,128)S(1)} %all-to-all-done.12.grads_ref, f32[8,640]{1,0:T(8,128)S(1)} %get-tuple-element.153.stat_ref.stat2_ref.stat02_ref, ...), custom_call_target="tpu_custom_call" | custom-call | flops 1000000000 | bytes 1000000 | tf_op jit(solution)/shard_map/pallas_call | solution.py:1157
  291.3 8.6 %all-to-all-done.14 = f32[16,12,8,128]{3,2,1,0:T(8,128)} async-done(((f32[16,12,8,128]{3,2,1,0:T(8,128)}), f32[16,12,8,128]{3,2,1,0:T(8,128)}, u32[]{:S(2)}, u32[]{:S(2)}) %all-to-all-start.14) | async-done | bytes 786464 | tf_op jit(solution)/shard_map/all_to_all | solution.py:1140
  301.2 2.6 all-to-all-start.15
  303.8 1.7 bitcast_add_fusion.2
  305.5 6.8 %all-to-all-done.15.zero_ref = f32[32,2,640]{2,1,0:T(2,128)S(1)} async-done(((f32[32,2,640]{2,1,0:T(2,128)}), f32[32,2,640]{2,1,0:T(2,128)S(1)}, u32[]{:S(2)}, u32[]{:S(2)}) %all-to-all-start.15) | async-done | bytes 163872 | tf_op jit(solution)/shard_map/all_to_all | solution.py:1113
  313.1 3.5 %all-to-all-start.16 = ((f32[16,4,8,128]{3,2,1,0:T(8,128)}), f32[16,4,8,128]{3,2,1,0:T(8,128)S(1)}, u32[]{:S(2)}, u32[]{:S(2)}) async-start(f32[16,4,8,128]{3,2,1,0:T(8,128)} %bitcast.18), calls=%async_computation.16 | async-start | bytes 524288 | tf_op jit(solution)/shard_map/all_to_all | solution.py:1135
  317.4 7.8 %shard_map.326 = (f32[112,2048]{1,0:T(8,128)}, f32[2,112,640]{2,1,0:T(8,128)S(1)}, f32[16,640]{1,0:T(8,128)S(1)}, f32[4,640]{1,0:T(4,128)}, f32[4,640]{1,0:T(4,1...) custom-call(s32[2]{0:T(128)S(1)} %copy-done.7, ...), custom_call_target="tpu_custom_call" | custom-call | flops 1000000000 | bytes 1000000 | tf_op jit(solution)/shard_map/pallas_call | solution.py:1157
  325.1 3.1 all-to-all-done.16
  328.3 14.6 %all_to_all.95 = f32[16,4,8,128]{3,2,1,0:T(8,128)S(1)} all-to-all(f32[16,4,8,128]{3,2,1,0:T(8,128)S(1)} %broadcast_in_dim.14), channel_id=1, replica_groups=mesh['dp'=4,'z'=4,'core'=2] {'dp','z'}, dimensions={0} | all-to-all | bytes 524288 | tf_op jit(solution)/shard_map/all_to_all | solution.py:1140
  342.9 1.5 collective-permute-done.5.late_other_ref
  344.4 3.2 shard_map.327
  (72 shorter events, 9.8 us)
Async XLA Ops:
  0.7 1.1 copy-start
  1.7 0.7 copy-start.6
  2.4 1.2 copy-start.14
  3.6 10.8 %copy-start.19 = (f32[2,45,640]{2,0,1:T(2,128)S(1)}, f32[2,45,640]{2,0,1:T(2,128)}, u32[]{:S(2)}) copy-start(f32[2,45,640]{2,0,1:T(2,128)} %param.27) | copy-start | bytes 691204
  3.6 10.8 %copy-start.7 = (s32[2]{0:T(128)S(1)}, s32[2]{0:T(128)}, u32[]{:S(2)}) copy-start(s32[2]{0:T(128)} %counts_ref.25) | copy-start | bytes 28
  3.6 10.9 %copy-start.15 = (f32[112,2048]{1,0:T(8,128)S(1)}, f32[112,2048]{1,0:T(8,128)}, u32[]{:S(2)}) copy-start(f32[112,2048]{1,0:T(8,128)} %video_ref.3) | copy-start | bytes 2752516
  3.6 10.9 %copy-start.16 = (f32[112,512]{1,0:T(8,128)S(1)}, f32[112,512]{1,0:T(8,128)}, u32[]{:S(2)}) copy-start(f32[112,512]{1,0:T(8,128)} %cot_ref.1) | copy-start | bytes 688132
  7.1 16.1 %all-to-all-start = ((f32[32,2,768]{2,1,0:T(2,128)}), f32[32,2,768]{2,1,0:T(2,128)S(1)}, u32[]{:S(2)}, u32[]{:S(2)}) async-start(f32[32,2,768]{2,1,0:T(2,128)} %get-tuple-element.120), calls=%async_computation | async-start | bytes 393216 | tf_op jit(solution)/shard_map/all_to_all | solution.py:1113
  14.4 8.7 %copy-start.1 = (f32[2,640,112]{1,2,0:T(8,128)S(1)}, f32[2,640,112]{1,2,0:T(8,128)}, u32[]{:S(2)}) copy-start(f32[2,640,112]{1,2,0:T(8,128)} %param.22) | copy-start | bytes 1720324
  14.4 8.7 %copy-start.4 = (f32[4,640]{1,0:T(4,128)S(1)}, f32[4,640]{1,0:T(4,128)}, u32[]{:S(2)}) copy-start(f32[4,640]{1,0:T(4,128)} %gain_ref.19) | copy-start | bytes 30724
  14.5 8.7 %copy-start.5 = (f32[4,640]{1,0:T(4,128)S(1)}, f32[4,640]{1,0:T(4,128)}, u32[]{:S(2)}) copy-start(f32[4,640]{1,0:T(4,128)} %bias_ref.17) | copy-start | bytes 30724
  23.1 31.4 %copy-start.2 = (f32[2,160,640]{2,1,0:T(8,128)S(1)}, f32[2,160,640]{2,1,0:T(8,128)}, u32[]{:S(2)}) copy-start(f32[2,160,640]{2,1,0:T(8,128)} %down_ref.7) | copy-start | bytes 2457604
  23.1 31.4 %copy-start.3 = (f32[2,112,640]{2,1,0:T(8,128)S(1)}, f32[2,112,640]{2,1,0:T(8,128)}, u32[]{:S(2)}) copy-start(f32[2,112,640]{2,1,0:T(8,128)} %proj_ref.7) | copy-start | bytes 1720324
  23.1 31.4 %copy-start.8 = (f32[2,640]{1,0:T(2,128)S(1)}, f32[2,640]{1,0:T(2,128)}, u32[]{:S(2)}) copy-start(f32[2,640]{1,0:T(2,128)} %upb_ref.3) | copy-start | bytes 15364
  23.2 31.4 %copy-start.11 = (f32[2,160]{1,0:T(2,128)S(1)}, f32[2,160]{1,0:T(2,128)}, u32[]{:S(2)}) copy-start(f32[2,160]{1,0:T(2,128)} %downb_ref.3) | copy-start | bytes 3844
  54.5 15.1 %copy-start.20 = (f32[2,112]{1,0:T(2,128)S(1)}, f32[2,112]{1,0:T(2,128)}, u32[]{:S(2)}) copy-start(f32[2,112]{1,0:T(2,128)} %param.25) | copy-start | bytes 2692
  54.6 15.1 %copy-start.21 = (f32[2,112]{1,0:T(2,128)S(1)}, f32[2,112]{1,0:T(2,128)}, u32[]{:S(2)}) copy-start(f32[2,112]{1,0:T(2,128)} %param.26) | copy-start | bytes 2692
  67.1 9.8 %all-to-all-start.2 = ((f32[32,2,128]{2,1,0:T(2,128)}), f32[32,2,128]{2,1,0:T(2,128)S(1)}, u32[]{:S(2)}, u32[]{:S(2)}) async-start(f32[32,2,128]{2,1,0:T(2,128)} %get-tuple-element.126), calls=%async_computation.2 | async-start | bytes 65536 | tf_op jit(solution)/shard_map/all_to_all | solution.py:1113
  92.9 14.4 %all-to-all-start.4 = ((f32[32,2,8,128]{3,2,1,0:T(8,128)}), f32[32,2,8,128]{3,2,1,0:T(8,128)S(1)}, u32[]{:S(2)}, u32[]{:S(2)}) async-start(f32[32,2,8,128]{3,2,1,0:T(8,128)} %bitcast.2), calls=%async_computation.4 | async-start | bytes 524288 | tf_op jit(solution)/shard_map/all_to_all | solution.py:1135
  136.9 13.0 %all-to-all-start.7 = ((f32[32,2,8,128]{3,2,1,0:T(8,128)}), f32[32,2,8,128]{3,2,1,0:T(8,128)S(1)}, u32[]{:S(2)}, u32[]{:S(2)}) async-start(f32[32,2,8,128]{3,2,1,0:T(8,128)} %broadcast_in_dim.10), calls=%async_computation.7 | async-start | bytes 524288 | tf_op jit(solution)/shard_map/all_to_all | solution.py:1140
  147.3 7.3 %copy-start.17 = (f32[288,8,128]{2,1,0:T(8,128)S(1)}, f32[288,8,128]{2,1,0:T(8,128)}, u32[]{:S(2)}) copy-start(f32[288,8,128]{2,1,0:T(8,128)} %get-tuple-element.155) | copy-start | bytes 3538948
  151.0 3.6 %collective-permute-start = (f32[144,8,128]{2,1,0:T(8,128)S(1)}, f32[144,8,128]{2,1,0:T(8,128)}, u32[]{:S(2)}, u32[]{:S(2)}) collective-permute-start(f32[144,8,128]{2,1,0:T(8,128)S(1)} %dynamic-slice_bitcast_fusion.1), channel_id=1, source_target_pairs={{0,1},{1,0},{2,3},{3,2},{4,5},{5,4},{6,7},{7,6},{8,9},{9,8},{10,11... | collective-permute-start | bytes 1769480 | tf_op jit(solution)/shard_map/ppermute | solution.py:1121
  151.4 11.7 %all-to-all-start.8 = ((f32[32,2,640]{2,1,0:T(2,128)}), f32[32,2,640]{2,1,0:T(2,128)S(1)}, u32[]{:S(2)}, u32[]{:S(2)}) async-start(f32[32,2,640]{2,1,0:T(2,128)} %get-tuple-element.154), calls=%async_computation.8 | async-start | bytes 327680 | tf_op jit(solution)/shard_map/all_to_all | solution.py:1113
  163.1 22.3 %all-to-all-start.9 = ((f32[16,9,8,128]{3,2,1,0:T(8,128)}), f32[16,9,8,128]{3,2,1,0:T(8,128)S(1)}, u32[]{:S(2)}, u32[]{:S(2)}) async-start(f32[16,9,8,128]{3,2,1,0:T(8,128)} %bitcast.7), calls=%async_computation.9 | async-start | bytes 1179648 | tf_op jit(solution)/shard_map/all_to_all | solution.py:1135
  202.2 28.0 %all-to-all-start.11 = ((f32[16,9,8,128]{3,2,1,0:T(8,128)}), f32[16,9,8,128]{3,2,1,0:T(8,128)S(1)}, u32[]{:S(2)}, u32[]{:S(2)}) async-start(f32[16,9,8,128]{3,2,1,0:T(8,128)} %broadcast_in_dim.12), calls=%async_computation.11 | async-start | bytes 1179648 | tf_op jit(solution)/shard_map/all_to_all | solution.py:1140
  229.5 6.3 %collective-permute-start.1 = (f32[192,8,128]{2,1,0:T(8,128)}, f32[192,8,128]{2,1,0:T(8,128)S(1)}, u32[]{:S(2)}, u32[]{:S(2)}) collective-permute-start(f32[192,8,128]{2,1,0:T(8,128)} %dynamic-slice_bitcast_fusion), channel_id=1, source_target_pairs={{0,1},{1,0},{2,3},{3,2},{4,5},{5,4},{6,7},{7,6},{8,9},{9,8},{10,11... | collective-permute-start | bytes 2359304 | tf_op jit(solution)/shard_map/ppermute | solution.py:1121
  230.2 14.1 %collective-permute-start.2 = (f32[144,8,128]{2,1,0:T(8,128)S(1)}, f32[144,8,128]{2,1,0:T(8,128)}, u32[]{:S(2)}, u32[]{:S(2)}) collective-permute-start(f32[144,8,128]{2,1,0:T(8,128)S(1)} %bitcast.39), channel_id=1, source_target_pairs={{0,1},{1,0},{2,3},{3,2},{4,5},{5,4},{6,7},{7,6},{8,9},{9,8},{10,11... | collective-permute-start | bytes 1769480 | tf_op jit(solution)/shard_map/ppermute | solution.py:1121
  230.2 14.0 %all-to-all-start.12 = ((f32[32,2,640]{2,1,0:T(2,128)}), f32[32,2,640]{2,1,0:T(2,128)S(1)}, u32[]{:S(2)}, u32[]{:S(2)}) async-start(f32[32,2,640]{2,1,0:T(2,128)} %get-tuple-element.174), calls=%async_computation.12 | async-start | bytes 327680 | tf_op jit(solution)/shard_map/all_to_all | solution.py:1113
  244.3 27.2 %all-to-all-start.13 = ((f32[16,12,8,128]{3,2,1,0:T(8,128)}), f32[16,12,8,128]{3,2,1,0:T(8,128)}, u32[]{:S(2)}, u32[]{:S(2)}) async-start(f32[16,12,8,128]{3,2,1,0:T(8,128)} %bitcast.12), calls=%async_computation.13 | async-start | bytes 1572864 | tf_op jit(solution)/shard_map/all_to_all | solution.py:1135
  273.6 26.4 %all-to-all-start.14 = ((f32[16,12,8,128]{3,2,1,0:T(8,128)}), f32[16,12,8,128]{3,2,1,0:T(8,128)}, u32[]{:S(2)}, u32[]{:S(2)}) async-start(f32[16,12,8,128]{3,2,1,0:T(8,128)} %broadcast_in_dim.13), calls=%async_computation.14 | async-start | bytes 1572864 | tf_op jit(solution)/shard_map/all_to_all | solution.py:1140
  291.3 26.0 %copy-start.9 = (f32[4,640]{1,0:T(4,128)S(1)}, f32[4,640]{1,0:T(4,128)}, u32[]{:S(2)}) copy-start(f32[4,640]{1,0:T(4,128)} %means_ref.1) | copy-start | bytes 30724
  291.3 26.1 %copy-start.10 = (f32[4,640]{1,0:T(4,128)S(1)}, f32[4,640]{1,0:T(4,128)}, u32[]{:S(2)}) copy-start(f32[4,640]{1,0:T(4,128)} %vars_ref.1) | copy-start | bytes 30724
  291.3 26.1 %copy-start.12 = (f32[2,112]{1,0:T(2,128)S(1)}, f32[2,112]{1,0:T(2,128)}, u32[]{:S(2)}) copy-start(f32[2,112]{1,0:T(2,128)} %nmeans_ref.1) | copy-start | bytes 2692
  291.3 26.1 %copy-start.13 = (f32[2,112]{1,0:T(2,128)S(1)}, f32[2,112]{1,0:T(2,128)}, u32[]{:S(2)}) copy-start(f32[2,112]{1,0:T(2,128)} %nvars_ref.1) | copy-start | bytes 2692
  300.0 12.3 %collective-permute-start.4 = (f32[192,8,128]{2,1,0:T(8,128)}, f32[192,8,128]{2,1,0:T(8,128)S(1)}, u32[]{:S(2)}, u32[]{:S(2)}) collective-permute-start(f32[192,8,128]{2,1,0:T(8,128)} %bitcast.13.pack0_ref), channel_id=1, source_target_pairs={{0,1},{1,0},{2,3},{3,2},{4,5},{5,4},{6,7},{7,6},{8,9},{9,8},{10,11... | collective-permute-start | bytes 2359304 | tf_op jit(solution)/shard_map/ppermute | solution.py:1121
  300.7 3.1 collective-permute-start.3
  301.2 11.1 %all-to-all-start.15 = ((f32[32,2,640]{2,1,0:T(2,128)}), f32[32,2,640]{2,1,0:T(2,128)S(1)}, u32[]{:S(2)}, u32[]{:S(2)}) async-start(f32[32,2,640]{2,1,0:T(2,128)} %get-tuple-element.192), calls=%async_computation.15 | async-start | bytes 327680 | tf_op jit(solution)/shard_map/all_to_all | solution.py:1113
  312.2 0.9 copy-start.18
  313.1 15.1 %all-to-all-start.16 = ((f32[16,4,8,128]{3,2,1,0:T(8,128)}), f32[16,4,8,128]{3,2,1,0:T(8,128)S(1)}, u32[]{:S(2)}, u32[]{:S(2)}) async-start(f32[16,4,8,128]{3,2,1,0:T(8,128)} %bitcast.18), calls=%async_computation.16 | async-start | bytes 524288 | tf_op jit(solution)/shard_map/all_to_all | solution.py:1135
  342.9 1.5 collective-permute-start.5

commit v4 on v3

--- a/solution.py
+++ b/solution.py
@@ -447,8 +447,8 @@
     return jnp.where(t < total, 1.0, 0.0).astype(F32)
 
 
-def each_frame(count, body, init, unroll=2):
-    return lax.fori_loop(0, count, body, init, unroll=unroll)
+def each_frame(count, body, init):
+    return lax.fori_loop(0, count, body, init, unroll=min(4, count))
 
 
 def lanes_of(ref, tile):
@@ -552,7 +552,7 @@
 
 def squeeze_backward_body(
     block, counts_ref, stat_ref, d_ref, gain_ref, bias_ref, down_ref, up_ref, proj_ref, gates_ref, running_ref,
-    pre_ref, dy2_ref, send_ref, pack_ref, dz3_ref, dz3t_ref, excited_ref, dexc_ref, dgate_ref, head,
+    pre_ref, dy2_ref, send_ref, pack_ref, dz3_ref, dz3t_ref, total_ref, dexc_ref, dgate_ref, head,
 ):
     total = live_frames(counts_ref)
     per_frame = HALF_ROWS if block else FULL_ROWS
@@ -593,11 +593,12 @@
                 dgate_ref[tile, pl.ds(t, 1), :] = tile_sum(own * second)
                 parts.append(second.reshape(pixels, LANES) * pick_row(gates, t))
             excited = parts[0] if group == 1 else jnp.concatenate(parts, axis=0)
-            excited_ref[flat, :] = side_by_side(excited)
+            total_ref[...] = total_ref[...] + plain_dot(dz3t_ref[:, flat], side_by_side(excited))
             return inside
 
+        total_ref[...] = jnp.zeros_like(total_ref)
         each_frame(chunks, chunk, 0)
-        dproj = fold_square(plain_dot(dz3t_ref[...], excited_ref[...]))
+        dproj = fold_square(total_ref[...])
         pack_ref[pl.ds(tile * per_tile, narrow // 8)] = dproj[0:narrow].reshape(narrow // 8, 8, LANES)
         return carry
 
@@ -681,7 +682,7 @@
 def squeeze_one_backward_kernel(
     counts_ref, third_ref, z_ref, cot_ref, ngain_ref, nbias_ref, stat_ref, d_ref, gain_ref, bias_ref, down_ref,
     up_ref, proj_ref, gates_ref, running_ref, pre_ref, act_ref, nsum_ref, dy2_ref, send_ref, pack_ref,
-    dz3_ref, dz3t_ref, excited_ref, dexc_ref, dgate_ref,
+    dz3_ref, dz3t_ref, total_ref, dexc_ref, dgate_ref,
 ):
     total = live_frames(counts_ref)
     pixels = HALF_ROWS * 8
@@ -707,7 +708,7 @@
 
     squeeze_backward_body(
         1, counts_ref, stat_ref, d_ref, gain_ref, bias_ref, down_ref, up_ref, proj_ref, gates_ref, running_ref,
-        pre_ref, dy2_ref, send_ref, pack_ref, dz3_ref, dz3t_ref, excited_ref, dexc_ref, dgate_ref, head,
+        pre_ref, dy2_ref, send_ref, pack_ref, dz3_ref, dz3t_ref, total_ref, dexc_ref, dgate_ref, head,
     )
 
 
@@ -726,7 +727,7 @@
 def squeeze_zero_backward_kernel(
     counts_ref, top_ref, stat1_ref, gram_ref, nstat_ref, dxpre_ref, x1_ref, z_ref, ngain_ref, w_ref, gains_ref, q_one_ref,
     stat_ref, d_ref, gain_ref, bias_ref, down_ref, up_ref, proj_ref, gates_ref, running_ref, pre_ref,
-    dx1_ref, nsum_ref, dy2_ref, send_ref, pack_ref, dz3_ref, dz3t_ref, excited_ref, dexc_ref, dgate_ref,
+    dx1_ref, nsum_ref, dy2_ref, send_ref, pack_ref, dz3_ref, dz3t_ref, total_ref, dexc_ref, dgate_ref,
 ):
     total = live_frames(counts_ref)
     width = gains_ref.shape[1]
@@ -767,7 +768,7 @@
 
     squeeze_backward_body(
         0, counts_ref, stat_ref, d_ref, gain_ref, bias_ref, down_ref, up_ref, proj_ref, gates_ref, running_ref,
-        pre_ref, dy2_ref, send_ref, pack_ref, dz3_ref, dz3t_ref, excited_ref, dexc_ref, dgate_ref, head,
+        pre_ref, dy2_ref, send_ref, pack_ref, dz3_ref, dz3t_ref, total_ref, dexc_ref, dgate_ref, head,
     )
 
 def back_full(t, k, a_ref, w_ref, z_ref, raw_ref, f_ref, dw_ref, fresh):
@@ -852,7 +853,7 @@
 def depth_backward_kernel(
     block, before, final, counts_ref, grads_ref, stat2_ref, stat_ref, nstat_ref, dy2_ref, d_ref, e_ref, a_ref, columns_ref, w_ref,
     gain_ref, bias_ref, taps_ref, z3_ref, dx_in_ref, sums_in_ref, list_in_ref, dxpre_ref, send_ref, q_ref, grad_rows_ref,
-    z_ref, f_ref, taps8_ref, dw_ref, pair_ref, *raw_refs,
+    z_ref, f_ref, taps8_ref, dw_ref, total_ref, *raw_refs,
 ):
     tile = pl.program_id(0)
     tiles = pl.num_programs(0)
@@ -936,7 +937,8 @@
         return lax.fori_loop(1, last + 1, lag, carry)
 
     lax.fori_loop(0, total, frame, 0)
-    square = right_square_t(pad_rows(w_ref[0]))
+    square = right_square_t(pad_rows(w_ref[0]) * scale_one)
+    total_ref[...] = jnp.zeros_like(total_ref)
 
     def finish(t, carry):
         rows = pl.ds(pl.multiple_of(t * FULL_ROWS, FULL_ROWS), FULL_ROWS)
@@ -948,9 +950,9 @@
         summed = carry[0] + jnp.sum(dy, axis=0)
         cross = carry[1] + jnp.sum(dy * (values - average_one), axis=0)
         dy = dy.reshape(256, LANES)
-        pair_ref[flat, :] = side_by_side(dy)
-        scaled = side_by_side(dy * scale_one)
-        dxpre_ref[flat, :] = dxpre_ref[flat, :] + fold_right(plain_dot(scaled, square, NT))
+        both = side_by_side(dy)
+        total_ref[...] = total_ref[...] + plain_dot(columns_ref[:, flat], both)
+        dxpre_ref[flat, :] = dxpre_ref[flat, :] + fold_right(plain_dot(both, square, NT))
         return (summed, cross)
 
     zero = jnp.zeros((8, LANES), F32)
@@ -960,7 +962,7 @@
         send_all(send_ref, rows, pl.ds(pl.multiple_of((tile + before) * LANES, LANES), LANES))
     else:
         send_ref[...] = rows8(rows[0:1], rows[1:2])
-    gathered = fold_square(plain_dot(columns_ref[...], pair_ref[...]))
+    gathered = fold_square(total_ref[...])
     narrow = w_ref.shape[1]
     dtaps = jnp.sum(dw_ref[...], axis=1)
     parts = (dtaps,) if half else pair_taps(dtaps)
@@ -1049,8 +1051,26 @@
     newnv_ref[...] = (1.0 - momentum) * nvars_ref[...] + momentum * variances
 
 
-def gradient_kernel(
-    core_ref, pack0_ref, pack0_other_ref, pack1_ref, pack1_other_ref, late_ref, late_other_ref, less_ref, factor_ref,
+def list_rows(core_ref, pair, at, count):
+    first_core = core_ref[0] == 0
+    mine, other = pair
+    half = mine.shape[0]
+    pieces = []
+    if at < half:
+        size = min(count, half - at)
+        here = slice(at, at + size)
+        pieces.append(jnp.where(first_core, mine[here], other[here]))
+        count = count - size
+        at = at + size
+    if count:
+        here = slice(at - half, at - half + count)
+        pieces.append(jnp.where(first_core, other[here], mine[here]))
+    values = pieces[0] if len(pieces) == 1 else jnp.concatenate(pieces, axis=0)
+    return values.reshape(-1, LANES)
+
+
+def lists_kernel(
+    core_ref, pack0_ref, pack0_other_ref, pack1_ref, pack1_other_ref, less_ref, factor_ref,
     dw_ref, dtaps_ref, ddown_ref, dup_ref, dproj_ref, dupb_ref, ddownb_ref,
 ):
     narrow = dw_ref.shape[1]
@@ -1059,50 +1079,40 @@
     tiles = dw_ref.shape[2] // LANES
     per_pack = pack_tiles(narrow, squeeze)
     per_tile = narrow // 8 + -(-taps // 8)
-    first_core = core_ref[0] == 0
-
-    def rows_of(pair, at, count):
-        mine, other = pair
-        half = mine.shape[0]
-        pieces = []
-        if at < half:
-            size = min(count, half - at)
-            here = slice(at, at + size)
-            pieces.append(jnp.where(first_core, mine[here], other[here]))
-            count = count - size
-            at = at + size
-        if count:
-            here = slice(at - half, at - half + count)
-            pieces.append(jnp.where(first_core, other[here], mine[here]))
-        values = pieces[0] if len(pieces) == 1 else jnp.concatenate(pieces, axis=0)
-        return values.reshape(-1, LANES)
-
     packs = ((pack0_ref, pack0_other_ref), (pack1_ref, pack1_other_ref))
-    lists = ((late_ref, late_other_ref), packs[0])
     for block in range(2):
         down_rows = []
         for tile in range(tiles):
             lanes = slice(tile * LANES, (tile + 1) * LANES)
             at = tile * per_pack
-            dproj_ref[block, :, lanes] = rows_of(packs[block], at, narrow // 8)
+            dproj_ref[block, :, lanes] = list_rows(core_ref, packs[block], at, narrow // 8)
             at = at + narrow // 8
-            ddown_ref[block, :, lanes] = rows_of(packs[block], at, squeeze // 8)
+            ddown_ref[block, :, lanes] = list_rows(core_ref, packs[block], at, squeeze // 8)
             at = at + squeeze // 8
-            dup_ref[block, :, lanes] = rows_of(packs[block], at, squeeze // 8)
-            biases = rows_of(packs[block], at + squeeze // 8, 1)
+            dup_ref[block, :, lanes] = list_rows(core_ref, packs[block], at, squeeze // 8)
+            biases = list_rows(core_ref, packs[block], at + squeeze // 8, 1)
             dupb_ref[block : block + 1, lanes] = biases[0:1]
             down_rows.append(biases[1:2])
-            values = rows_of(lists[block], (per_pack * tiles if block else 0) + tile * per_tile, per_tile)
-            dw = values[0:narrow] * factor_ref[8 * block : 8 * block + 1, lanes] - less_ref[block, :, lanes]
-            dw_ref[block, :, lanes] = dw
-            if block:
-                dtaps_ref[block, :, lanes] = values[narrow : narrow + taps]
-                continue
-            for r in range(3):
-                for k in range(LAGS):
-                    source = narrow + r * 3 * LAGS + 3 * k
-                    dtaps_ref[block, k * 9 + 3 * r : k * 9 + 3 * r + 3, lanes] = values[source : source + 3]
         ddownb_ref[block : block + 1, :] = jnp.concatenate(down_rows, axis=1)[:, 0:squeeze]
+    for tile in range(tiles):
+        lanes = slice(tile * LANES, (tile + 1) * LANES)
+        values = list_rows(core_ref, packs[0], per_pack * tiles + tile * per_tile, per_tile)
+        dw_ref[0, :, lanes] = values[0:narrow] * factor_ref[8:9, lanes] - less_ref[0, :, lanes]
+        dtaps_ref[0, :, lanes] = values[narrow : narrow + taps]
+
+
+def last_kernel(core_ref, late_ref, late_other_ref, less_ref, factor_ref, _, __, dw_ref, dtaps_ref):
+    narrow = dw_ref.shape[1]
+    taps = dtaps_ref.shape[1]
+    per_tile = narrow // 8 + -(-taps // 8)
+    for tile in range(dw_ref.shape[2] // LANES):
+        lanes = slice(tile * LANES, (tile + 1) * LANES)
+        values = list_rows(core_ref, (late_ref, late_other_ref), tile * per_tile, per_tile)
+        dw_ref[0, :, lanes] = values[0:narrow] * factor_ref[0:1, lanes] - less_ref[0, :, lanes]
+        for r in range(3):
+            for k in range(LAGS):
+                source = narrow + r * 3 * LAGS + 3 * k
+                dtaps_ref[0, k * 9 + 3 * r : k * 9 + 3 * r + 3, lanes] = values[source : source + 3]
 
 
 AXES = ("dp", "z", "core")
@@ -1153,7 +1163,7 @@
 SCALARS = pl.BlockSpec(memory_space=pltpu.SMEM)
 
 
-def call(kernel, grid, in_specs, out_specs, out_shape, scratch, args):
+def call(kernel, grid, in_specs, out_specs, out_shape, scratch, args, vmem=VMEM_BYTES, aliases=None):
     return pl.pallas_call(
         kernel,
         grid=grid,
@@ -1161,7 +1171,8 @@
         out_specs=out_specs,
         out_shape=out_shape,
         scratch_shapes=scratch,
-        compiler_params=pltpu.CompilerParams(vmem_limit_bytes=VMEM_BYTES),
+        compiler_params=pltpu.CompilerParams(vmem_limit_bytes=vmem),
+        input_output_aliases=aliases or {},
         cost_estimate=pl.CostEstimate(
             flops=1_000_000_000, bytes_accessed=1_000_000, transcendentals=0
         ),
@@ -1243,7 +1254,7 @@
         gram_kernel, (1,), [SCALARS, whole(video), of_block(0, cin, width)],
         [fixed(LANES + 8, LANES), fixed(devices, 2, width + LANES)],
         [shape(LANES + 8, LANES), shape(devices, 2, width + LANES)],
-        [], (frame_counts, video, w_t),
+        [], (frame_counts, video, w_t), vmem=60 * 1024 * 1024,
     )
     x, x_rows, x_columns, cot = simple_call(
         prepare_kernel, 1, (frame_counts, video, cotangent),
@@ -1337,7 +1348,7 @@
         outs = [fixed(8, LANES)] + wide_outs + [fixed(packed, 8, LANES)]
         shapes = [shape(8, LANES), shape(rows, 8, width), shape(devices, 2, width), shape(packed, 8, LANES)]
         scratch = [pltpu.VMEM((rows * 8, 2 * LANES), low), pltpu.VMEM((2 * LANES, rows * 8), low),
-                   pltpu.VMEM((rows * 8, 2 * LANES), low), pltpu.VMEM((tiles, rows, 8, LANES), F32),
+                   pltpu.VMEM((2 * LANES, 2 * LANES), F32), pltpu.VMEM((tiles, rows, 8, LANES), F32),
                    pltpu.VMEM((tiles, frames, LANES), F32)]
         return (ins, outs, shapes, scratch)
 
@@ -1391,7 +1402,7 @@
             [fixed(pixels, LANES), send_spec, fixed(listed, 8, LANES), tile_rows(8)],
             [shape(pixels, LANES), shape(*send), shape(listed, 8, LANES), shape(8, count * LANES)],
             [pltpu.VMEM(z_shape, F32), pltpu.VMEM(f_shape, F32), pltpu.VMEM(taps_shape, F32), pltpu.VMEM(taps_shape, F32),
-             pltpu.VMEM((pixels, 2 * LANES), low)]
+             pltpu.VMEM((2 * LANES, 2 * LANES), F32)]
             + ([] if block else [pltpu.VMEM((frames, 4, 2, PAIRS, 8, LANES), F32)]),
             (frame_counts, sums, stat2, stat, nstat, dy2, depth, expanded, planes, columns, w_t, wide_gains, wide_biases,
              depth_weight, z_zero, dx_in, sums_in, list_in),
@@ -1445,12 +1456,24 @@
     )
     less, late = together(less, late)
     late = share_back(late)
+    list_shapes = [
+        shape(2, cin, width), shape(2, taps, width), shape(2, squeeze, width), shape(2, squeeze, width),
+        shape(2, cin, width), shape(2, width), shape(2, squeeze),
+    ]
+    list_args = (core, pack_zero, pack_zero_other, pack_one, pack_one_other, less, factor)
+    dw_t, dtaps, ddown, dup, dproj, dupb, ddownb = call(
+        lists_kernel, (1,), [SCALARS] + [whole(array) for array in list_args[1:5]] + [of_block(1, cin, width), whole(factor)],
+        [of_block(1, cin, width), of_block(1, taps, width)] + [whole(item) for item in list_shapes[2:]], list_shapes, [],
+        list_args,
+    )
+    dw_t, late = together(dw_t, late)
     late_other = swap_cores(late)
-    dw_t, dtaps, ddown, dup, dproj, dupb, ddownb = simple_call(
-        gradient_kernel, 1,
-        (core, pack_zero, pack_zero_other, pack_one, pack_one_other, late, late_other, less, factor),
-        [shape(2, cin, width), shape(2, taps, width), shape(2, squeeze, width), shape(2, squeeze, width),
-         shape(2, cin, width), shape(2, width), shape(2, squeeze)],
+    stay = pl.BlockSpec(memory_space=pl.ANY)
+    dw_t, dtaps = call(
+        last_kernel, (1,),
+        [SCALARS, whole(late), whole(late_other), of_block(0, cin, width), whole(factor), stay, stay],
+        [of_block(0, cin, width), of_block(0, taps, width)], list_shapes[0:2], [],
+        (core, late, late_other, less, factor, dw_t, dtaps), aliases={5: 0, 6: 1},
     )
     return (
         activations, video_grad, jnp.swapaxes(dw_t, 1, 2), wgain, wbias, ngain, nbias, dtaps, ddown, ddownb,

time: 350 us -> 333 us (0.951)
  blocking collectives: 78.8 us -> 60.3 us
  waiting for transfers between devices: 53.8 us -> 67.4 us
  Pallas kernels: 148 us -> 137 us
  local copies, waits for them, and re-layouts: 11.2 us -> 7.39 us
  starting transfers between devices: 47.6 us -> 51.2 us
    all_to_all x1 -> x0, blocking collectives: 14.6 us -> none  [share_back(): lax.all_to_all(jnp.broadcast_to(own[None], pieces.shape), names, 0, 0, ti...]
    pallas_call x14 -> x15, Pallas kernels: 148 us -> 137 us  [call(): pl.pallas_call(kernel, grid=grid, in_specs=in_specs, out_specs=out_specs,...]
    all_to_all x3 -> x4, waiting for transfers between devices: 11.2 us -> 19.6 us  [share_back(): lax.all_to_all(jnp.broadcast_to(own[None], pieces.shape), names, 0, 0, ti...]
    all_to_all x4, waiting for transfers between devices: 9.1 us -> 13.3 us  [share_out(): lax.all_to_all(tiles.reshape(count, -1, *tiles.shape[1:]), names, 0, 0, t...]
    all_to_all x5, blocking collectives: 64.1 us -> 60.3 us  [exchange(): return lax.all_to_all(send, AXES, 0, 0, tiled=True)]
    unnamed x46 -> x40, local copies, waits for them, and re-layouts: 4.7 us -> 0.93 us
    all_to_all x3 -> x4, starting transfers between devices: 10.7 us -> 14.2 us  [share_back(): lax.all_to_all(jnp.broadcast_to(own[None], pieces.shape), names, 0, 0, ti...]
  transfers between devices with their start and end apart: 18 -> 19, of which waited for: 10 -> 12; matrix products, arithmetic and copies ran while one was open for 2% -> 2% of each run, Pallas kernels for 29% -> 29%
where the time goes in v4:
time: 333 us; the launch traced here: 331 us
  Pallas kernels  137 us (41%)
  waiting for transfers between devices  67.4 us (20%)
  blocking collectives  60.3 us (18%)
  starting transfers between devices  51.2 us (15%)
  local copies, waits for them, and re-layouts  7.39 us (2%)
  other arithmetic  6.13 us (2%)
    pallas_call x15, Pallas kernels, call(): pl.pallas_call(kernel, grid=grid, in_specs=in_specs, out_specs=out_specs,...  137 us
    all_to_all x5, blocking collectives, exchange(): return lax.all_to_all(send, AXES, 0, 0, tiled=True)  60.3 us
    all_to_all x5, waiting for transfers between devices, exchange(): return lax.all_to_all(send, AXES, 0, 0, tiled=True)  33 us
    all_to_all x5, starting transfers between devices, exchange(): return lax.all_to_all(send, AXES, 0, 0, tiled=True)  21.2 us
    all_to_all x4, waiting for transfers between devices, share_back(): lax.all_to_all(jnp.broadcast_to(own[None], pieces.shape), names, 0, 0, ti...  19.6 us
    all_to_all x4, starting transfers between devices, share_back(): lax.all_to_all(jnp.broadcast_to(own[None], pieces.shape), names, 0, 0, ti...  14.2 us
    all_to_all x4, starting transfers between devices, share_out(): lax.all_to_all(tiles.reshape(count, -1, *tiles.shape[1:]), names, 0, 0, t...  14 us
    all_to_all x4, waiting for transfers between devices, share_out(): lax.all_to_all(tiles.reshape(count, -1, *tiles.shape[1:]), names, 0, 0, t...  13.3 us
  transfers between devices with their start and end apart: 19, of which 12 were waited for; matrix products, arithmetic and copies ran while one was open for 2% of the time, Pallas kernels for 29%

profile of v4, /device:TPU:0, one launch (start us, length us, event | category | flops | bytes accessed | tf_op | source)
XLA Modules:
  0.0 331.1 jit_solution(17466634595806304734)
XLA Ops:
  0.7 3.9 %shard_map.314 = (f32[136,128]{1,0:T(8,128)}, f32[32,2,768]{2,1,0:T(2,128)}) custom-call(s32[2]{0:T(128)} %counts_ref.25, f32[112,2048]{1,0:T(8,128)} %video_ref.3, f32[2,112,640]{2,1,0:T(8,128)} %bitcast.28), custom_call_target="tpu_custom_call" | custom-call | flops 1000000000 | bytes 1000000 | tf_op jit(solution)/shard_map/pallas_call | solution.py:1167
  4.6 7.3 %all-to-all-start = ((f32[32,2,768]{2,1,0:T(2,128)}), f32[32,2,768]{2,1,0:T(2,128)S(1)}, u32[]{:S(2)}, u32[]{:S(2)}) async-start(f32[32,2,768]{2,1,0:T(2,128)} %get-tuple-element.124), calls=%async_computation | async-start | bytes 393216 | tf_op jit(solution)/shard_map/all_to_all | solution.py:1123
  12.0 3.4 %shard_map.315 = (f32[2048,128]{1,0:T(8,128)}, bf16[2048,256]{1,0:T(8,128)(2,1)}, bf16[256,2048]{1,0:T(8,128)(2,1)}, f32[512,128]{1,0:T(8,128)S(1)}) custom-call(s32[2]{0:T(128)S(1)} %copy-done.5, f32[112,2048]{1,0:T(8,128)S(1)} %copy-done.12, f32[112,512]{1,0:T(8,128)S(1)} %copy-done.13), custom_call_target="tpu_custom_call" | custom-call | flops 1000000000 | bytes 1000000 | tf_op jit(solution)/shard_map/pallas_call | solution.py:1167
  15.4 5.3 %all-to-all-done.sums_ref.count_ref = f32[32,2,768]{2,1,0:T(2,128)S(1)} async-done(((f32[32,2,768]{2,1,0:T(2,128)}), f32[32,2,768]{2,1,0:T(2,128)S(1)}, u32[]{:S(2)}, u32[]{:S(2)}) %all-to-all-start) | async-done | bytes 196640 | tf_op jit(solution)/shard_map/all_to_all | solution.py:1123
  20.7 16.7 %shard_map.316 = (f32[256,8,640]{2,1,0:T(8,128)}, f32[256,8,640]{2,1,0:T(8,128)}, f32[8,640]{1,0:T(8,128)S(1)}, f32[32,2,640]{2,1,0:T(2,128)S(1)}, f32[8,2,4,8,8,640]{5,4,3,2,1,0:T(8,128)}) custom-call(s32[2]{0:T(128)S(1)} %copy-done.5, f32[32,2,768]{2,1,0:T(2,128)S(1)} %all-to-all-done.sums_ref.count_ref, ...), custom_call_target="tpu_custom_call" | custom-call | flops 1000000000 | bytes 1000000 | tf_op jit(solution)/shard_map/pallas_call | solution.py:1167
  37.4 13.5 %all_to_all.90.sums_ref = f32[32,2,640]{2,1,0:T(2,128)S(1)} all-to-all(f32[32,2,640]{2,1,0:T(2,128)S(1)} %get-tuple-element.126), channel_id=1, replica_groups=mesh['dp'=4,'z'=4,'core'=2] {'dp','z','core'}, dimensions={0} | all-to-all | bytes 327680 | tf_op jit(solution)/shard_map/all_to_all | solution.py:1123
  51.0 10.5 %shard_map.317 = (f32[2048,128]{1,0:T(8,128)}, f32[8,640]{1,0:T(8,128)S(1)}, f32[8,640]{1,0:T(8,128)S(1)}, f32[8,160]{1,0:T(8,128)S(1)}, f32[8,640]{1,0:T(8,128)S(1)}, /*index=5*/f32[32,2,128]{2,1,0:T(2,128)}) custom-call(s32[2]{0:T(128)S(1)} %copy-done.5, f32[32,2,640]{2,1,0:T(2,128)S(1)} %all_to_all.90.sums_ref, ...), custom_call_target="tpu_custom_call" | custom-call | flops 1000000000 | bytes 1000000 | tf_op jit(solution)/shard_map/pallas_call | solution.py:1167
  61.4 2.6 all-to-all-start.2
  64.1 7.2 %all-to-all-done.2.sums_ref = f32[32,2,128]{2,1,0:T(2,128)S(1)} async-done(((f32[32,2,128]{2,1,0:T(2,128)}), f32[32,2,128]{2,1,0:T(2,128)S(1)}, u32[]{:S(2)}, u32[]{:S(2)}) %all-to-all-start.2) | async-done | bytes 32800 | tf_op jit(solution)/shard_map/all_to_all | solution.py:1123
  71.3 5.3 %shard_map.318 = (f32[2048,128]{1,0:T(8,128)}, bf16[2048,256]{1,0:T(8,128)(2,1)}, bf16[256,2048]{1,0:T(8,128)(2,1)}, f32[64,8,128]{2,1,0:T(8,128)}, f32[8,128]{1,0:T(8,128)S(1)}, /*index=5*/f32[32,2,640]{2,1,0:T(2,128)S(1)}) custom-call(s32[2]{0:T(128)S(1)} %copy-done.5, f32[32,2,128]{2,1,0:T(2,128)S(1)} %all-to-all-done.2.sums_ref, ...), custom_call_target="tpu_custom_call" | custom-call | flops 1000000000 | bytes 1000000 | tf_op jit(solution)/shard_map/pallas_call | solution.py:1167
  76.5 10.2 %all_to_all.91.sums_ref = f32[32,2,640]{2,1,0:T(2,128)S(1)} all-to-all(f32[32,2,640]{2,1,0:T(2,128)S(1)} %get-tuple-element.134), channel_id=1, replica_groups=mesh['dp'=4,'z'=4,'core'=2] {'dp','z','core'}, dimensions={0} | all-to-all | bytes 327680 | tf_op jit(solution)/shard_map/all_to_all | solution.py:1123
  86.7 2.6 all-to-all-start.4
  89.3 10.5 %shard_map.319 = (f32[256,8,640]{2,1,0:T(8,128)}, f32[64,8,640]{2,1,0:T(8,128)}, f32[8,640]{1,0:T(8,128)S(1)}, f32[32,2,640]{2,1,0:T(2,128)S(1)}, f32[8,3,18,8,640]{4,3,2,1,0:T(8,128)}) custom-call(s32[2]{0:T(128)S(1)} %copy-done.5, f32[32,2,640]{2,1,0:T(2,128)S(1)} %all_to_all.91.sums_ref, f32[8,128]{1,0:T(8,128)S(1)} %get-tuple-element.137.count_ref.nstat_ref, ...), custom_call_target="tpu_custom_call" | custom-call | flops 1000000000 | bytes 1000000 | tf_op jit(solution)/shard_map/pallas_call | solution.py:1167
  99.8 14.3 %all_to_all.92.sums_ref = f32[32,2,640]{2,1,0:T(2,128)S(1)} all-to-all(f32[32,2,640]{2,1,0:T(2,128)S(1)} %get-tuple-element.141), channel_id=1, replica_groups=mesh['dp'=4,'z'=4,'core'=2] {'dp','z','core'}, dimensions={0} | all-to-all | bytes 327680 | tf_op jit(solution)/shard_map/all_to_all | solution.py:1123
  114.1 4.5 %shard_map.320 = (f32[512,128]{1,0:T(8,128)S(1)}, f32[8,640]{1,0:T(8,128)S(1)}, f32[8,640]{1,0:T(8,128)S(1)}, f32[8,160]{1,0:T(8,128)S(1)}, f32[8,640]{1,0:T(8,128)S(1)}, /*index=5*/f32[32,4,128]{2,1,0:T(4,128)S(1)}) custom-call(s32[2]{0:T(128)S(1)} %copy-done.5, f32[32,2,640]{2,1,0:T(2,128)S(1)} %all_to_all.92.sums_ref, ...), custom_call_target="tpu_custom_call" | custom-call | flops 1000000000 | bytes 1000000 | tf_op jit(solution)/shard_map/pallas_call | solution.py:1167
  118.6 9.5 %all_to_all.93.third_ref = f32[32,4,128]{2,1,0:T(4,128)S(1)} all-to-all(f32[32,4,128]{2,1,0:T(4,128)S(1)} %get-tuple-element.144), channel_id=1, replica_groups=mesh['dp'=4,'z'=4,'core'=2] {'dp','z','core'}, dimensions={0} | all-to-all | bytes 131072 | tf_op jit(solution)/shard_map/all_to_all | solution.py:1123
  128.9 2.6 all-to-all-start.7
  131.5 7.9 %shard_map.321 = (f32[112,512]{1,0:T(8,128)}, f32[8,128]{1,0:T(8,128)S(1)}, f32[64,8,640]{2,1,0:T(8,128)}, f32[32,2,640]{2,1,0:T(2,128)}, f32[288,8,128]{2,1,0:T(8,128)}) custom-call(s32[2]{0:T(128)S(1)} %copy-done.5, f32[32,4,128]{2,1,0:T(4,128)S(1)} %all_to_all.93.third_ref, f32[512,128]{1,0:T(8,128)S(1)} %get-tuple-element.147.z_ref, ...), custom_call_target="tpu_custom_call" | custom-call | flops 1000000000 | bytes 1000000 | tf_op jit(solution)/shard_map/pallas_call | solution.py:1167
  139.3 2.5 all-to-all-done.7
  143.4 3.2 all-to-all-start.8
  146.6 1.9 bitcast_add_fusion.1
  148.6 6.5 %all-to-all-done.8.grads_ref = f32[32,2,640]{2,1,0:T(2,128)S(1)} async-done(((f32[32,2,640]{2,1,0:T(2,128)}), f32[32,2,640]{2,1,0:T(2,128)S(1)}, u32[]{:S(2)}, u32[]{:S(2)}) %all-to-all-start.8) | async-done | bytes 163872 | tf_op jit(solution)/shard_map/all_to_all | solution.py:1123
  155.1 3.6 %all-to-all-start.9 = ((f32[16,9,8,128]{3,2,1,0:T(8,128)}), f32[16,9,8,128]{3,2,1,0:T(8,128)S(1)}, u32[]{:S(2)}, u32[]{:S(2)}) async-start(f32[16,9,8,128]{3,2,1,0:T(8,128)} %bitcast.7), calls=%async_computation.9 | async-start | bytes 1179648 | tf_op jit(solution)/shard_map/all_to_all | solution.py:1145
  158.7 15.8 %shard_map.322 = (f32[2048,128]{1,0:T(8,128)}, f32[32,2,768]{2,1,0:T(2,128)S(1)}, f32[100,8,128]{2,1,0:T(8,128)S(1)}, f32[8,640]{1,0:T(8,128)S(1)}) custom-call(s32[2]{0:T(128)S(1)} %copy-done.5, f32[32,2,640]{2,1,0:T(2,128)S(1)} %all-to-all-done.8.grads_ref, f32[8,640]{1,0:T(8,128)S(1)} %get-tuple-element.148.stat_ref.stat2_ref.stat12_ref, ...), custom_call_target="tpu_custom_call" | custom-call | flops 1000000000 | bytes 1000000 | tf_op jit(solution)/shard_map/pallas_call | solution.py:1167
  174.5 2.7 all-to-all-done.9
  177.2 12.8 %all_to_all.94.top_ref.one_ref = f32[32,2,768]{2,1,0:T(2,128)S(1)} all-to-all(f32[32,2,768]{2,1,0:T(2,128)S(1)} %get-tuple-element.167), channel_id=1, replica_groups=mesh['dp'=4,'z'=4,'core'=2] {'dp','z','core'}, dimensions={0} | all-to-all | bytes 393216 | tf_op jit(solution)/shard_map/all_to_all | solution.py:1123
  190.9 3.8 %all-to-all-start.11 = ((f32[16,9,8,128]{3,2,1,0:T(8,128)}), f32[16,9,8,128]{3,2,1,0:T(8,128)S(1)}, u32[]{:S(2)}, u32[]{:S(2)}) async-start(f32[16,9,8,128]{3,2,1,0:T(8,128)} %broadcast_in_dim.12), calls=%async_computation.11 | async-start | bytes 1179648 | tf_op jit(solution)/shard_map/all_to_all | solution.py:1150
  194.7 18.8 %shard_map.323 = (f32[2048,128]{1,0:T(8,128)}, f32[8,128]{1,0:T(8,128)S(1)}, f32[256,8,640]{2,1,0:T(8,128)}, f32[32,2,640]{2,1,0:T(2,128)}, f32[384,8,128]{2,1,0:T(8,128)}) custom-call(s32[2]{0:T(128)S(1)} %copy-done.5, f32[32,2,768]{2,1,0:T(2,128)S(1)} %all_to_all.94.top_ref.one_ref, f32[8,640]{1,0:T(8,128)S(1)} %get-tuple-element.142.stat_ref.stat1_ref.stat11_ref, ...), custom_call_target="tpu_custom_call" | custom-call | flops 1000000000 | bytes 1000000 | tf_op jit(solution)/shard_map/pallas_call | solution.py:1167
  213.5 2.1 dynamic-slice_bitcast_fusion
  216.3 5.6 %all-to-all-start.12 = ((f32[32,2,640]{2,1,0:T(2,128)}), f32[32,2,640]{2,1,0:T(2,128)S(1)}, u32[]{:S(2)}, u32[]{:S(2)}) async-start(f32[32,2,640]{2,1,0:T(2,128)} %get-tuple-element.178), calls=%async_computation.12 | async-start | bytes 327680 | tf_op jit(solution)/shard_map/all_to_all | solution.py:1123
  221.9 2.2 bitcast_add_fusion
  224.1 6.3 %all-to-all-done.12.grads_ref = f32[32,2,640]{2,1,0:T(2,128)S(1)} async-done(((f32[32,2,640]{2,1,0:T(2,128)}), f32[32,2,640]{2,1,0:T(2,128)S(1)}, u32[]{:S(2)}, u32[]{:S(2)}) %all-to-all-start.12) | async-done | bytes 163872 | tf_op jit(solution)/shard_map/all_to_all | solution.py:1123
  230.4 4.3 %all-to-all-start.13 = ((f32[16,12,8,128]{3,2,1,0:T(8,128)}), f32[16,12,8,128]{3,2,1,0:T(8,128)}, u32[]{:S(2)}, u32[]{:S(2)}) async-start(f32[16,12,8,128]{3,2,1,0:T(8,128)} %bitcast.12), calls=%async_computation.13 | async-start | bytes 1572864 | tf_op jit(solution)/shard_map/all_to_all | solution.py:1145
  234.7 15.7 %shard_map.324 = (f32[2048,128]{1,0:T(8,128)}, f32[8,384]{1,0:T(8,128)S(1)}, f32[60,8,128]{2,1,0:T(8,128)S(1)}, f32[8,384]{1,0:T(8,128)S(1)}) custom-call(s32[2]{0:T(128)S(1)} %copy-done.5, f32[32,2,640]{2,1,0:T(2,128)S(1)} %all-to-all-done.12.grads_ref, f32[8,640]{1,0:T(8,128)S(1)} %get-tuple-element.157.stat_ref.stat2_ref.stat02_ref, ...), custom_call_target="tpu_custom_call" | custom-call | flops 1000000000 | bytes 1000000 | tf_op jit(solution)/shard_map/pallas_call | solution.py:1167
  250.4 7.2 %all-to-all-done.13 = f32[16,12,8,128]{3,2,1,0:T(8,128)} async-done(((f32[16,12,8,128]{3,2,1,0:T(8,128)}), f32[16,12,8,128]{3,2,1,0:T(8,128)}, u32[]{:S(2)}, u32[]{:S(2)}) %all-to-all-start.13) | async-done | bytes 786464 | tf_op jit(solution)/shard_map/all_to_all | solution.py:1145
  257.6 1.2 reduce_sum.38
  259.7 4.3 %all-to-all-start.14 = ((f32[16,12,8,128]{3,2,1,0:T(8,128)}), f32[16,12,8,128]{3,2,1,0:T(8,128)}, u32[]{:S(2)}, u32[]{:S(2)}) async-start(f32[16,12,8,128]{3,2,1,0:T(8,128)} %broadcast_in_dim.13), calls=%async_computation.14 | async-start | bytes 1572864 | tf_op jit(solution)/shard_map/all_to_all | solution.py:1150
  264.0 12.8 %shard_map.325 = (f32[2048,128]{1,0:T(8,128)}, f32[32,2,640]{2,1,0:T(2,128)}, f32[128,8,128]{2,1,0:T(8,128)S(1)}, f32[8,256]{1,0:T(8,128)S(1)}) custom-call(s32[2]{0:T(128)S(1)} %copy-done.5, f32[32,2,640]{2,1,0:T(2,128)S(1)} %all-to-all-done.12.grads_ref, f32[8,640]{1,0:T(8,128)S(1)} %get-tuple-element.157.stat_ref.stat2_ref.stat02_ref, ...), custom_call_target="tpu_custom_call" | custom-call | flops 1000000000 | bytes 1000000 | tf_op jit(solution)/shard_map/pallas_call | solution.py:1167
  276.8 9.3 %all-to-all-done.14 = f32[16,12,8,128]{3,2,1,0:T(8,128)} async-done(((f32[16,12,8,128]{3,2,1,0:T(8,128)}), f32[16,12,8,128]{3,2,1,0:T(8,128)}, u32[]{:S(2)}, u32[]{:S(2)}) %all-to-all-start.14) | async-done | bytes 786464 | tf_op jit(solution)/shard_map/all_to_all | solution.py:1150
  286.7 2.6 all-to-all-start.15
  290.0 7.7 %all-to-all-done.15.zero_ref = f32[32,2,640]{2,1,0:T(2,128)S(1)} async-done(((f32[32,2,640]{2,1,0:T(2,128)}), f32[32,2,640]{2,1,0:T(2,128)S(1)}, u32[]{:S(2)}, u32[]{:S(2)}) %all-to-all-start.15) | async-done | bytes 163872 | tf_op jit(solution)/shard_map/all_to_all | solution.py:1123
  297.7 3.5 %all-to-all-start.16 = ((f32[16,4,8,128]{3,2,1,0:T(8,128)}), f32[16,4,8,128]{3,2,1,0:T(8,128)S(1)}, u32[]{:S(2)}, u32[]{:S(2)}) async-start(f32[16,4,8,128]{3,2,1,0:T(8,128)} %bitcast.18), calls=%async_computation.16 | async-start | bytes 524288 | tf_op jit(solution)/shard_map/all_to_all | solution.py:1145
  302.0 7.4 %shard_map.326 = (f32[112,2048]{1,0:T(8,128)}, f32[2,112,640]{2,1,0:T(8,128)S(1)}, f32[16,640]{1,0:T(8,128)S(1)}, f32[4,640]{1,0:T(4,128)}, f32[4,640]{1,0:T(4,1...) custom-call(s32[2]{0:T(128)S(1)} %copy-done.5, ...), custom_call_target="tpu_custom_call" | custom-call | flops 1000000000 | bytes 1000000 | tf_op jit(solution)/shard_map/pallas_call | solution.py:1167
  309.4 3.4 %all-to-all-done.16 = f32[16,4,8,128]{3,2,1,0:T(8,128)S(1)} async-done(((f32[16,4,8,128]{3,2,1,0:T(8,128)}), f32[16,4,8,128]{3,2,1,0:T(8,128)S(1)}, u32[]{:S(2)}, u32[]{:S(2)}) %all-to-all-start.16) | async-done | bytes 262176 | tf_op jit(solution)/shard_map/all_to_all | solution.py:1145
  313.5 3.5 %all-to-all-start.17 = ((f32[16,4,8,128]{3,2,1,0:T(8,128)}), f32[16,4,8,128]{3,2,1,0:T(8,128)S(1)}, u32[]{:S(2)}, u32[]{:S(2)}) async-start(f32[16,4,8,128]{3,2,1,0:T(8,128)} %broadcast_in_dim.14), calls=%async_computation.17 | async-start | bytes 524288 | tf_op jit(solution)/shard_map/all_to_all | solution.py:1150
  317.1 3.1 shard_map.327
  320.2 7.8 %all-to-all-done.17 = f32[16,4,8,128]{3,2,1,0:T(8,128)S(1)} async-done(((f32[16,4,8,128]{3,2,1,0:T(8,128)}), f32[16,4,8,128]{3,2,1,0:T(8,128)S(1)}, u32[]{:S(2)}, u32[]{:S(2)}) %all-to-all-start.17) | async-done | bytes 262176 | tf_op jit(solution)/shard_map/all_to_all | solution.py:1150
  328.0 1.5 collective-permute-done.5.late_other_ref
  (68 shorter events, 8.7 us)
Async XLA Ops:
  0.7 11.3 %copy-start.16 = (f32[2,45,640]{2,0,1:T(2,128)S(1)}, f32[2,45,640]{2,0,1:T(2,128)}, u32[]{:S(2)}) copy-start(f32[2,45,640]{2,0,1:T(2,128)} %param.27) | copy-start | bytes 691204
  0.7 11.3 %copy-start.5 = (s32[2]{0:T(128)S(1)}, s32[2]{0:T(128)}, u32[]{:S(2)}) copy-start(s32[2]{0:T(128)} %counts_ref.25) | copy-start | bytes 28
  0.7 11.3 %copy-start.12 = (f32[112,2048]{1,0:T(8,128)S(1)}, f32[112,2048]{1,0:T(8,128)}, u32[]{:S(2)}) copy-start(f32[112,2048]{1,0:T(8,128)} %video_ref.3) | copy-start | bytes 2752516
  0.7 11.3 %copy-start.13 = (f32[112,512]{1,0:T(8,128)S(1)}, f32[112,512]{1,0:T(8,128)}, u32[]{:S(2)}) copy-start(f32[112,512]{1,0:T(8,128)} %cot_ref.1) | copy-start | bytes 688132
  4.6 16.1 %all-to-all-start = ((f32[32,2,768]{2,1,0:T(2,128)}), f32[32,2,768]{2,1,0:T(2,128)S(1)}, u32[]{:S(2)}, u32[]{:S(2)}) async-start(f32[32,2,768]{2,1,0:T(2,128)} %get-tuple-element.124), calls=%async_computation | async-start | bytes 393216 | tf_op jit(solution)/shard_map/all_to_all | solution.py:1123
  12.0 8.7 %copy-start = (f32[2,640,112]{1,2,0:T(8,128)S(1)}, f32[2,640,112]{1,2,0:T(8,128)}, u32[]{:S(2)}) copy-start(f32[2,640,112]{1,2,0:T(8,128)} %param.22) | copy-start | bytes 1720324
  12.0 8.7 %copy-start.3 = (f32[4,640]{1,0:T(4,128)S(1)}, f32[4,640]{1,0:T(4,128)}, u32[]{:S(2)}) copy-start(f32[4,640]{1,0:T(4,128)} %gain_ref.19) | copy-start | bytes 30724
  12.0 8.7 %copy-start.4 = (f32[4,640]{1,0:T(4,128)S(1)}, f32[4,640]{1,0:T(4,128)}, u32[]{:S(2)}) copy-start(f32[4,640]{1,0:T(4,128)} %bias_ref.17) | copy-start | bytes 30724
  20.7 30.2 %copy-start.1 = (f32[2,160,640]{2,1,0:T(8,128)S(1)}, f32[2,160,640]{2,1,0:T(8,128)}, u32[]{:S(2)}) copy-start(f32[2,160,640]{2,1,0:T(8,128)} %down_ref.7) | copy-start | bytes 2457604
  20.7 30.2 %copy-start.2 = (f32[2,112,640]{2,1,0:T(8,128)S(1)}, f32[2,112,640]{2,1,0:T(8,128)}, u32[]{:S(2)}) copy-start(f32[2,112,640]{2,1,0:T(8,128)} %proj_ref.7) | copy-start | bytes 1720324
  20.7 30.2 %copy-start.6 = (f32[2,640]{1,0:T(2,128)S(1)}, f32[2,640]{1,0:T(2,128)}, u32[]{:S(2)}) copy-start(f32[2,640]{1,0:T(2,128)} %upb_ref.3) | copy-start | bytes 15364
  20.7 30.2 %copy-start.9 = (f32[2,160]{1,0:T(2,128)S(1)}, f32[2,160]{1,0:T(2,128)}, u32[]{:S(2)}) copy-start(f32[2,160]{1,0:T(2,128)} %downb_ref.3) | copy-start | bytes 3844
  50.9 13.1 %copy-start.17 = (f32[2,112]{1,0:T(2,128)S(1)}, f32[2,112]{1,0:T(2,128)}, u32[]{:S(2)}) copy-start(f32[2,112]{1,0:T(2,128)} %param.25) | copy-start | bytes 2692
  50.9 13.1 %copy-start.18 = (f32[2,112]{1,0:T(2,128)S(1)}, f32[2,112]{1,0:T(2,128)}, u32[]{:S(2)}) copy-start(f32[2,112]{1,0:T(2,128)} %param.26) | copy-start | bytes 2692
  51.0 20.3 %copy-start.14 = (f32[136,128]{1,0:T(8,128)S(1)}, f32[136,128]{1,0:T(8,128)}, u32[]{:S(2)}) copy-start(f32[136,128]{1,0:T(8,128)} %get-tuple-element.131.gram0_ref) | copy-start | bytes 208900
  61.4 9.8 %all-to-all-start.2 = ((f32[32,2,128]{2,1,0:T(2,128)}), f32[32,2,128]{2,1,0:T(2,128)S(1)}, u32[]{:S(2)}, u32[]{:S(2)}) async-start(f32[32,2,128]{2,1,0:T(2,128)} %get-tuple-element.130), calls=%async_computation.2 | async-start | bytes 65536 | tf_op jit(solution)/shard_map/all_to_all | solution.py:1123
  86.7 13.1 %all-to-all-start.4 = ((f32[32,2,8,128]{3,2,1,0:T(8,128)}), f32[32,2,8,128]{3,2,1,0:T(8,128)S(1)}, u32[]{:S(2)}, u32[]{:S(2)}) async-start(f32[32,2,8,128]{3,2,1,0:T(8,128)} %bitcast.2), calls=%async_computation.4 | async-start | bytes 524288 | tf_op jit(solution)/shard_map/all_to_all | solution.py:1145
  128.9 13.0 %all-to-all-start.7 = ((f32[32,2,8,128]{3,2,1,0:T(8,128)}), f32[32,2,8,128]{3,2,1,0:T(8,128)S(1)}, u32[]{:S(2)}, u32[]{:S(2)}) async-start(f32[32,2,8,128]{3,2,1,0:T(8,128)} %broadcast_in_dim.10), calls=%async_computation.7 | async-start | bytes 524288 | tf_op jit(solution)/shard_map/all_to_all | solution.py:1150
  139.3 7.3 %copy-start.15 = (f32[288,8,128]{2,1,0:T(8,128)S(1)}, f32[288,8,128]{2,1,0:T(8,128)}, u32[]{:S(2)}) copy-start(f32[288,8,128]{2,1,0:T(8,128)} %get-tuple-element.159) | copy-start | bytes 3538948
  142.9 3.7 %collective-permute-start = (f32[144,8,128]{2,1,0:T(8,128)S(1)}, f32[144,8,128]{2,1,0:T(8,128)}, u32[]{:S(2)}, u32[]{:S(2)}) collective-permute-start(f32[144,8,128]{2,1,0:T(8,128)S(1)} %dynamic-slice_bitcast_fusion.1), channel_id=1, source_target_pairs={{0,1},{1,0},{2,3},{3,2},{4,5},{5,4},{6,7},{7,6},{8,9},{9,8},{10,11... | collective-permute-start | bytes 1769480 | tf_op jit(solution)/shard_map/ppermute | solution.py:1131
  143.4 11.7 %all-to-all-start.8 = ((f32[32,2,640]{2,1,0:T(2,128)}), f32[32,2,640]{2,1,0:T(2,128)S(1)}, u32[]{:S(2)}, u32[]{:S(2)}) async-start(f32[32,2,640]{2,1,0:T(2,128)} %get-tuple-element.158), calls=%async_computation.8 | async-start | bytes 327680 | tf_op jit(solution)/shard_map/all_to_all | solution.py:1123
  155.1 22.1 %all-to-all-start.9 = ((f32[16,9,8,128]{3,2,1,0:T(8,128)}), f32[16,9,8,128]{3,2,1,0:T(8,128)S(1)}, u32[]{:S(2)}, u32[]{:S(2)}) async-start(f32[16,9,8,128]{3,2,1,0:T(8,128)} %bitcast.7), calls=%async_computation.9 | async-start | bytes 1179648 | tf_op jit(solution)/shard_map/all_to_all | solution.py:1145
  190.9 25.4 %all-to-all-start.11 = ((f32[16,9,8,128]{3,2,1,0:T(8,128)}), f32[16,9,8,128]{3,2,1,0:T(8,128)S(1)}, u32[]{:S(2)}, u32[]{:S(2)}) async-start(f32[16,9,8,128]{3,2,1,0:T(8,128)} %broadcast_in_dim.12), calls=%async_computation.11 | async-start | bytes 1179648 | tf_op jit(solution)/shard_map/all_to_all | solution.py:1150
  215.6 6.4 %collective-permute-start.1 = (f32[192,8,128]{2,1,0:T(8,128)}, f32[192,8,128]{2,1,0:T(8,128)S(1)}, u32[]{:S(2)}, u32[]{:S(2)}) collective-permute-start(f32[192,8,128]{2,1,0:T(8,128)} %dynamic-slice_bitcast_fusion), channel_id=1, source_target_pairs={{0,1},{1,0},{2,3},{3,2},{4,5},{5,4},{6,7},{7,6},{8,9},{9,8},{10,11... | collective-permute-start | bytes 2359304 | tf_op jit(solution)/shard_map/ppermute | solution.py:1131
  216.3 14.1 %collective-permute-start.2 = (f32[144,8,128]{2,1,0:T(8,128)S(1)}, f32[144,8,128]{2,1,0:T(8,128)}, u32[]{:S(2)}, u32[]{:S(2)}) collective-permute-start(f32[144,8,128]{2,1,0:T(8,128)S(1)} %bitcast.39), channel_id=1, source_target_pairs={{0,1},{1,0},{2,3},{3,2},{4,5},{5,4},{6,7},{7,6},{8,9},{9,8},{10,11... | collective-permute-start | bytes 1769480 | tf_op jit(solution)/shard_map/ppermute | solution.py:1131
  216.3 14.1 %all-to-all-start.12 = ((f32[32,2,640]{2,1,0:T(2,128)}), f32[32,2,640]{2,1,0:T(2,128)S(1)}, u32[]{:S(2)}, u32[]{:S(2)}) async-start(f32[32,2,640]{2,1,0:T(2,128)} %get-tuple-element.178), calls=%async_computation.12 | async-start | bytes 327680 | tf_op jit(solution)/shard_map/all_to_all | solution.py:1123
  230.4 27.2 %all-to-all-start.13 = ((f32[16,12,8,128]{3,2,1,0:T(8,128)}), f32[16,12,8,128]{3,2,1,0:T(8,128)}, u32[]{:S(2)}, u32[]{:S(2)}) async-start(f32[16,12,8,128]{3,2,1,0:T(8,128)} %bitcast.12), calls=%async_computation.13 | async-start | bytes 1572864 | tf_op jit(solution)/shard_map/all_to_all | solution.py:1145
  259.7 26.4 %all-to-all-start.14 = ((f32[16,12,8,128]{3,2,1,0:T(8,128)}), f32[16,12,8,128]{3,2,1,0:T(8,128)}, u32[]{:S(2)}, u32[]{:S(2)}) async-start(f32[16,12,8,128]{3,2,1,0:T(8,128)} %broadcast_in_dim.13), calls=%async_computation.14 | async-start | bytes 1572864 | tf_op jit(solution)/shard_map/all_to_all | solution.py:1150
  276.8 25.2 %copy-start.7 = (f32[4,640]{1,0:T(4,128)S(1)}, f32[4,640]{1,0:T(4,128)}, u32[]{:S(2)}) copy-start(f32[4,640]{1,0:T(4,128)} %means_ref.1) | copy-start | bytes 30724
  276.8 25.2 %copy-start.8 = (f32[4,640]{1,0:T(4,128)S(1)}, f32[4,640]{1,0:T(4,128)}, u32[]{:S(2)}) copy-start(f32[4,640]{1,0:T(4,128)} %vars_ref.1) | copy-start | bytes 30724
  276.8 25.2 %copy-start.10 = (f32[2,112]{1,0:T(2,128)S(1)}, f32[2,112]{1,0:T(2,128)}, u32[]{:S(2)}) copy-start(f32[2,112]{1,0:T(2,128)} %nmeans_ref.1) | copy-start | bytes 2692
  276.8 25.2 %copy-start.11 = (f32[2,112]{1,0:T(2,128)S(1)}, f32[2,112]{1,0:T(2,128)}, u32[]{:S(2)}) copy-start(f32[2,112]{1,0:T(2,128)} %nvars_ref.1) | copy-start | bytes 2692
  286.1 11.7 %collective-permute-start.4 = (f32[192,8,128]{2,1,0:T(8,128)}, f32[192,8,128]{2,1,0:T(8,128)}, u32[]{:S(2)}, u32[]{:S(2)}) collective-permute-start(f32[192,8,128]{2,1,0:T(8,128)} %bitcast.13.pack0_ref), channel_id=1, source_target_pairs={{0,1},{1,0},{2,3},{3,2},{4,5},{5,4},{6,7},{7,6},{8,9},{9,8},{10,11... | collective-permute-start | bytes 2359304 | tf_op jit(solution)/shard_map/ppermute | solution.py:1131
  286.1 3.2 collective-permute-start.3
  286.7 11.1 %all-to-all-start.15 = ((f32[32,2,640]{2,1,0:T(2,128)}), f32[32,2,640]{2,1,0:T(2,128)S(1)}, u32[]{:S(2)}, u32[]{:S(2)}) async-start(f32[32,2,640]{2,1,0:T(2,128)} %get-tuple-element.196), calls=%async_computation.15 | async-start | bytes 327680 | tf_op jit(solution)/shard_map/all_to_all | solution.py:1123
  297.7 15.1 %all-to-all-start.16 = ((f32[16,4,8,128]{3,2,1,0:T(8,128)}), f32[16,4,8,128]{3,2,1,0:T(8,128)S(1)}, u32[]{:S(2)}, u32[]{:S(2)}) async-start(f32[16,4,8,128]{3,2,1,0:T(8,128)} %bitcast.18), calls=%async_computation.16 | async-start | bytes 524288 | tf_op jit(solution)/shard_map/all_to_all | solution.py:1145
  313.5 14.5 %all-to-all-start.17 = ((f32[16,4,8,128]{3,2,1,0:T(8,128)}), f32[16,4,8,128]{3,2,1,0:T(8,128)S(1)}, u32[]{:S(2)}, u32[]{:S(2)}) async-start(f32[16,4,8,128]{3,2,1,0:T(8,128)} %broadcast_in_dim.14), calls=%async_computation.17 | async-start | bytes 524288 | tf_op jit(solution)/shard_map/all_to_all | solution.py:1150
  328.0 1.5 collective-permute-start.5

commit v5 on v4

--- a/solution.py
+++ b/solution.py
@@ -448,7 +448,7 @@
 
 
 def each_frame(count, body, init):
-    return lax.fori_loop(0, count, body, init, unroll=min(4, count))
+    return lax.fori_loop(0, count, body, init, unroll=min(8, count))
 
 
 def lanes_of(ref, tile):
@@ -1053,24 +1053,39 @@
 
 def list_rows(core_ref, pair, at, count):
     first_core = core_ref[0] == 0
-    mine, other = pair
-    half = mine.shape[0]
+    mine, other = pair[0:2]
+    if len(pair) > 2:
+        share = pair[2]
+        half = mine.shape[0] * share
+
+        def run(ref, begin, size):
+            pieces = []
+            while size:
+                length = min(size, share - begin % share)
+                pieces.append(ref[begin // share, begin % share : begin % share + length])
+                begin = begin + length
+                size = size - length
+            return pieces[0] if len(pieces) == 1 else jnp.concatenate(pieces, axis=0)
+    else:
+        half = mine.shape[0]
+
+        def run(ref, begin, size):
+            return ref[begin : begin + size]
+
     pieces = []
     if at < half:
         size = min(count, half - at)
-        here = slice(at, at + size)
-        pieces.append(jnp.where(first_core, mine[here], other[here]))
+        pieces.append(jnp.where(first_core, run(mine, at, size), run(other, at, size)))
         count = count - size
         at = at + size
     if count:
-        here = slice(at - half, at - half + count)
-        pieces.append(jnp.where(first_core, other[here], mine[here]))
+        pieces.append(jnp.where(first_core, run(other, at - half, count), run(mine, at - half, count)))
     values = pieces[0] if len(pieces) == 1 else jnp.concatenate(pieces, axis=0)
     return values.reshape(-1, LANES)
 
 
 def lists_kernel(
-    core_ref, pack0_ref, pack0_other_ref, pack1_ref, pack1_other_ref, less_ref, factor_ref,
+    share, core_ref, pack0_ref, pack0_other_ref, pack1_ref, pack1_other_ref, less_ref, factor_ref,
     dw_ref, dtaps_ref, ddown_ref, dup_ref, dproj_ref, dupb_ref, ddownb_ref,
 ):
     narrow = dw_ref.shape[1]
@@ -1079,7 +1094,7 @@
     tiles = dw_ref.shape[2] // LANES
     per_pack = pack_tiles(narrow, squeeze)
     per_tile = narrow // 8 + -(-taps // 8)
-    packs = ((pack0_ref, pack0_other_ref), (pack1_ref, pack1_other_ref))
+    packs = ((pack0_ref, pack0_other_ref, share), (pack1_ref, pack1_other_ref))
     for block in range(2):
         down_rows = []
         for tile in range(tiles):
@@ -1427,20 +1442,16 @@
     pack_one_other = swap_cores(pack_one)
     sums, pack_zero, pack_one_other = together(exchange(sums), add_cores(pack_zero), pack_one_other)
     pack_zero = share_out(pack_zero)
-    first = tiles - tiles // 2
-    dxpre_zero, sums_in, late, grad_a = depth_backward(
-        0, 0, first, sums, stat02, stat01, dy2_zero, d_zero, e_zero, planes_zero, x_columns, nothing, nothing, nothing
-    )
-    dxpre_zero, pack_zero = together(dxpre_zero, pack_zero)
-    pack_zero = share_back(pack_zero)
-    dxpre_zero, sums, late, grad_b = depth_backward(
-        0, first, tiles, sums, stat02, stat01, dy2_zero, d_zero, e_zero, planes_zero, x_columns, dxpre_zero, sums_in, late
-    )
-    grad_zero = jnp.concatenate([grad_a, grad_b], axis=1)
+    dxpre_zero, sums, late, grad_zero = depth_backward(
+        0, 0, tiles, sums, stat02, stat01, dy2_zero, d_zero, e_zero, planes_zero, x_columns, nothing, nothing, nothing
+    )
     sums, pack_zero = together(sums, pack_zero)
-    pack_zero_other = swap_cores(pack_zero)
-    top_zero, late, pack_zero_other = together(exchange(sums), add_cores(late), pack_zero_other)
-    late = share_out(late)
+    top_zero, late = together(exchange(sums), add_cores(late))
+    own = jnp.sum(pack_zero, axis=0)
+    joint = jnp.concatenate(
+        [jnp.broadcast_to(own[None], pack_zero.shape), late.reshape(pack_zero.shape[0], -1, 8, LANES)], axis=1
+    )
+    joint = lax.all_to_all(joint, CHIPS, 0, 0, tiled=True)
     core = lax.axis_index("core").astype(jnp.int32).reshape(1)
     final_args = (
         frame_counts, momentum_index, gram, stat01, stat02, stat11, stat12, grad_zero, grad_one, top_one,
@@ -1454,15 +1465,16 @@
     video_grad, less, factor, wgain, wbias, ngain, nbias, newm, newv, newnm, newnv = simple_call(
         finish_kernel, 2, final_args, final_outs
     )
-    less, late = together(less, late)
-    late = share_back(late)
+    less, joint = together(less, joint)
+    joint_other = swap_cores(joint)
+    late = share_back(joint[:, own.shape[0] :])
     list_shapes = [
         shape(2, cin, width), shape(2, taps, width), shape(2, squeeze, width), shape(2, squeeze, width),
         shape(2, cin, width), shape(2, width), shape(2, squeeze),
     ]
-    list_args = (core, pack_zero, pack_zero_other, pack_one, pack_one_other, less, factor)
+    list_args = (core, joint, joint_other, pack_one, pack_one_other, less, factor)
     dw_t, dtaps, ddown, dup, dproj, dupb, ddownb = call(
-        lists_kernel, (1,), [SCALARS] + [whole(array) for array in list_args[1:5]] + [of_block(1, cin, width), whole(factor)],
+        functools.partial(lists_kernel, own.shape[0]), (1,), [SCALARS] + [whole(array) for array in list_args[1:5]] + [of_block(1, cin, width), whole(factor)],
         [of_block(1, cin, width), of_block(1, taps, width)] + [whole(item) for item in list_shapes[2:]], list_shapes, [],
         list_args,
     )

time: 333 us -> 325 us (0.976)
  Pallas kernels: 137 us -> 130 us
    all_to_all x0 -> x1, waiting for transfers between devices: none -> 20.8 us  [local(): joint = lax.all_to_all(joint, CHIPS, 0, 0, tiled=True)]
    all_to_all x4 -> x3, waiting for transfers between devices: 13.3 us -> 2.84 us  [share_out(): lax.all_to_all(tiles.reshape(count, -1, *tiles.shape[1:]), names, 0, 0, t...]
    all_to_all x4 -> x3, waiting for transfers between devices: 19.6 us -> 10.7 us  [share_back(): lax.all_to_all(jnp.broadcast_to(own[None], pieces.shape), names, 0, 0, ti...]
    pallas_call x15 -> x14, Pallas kernels: 137 us -> 130 us  [call(): pl.pallas_call(kernel, grid=grid, in_specs=in_specs, out_specs=out_specs,...]
    all_to_all x5, starting transfers between devices: 21.2 us -> 26.2 us  [exchange(): return lax.all_to_all(send, AXES, 0, 0, tiled=True)]
    all_to_all x0 -> x1, starting transfers between devices: none -> 4.71 us  [local(): joint = lax.all_to_all(joint, CHIPS, 0, 0, tiled=True)]
    all_to_all x4 -> x3, starting transfers between devices: 14.2 us -> 9.85 us  [share_back(): lax.all_to_all(jnp.broadcast_to(own[None], pieces.shape), names, 0, 0, ti...]
    all_to_all x4 -> x3, starting transfers between devices: 14 us -> 9.97 us  [share_out(): lax.all_to_all(tiles.reshape(count, -1, *tiles.shape[1:]), names, 0, 0, t...]
  transfers between devices with their start and end apart: 19 -> 18, of which waited for: 12 -> 11; matrix products, arithmetic and copies ran while one was open for 2% -> 3% of each run, Pallas kernels for 29% -> 28%
where the time goes in v5:
time: 325 us
  Pallas kernels  130 us (40%)
  waiting for transfers between devices  66.7 us (21%)
  blocking collectives  57.3 us (18%)
  starting transfers between devices  52.4 us (16%)
  local copies, waits for them, and re-layouts  8.39 us (3%)
  other arithmetic  7.94 us (2%)
    pallas_call x14, Pallas kernels, call(): pl.pallas_call(kernel, grid=grid, in_specs=in_specs, out_specs=out_specs,...  130 us
    all_to_all x5, blocking collectives, exchange(): return lax.all_to_all(send, AXES, 0, 0, tiled=True)  57.3 us
    all_to_all x5, waiting for transfers between devices, exchange(): return lax.all_to_all(send, AXES, 0, 0, tiled=True)  30.9 us
    all_to_all x5, starting transfers between devices, exchange(): return lax.all_to_all(send, AXES, 0, 0, tiled=True)  26.2 us
    all_to_all x1, waiting for transfers between devices, local(): joint = lax.all_to_all(joint, CHIPS, 0, 0, tiled=True)  20.8 us
    all_to_all x3, waiting for transfers between devices, share_back(): lax.all_to_all(jnp.broadcast_to(own[None], pieces.shape), names, 0, 0, ti...  10.7 us
    all_to_all x3, starting transfers between devices, share_out(): lax.all_to_all(tiles.reshape(count, -1, *tiles.shape[1:]), names, 0, 0, t...  9.97 us
    all_to_all x3, starting transfers between devices, share_back(): lax.all_to_all(jnp.broadcast_to(own[None], pieces.shape), names, 0, 0, ti...  9.85 us
  transfers between devices with their start and end apart: 18, of which 11 were waited for; matrix products, arithmetic and copies ran while one was open for 3% of the time, Pallas kernels for 28%

profile of v5, /device:TPU:0, one launch (start us, length us, event | category | flops | bytes accessed | tf_op | source)
XLA Modules:
  0.0 324.8 jit_solution(1178396035759549883)
XLA Ops:
  0.7 3.6 %shard_map.314 = (f32[136,128]{1,0:T(8,128)}, f32[32,2,768]{2,1,0:T(2,128)}) custom-call(s32[2]{0:T(128)} %counts_ref.23, f32[112,2048]{1,0:T(8,128)} %video_ref.3, f32[2,112,640]{2,1,0:T(8,128)} %bitcast.27), custom_call_target="tpu_custom_call" | custom-call | flops 1000000000 | bytes 1000000 | tf_op jit(solution)/shard_map/pallas_call | solution.py:1182
  4.3 7.3 %all-to-all-start = ((f32[32,2,768]{2,1,0:T(2,128)}), f32[32,2,768]{2,1,0:T(2,128)S(1)}, u32[]{:S(2)}, u32[]{:S(2)}) async-start(f32[32,2,768]{2,1,0:T(2,128)} %get-tuple-element.117), calls=%async_computation | async-start | bytes 393216 | tf_op jit(solution)/shard_map/all_to_all | solution.py:1138
  11.6 1.2 copy-done.12
  12.8 3.4 %shard_map.315 = (f32[2048,128]{1,0:T(8,128)}, bf16[2048,256]{1,0:T(8,128)(2,1)}, bf16[256,2048]{1,0:T(8,128)(2,1)}, f32[512,128]{1,0:T(8,128)S(1)}) custom-call(s32[2]{0:T(128)S(1)} %copy-done.5, f32[112,2048]{1,0:T(8,128)S(1)} %copy-done.12, f32[112,512]{1,0:T(8,128)S(1)} %copy-done.13), custom_call_target="tpu_custom_call" | custom-call | flops 1000000000 | bytes 1000000 | tf_op jit(solution)/shard_map/pallas_call | solution.py:1182
  16.2 4.1 %all-to-all-done.sums_ref.count_ref = f32[32,2,768]{2,1,0:T(2,128)S(1)} async-done(((f32[32,2,768]{2,1,0:T(2,128)}), f32[32,2,768]{2,1,0:T(2,128)S(1)}, u32[]{:S(2)}, u32[]{:S(2)}) %all-to-all-start) | async-done | bytes 196640 | tf_op jit(solution)/shard_map/all_to_all | solution.py:1138
  20.4 16.8 %shard_map.316 = (f32[256,8,640]{2,1,0:T(8,128)}, f32[256,8,640]{2,1,0:T(8,128)}, f32[8,640]{1,0:T(8,128)S(1)}, f32[32,2,640]{2,1,0:T(2,128)S(1)}, f32[8,2,4,8,8,640]{5,4,3,2,1,0:T(8,128)}) custom-call(s32[2]{0:T(128)S(1)} %copy-done.5, f32[32,2,768]{2,1,0:T(2,128)S(1)} %all-to-all-done.sums_ref.count_ref, ...), custom_call_target="tpu_custom_call" | custom-call | flops 1000000000 | bytes 1000000 | tf_op jit(solution)/shard_map/pallas_call | solution.py:1182
  37.2 11.9 %all_to_all.85.sums_ref = f32[32,2,640]{2,1,0:T(2,128)S(1)} all-to-all(f32[32,2,640]{2,1,0:T(2,128)S(1)} %get-tuple-element.119), channel_id=1, replica_groups=mesh['dp'=4,'z'=4,'core'=2] {'dp','z','core'}, dimensions={0} | all-to-all | bytes 327680 | tf_op jit(solution)/shard_map/all_to_all | solution.py:1138
  49.1 9.3 %shard_map.317 = (f32[2048,128]{1,0:T(8,128)}, f32[8,640]{1,0:T(8,128)S(1)}, f32[8,640]{1,0:T(8,128)S(1)}, f32[8,160]{1,0:T(8,128)S(1)}, f32[8,640]{1,0:T(8,128)S(1)}, /*index=5*/f32[32,2,128]{2,1,0:T(2,128)}) custom-call(s32[2]{0:T(128)S(1)} %copy-done.5, f32[32,2,640]{2,1,0:T(2,128)S(1)} %all_to_all.85.sums_ref, ...), custom_call_target="tpu_custom_call" | custom-call | flops 1000000000 | bytes 1000000 | tf_op jit(solution)/shard_map/pallas_call | solution.py:1182
  58.4 2.6 all-to-all-start.2
  61.0 7.2 %all-to-all-done.2.sums_ref = f32[32,2,128]{2,1,0:T(2,128)S(1)} async-done(((f32[32,2,128]{2,1,0:T(2,128)}), f32[32,2,128]{2,1,0:T(2,128)S(1)}, u32[]{:S(2)}, u32[]{:S(2)}) %all-to-all-start.2) | async-done | bytes 32800 | tf_op jit(solution)/shard_map/all_to_all | solution.py:1138
  68.2 4.8 %shard_map.318 = (f32[2048,128]{1,0:T(8,128)}, bf16[2048,256]{1,0:T(8,128)(2,1)}, bf16[256,2048]{1,0:T(8,128)(2,1)}, f32[64,8,128]{2,1,0:T(8,128)}, f32[8,128]{1,0:T(8,128)S(1)}, /*index=5*/f32[32,2,640]{2,1,0:T(2,128)S(1)}) custom-call(s32[2]{0:T(128)S(1)} %copy-done.5, f32[32,2,128]{2,1,0:T(2,128)S(1)} %all-to-all-done.2.sums_ref, ...), custom_call_target="tpu_custom_call" | custom-call | flops 1000000000 | bytes 1000000 | tf_op jit(solution)/shard_map/pallas_call | solution.py:1182
  73.0 10.2 %all_to_all.86.sums_ref = f32[32,2,640]{2,1,0:T(2,128)S(1)} all-to-all(f32[32,2,640]{2,1,0:T(2,128)S(1)} %get-tuple-element.127), channel_id=1, replica_groups=mesh['dp'=4,'z'=4,'core'=2] {'dp','z','core'}, dimensions={0} | all-to-all | bytes 327680 | tf_op jit(solution)/shard_map/all_to_all | solution.py:1138
  83.2 2.6 all-to-all-start.4
  85.8 10.3 %shard_map.319 = (f32[256,8,640]{2,1,0:T(8,128)}, f32[64,8,640]{2,1,0:T(8,128)}, f32[8,640]{1,0:T(8,128)S(1)}, f32[32,2,640]{2,1,0:T(2,128)S(1)}, f32[8,3,18,8,640]{4,3,2,1,0:T(8,128)}) custom-call(s32[2]{0:T(128)S(1)} %copy-done.5, f32[32,2,640]{2,1,0:T(2,128)S(1)} %all_to_all.86.sums_ref, f32[8,128]{1,0:T(8,128)S(1)} %get-tuple-element.130.count_ref.nstat_ref, ...), custom_call_target="tpu_custom_call" | custom-call | flops 1000000000 | bytes 1000000 | tf_op jit(solution)/shard_map/pallas_call | solution.py:1182
  96.1 14.0 %all_to_all.87.sums_ref = f32[32,2,640]{2,1,0:T(2,128)S(1)} all-to-all(f32[32,2,640]{2,1,0:T(2,128)S(1)} %get-tuple-element.134), channel_id=1, replica_groups=mesh['dp'=4,'z'=4,'core'=2] {'dp','z','core'}, dimensions={0} | all-to-all | bytes 327680 | tf_op jit(solution)/shard_map/all_to_all | solution.py:1138
  110.1 4.5 %shard_map.320 = (f32[512,128]{1,0:T(8,128)S(1)}, f32[8,640]{1,0:T(8,128)S(1)}, f32[8,640]{1,0:T(8,128)S(1)}, f32[8,160]{1,0:T(8,128)S(1)}, f32[8,640]{1,0:T(8,128)S(1)}, /*index=5*/f32[32,4,128]{2,1,0:T(4,128)S(1)}) custom-call(s32[2]{0:T(128)S(1)} %copy-done.5, f32[32,2,640]{2,1,0:T(2,128)S(1)} %all_to_all.87.sums_ref, ...), custom_call_target="tpu_custom_call" | custom-call | flops 1000000000 | bytes 1000000 | tf_op jit(solution)/shard_map/pallas_call | solution.py:1182
  114.6 9.5 %all_to_all.88.third_ref = f32[32,4,128]{2,1,0:T(4,128)S(1)} all-to-all(f32[32,4,128]{2,1,0:T(4,128)S(1)} %get-tuple-element.137), channel_id=1, replica_groups=mesh['dp'=4,'z'=4,'core'=2] {'dp','z','core'}, dimensions={0} | all-to-all | bytes 131072 | tf_op jit(solution)/shard_map/all_to_all | solution.py:1138
  124.9 2.6 all-to-all-start.7
  127.5 7.8 %shard_map.321 = (f32[112,512]{1,0:T(8,128)}, f32[8,128]{1,0:T(8,128)S(1)}, f32[64,8,640]{2,1,0:T(8,128)}, f32[32,2,640]{2,1,0:T(2,128)}, f32[288,8,128]{2,1,0:T(8,128)}) custom-call(s32[2]{0:T(128)S(1)} %copy-done.5, f32[32,4,128]{2,1,0:T(4,128)S(1)} %all_to_all.88.third_ref, f32[512,128]{1,0:T(8,128)S(1)} %get-tuple-element.140.z_ref, ...), custom_call_target="tpu_custom_call" | custom-call | flops 1000000000 | bytes 1000000 | tf_op jit(solution)/shard_map/pallas_call | solution.py:1182
  135.3 2.5 all-to-all-done.7
  137.9 1.1 dynamic-slice_bitcast_fusion.1
  139.4 3.2 all-to-all-start.8
  142.6 2.0 bitcast_add_fusion.1
  144.6 6.5 %all-to-all-done.8.grads_ref = f32[32,2,640]{2,1,0:T(2,128)S(1)} async-done(((f32[32,2,640]{2,1,0:T(2,128)}), f32[32,2,640]{2,1,0:T(2,128)S(1)}, u32[]{:S(2)}, u32[]{:S(2)}) %all-to-all-start.8) | async-done | bytes 163872 | tf_op jit(solution)/shard_map/all_to_all | solution.py:1138
  151.1 3.8 %all-to-all-start.9 = ((f32[16,9,8,128]{3,2,1,0:T(8,128)}), f32[16,9,8,128]{3,2,1,0:T(8,128)S(1)}, u32[]{:S(2)}, u32[]{:S(2)}) async-start(f32[16,9,8,128]{3,2,1,0:T(8,128)} %bitcast.7), calls=%async_computation.9 | async-start | bytes 1179648 | tf_op jit(solution)/shard_map/all_to_all | solution.py:1160
  154.9 15.6 %shard_map.322 = (f32[2048,128]{1,0:T(8,128)}, f32[32,2,768]{2,1,0:T(2,128)S(1)}, f32[100,8,128]{2,1,0:T(8,128)S(1)}, f32[8,640]{1,0:T(8,128)S(1)}) custom-call(s32[2]{0:T(128)S(1)} %copy-done.5, f32[32,2,640]{2,1,0:T(2,128)S(1)} %all-to-all-done.8.grads_ref, f32[8,640]{1,0:T(8,128)S(1)} %get-tuple-element.141.stat_ref.stat2_ref.stat12_ref, ...), custom_call_target="tpu_custom_call" | custom-call | flops 1000000000 | bytes 1000000 | tf_op jit(solution)/shard_map/pallas_call | solution.py:1182
  170.4 2.8 all-to-all-done.9
  173.2 11.8 %all_to_all.89.top_ref.one_ref = f32[32,2,768]{2,1,0:T(2,128)S(1)} all-to-all(f32[32,2,768]{2,1,0:T(2,128)S(1)} %get-tuple-element.160), channel_id=1, replica_groups=mesh['dp'=4,'z'=4,'core'=2] {'dp','z','core'}, dimensions={0} | all-to-all | bytes 393216 | tf_op jit(solution)/shard_map/all_to_all | solution.py:1138
  185.9 3.7 %all-to-all-start.11 = ((f32[16,9,8,128]{3,2,1,0:T(8,128)}), f32[16,9,8,128]{3,2,1,0:T(8,128)S(1)}, u32[]{:S(2)}, u32[]{:S(2)}) async-start(f32[16,9,8,128]{3,2,1,0:T(8,128)} %broadcast_in_dim.12), calls=%async_computation.11 | async-start | bytes 1179648 | tf_op jit(solution)/shard_map/all_to_all | solution.py:1165
  189.7 17.9 %shard_map.323 = (f32[2048,128]{1,0:T(8,128)}, f32[8,128]{1,0:T(8,128)S(1)}, f32[256,8,640]{2,1,0:T(8,128)}, f32[32,2,640]{2,1,0:T(2,128)}, f32[384,8,128]{2,1,0:T(8,128)}) custom-call(s32[2]{0:T(128)S(1)} %copy-done.5, f32[32,2,768]{2,1,0:T(2,128)S(1)} %all_to_all.89.top_ref.one_ref, f32[8,640]{1,0:T(8,128)S(1)} %get-tuple-element.135.stat_ref.stat1_ref.stat11_ref, ...), custom_call_target="tpu_custom_call" | custom-call | flops 1000000000 | bytes 1000000 | tf_op jit(solution)/shard_map/pallas_call | solution.py:1182
  207.6 2.1 dynamic-slice_bitcast_fusion
  210.3 5.7 %all-to-all-start.12 = ((f32[32,2,640]{2,1,0:T(2,128)}), f32[32,2,640]{2,1,0:T(2,128)S(1)}, u32[]{:S(2)}, u32[]{:S(2)}) async-start(f32[32,2,640]{2,1,0:T(2,128)} %get-tuple-element.171), calls=%async_computation.12 | async-start | bytes 327680 | tf_op jit(solution)/shard_map/all_to_all | solution.py:1138
  216.0 2.1 bitcast_add_fusion
  218.2 6.3 %all-to-all-done.12.grads_ref = f32[32,2,640]{2,1,0:T(2,128)S(1)} async-done(((f32[32,2,640]{2,1,0:T(2,128)}), f32[32,2,640]{2,1,0:T(2,128)S(1)}, u32[]{:S(2)}, u32[]{:S(2)}) %all-to-all-start.12) | async-done | bytes 163872 | tf_op jit(solution)/shard_map/all_to_all | solution.py:1138
  224.5 3.6 %all-to-all-start.13 = ((f32[16,12,8,128]{3,2,1,0:T(8,128)}), f32[16,12,8,128]{3,2,1,0:T(8,128)S(1)}, u32[]{:S(2)}, u32[]{:S(2)}) async-start(f32[16,12,8,128]{3,2,1,0:T(8,128)} %bitcast.12), calls=%async_computation.13 | async-start | bytes 1572864 | tf_op jit(solution)/shard_map/all_to_all | solution.py:1160
  228.1 25.6 %shard_map.324 = (f32[2048,128]{1,0:T(8,128)}, f32[32,2,640]{2,1,0:T(2,128)}, f32[128,8,128]{2,1,0:T(8,128)S(1)}, f32[8,640]{1,0:T(8,128)S(1)}) custom-call(s32[2]{0:T(128)S(1)} %copy-done.5, f32[32,2,640]{2,1,0:T(2,128)S(1)} %all-to-all-done.12.grads_ref, f32[8,640]{1,0:T(8,128)S(1)} %get-tuple-element.150.stat_ref.stat2_ref.stat02_ref, ...), custom_call_target="tpu_custom_call" | custom-call | flops 1000000000 | bytes 1000000 | tf_op jit(solution)/shard_map/pallas_call | solution.py:1182
  254.9 7.4 %all-to-all-start.14 = ((f32[32,2,640]{2,1,0:T(2,128)}), f32[32,2,640]{2,1,0:T(2,128)S(1)}, u32[]{:S(2)}, u32[]{:S(2)}) async-start(f32[32,2,640]{2,1,0:T(2,128)} %get-tuple-element.183), calls=%async_computation.14 | async-start | bytes 327680 | tf_op jit(solution)/shard_map/all_to_all | solution.py:1138
  262.4 1.7 bitcast_add_fusion.2
  264.1 6.7 %all-to-all-done.14.zero_ref = f32[32,2,640]{2,1,0:T(2,128)S(1)} async-done(((f32[32,2,640]{2,1,0:T(2,128)}), f32[32,2,640]{2,1,0:T(2,128)S(1)}, u32[]{:S(2)}, u32[]{:S(2)}) %all-to-all-start.14) | async-done | bytes 163872 | tf_op jit(solution)/shard_map/all_to_all | solution.py:1138
  270.9 1.1 pad_maximum_fusion
  272.0 4.7 %all-to-all-start.15 = ((f32[16,16,8,128]{3,2,1,0:T(8,128)}), f32[16,16,8,128]{3,2,1,0:T(8,128)}, u32[]{:S(2)}, u32[]{:S(2)}) async-start(f32[16,16,8,128]{3,2,1,0:T(8,128)} %pad_maximum_fusion), calls=%async_computation.15 | async-start | bytes 2097152 | tf_op jit(solution)/shard_map/all_to_all | solution.py:1454
  277.4 6.8 %shard_map.325 = (f32[112,2048]{1,0:T(8,128)}, f32[2,112,640]{2,1,0:T(8,128)S(1)}, f32[16,640]{1,0:T(8,128)S(1)}, f32[4,640]{1,0:T(4,128)}, f32[4,640]{1,0:T(4,1...) custom-call(s32[2]{0:T(128)S(1)} %copy-done.5, ...), custom_call_target="tpu_custom_call" | custom-call | flops 1000000000 | bytes 1000000 | tf_op jit(solution)/shard_map/pallas_call | solution.py:1182
  284.2 20.8 %all-to-all-done.15.pack0_ref = f32[16,16,8,128]{3,2,1,0:T(8,128)} async-done(((f32[16,16,8,128]{3,2,1,0:T(8,128)}), f32[16,16,8,128]{3,2,1,0:T(8,128)}, u32[]{:S(2)}, u32[]{:S(2)}) %all-to-all-start.15) | async-done | bytes 1048608 | tf_op jit(solution)/shard_map/all_to_all | solution.py:1454
  305.0 1.0 slice_reduce_fusion
  306.7 3.5 %all-to-all-start.16 = ((f32[16,4,8,128]{3,2,1,0:T(8,128)}), f32[16,4,8,128]{3,2,1,0:T(8,128)S(1)}, u32[]{:S(2)}, u32[]{:S(2)}) async-start(f32[16,4,8,128]{3,2,1,0:T(8,128)} %broadcast_in_dim.14), calls=%async_computation.16 | async-start | bytes 524288 | tf_op jit(solution)/shard_map/all_to_all | solution.py:1165
  310.2 3.3 %shard_map.326 = (f32[2,112,640]{2,1,0:T(8,128)}, f32[2,45,640]{2,1,0:T(8,128)S(1)}, f32[2,160,640]{2,1,0:T(8,128)}, f32[2,160,640]{2,1,0:T(8,128)}, f32[2,112,6...) custom-call(s32[1]{0:T(128)} %bitcast.16.core_ref, f32[16,16,8,128]{3,2,1,0:T(8,128)} %all-to-all-done.15.pack0_ref, ...), custom_call_target="tpu_custom_call" | custom-call | flops 1000000000 | bytes 1000000 | tf_op jit(solution)/shard_map/pallas_call | solution.py:1182
  313.6 8.2 %all-to-all-done.16 = f32[16,4,8,128]{3,2,1,0:T(8,128)S(1)} async-done(((f32[16,4,8,128]{3,2,1,0:T(8,128)}), f32[16,4,8,128]{3,2,1,0:T(8,128)S(1)}, u32[]{:S(2)}, u32[]{:S(2)}) %all-to-all-start.16) | async-done | bytes 262176 | tf_op jit(solution)/shard_map/all_to_all | solution.py:1165
  321.7 1.5 collective-permute-done.5.late_other_ref
  (67 shorter events, 6.7 us)
Async XLA Ops:
  0.7 10.9 %copy-start.17 = (f32[2,45,640]{2,0,1:T(2,128)S(1)}, f32[2,45,640]{2,0,1:T(2,128)}, u32[]{:S(2)}) copy-start(f32[2,45,640]{2,0,1:T(2,128)} %param.27) | copy-start | bytes 691204
  0.7 11.0 %copy-start.5 = (s32[2]{0:T(128)S(1)}, s32[2]{0:T(128)}, u32[]{:S(2)}) copy-start(s32[2]{0:T(128)} %counts_ref.23) | copy-start | bytes 28
  0.7 11.0 %copy-start.13 = (f32[112,512]{1,0:T(8,128)S(1)}, f32[112,512]{1,0:T(8,128)}, u32[]{:S(2)}) copy-start(f32[112,512]{1,0:T(8,128)} %cot_ref.1) | copy-start | bytes 688132
  4.3 16.1 %all-to-all-start = ((f32[32,2,768]{2,1,0:T(2,128)}), f32[32,2,768]{2,1,0:T(2,128)S(1)}, u32[]{:S(2)}, u32[]{:S(2)}) async-start(f32[32,2,768]{2,1,0:T(2,128)} %get-tuple-element.117), calls=%async_computation | async-start | bytes 393216 | tf_op jit(solution)/shard_map/all_to_all | solution.py:1138
  11.6 1.2 copy-start.12
  12.8 7.5 %copy-start.1 = (f32[2,640,112]{1,2,0:T(8,128)S(1)}, f32[2,640,112]{1,2,0:T(8,128)}, u32[]{:S(2)}) copy-start(f32[2,640,112]{1,2,0:T(8,128)} %param.22) | copy-start | bytes 1720324
  12.8 7.5 %copy-start.3 = (f32[4,640]{1,0:T(4,128)S(1)}, f32[4,640]{1,0:T(4,128)}, u32[]{:S(2)}) copy-start(f32[4,640]{1,0:T(4,128)} %gain_ref.17) | copy-start | bytes 30724
  12.8 7.5 %copy-start.4 = (f32[4,640]{1,0:T(4,128)S(1)}, f32[4,640]{1,0:T(4,128)}, u32[]{:S(2)}) copy-start(f32[4,640]{1,0:T(4,128)} %bias_ref.15) | copy-start | bytes 30724
  20.3 28.7 %copy-start = (f32[2,160,640]{2,1,0:T(8,128)S(1)}, f32[2,160,640]{2,1,0:T(8,128)}, u32[]{:S(2)}) copy-start(f32[2,160,640]{2,1,0:T(8,128)} %down_ref.7) | copy-start | bytes 2457604
  20.4 28.7 %copy-start.2 = (f32[2,112,640]{2,1,0:T(8,128)S(1)}, f32[2,112,640]{2,1,0:T(8,128)}, u32[]{:S(2)}) copy-start(f32[2,112,640]{2,1,0:T(8,128)} %proj_ref.7) | copy-start | bytes 1720324
  20.4 28.7 %copy-start.6 = (f32[2,640]{1,0:T(2,128)S(1)}, f32[2,640]{1,0:T(2,128)}, u32[]{:S(2)}) copy-start(f32[2,640]{1,0:T(2,128)} %upb_ref.3) | copy-start | bytes 15364
  20.4 28.7 %copy-start.9 = (f32[2,160]{1,0:T(2,128)S(1)}, f32[2,160]{1,0:T(2,128)}, u32[]{:S(2)}) copy-start(f32[2,160]{1,0:T(2,128)} %downb_ref.3) | copy-start | bytes 3844
  49.1 11.9 %copy-start.18 = (f32[2,112]{1,0:T(2,128)S(1)}, f32[2,112]{1,0:T(2,128)}, u32[]{:S(2)}) copy-start(f32[2,112]{1,0:T(2,128)} %param.25) | copy-start | bytes 2692
  49.1 11.9 %copy-start.19 = (f32[2,112]{1,0:T(2,128)S(1)}, f32[2,112]{1,0:T(2,128)}, u32[]{:S(2)}) copy-start(f32[2,112]{1,0:T(2,128)} %param.26) | copy-start | bytes 2692
  49.1 19.1 %copy-start.14 = (f32[136,128]{1,0:T(8,128)S(1)}, f32[136,128]{1,0:T(8,128)}, u32[]{:S(2)}) copy-start(f32[136,128]{1,0:T(8,128)} %get-tuple-element.124.gram0_ref) | copy-start | bytes 208900
  58.4 9.8 %all-to-all-start.2 = ((f32[32,2,128]{2,1,0:T(2,128)}), f32[32,2,128]{2,1,0:T(2,128)S(1)}, u32[]{:S(2)}, u32[]{:S(2)}) async-start(f32[32,2,128]{2,1,0:T(2,128)} %get-tuple-element.123), calls=%async_computation.2 | async-start | bytes 65536 | tf_op jit(solution)/shard_map/all_to_all | solution.py:1138
  83.2 13.0 %all-to-all-start.4 = ((f32[32,2,8,128]{3,2,1,0:T(8,128)}), f32[32,2,8,128]{3,2,1,0:T(8,128)S(1)}, u32[]{:S(2)}, u32[]{:S(2)}) async-start(f32[32,2,8,128]{3,2,1,0:T(8,128)} %bitcast.2), calls=%async_computation.4 | async-start | bytes 524288 | tf_op jit(solution)/shard_map/all_to_all | solution.py:1160
  124.9 13.0 %all-to-all-start.7 = ((f32[32,2,8,128]{3,2,1,0:T(8,128)}), f32[32,2,8,128]{3,2,1,0:T(8,128)S(1)}, u32[]{:S(2)}, u32[]{:S(2)}) async-start(f32[32,2,8,128]{3,2,1,0:T(8,128)} %broadcast_in_dim.10), calls=%async_computation.7 | async-start | bytes 524288 | tf_op jit(solution)/shard_map/all_to_all | solution.py:1165
  135.3 7.3 %copy-start.15 = (f32[288,8,128]{2,1,0:T(8,128)S(1)}, f32[288,8,128]{2,1,0:T(8,128)}, u32[]{:S(2)}) copy-start(f32[288,8,128]{2,1,0:T(8,128)} %get-tuple-element.152) | copy-start | bytes 3538948
  139.0 3.6 %collective-permute-start = (f32[144,8,128]{2,1,0:T(8,128)S(1)}, f32[144,8,128]{2,1,0:T(8,128)}, u32[]{:S(2)}, u32[]{:S(2)}) collective-permute-start(f32[144,8,128]{2,1,0:T(8,128)S(1)} %dynamic-slice_bitcast_fusion.1), channel_id=1, source_target_pairs={{0,1},{1,0},{2,3},{3,2},{4,5},{5,4},{6,7},{7,6},{8,9},{9,8},{10,11... | collective-permute-start | bytes 1769480 | tf_op jit(solution)/shard_map/ppermute | solution.py:1146
  139.4 11.7 %all-to-all-start.8 = ((f32[32,2,640]{2,1,0:T(2,128)}), f32[32,2,640]{2,1,0:T(2,128)S(1)}, u32[]{:S(2)}, u32[]{:S(2)}) async-start(f32[32,2,640]{2,1,0:T(2,128)} %get-tuple-element.151), calls=%async_computation.8 | async-start | bytes 327680 | tf_op jit(solution)/shard_map/all_to_all | solution.py:1138
  151.1 22.1 %all-to-all-start.9 = ((f32[16,9,8,128]{3,2,1,0:T(8,128)}), f32[16,9,8,128]{3,2,1,0:T(8,128)S(1)}, u32[]{:S(2)}, u32[]{:S(2)}) async-start(f32[16,9,8,128]{3,2,1,0:T(8,128)} %bitcast.7), calls=%async_computation.9 | async-start | bytes 1179648 | tf_op jit(solution)/shard_map/all_to_all | solution.py:1160
  185.9 24.3 %all-to-all-start.11 = ((f32[16,9,8,128]{3,2,1,0:T(8,128)}), f32[16,9,8,128]{3,2,1,0:T(8,128)S(1)}, u32[]{:S(2)}, u32[]{:S(2)}) async-start(f32[16,9,8,128]{3,2,1,0:T(8,128)} %broadcast_in_dim.12), calls=%async_computation.11 | async-start | bytes 1179648 | tf_op jit(solution)/shard_map/all_to_all | solution.py:1165
  209.6 6.4 %collective-permute-start.1 = (f32[192,8,128]{2,1,0:T(8,128)}, f32[192,8,128]{2,1,0:T(8,128)S(1)}, u32[]{:S(2)}, u32[]{:S(2)}) collective-permute-start(f32[192,8,128]{2,1,0:T(8,128)} %dynamic-slice_bitcast_fusion), channel_id=1, source_target_pairs={{0,1},{1,0},{2,3},{3,2},{4,5},{5,4},{6,7},{7,6},{8,9},{9,8},{10,11... | collective-permute-start | bytes 2359304 | tf_op jit(solution)/shard_map/ppermute | solution.py:1146
  210.3 14.2 %collective-permute-start.2 = (f32[144,8,128]{2,1,0:T(8,128)S(1)}, f32[144,8,128]{2,1,0:T(8,128)}, u32[]{:S(2)}, u32[]{:S(2)}) collective-permute-start(f32[144,8,128]{2,1,0:T(8,128)S(1)} %bitcast.37), channel_id=1, source_target_pairs={{0,1},{1,0},{2,3},{3,2},{4,5},{5,4},{6,7},{7,6},{8,9},{9,8},{10,11... | collective-permute-start | bytes 1769480 | tf_op jit(solution)/shard_map/ppermute | solution.py:1146
  210.3 14.2 %all-to-all-start.12 = ((f32[32,2,640]{2,1,0:T(2,128)}), f32[32,2,640]{2,1,0:T(2,128)S(1)}, u32[]{:S(2)}, u32[]{:S(2)}) async-start(f32[32,2,640]{2,1,0:T(2,128)} %get-tuple-element.171), calls=%async_computation.12 | async-start | bytes 327680 | tf_op jit(solution)/shard_map/all_to_all | solution.py:1138
  224.5 30.5 %all-to-all-start.13 = ((f32[16,12,8,128]{3,2,1,0:T(8,128)}), f32[16,12,8,128]{3,2,1,0:T(8,128)S(1)}, u32[]{:S(2)}, u32[]{:S(2)}) async-start(f32[16,12,8,128]{3,2,1,0:T(8,128)} %bitcast.12), calls=%async_computation.13 | async-start | bytes 1572864 | tf_op jit(solution)/shard_map/all_to_all | solution.py:1160
  254.4 8.0 %collective-permute-start.3 = (f32[64,8,128]{2,1,0:T(8,128)}, f32[64,8,128]{2,1,0:T(8,128)}, u32[]{:S(2)}, u32[]{:S(2)}) collective-permute-start(f32[64,8,128]{2,1,0:T(8,128)} %dynamic-slice_bitcast_fusion.2), channel_id=1, source_target_pairs={{0,1},{1,0},{2,3},{3,2},{4,5},{5,4},{6,7},{7,6},{8,9},{9,8},{10,11... | collective-permute-start | bytes 786440 | tf_op jit(solution)/shard_map/ppermute | solution.py:1146
  254.9 15.9 %all-to-all-start.14 = ((f32[32,2,640]{2,1,0:T(2,128)}), f32[32,2,640]{2,1,0:T(2,128)S(1)}, u32[]{:S(2)}, u32[]{:S(2)}) async-start(f32[32,2,640]{2,1,0:T(2,128)} %get-tuple-element.183), calls=%async_computation.14 | async-start | bytes 327680 | tf_op jit(solution)/shard_map/all_to_all | solution.py:1138
  264.1 6.8 %copy-start.16 = (f32[64,8,128]{2,1,0:T(8,128)S(1)}, f32[64,8,128]{2,1,0:T(8,128)}, u32[]{:S(2)}) copy-start(f32[64,8,128]{2,1,0:T(8,128)} %bitcast_add_fusion.2) | copy-start | bytes 786436
  272.0 5.4 %copy-start.7 = (f32[4,640]{1,0:T(4,128)S(1)}, f32[4,640]{1,0:T(4,128)}, u32[]{:S(2)}) copy-start(f32[4,640]{1,0:T(4,128)} %means_ref.1) | copy-start | bytes 30724
  272.0 5.4 %copy-start.8 = (f32[4,640]{1,0:T(4,128)S(1)}, f32[4,640]{1,0:T(4,128)}, u32[]{:S(2)}) copy-start(f32[4,640]{1,0:T(4,128)} %vars_ref.1) | copy-start | bytes 30724
  272.0 5.4 %copy-start.10 = (f32[2,112]{1,0:T(2,128)S(1)}, f32[2,112]{1,0:T(2,128)}, u32[]{:S(2)}) copy-start(f32[2,112]{1,0:T(2,128)} %nmeans_ref.1) | copy-start | bytes 2692
  272.0 5.4 %copy-start.11 = (f32[2,112]{1,0:T(2,128)S(1)}, f32[2,112]{1,0:T(2,128)}, u32[]{:S(2)}) copy-start(f32[2,112]{1,0:T(2,128)} %nvars_ref.1) | copy-start | bytes 2692
  272.0 33.0 %all-to-all-start.15 = ((f32[16,16,8,128]{3,2,1,0:T(8,128)}), f32[16,16,8,128]{3,2,1,0:T(8,128)}, u32[]{:S(2)}, u32[]{:S(2)}) async-start(f32[16,16,8,128]{3,2,1,0:T(8,128)} %pad_maximum_fusion), calls=%async_computation.15 | async-start | bytes 2097152 | tf_op jit(solution)/shard_map/all_to_all | solution.py:1454
  305.0 5.3 %collective-permute-start.4 = (f32[16,16,8,128]{3,2,1,0:T(8,128)}, f32[16,16,8,128]{3,2,1,0:T(8,128)}, u32[]{:S(2)}, u32[]{:S(2)}) collective-permute-start(f32[16,16,8,128]{3,2,1,0:T(8,128)} %all-to-all-done.15.pack0_ref), channel_id=1, source_target_pairs={{0,1},{1,0},{2,3},{3,2},{4,5},{5,4},{6,7},{7,6},{8,9},{9,8},{10,11... | collective-permute-start | bytes 3145736 | tf_op jit(solution)/shard_map/ppermute | solution.py:1146
  306.7 15.0 %all-to-all-start.16 = ((f32[16,4,8,128]{3,2,1,0:T(8,128)}), f32[16,4,8,128]{3,2,1,0:T(8,128)S(1)}, u32[]{:S(2)}, u32[]{:S(2)}) async-start(f32[16,4,8,128]{3,2,1,0:T(8,128)} %broadcast_in_dim.14), calls=%async_computation.16 | async-start | bytes 524288 | tf_op jit(solution)/shard_map/all_to_all | solution.py:1165
  321.7 1.5 collective-permute-start.5

commit v6 on v5

--- a/solution.py
+++ b/solution.py
@@ -496,7 +496,7 @@
         return carry
 
     if block:
-        lax.fori_loop(0, tiles, activate, 0)
+        lax.fori_loop(0, tiles, activate, 0, unroll=tiles)
     else:
         activate(step, 0)
 
@@ -529,7 +529,7 @@
         pre_ref[...] = pre
         gates_ref[...] = sigmoid(skinny_dot(pre * sigmoid(pre), up_ref[0]) + upb_ref[block : block + 1, :])
         z_ref[...] = jnp.zeros_like(z_ref)
-        lax.fori_loop(0, tiles, project, 0)
+        lax.fori_loop(0, tiles, project, 0, unroll=tiles if block else 1)
 
         def chunk(index, carry):
             at = pl.ds(pl.multiple_of(index * 256, 256), 256)
@@ -546,13 +546,37 @@
         send_all(send_ref, rows, slice(0, LANES))
 
 
+def put_lists(core_ref, refs, writes):
+    size = refs[0].shape[0]
+
+    for core in range(2):
+        @pl.when(core_ref[0] == core)
+        def write(core=core):
+            for at, values in writes:
+                for half in range(2):
+                    begin = max(at, half * size)
+                    end = min(at + values.shape[0], (half + 1) * size)
+                    if begin < end:
+                        refs[half ^ core][begin - half * size : end - half * size] = values[begin - at : end - at]
+
+
+def put_tile_list(core_ref, refs, at, values):
+    size = refs[0].shape[0]
+    half = jnp.where(at >= size, 1, 0)
+    place = pl.ds(at - half * size, values.shape[0])
+    for other in range(2):
+        @pl.when((core_ref[0] == half) == (other == 0))
+        def write(other=other):
+            refs[other][place] = values
+
+
 def pack_tiles(narrow, squeeze):
     return narrow // 8 + 2 * (squeeze // 8) + 1
 
 
 def squeeze_backward_body(
     block, counts_ref, stat_ref, d_ref, gain_ref, bias_ref, down_ref, up_ref, proj_ref, gates_ref, running_ref,
-    pre_ref, dy2_ref, send_ref, pack_ref, dz3_ref, dz3t_ref, total_ref, dexc_ref, dgate_ref, head,
+    pre_ref, dy2_ref, send_ref, core_ref, list_refs, dz3_ref, dz3t_ref, total_ref, dexc_ref, dgate_ref, head,
 ):
     total = live_frames(counts_ref)
     per_frame = HALF_ROWS if block else FULL_ROWS
@@ -599,7 +623,7 @@
         total_ref[...] = jnp.zeros_like(total_ref)
         each_frame(chunks, chunk, 0)
         dproj = fold_square(total_ref[...])
-        pack_ref[pl.ds(tile * per_tile, narrow // 8)] = dproj[0:narrow].reshape(narrow // 8, 8, LANES)
+        put_tile_list(core_ref, list_refs, tile * per_tile, dproj[0:narrow].reshape(narrow // 8, 8, LANES))
         return carry
 
     def squeeze_part():
@@ -616,13 +640,15 @@
         dpre_row = jnp.sum(dpre, axis=0, keepdims=True)
         dpre_row = jnp.concatenate([dpre_row, jnp.zeros((1, du.shape[1] - squeeze), F32)], axis=1)
         biases = rows8(jnp.sum(du, axis=0, keepdims=True), dpre_row)
+        writes = []
         for index in range(tiles):
             own = slice(index * LANES, (index + 1) * LANES)
             at = index * per_tile + narrow // 8
-            pack_ref[at : at + squeeze // 8] = ddown[:, own].reshape(squeeze // 8, 8, LANES)
+            writes.append((at, ddown[:, own].reshape(squeeze // 8, 8, LANES)))
             at = at + squeeze // 8
-            pack_ref[at : at + squeeze // 8] = dup[:, own].reshape(squeeze // 8, 8, LANES)
-            pack_ref[at + squeeze // 8] = biases[:, own]
+            writes.append((at, dup[:, own].reshape(squeeze // 8, 8, LANES)))
+            writes.append((at + squeeze // 8, biases[:, own].reshape(1, 8, LANES)))
+        put_lists(core_ref, list_refs, writes)
         drunning = skinny_dot(dpre, down_ref[0])
         dpooled = exact_dot(running_matrix(counts_ref, frames), drunning, TN) * (1.0 / pixels)
         for index in range(tiles):
@@ -655,9 +681,9 @@
 
     if block:
         head()
-        lax.fori_loop(0, tiles, excite, 0)
+        lax.fori_loop(0, tiles, excite, 0, unroll=tiles)
         squeeze_part()
-        lax.fori_loop(0, tiles, slope, 0)
+        lax.fori_loop(0, tiles, slope, 0, unroll=tiles)
     else:
         phase = pl.program_id(0)
         tile = pl.program_id(1)
@@ -680,8 +706,8 @@
 
 
 def squeeze_one_backward_kernel(
-    counts_ref, third_ref, z_ref, cot_ref, ngain_ref, nbias_ref, stat_ref, d_ref, gain_ref, bias_ref, down_ref,
-    up_ref, proj_ref, gates_ref, running_ref, pre_ref, act_ref, nsum_ref, dy2_ref, send_ref, pack_ref,
+    counts_ref, core_ref, third_ref, z_ref, cot_ref, ngain_ref, nbias_ref, stat_ref, d_ref, gain_ref, bias_ref, down_ref,
+    up_ref, proj_ref, gates_ref, running_ref, pre_ref, act_ref, nsum_ref, dy2_ref, send_ref, mine_ref, theirs_ref,
     dz3_ref, dz3t_ref, total_ref, dexc_ref, dgate_ref,
 ):
     total = live_frames(counts_ref)
@@ -708,7 +734,7 @@
 
     squeeze_backward_body(
         1, counts_ref, stat_ref, d_ref, gain_ref, bias_ref, down_ref, up_ref, proj_ref, gates_ref, running_ref,
-        pre_ref, dy2_ref, send_ref, pack_ref, dz3_ref, dz3t_ref, total_ref, dexc_ref, dgate_ref, head,
+        pre_ref, dy2_ref, send_ref, core_ref, (mine_ref, theirs_ref), dz3_ref, dz3t_ref, total_ref, dexc_ref, dgate_ref, head,
     )
 
 
@@ -725,16 +751,16 @@
 
 
 def squeeze_zero_backward_kernel(
-    counts_ref, top_ref, stat1_ref, gram_ref, nstat_ref, dxpre_ref, x1_ref, z_ref, ngain_ref, w_ref, gains_ref, q_one_ref,
+    counts_ref, core_ref, top_ref, stat1_ref, gram_ref, nstat_ref, dxpre_ref, x1_ref, z_ref, ngain_ref, w_ref, gains_ref, q_one_ref,
     stat_ref, d_ref, gain_ref, bias_ref, down_ref, up_ref, proj_ref, gates_ref, running_ref, pre_ref,
-    dx1_ref, nsum_ref, dy2_ref, send_ref, pack_ref, dz3_ref, dz3t_ref, total_ref, dexc_ref, dgate_ref,
+    dx1_ref, nsum_ref, dy2_ref, send_ref, mine_ref, theirs_ref, dz3_ref, dz3t_ref, total_ref, dexc_ref, dgate_ref,
 ):
     total = live_frames(counts_ref)
     width = gains_ref.shape[1]
 
     def head():
         start = pack_tiles(proj_ref.shape[1], down_ref.shape[1]) * (width // LANES)
-        pack_ref[start : start + q_one_ref.shape[0]] = q_one_ref[...]
+        put_lists(core_ref, (mine_ref, theirs_ref), [(start, q_one_ref)])
         count = stat_ref[2:3, :]
         wide_count = jnp.broadcast_to(count[:, 0:1], (1, width))
         sums = row_total(top_ref, slice(0, width))
@@ -768,7 +794,7 @@
 
     squeeze_backward_body(
         0, counts_ref, stat_ref, d_ref, gain_ref, bias_ref, down_ref, up_ref, proj_ref, gates_ref, running_ref,
-        pre_ref, dy2_ref, send_ref, pack_ref, dz3_ref, dz3t_ref, total_ref, dexc_ref, dgate_ref, head,
+        pre_ref, dy2_ref, send_ref, core_ref, (mine_ref, theirs_ref), dz3_ref, dz3t_ref, total_ref, dexc_ref, dgate_ref, head,
     )
 
 def back_full(t, k, a_ref, w_ref, z_ref, raw_ref, f_ref, dw_ref, fresh):
@@ -1222,6 +1248,7 @@
     full_rows = frames * FULL_ROWS
     half_rows = frames * HALF_ROWS
     low = jnp.bfloat16
+    core = lax.axis_index("core").astype(jnp.int32).reshape(1)
 
     def round_up(count):
         return -(-count // devices) * devices
@@ -1360,23 +1387,23 @@
             ins[6] = early(weight_at(block, cin))
         packed = round_up(tiles * (pack_tiles(cin, squeeze) + (0 if block else q_tiles)))
         wide_outs = [fixed(rows, 8, width), fixed(devices, 2, width)] if block else [late(cube_at(rows)), late(sums_at(2))]
-        outs = [fixed(8, LANES)] + wide_outs + [fixed(packed, 8, LANES)]
-        shapes = [shape(8, LANES), shape(rows, 8, width), shape(devices, 2, width), shape(packed, 8, LANES)]
+        outs = [fixed(8, LANES)] + wide_outs + [fixed(packed // 2, 8, LANES)] * 2
+        shapes = [shape(8, LANES), shape(rows, 8, width), shape(devices, 2, width)] + [shape(packed // 2, 8, LANES)] * 2
         scratch = [pltpu.VMEM((rows * 8, 2 * LANES), low), pltpu.VMEM((2 * LANES, rows * 8), low),
                    pltpu.VMEM((2 * LANES, 2 * LANES), F32), pltpu.VMEM((tiles, rows, 8, LANES), F32),
                    pltpu.VMEM((tiles, frames, LANES), F32)]
         return (ins, outs, shapes, scratch)
 
     ins, outs, shapes, scratch = backward_specs(1)
-    activations, nsum_one, dy2_one, sums, pack_one = call(
+    activations, nsum_one, dy2_one, sums, pack_one, theirs = call(
         squeeze_one_backward_kernel, (1,),
-        [SCALARS, whole(third), whole(z_one), whole(cot), whole(ngains), whole(nbiases)] + ins,
+        [SCALARS, SCALARS, whole(third), whole(z_one), whole(cot), whole(ngains), whole(nbiases)] + ins,
         [fixed(cin, half_pixels)] + outs, [shape(cin, half_pixels)] + shapes, scratch,
-        (frame_counts, third, z_one, cot, ngains, nbiases, stat12, d_one, wide_gains, wide_biases, squeeze_weight, up_t,
+        (frame_counts, core, third, z_one, cot, ngains, nbiases, stat12, d_one, wide_gains, wide_biases, squeeze_weight, up_t,
          project_weight, gates_one, running_one, pre_one),
     )
-    sums, pack_one, gram = together(sums, pack_one, gram)
-    sums, pack_one = together(exchange(sums), add_cores(pack_one))
+    sums, theirs, gram = together(sums, theirs, gram)
+    sums, pack_one = together(exchange(sums), pack_one + swap_cores(theirs))
     pack_one = share_out(pack_one)
     nothing = jnp.zeros((8, LANES), F32)
 
@@ -1430,17 +1457,19 @@
     top_one, pack_one = together(exchange(sums), pack_one)
     pack_one = share_back(pack_one)
     ins, outs, shapes, scratch = backward_specs(0)
-    dx1, nsum_zero, dy2_zero, sums, pack_zero = call(
+    dx1, nsum_zero, dy2_zero, sums, pack_zero, theirs = call(
         squeeze_zero_backward_kernel, (2, tiles),
-        [SCALARS, whole(top_one), whole(stat11), whole(gram), whole(nstat), whole(dxpre_one), whole(x1), whole(z_zero),
+        [SCALARS, SCALARS, whole(top_one), whole(stat11), whole(gram), whole(nstat), whole(dxpre_one), whole(x1), whole(z_zero),
          whole(ngains), of_block(1, cin, width), whole(wide_gains), whole(q_one)] + ins,
         [fixed(pixels, LANES)] + outs, [shape(pixels, LANES)] + shapes, scratch,
-        (frame_counts, top_one, stat11, gram, nstat, dxpre_one, x1, z_zero, ngains, w_t, wide_gains, q_one, stat02, d_zero,
+        (frame_counts, core, top_one, stat11, gram, nstat, dxpre_one, x1, z_zero, ngains, w_t, wide_gains, q_one, stat02, d_zero,
          wide_gains, wide_biases, squeeze_weight, up_t, project_weight, gates_zero, running_zero, pre_zero),
     )
     sums, pack_one = together(sums, pack_one)
     pack_one_other = swap_cores(pack_one)
-    sums, pack_zero, pack_one_other = together(exchange(sums), add_cores(pack_zero), pack_one_other)
+    sums, pack_zero, pack_one_other = together(
+        exchange(sums), pack_zero + swap_cores(theirs), pack_one_other
+    )
     pack_zero = share_out(pack_zero)
     dxpre_zero, sums, late, grad_zero = depth_backward(
         0, 0, tiles, sums, stat02, stat01, dy2_zero, d_zero, e_zero, planes_zero, x_columns, nothing, nothing, nothing
@@ -1452,7 +1481,6 @@
         [jnp.broadcast_to(own[None], pack_zero.shape), late.reshape(pack_zero.shape[0], -1, 8, LANES)], axis=1
     )
     joint = lax.all_to_all(joint, CHIPS, 0, 0, tiled=True)
-    core = lax.axis_index("core").astype(jnp.int32).reshape(1)
     final_args = (
         frame_counts, momentum_index, gram, stat01, stat02, stat11, stat12, grad_zero, grad_one, top_one,
         top_zero, nsum_zero, nsum_one, dxpre_zero, x, dx1, w_t, wide_gains, wide_means, wide_variances, narrow_means,

time: 325 us -> 324 us (level)
  Pallas kernels: 130 us -> 123 us
    pallas_call x14, Pallas kernels: 130 us -> 123 us  [call(): pl.pallas_call(kernel, grid=grid, in_specs=in_specs, out_specs=out_specs,...]
    add x3 -> x1, other arithmetic: 5.79 us -> 1.69 us  [add_cores(): mine + swap_cores(lax.dynamic_index_in_dim(pair, 1 - core, 0, keepdims=Fa...]
  transfers between devices with their start and end apart: 18 -> 18, of which waited for: 11 -> 11; matrix products, arithmetic and copies ran while one was open for 3% -> 3% of each run, Pallas kernels for 28% -> 27%
where the time goes in v6:
time: 324 us; the launch traced here: 322 us
  Pallas kernels  123 us (38%)
  waiting for transfers between devices  67.2 us (21%)
  blocking collectives  59.6 us (18%)
  starting transfers between devices  54.8 us (17%)
  other arithmetic  7.82 us (2%)
  local copies, waits for them, and re-layouts  7.75 us (2%)
    pallas_call x14, Pallas kernels, call(): pl.pallas_call(kernel, grid=grid, in_specs=in_specs, out_specs=out_specs,...  123 us
    all_to_all x5, blocking collectives, exchange(): return lax.all_to_all(send, AXES, 0, 0, tiled=True)  59.6 us
    all_to_all x5, waiting for transfers between devices, exchange(): return lax.all_to_all(send, AXES, 0, 0, tiled=True)  29.5 us
    all_to_all x5, starting transfers between devices, exchange(): return lax.all_to_all(send, AXES, 0, 0, tiled=True)  27.7 us
    all_to_all x1, waiting for transfers between devices, local(): joint = lax.all_to_all(joint, CHIPS, 0, 0, tiled=True)  20.8 us
    all_to_all x3, waiting for transfers between devices, share_back(): lax.all_to_all(jnp.broadcast_to(own[None], pieces.shape), names, 0, 0, ti...  10.9 us
    all_to_all x3, starting transfers between devices, share_back(): lax.all_to_all(jnp.broadcast_to(own[None], pieces.shape), names, 0, 0, ti...  9.85 us
    all_to_all x3, starting transfers between devices, share_out(): lax.all_to_all(tiles.reshape(count, -1, *tiles.shape[1:]), names, 0, 0, t...  9.79 us
  transfers between devices with their start and end apart: 18, of which 11 were waited for; matrix products, arithmetic and copies ran while one was open for 3% of the time, Pallas kernels for 27%

profile of v6, /device:TPU:0, one launch (start us, length us, event | category | flops | bytes accessed | tf_op | source)
XLA Modules:
  0.0 321.9 jit_solution(16213224405246161071)
XLA Ops:
  0.7 3.7 %shard_map.314 = (f32[136,128]{1,0:T(8,128)}, f32[32,2,768]{2,1,0:T(2,128)}) custom-call(s32[2]{0:T(128)} %counts_ref.23, f32[112,2048]{1,0:T(8,128)} %video_ref.3, f32[2,112,640]{2,1,0:T(8,128)} %bitcast.17), custom_call_target="tpu_custom_call" | custom-call | flops 1000000000 | bytes 1000000 | tf_op jit(solution)/shard_map/pallas_call | solution.py:1208
  4.4 7.3 %all-to-all-start = ((f32[32,2,768]{2,1,0:T(2,128)}), f32[32,2,768]{2,1,0:T(2,128)S(1)}, u32[]{:S(2)}, u32[]{:S(2)}) async-start(f32[32,2,768]{2,1,0:T(2,128)} %get-tuple-element.119), calls=%async_computation | async-start | bytes 393216 | tf_op jit(solution)/shard_map/all_to_all | solution.py:1164
  11.7 1.0 copy.38.taps_ref
  13.3 1.2 copy-done.13
  14.5 0.9 copy-done.14
  15.4 3.4 %shard_map.315 = (f32[2048,128]{1,0:T(8,128)}, bf16[2048,256]{1,0:T(8,128)(2,1)}, bf16[256,2048]{1,0:T(8,128)(2,1)}, f32[512,128]{1,0:T(8,128)S(1)}) custom-call(s32[2]{0:T(128)S(1)} %copy-done.5, f32[112,2048]{1,0:T(8,128)S(1)} %copy-done.13, f32[112,512]{1,0:T(8,128)S(1)} %copy-done.14), custom_call_target="tpu_custom_call" | custom-call | flops 1000000000 | bytes 1000000 | tf_op jit(solution)/shard_map/pallas_call | solution.py:1208
  18.8 1.6 all-to-all-done.sums_ref.count_ref
  20.5 14.9 %shard_map.316 = (f32[256,8,640]{2,1,0:T(8,128)}, f32[256,8,640]{2,1,0:T(8,128)}, f32[8,640]{1,0:T(8,128)S(1)}, f32[32,2,640]{2,1,0:T(2,128)S(1)}, f32[8,2,4,8,8,640]{5,4,3,2,1,0:T(8,128)}) custom-call(s32[2]{0:T(128)S(1)} %copy-done.6, f32[32,2,768]{2,1,0:T(2,128)S(1)} %all-to-all-done.sums_ref.count_ref, ...), custom_call_target="tpu_custom_call" | custom-call | flops 1000000000 | bytes 1000000 | tf_op jit(solution)/shard_map/pallas_call | solution.py:1208
  35.5 14.5 %all_to_all.85.sums_ref = f32[32,2,640]{2,1,0:T(2,128)S(1)} all-to-all(f32[32,2,640]{2,1,0:T(2,128)S(1)} %get-tuple-element.121), channel_id=1, replica_groups=mesh['dp'=4,'z'=4,'core'=2] {'dp','z','core'}, dimensions={0} | all-to-all | bytes 327680 | tf_op jit(solution)/shard_map/all_to_all | solution.py:1164
  50.0 9.3 %shard_map.317 = (f32[2048,128]{1,0:T(8,128)}, f32[8,640]{1,0:T(8,128)S(1)}, f32[8,640]{1,0:T(8,128)S(1)}, f32[8,160]{1,0:T(8,128)S(1)}, f32[8,640]{1,0:T(8,128)S(1)}, /*index=5*/f32[32,2,128]{2,1,0:T(2,128)}) custom-call(s32[2]{0:T(128)S(1)} %copy-done.6, f32[32,2,640]{2,1,0:T(2,128)S(1)} %all_to_all.85.sums_ref, ...), custom_call_target="tpu_custom_call" | custom-call | flops 1000000000 | bytes 1000000 | tf_op jit(solution)/shard_map/pallas_call | solution.py:1208
  59.3 2.6 all-to-all-start.2
  61.9 7.2 %all-to-all-done.2.sums_ref = f32[32,2,128]{2,1,0:T(2,128)S(1)} async-done(((f32[32,2,128]{2,1,0:T(2,128)}), f32[32,2,128]{2,1,0:T(2,128)S(1)}, u32[]{:S(2)}, u32[]{:S(2)}) %all-to-all-start.2) | async-done | bytes 32800 | tf_op jit(solution)/shard_map/all_to_all | solution.py:1164
  69.1 4.8 %shard_map.318 = (f32[2048,128]{1,0:T(8,128)}, bf16[2048,256]{1,0:T(8,128)(2,1)}, bf16[256,2048]{1,0:T(8,128)(2,1)}, f32[64,8,128]{2,1,0:T(8,128)}, f32[8,128]{1,0:T(8,128)S(1)}, /*index=5*/f32[32,2,640]{2,1,0:T(2,128)S(1)}) custom-call(s32[2]{0:T(128)S(1)} %copy-done.6, f32[32,2,128]{2,1,0:T(2,128)S(1)} %all-to-all-done.2.sums_ref, ...), custom_call_target="tpu_custom_call" | custom-call | flops 1000000000 | bytes 1000000 | tf_op jit(solution)/shard_map/pallas_call | solution.py:1208
  73.9 10.2 %all_to_all.86.sums_ref = f32[32,2,640]{2,1,0:T(2,128)S(1)} all-to-all(f32[32,2,640]{2,1,0:T(2,128)S(1)} %get-tuple-element.129), channel_id=1, replica_groups=mesh['dp'=4,'z'=4,'core'=2] {'dp','z','core'}, dimensions={0} | all-to-all | bytes 327680 | tf_op jit(solution)/shard_map/all_to_all | solution.py:1164
  84.1 2.6 all-to-all-start.4
  86.6 10.1 %shard_map.319 = (f32[256,8,640]{2,1,0:T(8,128)}, f32[64,8,640]{2,1,0:T(8,128)}, f32[8,640]{1,0:T(8,128)S(1)}, f32[32,2,640]{2,1,0:T(2,128)S(1)}, f32[8,3,18,8,640]{4,3,2,1,0:T(8,128)}) custom-call(s32[2]{0:T(128)S(1)} %copy-done.6, f32[32,2,640]{2,1,0:T(2,128)S(1)} %all_to_all.86.sums_ref, f32[8,128]{1,0:T(8,128)S(1)} %get-tuple-element.132.count_ref.nstat_ref, ...), custom_call_target="tpu_custom_call" | custom-call | flops 1000000000 | bytes 1000000 | tf_op jit(solution)/shard_map/pallas_call | solution.py:1208
  97.0 13.8 %all_to_all.87.sums_ref = f32[32,2,640]{2,1,0:T(2,128)S(1)} all-to-all(f32[32,2,640]{2,1,0:T(2,128)S(1)} %get-tuple-element.136), channel_id=1, replica_groups=mesh['dp'=4,'z'=4,'core'=2] {'dp','z','core'}, dimensions={0} | all-to-all | bytes 327680 | tf_op jit(solution)/shard_map/all_to_all | solution.py:1164
  110.8 3.4 %shard_map.320 = (f32[512,128]{1,0:T(8,128)S(1)}, f32[8,640]{1,0:T(8,128)S(1)}, f32[8,640]{1,0:T(8,128)S(1)}, f32[8,160]{1,0:T(8,128)S(1)}, f32[8,640]{1,0:T(8,128)S(1)}, /*index=5*/f32[32,4,128]{2,1,0:T(4,128)S(1)}) custom-call(s32[2]{0:T(128)S(1)} %copy-done.6, f32[32,2,640]{2,1,0:T(2,128)S(1)} %all_to_all.87.sums_ref, ...), custom_call_target="tpu_custom_call" | custom-call | flops 1000000000 | bytes 1000000 | tf_op jit(solution)/shard_map/pallas_call | solution.py:1208
  114.2 9.5 %all_to_all.88.third_ref = f32[32,4,128]{2,1,0:T(4,128)S(1)} all-to-all(f32[32,4,128]{2,1,0:T(4,128)S(1)} %get-tuple-element.139), channel_id=1, replica_groups=mesh['dp'=4,'z'=4,'core'=2] {'dp','z','core'}, dimensions={0} | all-to-all | bytes 131072 | tf_op jit(solution)/shard_map/all_to_all | solution.py:1164
  124.5 2.6 all-to-all-start.7
  127.1 7.6 %shard_map.321 = (f32[112,512]{1,0:T(8,128)}, f32[8,128]{1,0:T(8,128)S(1)}, f32[64,8,640]{2,1,0:T(8,128)}, f32[32,2,640]{2,1,0:T(2,128)}, f32[144,8,128]{2,1,0:T(8,128)S(1)}, /*index=5*/f32[144,8,128]{2,1,0:T(8,128)}) custom-call(s32[2]{0:T(128)S(1)} %copy-done.6, s32[1]{0:T(128)} %bitcast.core_ref, f32[32,4,128]{2,1,0:T(4,128)S(1)} %all_to_all.88.third_ref, ...), custom_call_target="tpu_custom_call" | custom-call | flops 1000000000 | bytes 1000000 | tf_op jit(solution)/shard_map/pallas_call | solution.py:1208
  134.7 2.8 all-to-all-done.7
  137.8 2.9 all-to-all-start.8
  141.6 7.6 %all-to-all-done.8.grads_ref = f32[32,2,640]{2,1,0:T(2,128)S(1)} async-done(((f32[32,2,640]{2,1,0:T(2,128)}), f32[32,2,640]{2,1,0:T(2,128)S(1)}, u32[]{:S(2)}, u32[]{:S(2)}) %all-to-all-start.8) | async-done | bytes 163872 | tf_op jit(solution)/shard_map/all_to_all | solution.py:1164
  149.2 3.6 %all-to-all-start.9 = ((f32[16,9,8,128]{3,2,1,0:T(8,128)}), f32[16,9,8,128]{3,2,1,0:T(8,128)S(1)}, u32[]{:S(2)}, u32[]{:S(2)}) async-start(f32[16,9,8,128]{3,2,1,0:T(8,128)} %bitcast.5), calls=%async_computation.9 | async-start | bytes 1179648 | tf_op jit(solution)/shard_map/all_to_all | solution.py:1186
  152.8 14.4 %shard_map.322 = (f32[2048,128]{1,0:T(8,128)}, f32[32,2,768]{2,1,0:T(2,128)S(1)}, f32[100,8,128]{2,1,0:T(8,128)S(1)}, f32[8,640]{1,0:T(8,128)S(1)}) custom-call(s32[2]{0:T(128)S(1)} %copy-done.6, f32[32,2,640]{2,1,0:T(2,128)S(1)} %all-to-all-done.8.grads_ref, f32[8,640]{1,0:T(8,128)S(1)} %get-tuple-element.143.stat_ref.stat2_ref.stat12_ref, ...), custom_call_target="tpu_custom_call" | custom-call | flops 1000000000 | bytes 1000000 | tf_op jit(solution)/shard_map/pallas_call | solution.py:1208
  167.1 4.2 %all-to-all-done.9 = f32[16,9,8,128]{3,2,1,0:T(8,128)S(1)} async-done(((f32[16,9,8,128]{3,2,1,0:T(8,128)}), f32[16,9,8,128]{3,2,1,0:T(8,128)S(1)}, u32[]{:S(2)}, u32[]{:S(2)}) %all-to-all-start.9) | async-done | bytes 589856 | tf_op jit(solution)/shard_map/all_to_all | solution.py:1186
  171.3 11.6 %all_to_all.89.top_ref.one_ref = f32[32,2,768]{2,1,0:T(2,128)S(1)} all-to-all(f32[32,2,768]{2,1,0:T(2,128)S(1)} %get-tuple-element.163), channel_id=1, replica_groups=mesh['dp'=4,'z'=4,'core'=2] {'dp','z','core'}, dimensions={0} | all-to-all | bytes 393216 | tf_op jit(solution)/shard_map/all_to_all | solution.py:1164
  183.8 3.7 %all-to-all-start.11 = ((f32[16,9,8,128]{3,2,1,0:T(8,128)}), f32[16,9,8,128]{3,2,1,0:T(8,128)S(1)}, u32[]{:S(2)}, u32[]{:S(2)}) async-start(f32[16,9,8,128]{3,2,1,0:T(8,128)} %broadcast_in_dim.12), calls=%async_computation.11 | async-start | bytes 1179648 | tf_op jit(solution)/shard_map/all_to_all | solution.py:1191
  187.5 18.1 %shard_map.323 = (f32[2048,128]{1,0:T(8,128)}, f32[8,128]{1,0:T(8,128)S(1)}, f32[256,8,640]{2,1,0:T(8,128)}, f32[32,2,640]{2,1,0:T(2,128)}, f32[192,8,128]{2,1,0:T(8,128)}, /*index=5*/f32[192,8,128]{2,1,0:T(8,128)}) custom-call(s32[2]{0:T(128)S(1)} %copy-done.6, s32[1]{0:T(128)} %bitcast.core_ref, f32[32,2,768]{2,1,0:T(2,128)S(1)} %all_to_all.89.top_ref.one_ref, ...), custom_call_target="tpu_custom_call" | custom-call | flops 1000000000 | bytes 1000000 | tf_op jit(solution)/shard_map/pallas_call | solution.py:1208
  206.5 5.6 %all-to-all-start.12 = ((f32[32,2,640]{2,1,0:T(2,128)}), f32[32,2,640]{2,1,0:T(2,128)S(1)}, u32[]{:S(2)}, u32[]{:S(2)}) async-start(f32[32,2,640]{2,1,0:T(2,128)} %get-tuple-element.174), calls=%async_computation.12 | async-start | bytes 327680 | tf_op jit(solution)/shard_map/all_to_all | solution.py:1164
  212.1 2.1 add.22
  214.3 6.3 %all-to-all-done.12.grads_ref = f32[32,2,640]{2,1,0:T(2,128)S(1)} async-done(((f32[32,2,640]{2,1,0:T(2,128)}), f32[32,2,640]{2,1,0:T(2,128)S(1)}, u32[]{:S(2)}, u32[]{:S(2)}) %all-to-all-start.12) | async-done | bytes 163872 | tf_op jit(solution)/shard_map/all_to_all | solution.py:1164
  220.6 3.6 %all-to-all-start.13 = ((f32[16,12,8,128]{3,2,1,0:T(8,128)}), f32[16,12,8,128]{3,2,1,0:T(8,128)S(1)}, u32[]{:S(2)}, u32[]{:S(2)}) async-start(f32[16,12,8,128]{3,2,1,0:T(8,128)} %bitcast.37), calls=%async_computation.13 | async-start | bytes 1572864 | tf_op jit(solution)/shard_map/all_to_all | solution.py:1186
  224.2 22.6 %shard_map.324 = (f32[2048,128]{1,0:T(8,128)}, f32[32,2,640]{2,1,0:T(2,128)}, f32[128,8,128]{2,1,0:T(8,128)S(1)}, f32[8,640]{1,0:T(8,128)S(1)}) custom-call(s32[2]{0:T(128)S(1)} %copy-done.6, f32[32,2,640]{2,1,0:T(2,128)S(1)} %all-to-all-done.12.grads_ref, f32[8,640]{1,0:T(8,128)S(1)} %get-tuple-element.152.stat_ref.stat2_ref.stat02_ref, ...), custom_call_target="tpu_custom_call" | custom-call | flops 1000000000 | bytes 1000000 | tf_op jit(solution)/shard_map/pallas_call | solution.py:1208
  247.6 1.7 collective-permute-start.3
  249.3 9.3 %all-to-all-start.14 = ((f32[32,2,640]{2,1,0:T(2,128)}), f32[32,2,640]{2,1,0:T(2,128)S(1)}, u32[]{:S(2)}, u32[]{:S(2)}) async-start(f32[32,2,640]{2,1,0:T(2,128)} %get-tuple-element.187), calls=%async_computation.14 | async-start | bytes 327680 | tf_op jit(solution)/shard_map/all_to_all | solution.py:1164
  258.7 1.7 bitcast_add_fusion
  260.4 6.7 %all-to-all-done.14.zero_ref = f32[32,2,640]{2,1,0:T(2,128)S(1)} async-done(((f32[32,2,640]{2,1,0:T(2,128)}), f32[32,2,640]{2,1,0:T(2,128)S(1)}, u32[]{:S(2)}, u32[]{:S(2)}) %all-to-all-start.14) | async-done | bytes 163872 | tf_op jit(solution)/shard_map/all_to_all | solution.py:1164
  267.2 2.0 pad_maximum_fusion
  269.2 4.6 %all-to-all-start.15 = ((f32[16,16,8,128]{3,2,1,0:T(8,128)}), f32[16,16,8,128]{3,2,1,0:T(8,128)}, u32[]{:S(2)}, u32[]{:S(2)}) async-start(f32[16,16,8,128]{3,2,1,0:T(8,128)} %pad_maximum_fusion), calls=%async_computation.15 | async-start | bytes 2097152 | tf_op jit(solution)/shard_map/all_to_all | solution.py:1483
  274.5 6.8 %shard_map.325 = (f32[112,2048]{1,0:T(8,128)}, f32[2,112,640]{2,1,0:T(8,128)S(1)}, f32[16,640]{1,0:T(8,128)S(1)}, f32[4,640]{1,0:T(4,128)}, f32[4,640]{1,0:T(4,1...) custom-call(s32[2]{0:T(128)S(1)} %copy-done.6, ...), custom_call_target="tpu_custom_call" | custom-call | flops 1000000000 | bytes 1000000 | tf_op jit(solution)/shard_map/pallas_call | solution.py:1208
  281.3 20.8 %all-to-all-done.15.pack0_ref = f32[16,16,8,128]{3,2,1,0:T(8,128)} async-done(((f32[16,16,8,128]{3,2,1,0:T(8,128)}), f32[16,16,8,128]{3,2,1,0:T(8,128)}, u32[]{:S(2)}, u32[]{:S(2)}) %all-to-all-start.15) | async-done | bytes 1048608 | tf_op jit(solution)/shard_map/all_to_all | solution.py:1483
  302.1 1.0 slice_reduce_fusion
  303.8 3.5 %all-to-all-start.16 = ((f32[16,4,8,128]{3,2,1,0:T(8,128)}), f32[16,4,8,128]{3,2,1,0:T(8,128)S(1)}, u32[]{:S(2)}, u32[]{:S(2)}) async-start(f32[16,4,8,128]{3,2,1,0:T(8,128)} %broadcast_in_dim.14), calls=%async_computation.16 | async-start | bytes 524288 | tf_op jit(solution)/shard_map/all_to_all | solution.py:1191
  307.3 3.3 %shard_map.326 = (f32[2,112,640]{2,1,0:T(8,128)}, f32[2,45,640]{2,1,0:T(8,128)S(1)}, f32[2,160,640]{2,1,0:T(8,128)}, f32[2,160,640]{2,1,0:T(8,128)}, f32[2,112,6...) custom-call(s32[1]{0:T(128)} %bitcast.core_ref, f32[16,16,8,128]{3,2,1,0:T(8,128)} %all-to-all-done.15.pack0_ref, ...), custom_call_target="tpu_custom_call" | custom-call | flops 1000000000 | bytes 1000000 | tf_op jit(solution)/shard_map/pallas_call | solution.py:1208
  310.6 8.2 %all-to-all-done.16 = f32[16,4,8,128]{3,2,1,0:T(8,128)S(1)} async-done(((f32[16,4,8,128]{3,2,1,0:T(8,128)}), f32[16,4,8,128]{3,2,1,0:T(8,128)S(1)}, u32[]{:S(2)}, u32[]{:S(2)}) %all-to-all-start.16) | async-done | bytes 262176 | tf_op jit(solution)/shard_map/all_to_all | solution.py:1191
  318.8 1.5 collective-permute-done.5.late_other_ref
  (61 shorter events, 8.0 us)
Async XLA Ops:
  0.7 19.8 %copy-start.1 = (f32[2,640,112]{1,2,0:T(8,128)S(1)}, f32[2,640,112]{1,2,0:T(8,128)}, u32[]{:S(2)}) copy-start(f32[2,640,112]{1,2,0:T(8,128)} %param.22) | copy-start | bytes 1720324
  0.7 19.8 %copy-start.6 = (s32[2]{0:T(128)S(1)}, s32[2]{0:T(128)}, u32[]{:S(2)}) copy-start(s32[2]{0:T(128)} %counts_ref.23) | copy-start | bytes 28
  0.7 19.8 %copy-start.3 = (f32[4,640]{1,0:T(4,128)S(1)}, f32[4,640]{1,0:T(4,128)}, u32[]{:S(2)}) copy-start(f32[4,640]{1,0:T(4,128)} %gain_ref.17) | copy-start | bytes 30724
  0.7 19.8 %copy-start.4 = (f32[4,640]{1,0:T(4,128)S(1)}, f32[4,640]{1,0:T(4,128)}, u32[]{:S(2)}) copy-start(f32[4,640]{1,0:T(4,128)} %bias_ref.15) | copy-start | bytes 30724
  0.7 49.3 %copy-start = (f32[2,160,640]{2,1,0:T(8,128)S(1)}, f32[2,160,640]{2,1,0:T(8,128)}, u32[]{:S(2)}) copy-start(f32[2,160,640]{2,1,0:T(8,128)} %down_ref.7) | copy-start | bytes 2457604
  0.7 49.3 %copy-start.2 = (f32[2,112,640]{2,1,0:T(8,128)S(1)}, f32[2,112,640]{2,1,0:T(8,128)}, u32[]{:S(2)}) copy-start(f32[2,112,640]{2,1,0:T(8,128)} %proj_ref.7) | copy-start | bytes 1720324
  0.7 49.3 %copy-start.7 = (f32[2,640]{1,0:T(2,128)S(1)}, f32[2,640]{1,0:T(2,128)}, u32[]{:S(2)}) copy-start(f32[2,640]{1,0:T(2,128)} %upb_ref.3) | copy-start | bytes 15364
  0.7 49.3 %copy-start.10 = (f32[2,160]{1,0:T(2,128)S(1)}, f32[2,160]{1,0:T(2,128)}, u32[]{:S(2)}) copy-start(f32[2,160]{1,0:T(2,128)} %downb_ref.3) | copy-start | bytes 3844
  4.4 16.1 %all-to-all-start = ((f32[32,2,768]{2,1,0:T(2,128)}), f32[32,2,768]{2,1,0:T(2,128)S(1)}, u32[]{:S(2)}, u32[]{:S(2)}) async-start(f32[32,2,768]{2,1,0:T(2,128)} %get-tuple-element.119), calls=%async_computation | async-start | bytes 393216 | tf_op jit(solution)/shard_map/all_to_all | solution.py:1164
  12.7 0.7 copy-start.5
  13.3 1.2 copy-start.13
  14.5 0.9 copy-start.14
  20.5 41.4 %copy-start.16 = (f32[2,112]{1,0:T(2,128)S(1)}, f32[2,112]{1,0:T(2,128)}, u32[]{:S(2)}) copy-start(f32[2,112]{1,0:T(2,128)} %param.25) | copy-start | bytes 2692
  20.5 41.4 %copy-start.17 = (f32[2,112]{1,0:T(2,128)S(1)}, f32[2,112]{1,0:T(2,128)}, u32[]{:S(2)}) copy-start(f32[2,112]{1,0:T(2,128)} %param.26) | copy-start | bytes 2692
  20.5 48.6 %copy-start.15 = (f32[136,128]{1,0:T(8,128)S(1)}, f32[136,128]{1,0:T(8,128)}, u32[]{:S(2)}) copy-start(f32[136,128]{1,0:T(8,128)} %get-tuple-element.126.gram0_ref) | copy-start | bytes 208900
  59.3 9.8 %all-to-all-start.2 = ((f32[32,2,128]{2,1,0:T(2,128)}), f32[32,2,128]{2,1,0:T(2,128)S(1)}, u32[]{:S(2)}, u32[]{:S(2)}) async-start(f32[32,2,128]{2,1,0:T(2,128)} %get-tuple-element.125), calls=%async_computation.2 | async-start | bytes 65536 | tf_op jit(solution)/shard_map/all_to_all | solution.py:1164
  84.1 13.0 %all-to-all-start.4 = ((f32[32,2,8,128]{3,2,1,0:T(8,128)}), f32[32,2,8,128]{3,2,1,0:T(8,128)S(1)}, u32[]{:S(2)}, u32[]{:S(2)}) async-start(f32[32,2,8,128]{3,2,1,0:T(8,128)} %bitcast.3), calls=%async_computation.4 | async-start | bytes 524288 | tf_op jit(solution)/shard_map/all_to_all | solution.py:1186
  124.5 13.0 %all-to-all-start.7 = ((f32[32,2,8,128]{3,2,1,0:T(8,128)}), f32[32,2,8,128]{3,2,1,0:T(8,128)S(1)}, u32[]{:S(2)}, u32[]{:S(2)}) async-start(f32[32,2,8,128]{3,2,1,0:T(8,128)} %broadcast_in_dim.10), calls=%async_computation.7 | async-start | bytes 524288 | tf_op jit(solution)/shard_map/all_to_all | solution.py:1191
  137.5 3.3 %collective-permute-start = (f32[144,8,128]{2,1,0:T(8,128)}, f32[144,8,128]{2,1,0:T(8,128)S(1)}, u32[]{:S(2)}, u32[]{:S(2)}) collective-permute-start(f32[144,8,128]{2,1,0:T(8,128)} %get-tuple-element.155), channel_id=1, source_target_pairs={{0,1},{1,0},{2,3},{3,2},{4,5},{5,4},{6,7},{7,6},{8,9},{9,8},{10,11... | collective-permute-start | bytes 1769480 | tf_op jit(solution)/shard_map/ppermute | solution.py:1172
  137.8 11.3 %all-to-all-start.8 = ((f32[32,2,640]{2,1,0:T(2,128)}), f32[32,2,640]{2,1,0:T(2,128)S(1)}, u32[]{:S(2)}, u32[]{:S(2)}) async-start(f32[32,2,640]{2,1,0:T(2,128)} %get-tuple-element.153), calls=%async_computation.8 | async-start | bytes 327680 | tf_op jit(solution)/shard_map/all_to_all | solution.py:1164
  149.2 22.1 %all-to-all-start.9 = ((f32[16,9,8,128]{3,2,1,0:T(8,128)}), f32[16,9,8,128]{3,2,1,0:T(8,128)S(1)}, u32[]{:S(2)}, u32[]{:S(2)}) async-start(f32[16,9,8,128]{3,2,1,0:T(8,128)} %bitcast.5), calls=%async_computation.9 | async-start | bytes 1179648 | tf_op jit(solution)/shard_map/all_to_all | solution.py:1186
  183.8 22.6 %all-to-all-start.11 = ((f32[16,9,8,128]{3,2,1,0:T(8,128)}), f32[16,9,8,128]{3,2,1,0:T(8,128)S(1)}, u32[]{:S(2)}, u32[]{:S(2)}) async-start(f32[16,9,8,128]{3,2,1,0:T(8,128)} %broadcast_in_dim.12), calls=%async_computation.11 | async-start | bytes 1179648 | tf_op jit(solution)/shard_map/all_to_all | solution.py:1191
  205.7 6.5 %collective-permute-start.1 = (f32[192,8,128]{2,1,0:T(8,128)}, f32[192,8,128]{2,1,0:T(8,128)S(1)}, u32[]{:S(2)}, u32[]{:S(2)}) collective-permute-start(f32[192,8,128]{2,1,0:T(8,128)} %get-tuple-element.176), channel_id=1, source_target_pairs={{0,1},{1,0},{2,3},{3,2},{4,5},{5,4},{6,7},{7,6},{8,9},{9,8},{10,11... | collective-permute-start | bytes 2359304 | tf_op jit(solution)/shard_map/ppermute | solution.py:1172
  206.4 14.2 %collective-permute-start.2 = (f32[144,8,128]{2,1,0:T(8,128)S(1)}, f32[144,8,128]{2,1,0:T(8,128)}, u32[]{:S(2)}, u32[]{:S(2)}) collective-permute-start(f32[144,8,128]{2,1,0:T(8,128)S(1)} %bitcast.27), channel_id=1, source_target_pairs={{0,1},{1,0},{2,3},{3,2},{4,5},{5,4},{6,7},{7,6},{8,9},{9,8},{10,11... | collective-permute-start | bytes 1769480 | tf_op jit(solution)/shard_map/ppermute | solution.py:1172
  206.5 14.1 %all-to-all-start.12 = ((f32[32,2,640]{2,1,0:T(2,128)}), f32[32,2,640]{2,1,0:T(2,128)S(1)}, u32[]{:S(2)}, u32[]{:S(2)}) async-start(f32[32,2,640]{2,1,0:T(2,128)} %get-tuple-element.174), calls=%async_computation.12 | async-start | bytes 327680 | tf_op jit(solution)/shard_map/all_to_all | solution.py:1164
  220.6 28.7 %all-to-all-start.13 = ((f32[16,12,8,128]{3,2,1,0:T(8,128)}), f32[16,12,8,128]{3,2,1,0:T(8,128)S(1)}, u32[]{:S(2)}, u32[]{:S(2)}) async-start(f32[16,12,8,128]{3,2,1,0:T(8,128)} %bitcast.37), calls=%async_computation.13 | async-start | bytes 1572864 | tf_op jit(solution)/shard_map/all_to_all | solution.py:1186
  246.8 27.6 %copy-start.8 = (f32[4,640]{1,0:T(4,128)S(1)}, f32[4,640]{1,0:T(4,128)}, u32[]{:S(2)}) copy-start(f32[4,640]{1,0:T(4,128)} %means_ref.1) | copy-start | bytes 30724
  246.8 27.6 %copy-start.9 = (f32[4,640]{1,0:T(4,128)S(1)}, f32[4,640]{1,0:T(4,128)}, u32[]{:S(2)}) copy-start(f32[4,640]{1,0:T(4,128)} %vars_ref.1) | copy-start | bytes 30724
  246.9 27.6 %copy-start.11 = (f32[2,112]{1,0:T(2,128)S(1)}, f32[2,112]{1,0:T(2,128)}, u32[]{:S(2)}) copy-start(f32[2,112]{1,0:T(2,128)} %nmeans_ref.1) | copy-start | bytes 2692
  246.9 27.6 %copy-start.12 = (f32[2,112]{1,0:T(2,128)S(1)}, f32[2,112]{1,0:T(2,128)}, u32[]{:S(2)}) copy-start(f32[2,112]{1,0:T(2,128)} %nvars_ref.1) | copy-start | bytes 2692
  247.6 11.1 %collective-permute-start.3 = (f32[64,8,128]{2,1,0:T(8,128)}, f32[64,8,128]{2,1,0:T(8,128)}, u32[]{:S(2)}, u32[]{:S(2)}) collective-permute-start(f32[64,8,128]{2,1,0:T(8,128)} %dynamic-slice_bitcast_fusion), channel_id=1, source_target_pairs={{0,1},{1,0},{2,3},{3,2},{4,5},{5,4},{6,7},{7,6},{8,9},{9,8},{10,11... | collective-permute-start | bytes 786440 | tf_op jit(solution)/shard_map/ppermute | solution.py:1172
  249.3 17.8 %all-to-all-start.14 = ((f32[32,2,640]{2,1,0:T(2,128)}), f32[32,2,640]{2,1,0:T(2,128)S(1)}, u32[]{:S(2)}, u32[]{:S(2)}) async-start(f32[32,2,640]{2,1,0:T(2,128)} %get-tuple-element.187), calls=%async_computation.14 | async-start | bytes 327680 | tf_op jit(solution)/shard_map/all_to_all | solution.py:1164
  269.2 32.8 %all-to-all-start.15 = ((f32[16,16,8,128]{3,2,1,0:T(8,128)}), f32[16,16,8,128]{3,2,1,0:T(8,128)}, u32[]{:S(2)}, u32[]{:S(2)}) async-start(f32[16,16,8,128]{3,2,1,0:T(8,128)} %pad_maximum_fusion), calls=%async_computation.15 | async-start | bytes 2097152 | tf_op jit(solution)/shard_map/all_to_all | solution.py:1483
  302.1 5.3 %collective-permute-start.4 = (f32[16,16,8,128]{3,2,1,0:T(8,128)}, f32[16,16,8,128]{3,2,1,0:T(8,128)}, u32[]{:S(2)}, u32[]{:S(2)}) collective-permute-start(f32[16,16,8,128]{3,2,1,0:T(8,128)} %all-to-all-done.15.pack0_ref), channel_id=1, source_target_pairs={{0,1},{1,0},{2,3},{3,2},{4,5},{5,4},{6,7},{7,6},{8,9},{9,8},{10,11... | collective-permute-start | bytes 3145736 | tf_op jit(solution)/shard_map/ppermute | solution.py:1172
  303.8 15.0 %all-to-all-start.16 = ((f32[16,4,8,128]{3,2,1,0:T(8,128)}), f32[16,4,8,128]{3,2,1,0:T(8,128)S(1)}, u32[]{:S(2)}, u32[]{:S(2)}) async-start(f32[16,4,8,128]{3,2,1,0:T(8,128)} %broadcast_in_dim.14), calls=%async_computation.16 | async-start | bytes 524288 | tf_op jit(solution)/shard_map/all_to_all | solution.py:1191
  318.8 1.5 collective-permute-start.5

commit v7 on v6

--- a/solution.py
+++ b/solution.py
@@ -877,8 +877,8 @@
 
 
 def depth_backward_kernel(
-    block, before, final, counts_ref, grads_ref, stat2_ref, stat_ref, nstat_ref, dy2_ref, d_ref, e_ref, a_ref, columns_ref, w_ref,
-    gain_ref, bias_ref, taps_ref, z3_ref, dx_in_ref, sums_in_ref, list_in_ref, dxpre_ref, send_ref, q_ref, grad_rows_ref,
+    block, counts_ref, grads_ref, stat2_ref, stat_ref, nstat_ref, dy2_ref, d_ref, e_ref, a_ref, columns_ref, w_ref,
+    gain_ref, bias_ref, taps_ref, z3_ref, dxpre_ref, send_ref, q_ref, grad_rows_ref,
     z_ref, f_ref, taps8_ref, dw_ref, total_ref, *raw_refs,
 ):
     tile = pl.program_id(0)
@@ -894,12 +894,9 @@
     def start():
         if half:
             clear_edges(z_ref)
-        if before:
-            dxpre_ref[...] = dx_in_ref[...]
-            send_all(send_ref, sums_in_ref[0:2, :], slice(0, before * LANES))
-            q_ref[0 : list_in_ref.shape[0]] = list_in_ref[...]
-        else:
-            dxpre_ref[...] = jnp.zeros_like(dxpre_ref)
+        dxpre_ref[...] = jnp.zeros_like(dxpre_ref)
+        if not half:
+            send_ref[...] = jnp.zeros_like(send_ref)
 
         def dead(t, carry):
             if half:
@@ -984,10 +981,12 @@
     zero = jnp.zeros((8, LANES), F32)
     summed, cross = each_frame(frames, finish, (zero, zero))
     rows = stack_rows(jnp.sum(summed, axis=0, keepdims=True), root_one * jnp.sum(cross, axis=0, keepdims=True))
-    if final:
-        send_all(send_ref, rows, pl.ds(pl.multiple_of((tile + before) * LANES, LANES), LANES))
+    if half:
+        send_all(send_ref, rows, pl.ds(pl.multiple_of(tile * LANES, LANES), LANES))
     else:
-        send_ref[...] = rows8(rows[0:1], rows[1:2])
+        spot = lax.broadcasted_iota(jnp.int32, (8, LANES), 0)
+        for index in range(2):
+            send_ref[index] = jnp.where(spot == tile, rows[index : index + 1], send_ref[index])
     gathered = fold_square(total_ref[...])
     narrow = w_ref.shape[1]
     dtaps = jnp.sum(dw_ref[...], axis=1)
@@ -995,7 +994,7 @@
     unused = jnp.zeros(((-taps) % 8, LANES), F32)
     values = jnp.concatenate((gathered[0:narrow],) + parts + (unused,), axis=0)
     listed = values.shape[0] // 8
-    q_ref[pl.ds((tile + before) * listed, listed)] = values.reshape(listed, 8, LANES)
+    q_ref[pl.ds(tile * listed, listed)] = values.reshape(listed, 8, LANES)
 
     if half:
         @pl.when(tile == tiles - 1)
@@ -1027,7 +1026,10 @@
     full = stat01_ref[2:3, :]
     count = full[:, 0:LANES]
     width = full.shape[1]
-    top_zero = row_total(zero_ref)
+    tiles = width // LANES
+    top_zero = stack_rows(
+        *(jnp.concatenate([zero_ref[index, tile : tile + 1, :] for tile in range(tiles)], axis=1) for index in range(2))
+    )
     top_one = row_total(one_ref, slice(0, width))
     w_zero = pad_rows(w_ref[0])
     matrix, shift = input_factors(top_zero, stat01_ref, full, gain_ref[0:1, :], w_zero)
@@ -1405,10 +1407,11 @@
     sums, theirs, gram = together(sums, theirs, gram)
     sums, pack_one = together(exchange(sums), pack_one + swap_cores(theirs))
     pack_one = share_out(pack_one)
-    nothing = jnp.zeros((8, LANES), F32)
-
-    def depth_backward(block, begin, end, sums, stat2, stat, dy2, depth, expanded, planes, columns, dx_in, sums_in, list_in):
+
+    def depth_backward(block, sums, stat2, stat, dy2, depth, expanded, planes, columns):
         rows = half_rows if block else full_rows
+        listed = tiles * q_tiles if block else round_up(tiles * q_tiles)
+        send = (devices, 2, width + LANES) if block else (2, 8, LANES)
         if block:
             taps_shape = (taps, 8, LANES)
             z_shape = (frames, 2, HALF_ROWS + 1, 8, LANES)
@@ -1417,41 +1420,22 @@
             taps_shape = (12 * LAGS, 8, LANES)
             z_shape = planes_shape(0, LANES, 4)
             f_shape = (frames, PAIRS, 4, 2, 8, LANES)
-        count = end - begin
-        final = end == tiles
-        listed = round_up(end * q_tiles) if final and not block else end * q_tiles
-        if final:
-            send = (devices, 2, width + (LANES if block else 0))
-            send_spec = fixed(*send)
-        else:
-            send = (8, count * LANES)
-            send_spec = tile_rows(8)
-
-        def wide_rows(rows):
-            return pl.BlockSpec((rows, LANES), lambda j: (0, j + begin))
-
-        def wide_cube(rows):
-            return pl.BlockSpec((rows, 8, LANES), lambda j: (0, 0, j + begin))
-
-        def wide_weight(rows):
-            return pl.BlockSpec((1, rows, LANES), lambda j: (block, 0, j + begin))
-
         return call(
-            functools.partial(depth_backward_kernel, block, begin, final), (count,),
-            [SCALARS, pl.BlockSpec((devices, 2, LANES), lambda j: (0, 0, j + begin)), wide_rows(8), wide_rows(8), whole(nstat),
-             wide_cube(rows), wide_cube(rows), wide_cube(full_rows), planes_of(block, 2, begin), whole(columns), wide_weight(cin), wide_rows(4),
-             wide_rows(4), wide_weight(taps), whole(z_zero), whole(dx_in), whole(sums_in), whole(list_in)],
-            [fixed(pixels, LANES), send_spec, fixed(listed, 8, LANES), tile_rows(8)],
-            [shape(pixels, LANES), shape(*send), shape(listed, 8, LANES), shape(8, count * LANES)],
+            functools.partial(depth_backward_kernel, block), (tiles,),
+            [SCALARS, tile_sums(), tile_rows(8), tile_rows(8), whole(nstat),
+             tile_cube(rows), tile_cube(rows), tile_cube(full_rows), planes_of(block, 2), whole(columns), weight_tile(block, cin), tile_rows(4),
+             tile_rows(4), weight_tile(block, taps), whole(z_zero)],
+            [fixed(pixels, LANES), fixed(*send), fixed(listed, 8, LANES), tile_rows(8)],
+            [shape(pixels, LANES), shape(*send), shape(listed, 8, LANES), shape(8, width)],
             [pltpu.VMEM(z_shape, F32), pltpu.VMEM(f_shape, F32), pltpu.VMEM(taps_shape, F32), pltpu.VMEM(taps_shape, F32),
              pltpu.VMEM((2 * LANES, 2 * LANES), F32)]
             + ([] if block else [pltpu.VMEM((frames, 4, 2, PAIRS, 8, LANES), F32)]),
             (frame_counts, sums, stat2, stat, nstat, dy2, depth, expanded, planes, columns, w_t, wide_gains, wide_biases,
-             depth_weight, z_zero, dx_in, sums_in, list_in),
+             depth_weight, z_zero),
         )
 
     dxpre_one, sums, q_one, grad_one = depth_backward(
-        1, 0, tiles, sums, stat12, stat11, dy2_one, d_one, e_one, planes_one, x1_columns, nothing, nothing, nothing
+        1, sums, stat12, stat11, dy2_one, d_one, e_one, planes_one, x1_columns
     )
     sums, pack_one = together(sums, pack_one)
     top_one, pack_one = together(exchange(sums), pack_one)
@@ -1471,16 +1455,25 @@
         exchange(sums), pack_zero + swap_cores(theirs), pack_one_other
     )
     pack_zero = share_out(pack_zero)
-    dxpre_zero, sums, late, grad_zero = depth_backward(
-        0, 0, tiles, sums, stat02, stat01, dy2_zero, d_zero, e_zero, planes_zero, x_columns, nothing, nothing, nothing
-    )
-    sums, pack_zero = together(sums, pack_zero)
-    top_zero, late = together(exchange(sums), add_cores(late))
+    dxpre_zero, top, late, grad_zero = depth_backward(
+        0, sums, stat02, stat01, dy2_zero, d_zero, e_zero, planes_zero, x_columns
+    )
+    top, pack_zero = together(top, pack_zero)
+    top = top + swap_cores(top)
+    late = add_cores(late)
     own = jnp.sum(pack_zero, axis=0)
+    chips = pack_zero.shape[0]
     joint = jnp.concatenate(
-        [jnp.broadcast_to(own[None], pack_zero.shape), late.reshape(pack_zero.shape[0], -1, 8, LANES)], axis=1
+        [jnp.broadcast_to(own[None], pack_zero.shape), late.reshape(chips, -1, 8, LANES),
+         jnp.broadcast_to(top[None], (chips,) + top.shape)], axis=1,
     )
     joint = lax.all_to_all(joint, CHIPS, 0, 0, tiled=True)
+    added = jnp.sum(joint[:, own.shape[0] :], axis=0)
+    top_zero = added[-2:]
+    late = lax.all_to_all(
+        jnp.broadcast_to(added[None, :-2], (chips, added.shape[0] - 2, 8, LANES)), CHIPS, 0, 0, tiled=True
+    ).reshape(-1, 8, LANES)
+    joint_other = swap_cores(joint)
     final_args = (
         frame_counts, momentum_index, gram, stat01, stat02, stat11, stat12, grad_zero, grad_one, top_one,
         top_zero, nsum_zero, nsum_one, dxpre_zero, x, dx1, w_t, wide_gains, wide_means, wide_variances, narrow_means,
@@ -1493,9 +1486,6 @@
     video_grad, less, factor, wgain, wbias, ngain, nbias, newm, newv, newnm, newnv = simple_call(
         finish_kernel, 2, final_args, final_outs
     )
-    less, joint = together(less, joint)
-    joint_other = swap_cores(joint)
-    late = share_back(joint[:, own.shape[0] :])
     list_shapes = [
         shape(2, cin, width), shape(2, taps, width), shape(2, squeeze, width), shape(2, squeeze, width),
         shape(2, cin, width), shape(2, width), shape(2, squeeze),

time: 324 us -> 314 us (0.969)
  blocking collectives: 59.6 us -> 93.8 us
  waiting for transfers between devices: 67.2 us -> 36.7 us
  starting transfers between devices: 54.8 us -> 47.1 us
  local copies, waits for them, and re-layouts: 7.75 us -> 3.35 us
    all_to_all x0 -> x1, blocking collectives: none -> 35.4 us  [local(): joint = lax.all_to_all(joint, CHIPS, 0, 0, tiled=True)]
    all_to_all x1, waiting for transfers between devices: 20.8 us -> 0.43 us  [local(): lax.all_to_all(jnp.broadcast_to(added[None, :-2], (chips, added.shape[0]...]
    all_to_all x5 -> x4, starting transfers between devices: 27.7 us -> 18.4 us  [exchange(): return lax.all_to_all(send, AXES, 0, 0, tiled=True)]
    all_to_all x3 -> x2, waiting for transfers between devices: 10.9 us -> 2.74 us  [share_back(): lax.all_to_all(jnp.broadcast_to(own[None], pieces.shape), names, 0, 0, ti...]
    ppermute x6 -> x7, starting transfers between devices: 2.91 us -> 8.2 us  [swap_cores(): return lax.ppermute(values, 'core', [(0, 1), (1, 0)])]
    unnamed x38, local copies, waits for them, and re-layouts: 4.61 us -> 0.92 us
    all_to_all x3 -> x2, starting transfers between devices: 9.85 us -> 6.32 us  [share_back(): lax.all_to_all(jnp.broadcast_to(own[None], pieces.shape), names, 0, 0, ti...]
    all_to_all x5 -> x4, waiting for transfers between devices: 29.5 us -> 26.4 us  [exchange(): return lax.all_to_all(send, AXES, 0, 0, tiled=True)]
  transfers between devices with their start and end apart: 18 -> 17, of which waited for: 11 -> 10; matrix products, arithmetic and copies ran while one was open for 3% -> 2% of each run, Pallas kernels for 27% -> 27%
where the time goes in v7:
time: 314 us; the launch traced here: 311 us
  Pallas kernels  123 us (39%)
  blocking collectives  93.8 us (30%)
  starting transfers between devices  47.1 us (15%)
  waiting for transfers between devices  36.7 us (12%)
  other arithmetic  5.4 us (2%)
  local copies, waits for them, and re-layouts  3.35 us (1%)
    pallas_call x14, Pallas kernels, call(): pl.pallas_call(kernel, grid=grid, in_specs=in_specs, out_specs=out_specs,...  123 us
    all_to_all x5, blocking collectives, exchange(): return lax.all_to_all(send, AXES, 0, 0, tiled=True)  58.4 us
    all_to_all x1, blocking collectives, local(): joint = lax.all_to_all(joint, CHIPS, 0, 0, tiled=True)  35.4 us
    all_to_all x4, waiting for transfers between devices, exchange(): return lax.all_to_all(send, AXES, 0, 0, tiled=True)  26.4 us
    all_to_all x4, starting transfers between devices, exchange(): return lax.all_to_all(send, AXES, 0, 0, tiled=True)  18.4 us
    all_to_all x3, starting transfers between devices, share_out(): lax.all_to_all(tiles.reshape(count, -1, *tiles.shape[1:]), names, 0, 0, t...  10.5 us
    ppermute x7, starting transfers between devices, swap_cores(): return lax.ppermute(values, 'core', [(0, 1), (1, 0)])  8.2 us
    all_to_all x2, starting transfers between devices, share_back(): lax.all_to_all(jnp.broadcast_to(own[None], pieces.shape), names, 0, 0, ti...  6.32 us
  transfers between devices with their start and end apart: 17, of which 10 were waited for; matrix products, arithmetic and copies ran while one was open for 2% of the time, Pallas kernels for 27%

profile of v7, /device:TPU:0, one launch (start us, length us, event | category | flops | bytes accessed | tf_op | source)
XLA Modules:
  0.0 311.4 jit_solution(3543798553836640138)
XLA Ops:
  0.7 3.6 %shard_map.314 = (f32[136,128]{1,0:T(8,128)}, f32[32,2,768]{2,1,0:T(2,128)}) custom-call(s32[2]{0:T(128)} %counts_ref.23, f32[112,2048]{1,0:T(8,128)} %video_ref.3, f32[2,112,640]{2,1,0:T(8,128)} %bitcast.17), custom_call_target="tpu_custom_call" | custom-call | flops 1000000000 | bytes 1000000 | tf_op jit(solution)/shard_map/pallas_call | solution.py:1210
  4.3 7.3 %all-to-all-start = ((f32[32,2,768]{2,1,0:T(2,128)}), f32[32,2,768]{2,1,0:T(2,128)S(1)}, u32[]{:S(2)}, u32[]{:S(2)}) async-start(f32[32,2,768]{2,1,0:T(2,128)} %get-tuple-element.115), calls=%async_computation | async-start | bytes 393216 | tf_op jit(solution)/shard_map/all_to_all | solution.py:1166
  11.7 3.4 %shard_map.315 = (f32[2048,128]{1,0:T(8,128)}, bf16[2048,256]{1,0:T(8,128)(2,1)}, bf16[256,2048]{1,0:T(8,128)(2,1)}, f32[512,128]{1,0:T(8,128)S(1)}) custom-call(s32[2]{0:T(128)S(1)} %copy-done.5, f32[112,2048]{1,0:T(8,128)S(1)} %copy-done.12, f32[112,512]{1,0:T(8,128)S(1)} %copy-done.13), custom_call_target="tpu_custom_call" | custom-call | flops 1000000000 | bytes 1000000 | tf_op jit(solution)/shard_map/pallas_call | solution.py:1210
  15.1 5.3 %all-to-all-done.sums_ref.count_ref = f32[32,2,768]{2,1,0:T(2,128)S(1)} async-done(((f32[32,2,768]{2,1,0:T(2,128)}), f32[32,2,768]{2,1,0:T(2,128)S(1)}, u32[]{:S(2)}, u32[]{:S(2)}) %all-to-all-start) | async-done | bytes 196640 | tf_op jit(solution)/shard_map/all_to_all | solution.py:1166
  20.4 15.9 %shard_map.316 = (f32[256,8,640]{2,1,0:T(8,128)}, f32[256,8,640]{2,1,0:T(8,128)}, f32[8,640]{1,0:T(8,128)S(1)}, f32[32,2,640]{2,1,0:T(2,128)S(1)}, f32[8,2,4,8,8,640]{5,4,3,2,1,0:T(8,128)}) custom-call(s32[2]{0:T(128)S(1)} %copy-done.5, f32[32,2,768]{2,1,0:T(2,128)S(1)} %all-to-all-done.sums_ref.count_ref, ...), custom_call_target="tpu_custom_call" | custom-call | flops 1000000000 | bytes 1000000 | tf_op jit(solution)/shard_map/pallas_call | solution.py:1210
  36.4 13.3 %all_to_all.80.sums_ref = f32[32,2,640]{2,1,0:T(2,128)S(1)} all-to-all(f32[32,2,640]{2,1,0:T(2,128)S(1)} %get-tuple-element.117), channel_id=1, replica_groups=mesh['dp'=4,'z'=4,'core'=2] {'dp','z','core'}, dimensions={0} | all-to-all | bytes 327680 | tf_op jit(solution)/shard_map/all_to_all | solution.py:1166
  49.7 9.4 %shard_map.317 = (f32[2048,128]{1,0:T(8,128)}, f32[8,640]{1,0:T(8,128)S(1)}, f32[8,640]{1,0:T(8,128)S(1)}, f32[8,160]{1,0:T(8,128)S(1)}, f32[8,640]{1,0:T(8,128)S(1)}, /*index=5*/f32[32,2,128]{2,1,0:T(2,128)}) custom-call(s32[2]{0:T(128)S(1)} %copy-done.5, f32[32,2,640]{2,1,0:T(2,128)S(1)} %all_to_all.80.sums_ref, ...), custom_call_target="tpu_custom_call" | custom-call | flops 1000000000 | bytes 1000000 | tf_op jit(solution)/shard_map/pallas_call | solution.py:1210
  59.1 2.6 all-to-all-start.2
  61.7 7.2 %all-to-all-done.2.sums_ref = f32[32,2,128]{2,1,0:T(2,128)S(1)} async-done(((f32[32,2,128]{2,1,0:T(2,128)}), f32[32,2,128]{2,1,0:T(2,128)S(1)}, u32[]{:S(2)}, u32[]{:S(2)}) %all-to-all-start.2) | async-done | bytes 32800 | tf_op jit(solution)/shard_map/all_to_all | solution.py:1166
  68.9 4.8 %shard_map.318 = (f32[2048,128]{1,0:T(8,128)}, bf16[2048,256]{1,0:T(8,128)(2,1)}, bf16[256,2048]{1,0:T(8,128)(2,1)}, f32[64,8,128]{2,1,0:T(8,128)}, f32[8,128]{1,0:T(8,128)S(1)}, /*index=5*/f32[32,2,640]{2,1,0:T(2,128)S(1)}) custom-call(s32[2]{0:T(128)S(1)} %copy-done.5, f32[32,2,128]{2,1,0:T(2,128)S(1)} %all-to-all-done.2.sums_ref, ...), custom_call_target="tpu_custom_call" | custom-call | flops 1000000000 | bytes 1000000 | tf_op jit(solution)/shard_map/pallas_call | solution.py:1210
  73.7 10.2 %all_to_all.81.sums_ref = f32[32,2,640]{2,1,0:T(2,128)S(1)} all-to-all(f32[32,2,640]{2,1,0:T(2,128)S(1)} %get-tuple-element.125), channel_id=1, replica_groups=mesh['dp'=4,'z'=4,'core'=2] {'dp','z','core'}, dimensions={0} | all-to-all | bytes 327680 | tf_op jit(solution)/shard_map/all_to_all | solution.py:1166
  83.8 2.6 all-to-all-start.4
  86.4 9.9 %shard_map.319 = (f32[256,8,640]{2,1,0:T(8,128)}, f32[64,8,640]{2,1,0:T(8,128)}, f32[8,640]{1,0:T(8,128)S(1)}, f32[32,2,640]{2,1,0:T(2,128)S(1)}, f32[8,3,18,8,640]{4,3,2,1,0:T(8,128)}) custom-call(s32[2]{0:T(128)S(1)} %copy-done.5, f32[32,2,640]{2,1,0:T(2,128)S(1)} %all_to_all.81.sums_ref, f32[8,128]{1,0:T(8,128)S(1)} %get-tuple-element.128.count_ref.nstat_ref, ...), custom_call_target="tpu_custom_call" | custom-call | flops 1000000000 | bytes 1000000 | tf_op jit(solution)/shard_map/pallas_call | solution.py:1210
  96.8 14.1 %all_to_all.82.sums_ref = f32[32,2,640]{2,1,0:T(2,128)S(1)} all-to-all(f32[32,2,640]{2,1,0:T(2,128)S(1)} %get-tuple-element.132), channel_id=1, replica_groups=mesh['dp'=4,'z'=4,'core'=2] {'dp','z','core'}, dimensions={0} | all-to-all | bytes 327680 | tf_op jit(solution)/shard_map/all_to_all | solution.py:1166
  110.9 3.4 %shard_map.320 = (f32[512,128]{1,0:T(8,128)S(1)}, f32[8,640]{1,0:T(8,128)S(1)}, f32[8,640]{1,0:T(8,128)S(1)}, f32[8,160]{1,0:T(8,128)S(1)}, f32[8,640]{1,0:T(8,128)S(1)}, /*index=5*/f32[32,4,128]{2,1,0:T(4,128)S(1)}) custom-call(s32[2]{0:T(128)S(1)} %copy-done.5, f32[32,2,640]{2,1,0:T(2,128)S(1)} %all_to_all.82.sums_ref, ...), custom_call_target="tpu_custom_call" | custom-call | flops 1000000000 | bytes 1000000 | tf_op jit(solution)/shard_map/pallas_call | solution.py:1210
  114.3 9.5 %all_to_all.83.third_ref = f32[32,4,128]{2,1,0:T(4,128)S(1)} all-to-all(f32[32,4,128]{2,1,0:T(4,128)S(1)} %get-tuple-element.135), channel_id=1, replica_groups=mesh['dp'=4,'z'=4,'core'=2] {'dp','z','core'}, dimensions={0} | all-to-all | bytes 131072 | tf_op jit(solution)/shard_map/all_to_all | solution.py:1166
  123.8 0.7 broadcast_in_dim.10
  124.5 2.6 all-to-all-start.7
  127.1 7.6 %shard_map.321 = (f32[112,512]{1,0:T(8,128)}, f32[8,128]{1,0:T(8,128)S(1)}, f32[64,8,640]{2,1,0:T(8,128)}, f32[32,2,640]{2,1,0:T(2,128)}, f32[144,8,128]{2,1,0:T(8,128)S(1)}, /*index=5*/f32[144,8,128]{2,1,0:T(8,128)}) custom-call(s32[2]{0:T(128)S(1)} %copy-done.5, s32[1]{0:T(128)} %bitcast.core_ref, f32[32,4,128]{2,1,0:T(4,128)S(1)} %all_to_all.83.third_ref, ...), custom_call_target="tpu_custom_call" | custom-call | flops 1000000000 | bytes 1000000 | tf_op jit(solution)/shard_map/pallas_call | solution.py:1210
  134.8 2.7 all-to-all-done.7
  137.9 2.9 all-to-all-start.8
  140.8 0.9 add.24
  141.7 7.6 %all-to-all-done.8.grads_ref = f32[32,2,640]{2,1,0:T(2,128)S(1)} async-done(((f32[32,2,640]{2,1,0:T(2,128)}), f32[32,2,640]{2,1,0:T(2,128)S(1)}, u32[]{:S(2)}, u32[]{:S(2)}) %all-to-all-start.8) | async-done | bytes 163872 | tf_op jit(solution)/shard_map/all_to_all | solution.py:1166
  149.2 3.6 %all-to-all-start.9 = ((f32[16,9,8,128]{3,2,1,0:T(8,128)}), f32[16,9,8,128]{3,2,1,0:T(8,128)S(1)}, u32[]{:S(2)}, u32[]{:S(2)}) async-start(f32[16,9,8,128]{3,2,1,0:T(8,128)} %bitcast.5), calls=%async_computation.9 | async-start | bytes 1179648 | tf_op jit(solution)/shard_map/all_to_all | solution.py:1188
  152.8 14.4 %shard_map.322 = (f32[2048,128]{1,0:T(8,128)}, f32[32,2,768]{2,1,0:T(2,128)S(1)}, f32[100,8,128]{2,1,0:T(8,128)S(1)}, f32[8,640]{1,0:T(8,128)S(1)}) custom-call(s32[2]{0:T(128)S(1)} %copy-done.5, f32[32,2,640]{2,1,0:T(2,128)S(1)} %all-to-all-done.8.grads_ref, f32[8,640]{1,0:T(8,128)S(1)} %get-tuple-element.139.stat_ref.stat2_ref.stat12_ref, ...), custom_call_target="tpu_custom_call" | custom-call | flops 1000000000 | bytes 1000000 | tf_op jit(solution)/shard_map/pallas_call | solution.py:1210
  167.2 4.2 %all-to-all-done.9 = f32[16,9,8,128]{3,2,1,0:T(8,128)S(1)} async-done(((f32[16,9,8,128]{3,2,1,0:T(8,128)}), f32[16,9,8,128]{3,2,1,0:T(8,128)S(1)}, u32[]{:S(2)}, u32[]{:S(2)}) %all-to-all-start.9) | async-done | bytes 589856 | tf_op jit(solution)/shard_map/all_to_all | solution.py:1188
  171.4 11.4 %all_to_all.84.top_ref.one_ref = f32[32,2,768]{2,1,0:T(2,128)S(1)} all-to-all(f32[32,2,768]{2,1,0:T(2,128)S(1)} %get-tuple-element.159), channel_id=1, replica_groups=mesh['dp'=4,'z'=4,'core'=2] {'dp','z','core'}, dimensions={0} | all-to-all | bytes 393216 | tf_op jit(solution)/shard_map/all_to_all | solution.py:1166
  182.8 0.9 broadcast_in_dim.11
  183.7 3.7 %all-to-all-start.11 = ((f32[16,9,8,128]{3,2,1,0:T(8,128)}), f32[16,9,8,128]{3,2,1,0:T(8,128)S(1)}, u32[]{:S(2)}, u32[]{:S(2)}) async-start(f32[16,9,8,128]{3,2,1,0:T(8,128)} %broadcast_in_dim.11), calls=%async_computation.11 | async-start | bytes 1179648 | tf_op jit(solution)/shard_map/all_to_all | solution.py:1193
  187.4 18.1 %shard_map.323 = (f32[2048,128]{1,0:T(8,128)}, f32[8,128]{1,0:T(8,128)S(1)}, f32[256,8,640]{2,1,0:T(8,128)}, f32[32,2,640]{2,1,0:T(2,128)}, f32[192,8,128]{2,1,0:T(8,128)}, /*index=5*/f32[192,8,128]{2,1,0:T(8,128)}) custom-call(s32[2]{0:T(128)S(1)} %copy-done.5, s32[1]{0:T(128)} %bitcast.core_ref, f32[32,2,768]{2,1,0:T(2,128)S(1)} %all_to_all.84.top_ref.one_ref, ...), custom_call_target="tpu_custom_call" | custom-call | flops 1000000000 | bytes 1000000 | tf_op jit(solution)/shard_map/pallas_call | solution.py:1210
  205.6 0.7 collective-permute-start.1
  206.4 5.6 %all-to-all-start.12 = ((f32[32,2,640]{2,1,0:T(2,128)}), f32[32,2,640]{2,1,0:T(2,128)S(1)}, u32[]{:S(2)}, u32[]{:S(2)}) async-start(f32[32,2,640]{2,1,0:T(2,128)} %get-tuple-element.170), calls=%async_computation.12 | async-start | bytes 327680 | tf_op jit(solution)/shard_map/all_to_all | solution.py:1166
  212.0 2.1 add.25
  214.2 6.3 %all-to-all-done.12.grads_ref = f32[32,2,640]{2,1,0:T(2,128)S(1)} async-done(((f32[32,2,640]{2,1,0:T(2,128)}), f32[32,2,640]{2,1,0:T(2,128)S(1)}, u32[]{:S(2)}, u32[]{:S(2)}) %all-to-all-start.12) | async-done | bytes 163872 | tf_op jit(solution)/shard_map/all_to_all | solution.py:1166
  220.5 4.3 %all-to-all-start.13 = ((f32[16,12,8,128]{3,2,1,0:T(8,128)}), f32[16,12,8,128]{3,2,1,0:T(8,128)}, u32[]{:S(2)}, u32[]{:S(2)}) async-start(f32[16,12,8,128]{3,2,1,0:T(8,128)} %bitcast.7), calls=%async_computation.13 | async-start | bytes 1572864 | tf_op jit(solution)/shard_map/all_to_all | solution.py:1188
  224.8 21.9 %shard_map.324 = (f32[2048,128]{1,0:T(8,128)}, f32[2,8,128]{2,1,0:T(8,128)S(1)}, f32[128,8,128]{2,1,0:T(8,128)S(1)}, f32[8,640]{1,0:T(8,128)S(1)}) custom-call(s32[2]{0:T(128)S(1)} %copy-done.5, f32[32,2,640]{2,1,0:T(2,128)S(1)} %all-to-all-done.12.grads_ref, f32[8,640]{1,0:T(8,128)S(1)} %get-tuple-element.148.stat_ref.stat2_ref.stat02_ref, ...), custom_call_target="tpu_custom_call" | custom-call | flops 1000000000 | bytes 1000000 | tf_op jit(solution)/shard_map/pallas_call | solution.py:1210
  246.7 6.7 %collective-permute-start.3 = (f32[64,8,128]{2,1,0:T(8,128)S(1)}, f32[64,8,128]{2,1,0:T(8,128)S(1)}, u32[]{:S(2)}, u32[]{:S(2)}) collective-permute-start(f32[64,8,128]{2,1,0:T(8,128)S(1)} %dynamic-slice_bitcast_fusion), channel_id=1, source_target_pairs={{0,1},{1,0},{2,3},{3,2},{4,5},{5,4},{6,7},{7,6},{8,9},{9,8},{10,11... | collective-permute-start | bytes 786440 | tf_op jit(solution)/shard_map/ppermute | solution.py:1174
  253.5 1.1 collective-permute-done.3
  254.6 1.2 reduce_sum.38
  256.0 35.4 %all_to_all.85.pack0_ref = f32[16,18,8,128]{3,2,1,0:T(8,128)} all-to-all(f32[16,18,8,128]{3,2,1,0:T(8,128)S(1)} %pad_maximum_fusion), channel_id=1, replica_groups=mesh['dp'=4,'z'=4,'core'=2] {'dp','z'}, dimensions={0} | all-to-all | bytes 2359296 | tf_op jit(solution)/shard_map/all_to_all | solution.py:1470
  291.4 1.0 slice_reduce_fusion
  292.5 0.7 broadcast_in_dim.14
  293.2 3.8 %all-to-all-start.15 = ((f32[16,4,8,128]{3,2,1,0:T(8,128)}), f32[16,4,8,128]{3,2,1,0:T(8,128)S(1)}, u32[]{:S(2)}, u32[]{:S(2)}) async-start(f32[16,4,8,128]{3,2,1,0:T(8,128)} %broadcast_in_dim.14), calls=%async_computation.15 | async-start | bytes 524288 | tf_op jit(solution)/shard_map/all_to_all | solution.py:1473
  297.7 6.7 %shard_map.325 = (f32[112,2048]{1,0:T(8,128)}, f32[2,112,640]{2,1,0:T(8,128)S(1)}, f32[16,640]{1,0:T(8,128)S(1)}, f32[4,640]{1,0:T(4,128)}, f32[4,640]{1,0:T(4,1...) custom-call(s32[2]{0:T(128)S(1)} %copy-done.5, ...), custom_call_target="tpu_custom_call" | custom-call | flops 1000000000 | bytes 1000000 | tf_op jit(solution)/shard_map/pallas_call | solution.py:1210
  304.4 3.4 %shard_map.326 = (f32[2,112,640]{2,1,0:T(8,128)}, f32[2,45,640]{2,1,0:T(8,128)S(1)}, f32[2,160,640]{2,1,0:T(8,128)}, f32[2,160,640]{2,1,0:T(8,128)}, f32[2,112,6...) custom-call(s32[1]{0:T(128)} %bitcast.core_ref, f32[16,18,8,128]{3,2,1,0:T(8,128)} %all_to_all.85.pack0_ref, ...), custom_call_target="tpu_custom_call" | custom-call | flops 1000000000 | bytes 1000000 | tf_op jit(solution)/shard_map/pallas_call | solution.py:1210
  308.4 1.4 collective-permute-done.6.late_other_ref
  309.8 0.8 shard_map.327
  310.6 0.8 copy.42
  (63 shorter events, 2.1 us)
Async XLA Ops:
  0.7 11.0 %copy-start.15 = (f32[2,45,640]{2,0,1:T(2,128)S(1)}, f32[2,45,640]{2,0,1:T(2,128)}, u32[]{:S(2)}) copy-start(f32[2,45,640]{2,0,1:T(2,128)} %param.27) | copy-start | bytes 691204
  0.7 11.0 %copy-start.5 = (s32[2]{0:T(128)S(1)}, s32[2]{0:T(128)}, u32[]{:S(2)}) copy-start(s32[2]{0:T(128)} %counts_ref.23) | copy-start | bytes 28
  0.7 11.0 %copy-start.12 = (f32[112,2048]{1,0:T(8,128)S(1)}, f32[112,2048]{1,0:T(8,128)}, u32[]{:S(2)}) copy-start(f32[112,2048]{1,0:T(8,128)} %video_ref.3) | copy-start | bytes 2752516
  0.7 11.0 %copy-start.13 = (f32[112,512]{1,0:T(8,128)S(1)}, f32[112,512]{1,0:T(8,128)}, u32[]{:S(2)}) copy-start(f32[112,512]{1,0:T(8,128)} %cot_ref.1) | copy-start | bytes 688132
  4.3 16.1 %all-to-all-start = ((f32[32,2,768]{2,1,0:T(2,128)}), f32[32,2,768]{2,1,0:T(2,128)S(1)}, u32[]{:S(2)}, u32[]{:S(2)}) async-start(f32[32,2,768]{2,1,0:T(2,128)} %get-tuple-element.115), calls=%async_computation | async-start | bytes 393216 | tf_op jit(solution)/shard_map/all_to_all | solution.py:1166
  11.7 8.7 %copy-start.2 = (f32[2,640,112]{1,2,0:T(8,128)S(1)}, f32[2,640,112]{1,2,0:T(8,128)}, u32[]{:S(2)}) copy-start(f32[2,640,112]{1,2,0:T(8,128)} %param.22) | copy-start | bytes 1720324
  11.7 8.7 %copy-start.3 = (f32[4,640]{1,0:T(4,128)S(1)}, f32[4,640]{1,0:T(4,128)}, u32[]{:S(2)}) copy-start(f32[4,640]{1,0:T(4,128)} %gain_ref.17) | copy-start | bytes 30724
  11.7 8.7 %copy-start.4 = (f32[4,640]{1,0:T(4,128)S(1)}, f32[4,640]{1,0:T(4,128)}, u32[]{:S(2)}) copy-start(f32[4,640]{1,0:T(4,128)} %bias_ref.15) | copy-start | bytes 30724
  20.4 29.3 %copy-start = (f32[2,160,640]{2,1,0:T(8,128)S(1)}, f32[2,160,640]{2,1,0:T(8,128)}, u32[]{:S(2)}) copy-start(f32[2,160,640]{2,1,0:T(8,128)} %down_ref.7) | copy-start | bytes 2457604
  20.4 29.3 %copy-start.1 = (f32[2,112,640]{2,1,0:T(8,128)S(1)}, f32[2,112,640]{2,1,0:T(8,128)}, u32[]{:S(2)}) copy-start(f32[2,112,640]{2,1,0:T(8,128)} %proj_ref.7) | copy-start | bytes 1720324
  20.4 29.2 %copy-start.6 = (f32[2,640]{1,0:T(2,128)S(1)}, f32[2,640]{1,0:T(2,128)}, u32[]{:S(2)}) copy-start(f32[2,640]{1,0:T(2,128)} %upb_ref.3) | copy-start | bytes 15364
  20.4 29.2 %copy-start.9 = (f32[2,160]{1,0:T(2,128)S(1)}, f32[2,160]{1,0:T(2,128)}, u32[]{:S(2)}) copy-start(f32[2,160]{1,0:T(2,128)} %downb_ref.3) | copy-start | bytes 3844
  49.7 12.0 %copy-start.16 = (f32[2,112]{1,0:T(2,128)S(1)}, f32[2,112]{1,0:T(2,128)}, u32[]{:S(2)}) copy-start(f32[2,112]{1,0:T(2,128)} %param.25) | copy-start | bytes 2692
  49.7 12.0 %copy-start.17 = (f32[2,112]{1,0:T(2,128)S(1)}, f32[2,112]{1,0:T(2,128)}, u32[]{:S(2)}) copy-start(f32[2,112]{1,0:T(2,128)} %param.26) | copy-start | bytes 2692
  49.7 19.2 %copy-start.14 = (f32[136,128]{1,0:T(8,128)S(1)}, f32[136,128]{1,0:T(8,128)}, u32[]{:S(2)}) copy-start(f32[136,128]{1,0:T(8,128)} %get-tuple-element.122.gram0_ref) | copy-start | bytes 208900
  59.1 9.8 %all-to-all-start.2 = ((f32[32,2,128]{2,1,0:T(2,128)}), f32[32,2,128]{2,1,0:T(2,128)S(1)}, u32[]{:S(2)}, u32[]{:S(2)}) async-start(f32[32,2,128]{2,1,0:T(2,128)} %get-tuple-element.121), calls=%async_computation.2 | async-start | bytes 65536 | tf_op jit(solution)/shard_map/all_to_all | solution.py:1166
  83.8 13.0 %all-to-all-start.4 = ((f32[32,2,8,128]{3,2,1,0:T(8,128)}), f32[32,2,8,128]{3,2,1,0:T(8,128)S(1)}, u32[]{:S(2)}, u32[]{:S(2)}) async-start(f32[32,2,8,128]{3,2,1,0:T(8,128)} %bitcast.3), calls=%async_computation.4 | async-start | bytes 524288 | tf_op jit(solution)/shard_map/all_to_all | solution.py:1188
  124.5 13.0 %all-to-all-start.7 = ((f32[32,2,8,128]{3,2,1,0:T(8,128)}), f32[32,2,8,128]{3,2,1,0:T(8,128)S(1)}, u32[]{:S(2)}, u32[]{:S(2)}) async-start(f32[32,2,8,128]{3,2,1,0:T(8,128)} %broadcast_in_dim.10), calls=%async_computation.7 | async-start | bytes 524288 | tf_op jit(solution)/shard_map/all_to_all | solution.py:1193
  137.5 3.3 %collective-permute-start = (f32[144,8,128]{2,1,0:T(8,128)}, f32[144,8,128]{2,1,0:T(8,128)S(1)}, u32[]{:S(2)}, u32[]{:S(2)}) collective-permute-start(f32[144,8,128]{2,1,0:T(8,128)} %get-tuple-element.151), channel_id=1, source_target_pairs={{0,1},{1,0},{2,3},{3,2},{4,5},{5,4},{6,7},{7,6},{8,9},{9,8},{10,11... | collective-permute-start | bytes 1769480 | tf_op jit(solution)/shard_map/ppermute | solution.py:1174
  137.9 11.4 %all-to-all-start.8 = ((f32[32,2,640]{2,1,0:T(2,128)}), f32[32,2,640]{2,1,0:T(2,128)S(1)}, u32[]{:S(2)}, u32[]{:S(2)}) async-start(f32[32,2,640]{2,1,0:T(2,128)} %get-tuple-element.149), calls=%async_computation.8 | async-start | bytes 327680 | tf_op jit(solution)/shard_map/all_to_all | solution.py:1166
  149.2 22.1 %all-to-all-start.9 = ((f32[16,9,8,128]{3,2,1,0:T(8,128)}), f32[16,9,8,128]{3,2,1,0:T(8,128)S(1)}, u32[]{:S(2)}, u32[]{:S(2)}) async-start(f32[16,9,8,128]{3,2,1,0:T(8,128)} %bitcast.5), calls=%async_computation.9 | async-start | bytes 1179648 | tf_op jit(solution)/shard_map/all_to_all | solution.py:1188
  183.7 22.6 %all-to-all-start.11 = ((f32[16,9,8,128]{3,2,1,0:T(8,128)}), f32[16,9,8,128]{3,2,1,0:T(8,128)S(1)}, u32[]{:S(2)}, u32[]{:S(2)}) async-start(f32[16,9,8,128]{3,2,1,0:T(8,128)} %broadcast_in_dim.11), calls=%async_computation.11 | async-start | bytes 1179648 | tf_op jit(solution)/shard_map/all_to_all | solution.py:1193
  205.6 6.5 %collective-permute-start.1 = (f32[192,8,128]{2,1,0:T(8,128)}, f32[192,8,128]{2,1,0:T(8,128)S(1)}, u32[]{:S(2)}, u32[]{:S(2)}) collective-permute-start(f32[192,8,128]{2,1,0:T(8,128)} %get-tuple-element.172), channel_id=1, source_target_pairs={{0,1},{1,0},{2,3},{3,2},{4,5},{5,4},{6,7},{7,6},{8,9},{9,8},{10,11... | collective-permute-start | bytes 2359304 | tf_op jit(solution)/shard_map/ppermute | solution.py:1174
  206.3 14.2 %collective-permute-start.2 = (f32[144,8,128]{2,1,0:T(8,128)S(1)}, f32[144,8,128]{2,1,0:T(8,128)}, u32[]{:S(2)}, u32[]{:S(2)}) collective-permute-start(f32[144,8,128]{2,1,0:T(8,128)S(1)} %bitcast.25), channel_id=1, source_target_pairs={{0,1},{1,0},{2,3},{3,2},{4,5},{5,4},{6,7},{7,6},{8,9},{9,8},{10,11... | collective-permute-start | bytes 1769480 | tf_op jit(solution)/shard_map/ppermute | solution.py:1174
  206.4 14.1 %all-to-all-start.12 = ((f32[32,2,640]{2,1,0:T(2,128)}), f32[32,2,640]{2,1,0:T(2,128)S(1)}, u32[]{:S(2)}, u32[]{:S(2)}) async-start(f32[32,2,640]{2,1,0:T(2,128)} %get-tuple-element.170), calls=%async_computation.12 | async-start | bytes 327680 | tf_op jit(solution)/shard_map/all_to_all | solution.py:1166
  220.5 32.9 %all-to-all-start.13 = ((f32[16,12,8,128]{3,2,1,0:T(8,128)}), f32[16,12,8,128]{3,2,1,0:T(8,128)}, u32[]{:S(2)}, u32[]{:S(2)}) async-start(f32[16,12,8,128]{3,2,1,0:T(8,128)} %bitcast.7), calls=%async_computation.13 | async-start | bytes 1572864 | tf_op jit(solution)/shard_map/all_to_all | solution.py:1188
  246.7 7.9 %collective-permute-start.3 = (f32[64,8,128]{2,1,0:T(8,128)S(1)}, f32[64,8,128]{2,1,0:T(8,128)S(1)}, u32[]{:S(2)}, u32[]{:S(2)}) collective-permute-start(f32[64,8,128]{2,1,0:T(8,128)S(1)} %dynamic-slice_bitcast_fusion), channel_id=1, source_target_pairs={{0,1},{1,0},{2,3},{3,2},{4,5},{5,4},{6,7},{7,6},{8,9},{9,8},{10,11... | collective-permute-start | bytes 786440 | tf_op jit(solution)/shard_map/ppermute | solution.py:1174
  253.4 2.4 collective-permute-start.4
  291.4 6.3 %copy-start.7 = (f32[4,640]{1,0:T(4,128)S(1)}, f32[4,640]{1,0:T(4,128)}, u32[]{:S(2)}) copy-start(f32[4,640]{1,0:T(4,128)} %means_ref.1) | copy-start | bytes 30724
  291.4 6.3 %copy-start.8 = (f32[4,640]{1,0:T(4,128)S(1)}, f32[4,640]{1,0:T(4,128)}, u32[]{:S(2)}) copy-start(f32[4,640]{1,0:T(4,128)} %vars_ref.1) | copy-start | bytes 30724
  291.4 6.3 %copy-start.10 = (f32[2,112]{1,0:T(2,128)S(1)}, f32[2,112]{1,0:T(2,128)}, u32[]{:S(2)}) copy-start(f32[2,112]{1,0:T(2,128)} %nmeans_ref.1) | copy-start | bytes 2692
  291.4 6.3 %copy-start.11 = (f32[2,112]{1,0:T(2,128)S(1)}, f32[2,112]{1,0:T(2,128)}, u32[]{:S(2)}) copy-start(f32[2,112]{1,0:T(2,128)} %nvars_ref.1) | copy-start | bytes 2692
  291.4 13.0 %collective-permute-start.5 = (f32[16,18,8,128]{3,2,1,0:T(8,128)}, f32[16,18,8,128]{3,2,1,0:T(8,128)}, u32[]{:S(2)}, u32[]{:S(2)}) collective-permute-start(f32[16,18,8,128]{3,2,1,0:T(8,128)} %all_to_all.85.pack0_ref), channel_id=1, source_target_pairs={{0,1},{1,0},{2,3},{3,2},{4,5},{5,4},{6,7},{7,6},{8,9},{9,8},{10,11... | collective-permute-start | bytes 3538952 | tf_op jit(solution)/shard_map/ppermute | solution.py:1174
  293.2 15.0 %all-to-all-start.15 = ((f32[16,4,8,128]{3,2,1,0:T(8,128)}), f32[16,4,8,128]{3,2,1,0:T(8,128)S(1)}, u32[]{:S(2)}, u32[]{:S(2)}) async-start(f32[16,4,8,128]{3,2,1,0:T(8,128)} %broadcast_in_dim.14), calls=%async_computation.15 | async-start | bytes 524288 | tf_op jit(solution)/shard_map/all_to_all | solution.py:1473
  308.2 1.5 collective-permute-start.6
